TPU v7x, 32 devices: a whole 2x2x4 slice. The times are simulated.
32 devices in a mesh: row: 8 (over z, y), col: 4 (over x, core).
Axes of the slice: x: 2, y: 2, z: 4, core: 2. Of those that a mesh axis runs over, the one named last changes fastest.
Arguments:
- tokens: bfloat16 [16384, 1024], P(('row', 'col')), may hold values from -6 to 6
- cotangent: bfloat16 [16384, 1024], P(('row', 'col')), may hold values from -6 to 6
- dest_slot: int32 [16384], replicated, may hold values from 0 to 16383, as said below
- lengths: int32 [32, 4], P(('row', 'col')), may hold values from 1 to 256, 512 in all within a row
- pad_mask: int32 [16384], P(('row', 'col')), may hold values 0 or 1
- based_gain: float32 [1024], replicated, may hold values from 0.1 to 1.9
- based_query: bfloat16 [1024, 256], P('row', 'col'), may hold values from -0.1875 to 0.1875
- based_key: bfloat16 [1024, 256], P('row', 'col'), may hold values from -0.1875 to 0.1875
- based_value: bfloat16 [1024, 1024], P('row', 'col'), may hold values from -0.1875 to 0.1875
- based_output: bfloat16 [1024, 1024], P('row', 'col'), may hold values from -1.5 to 1.5
- mlp_gain_one: float32 [1024], replicated, may hold values from 0.1 to 1.9
- mlp_gate_one: bfloat16 [1024, 2752], P('row', 'col'), may hold values from -0.1875 to 0.1875
- mlp_up_one: bfloat16 [1024, 2752], P('row', 'col'), may hold values from -0.1875 to 0.1875
- mlp_down_one: bfloat16 [2752, 1024], P('row', 'col'), may hold values from -0.109375 to 0.109375
- window_gain: float32 [1024], replicated, may hold values from 0.1 to 1.9
- window_query: bfloat16 [1024, 1024], P('row', 'col'), may hold values from -0.1875 to 0.1875
- window_key: bfloat16 [1024, 1024], P('row', 'col'), may hold values from -0.1875 to 0.1875
- window_value: bfloat16 [1024, 1024], P('row', 'col'), may hold values from -0.1875 to 0.1875
- window_output: bfloat16 [1024, 1024], P('row', 'col'), may hold values from -1 to 1
- mlp_gain_two: float32 [1024], replicated, may hold values from 0.1 to 1.9
- mlp_gate_two: bfloat16 [1024, 2752], P('row', 'col'), may hold values from -0.1875 to 0.1875
- mlp_up_two: bfloat16 [1024, 2752], P('row', 'col'), may hold values from -0.1875 to 0.1875
- mlp_down_two: bfloat16 [2752, 1024], P('row', 'col'), may hold values from -0.109375 to 0.109375
Outputs:
- output: bfloat16 [16384, 1024], P(('row', 'col'))
- tokens_grad: bfloat16 [16384, 1024], P(('row', 'col'))
- grad_based_gain: float32 [1024], replicated
- grad_based_query: float32 [1024, 256], P('row', 'col')
- grad_based_key: float32 [1024, 256], P('row', 'col')
- grad_based_value: float32 [1024, 1024], P('row', 'col')
- grad_based_output: float32 [1024, 1024], P('row', 'col')
- grad_mlp_gain_one: float32 [1024], replicated
- grad_mlp_gate_one: float32 [1024, 2752], P('row', 'col')
- grad_mlp_up_one: float32 [1024, 2752], P('row', 'col')
- grad_mlp_down_one: float32 [2752, 1024], P('row', 'col')
- grad_window_gain: float32 [1024], replicated
- grad_window_query: float32 [1024, 1024], P('row', 'col')
- grad_window_key: float32 [1024, 1024], P('row', 'col')
- grad_window_value: float32 [1024, 1024], P('row', 'col')
- grad_window_output: float32 [1024, 1024], P('row', 'col')
- grad_mlp_gain_two: float32 [1024], replicated
- grad_mlp_gate_two: float32 [1024, 2752], P('row', 'col')
- grad_mlp_up_two: float32 [1024, 2752], P('row', 'col')
- grad_mlp_down_two: float32 [2752, 1024], P('row', 'col')
Inputs may be any that keep to these rules, and one draw needn't show every extreme that they name: dest_slot is a permutation. Blocks of 512 rows are numbered in order; block b sends its tokens only to blocks b2 with b2 % 4 == b % 4, exactly 64 to each such block, itself included. `lengths`: row b lists the sequences of packed block b in order; each row sums to 512.
All inputs are finite; a program needn't handle non-finite values. No bound on the sum of `pad_mask` on one device may be relied on, other than what follows from the above.
Results may differ from a plain program's by a relative error of at most 0.025.
Values may be sent and summed in bfloat16 or wider, within the bound.
No kernel may reach another device: no remote copies, remote signals or barrier semaphores. Data moves between devices by JAX's collectives and lax.ppermute only.
A program may use at most 256 MiB of HBM per device.

v0:
```python
import jax
import jax.numpy as jnp
from jax import lax
from jax.sharding import PartitionSpec as P

HEADS = 16
FEAT = 16
HEAD_DIM = 64
WINDOW = 64
MAX_LEN = 256
QUERY_BLOCK_SIZE = 512


EPS = 1e-05


def rms_apply(residual, gain_vector):
    factor = lax.rsqrt(jnp.mean(residual * residual, axis=-1, keepdims=True) + EPS)
    return residual * factor * gain_vector


def rms_grad(residual, gain_vector, d_normed):
    _, pullback = jax.vjp(rms_apply, residual, gain_vector)
    return pullback(d_normed)


def swiglu(gate_pre, upward):
    return jax.nn.silu(gate_pre) * upward


def project(left_side, right_side):
    return jnp.dot(left_side, right_side, preferred_element_type=jnp.float32)


def project_back(gradient, right_side):
    return jnp.einsum("tc,rc->tr", gradient, right_side, preferred_element_type=jnp.float32)


def outer_sum(left_side, gradient):
    return jnp.einsum("tr,tc->rc", left_side, gradient, preferred_element_type=jnp.float32)


def pad_front(source, key_extent, fill_value):
    front_fill = jnp.full((key_extent,) + source.shape[1:], fill_value, source.dtype)
    return jnp.concatenate([front_fill, source], axis=0)


def key_rules(segment_pad, live_pad, block_first_row, key_extent, window_span):
    query_pos = block_first_row + jnp.arange(QUERY_BLOCK_SIZE, dtype=jnp.int32)
    key_pos = (
        block_first_row - key_extent + jnp.arange(key_extent + QUERY_BLOCK_SIZE, dtype=jnp.int32)
    )
    query_seg = segment_pad[
        block_first_row + key_extent : block_first_row + key_extent + QUERY_BLOCK_SIZE
    ]
    earlier = (key_pos[None, :] <= query_pos[:, None]) & (
        key_pos[None, :] > query_pos[:, None] - window_span
    )
    same_seq = query_seg[:, None] == segment_pad[None, :]
    usable = (live_pad[None, :] > 0) | (key_pos[None, :] == query_pos[:, None])
    return earlier & same_seq & usable


def based_forward(query_rows, keys_in, values_in, segment, live_keys):
    key_extent = MAX_LEN
    logit_scale = FEAT ** (-0.5)
    padded_keys = pad_front(keys_in, key_extent, 0.0)
    values_pad = pad_front(values_in, key_extent, 0.0)
    segment_pad = pad_front(segment, key_extent, -1)
    live_pad = pad_front(live_keys, key_extent, 0)
    allowed = key_rules(segment_pad, live_pad, 0, key_extent, key_extent).astype(jnp.float32)
    score_matrix = (
        jnp.einsum("nvx,ivx->vni", query_rows, padded_keys, preferred_element_type=jnp.float32)
        * logit_scale
    )
    weights = (1.0 + score_matrix + 0.5 * score_matrix * score_matrix) * allowed[None]
    totals = jnp.sum(weights, axis=-1)
    numerator = jnp.einsum(
        "hqk,khe->qhe", weights.astype(jnp.bfloat16), values_pad, preferred_element_type=jnp.float32
    )
    pieces = numerator / jnp.transpose(totals)[:, :, None]
    return (pieces, totals)


def based_backward(
    query_rows, keys_in, values_in, segment, live_keys, attended, totals, d_attended
):
    key_extent = MAX_LEN
    logit_scale = FEAT ** (-0.5)
    padded_keys = pad_front(keys_in, key_extent, 0.0)
    values_pad = pad_front(values_in, key_extent, 0.0)
    segment_pad = pad_front(segment, key_extent, -1)
    live_pad = pad_front(live_keys, key_extent, 0)
    spread = jnp.transpose(totals)
    d_numer = (d_attended / spread[:, :, None]).astype(jnp.bfloat16)
    d_total = -jnp.sum(d_attended * attended, axis=-1) / spread
    d_keys = jnp.zeros(padded_keys.shape, jnp.float32)
    d_values = jnp.zeros(values_pad.shape, jnp.float32)
    key_stop = key_extent + QUERY_BLOCK_SIZE
    allowed = key_rules(segment_pad, live_pad, 0, key_extent, key_extent).astype(jnp.float32)
    score_matrix = (
        jnp.einsum("nvx,ivx->vni", query_rows, padded_keys, preferred_element_type=jnp.float32)
        * logit_scale
    )
    weights = (1.0 + score_matrix + 0.5 * score_matrix * score_matrix) * allowed[None]
    d_weights = (
        jnp.einsum("qhe,khe->hqk", d_numer, values_pad, preferred_element_type=jnp.float32)
        + jnp.transpose(d_total)[:, :, None]
    )
    scores_gradient = (d_weights * allowed[None] * (1.0 + score_matrix)).astype(jnp.bfloat16)
    d_queries = (
        jnp.einsum("pdt,tpn->dpn", scores_gradient, padded_keys, preferred_element_type=jnp.float32)
        * logit_scale
    )
    d_keys = d_keys.at[0:key_stop].add(
        jnp.einsum("sje,jsn->esn", scores_gradient, query_rows, preferred_element_type=jnp.float32)
        * logit_scale
    )
    d_values = d_values.at[0:key_stop].add(
        jnp.einsum(
            "hqk,qhe->khe",
            weights.astype(jnp.bfloat16),
            d_numer,
            preferred_element_type=jnp.float32,
        )
    )
    return (d_queries, d_keys[key_extent:], d_values[key_extent:])


def window_forward(query_rows, keys_in, values_in, segment, live_keys):
    key_extent = WINDOW
    logit_scale = HEAD_DIM ** (-0.5)
    padded_keys = pad_front(keys_in, key_extent, 0.0)
    values_pad = pad_front(values_in, key_extent, 0.0)
    segment_pad = pad_front(segment, key_extent, -1)
    live_pad = pad_front(live_keys, key_extent, 0)
    allowed = key_rules(segment_pad, live_pad, 0, key_extent, key_extent)
    score_matrix = (
        jnp.einsum("nvx,ivx->vni", query_rows, padded_keys, preferred_element_type=jnp.float32)
        * logit_scale
    )
    masked = jnp.where(allowed[None], score_matrix, -1e30)
    peak_score = jnp.max(masked, axis=-1, keepdims=True)
    exponent = jnp.exp(masked - peak_score)
    row_total = jnp.sum(exponent, axis=-1, keepdims=True)
    weights = exponent / row_total
    pieces = jnp.einsum(
        "hqk,khe->qhe", weights.astype(jnp.bfloat16), values_pad, preferred_element_type=jnp.float32
    )
    logsums = (peak_score + jnp.log(row_total))[:, :, 0]
    return (pieces, logsums)


def window_backward(query_rows, keys_in, values_in, segment, live_keys, logsums, d_attended):
    key_extent = WINDOW
    logit_scale = HEAD_DIM ** (-0.5)
    padded_keys = pad_front(keys_in, key_extent, 0.0)
    values_pad = pad_front(values_in, key_extent, 0.0)
    segment_pad = pad_front(segment, key_extent, -1)
    live_pad = pad_front(live_keys, key_extent, 0)
    d_keys = jnp.zeros(padded_keys.shape, jnp.float32)
    d_values = jnp.zeros(values_pad.shape, jnp.float32)
    key_stop = key_extent + QUERY_BLOCK_SIZE
    allowed = key_rules(segment_pad, live_pad, 0, key_extent, key_extent)
    score_matrix = (
        jnp.einsum("nvx,ivx->vni", query_rows, padded_keys, preferred_element_type=jnp.float32)
        * logit_scale
    )
    weights = jnp.exp(
        jnp.where(allowed[None], score_matrix, -1e30) - logsums[:, 0:QUERY_BLOCK_SIZE, None]
    )
    d_values = d_values.at[0:key_stop].add(
        jnp.einsum(
            "hqk,qhe->khe",
            weights.astype(jnp.bfloat16),
            d_attended,
            preferred_element_type=jnp.float32,
        )
    )
    d_weights = jnp.einsum(
        "qhe,khe->hqk", d_attended, values_pad, preferred_element_type=jnp.float32
    )
    row_dot = jnp.sum(weights * d_weights, axis=-1, keepdims=True)
    scores_gradient = (weights * (d_weights - row_dot)).astype(jnp.bfloat16)
    d_queries = (
        jnp.einsum("pdt,tpn->dpn", scores_gradient, padded_keys, preferred_element_type=jnp.float32)
        * logit_scale
    )
    d_keys = d_keys.at[0:key_stop].add(
        jnp.einsum("sje,jsn->esn", scores_gradient, query_rows, preferred_element_type=jnp.float32)
        * logit_scale
    )
    return (d_queries, d_keys[key_extent:], d_values[key_extent:])


def fetch_layer(shards):
    wide_parts = (
        lax.all_gather(shards[0], "col", axis=1, tiled=True),
        lax.all_gather(shards[1], "col", axis=1, tiled=True),
        lax.all_gather(shards[2], "col", axis=1, tiled=True),
        lax.all_gather(shards[3], "col", axis=1, tiled=True),
        lax.all_gather(shards[4], "col", axis=1, tiled=True),
        lax.all_gather(shards[5], "col", axis=1, tiled=True),
        lax.all_gather(shards[6], "col", axis=1, tiled=True),
    )
    gathered = (
        lax.all_gather(wide_parts[0], "row", axis=0, tiled=True),
        lax.all_gather(wide_parts[1], "row", axis=0, tiled=True),
        lax.all_gather(wide_parts[2], "row", axis=0, tiled=True),
        lax.all_gather(wide_parts[3], "row", axis=0, tiled=True),
        lax.all_gather(wide_parts[4], "row", axis=0, tiled=True),
        lax.all_gather(wide_parts[5], "row", axis=0, tiled=True),
        lax.all_gather(wide_parts[6], "row", axis=0, tiled=True),
    )
    return gathered


def reduce_layer(grads):
    partial_sums = (
        lax.psum_scatter(
            grads[0].astype(jnp.bfloat16), "row", scatter_dimension=0, tiled=True
        ).astype(jnp.float32),
        lax.psum_scatter(
            grads[1].astype(jnp.bfloat16), "row", scatter_dimension=0, tiled=True
        ).astype(jnp.float32),
        lax.psum_scatter(
            grads[2].astype(jnp.bfloat16), "row", scatter_dimension=0, tiled=True
        ).astype(jnp.float32),
        lax.psum_scatter(
            grads[3].astype(jnp.bfloat16), "row", scatter_dimension=0, tiled=True
        ).astype(jnp.float32),
        lax.psum_scatter(
            grads[4].astype(jnp.bfloat16), "row", scatter_dimension=0, tiled=True
        ).astype(jnp.float32),
        lax.psum_scatter(
            grads[5].astype(jnp.bfloat16), "row", scatter_dimension=0, tiled=True
        ).astype(jnp.float32),
        lax.psum_scatter(
            grads[6].astype(jnp.bfloat16), "row", scatter_dimension=0, tiled=True
        ).astype(jnp.float32),
    )
    summed = (
        lax.psum_scatter(
            partial_sums[0].astype(jnp.bfloat16), "col", scatter_dimension=1, tiled=True
        ).astype(jnp.float32),
        lax.psum_scatter(
            partial_sums[1].astype(jnp.bfloat16), "col", scatter_dimension=1, tiled=True
        ).astype(jnp.float32),
        lax.psum_scatter(
            partial_sums[2].astype(jnp.bfloat16), "col", scatter_dimension=1, tiled=True
        ).astype(jnp.float32),
        lax.psum_scatter(
            partial_sums[3].astype(jnp.bfloat16), "col", scatter_dimension=1, tiled=True
        ).astype(jnp.float32),
        lax.psum_scatter(
            partial_sums[4].astype(jnp.bfloat16), "col", scatter_dimension=1, tiled=True
        ).astype(jnp.float32),
        lax.psum_scatter(
            partial_sums[5].astype(jnp.bfloat16), "col", scatter_dimension=1, tiled=True
        ).astype(jnp.float32),
        lax.psum_scatter(
            partial_sums[6].astype(jnp.bfloat16), "col", scatter_dimension=1, tiled=True
        ).astype(jnp.float32),
    )
    return summed


def layer_forward(residual, gain_att, gain_mlp, gathered, segment, live_keys, mixer_kind):
    w_query, w_key, w_value, w_out, w_gate, w_up, w_down = gathered
    tokens_here = residual.shape[0]
    normed = rms_apply(residual, gain_att).astype(jnp.bfloat16)
    query_rows = project(normed, w_query).astype(jnp.bfloat16)
    keys_in = project(normed, w_key).astype(jnp.bfloat16)
    values_in = project(normed, w_value).astype(jnp.bfloat16)
    feature_width = query_rows.shape[1] // HEADS
    query_heads = query_rows.reshape(tokens_here, HEADS, feature_width)
    key_heads = keys_in.reshape(tokens_here, HEADS, feature_width)
    value_heads = values_in.reshape(tokens_here, HEADS, HEAD_DIM)
    if mixer_kind == "based":
        attended, block_stats = based_forward(
            query_heads, key_heads, value_heads, segment, live_keys
        )
    else:
        attended, block_stats = window_forward(
            query_heads, key_heads, value_heads, segment, live_keys
        )
    mixed_out = attended.reshape(tokens_here, -1).astype(jnp.bfloat16)
    resid_mid = residual + project(mixed_out, w_out)
    normed_mlp = rms_apply(resid_mid, gain_mlp).astype(jnp.bfloat16)
    gate_pre = project(normed_mlp, w_gate)
    upward = project(normed_mlp, w_up)
    hidden = swiglu(gate_pre, upward).astype(jnp.bfloat16)
    resid_out = resid_mid + project(hidden, w_down)
    kept_state = (
        residual,
        normed,
        query_heads,
        key_heads,
        value_heads,
        attended,
        block_stats,
        mixed_out,
        resid_mid,
        normed_mlp,
        gate_pre,
        upward,
        hidden,
    )
    return (resid_out, kept_state)


def layer_backward(
    d_resid, kept_state, gathered, gain_att, gain_mlp, segment, live_keys, mixer_kind
):
    (
        residual,
        normed,
        query_heads,
        key_heads,
        value_heads,
        attended,
        block_stats,
        mixed_out,
        resid_mid,
        normed_mlp,
        gate_pre,
        upward,
        hidden,
    ) = kept_state
    w_query, w_key, w_value, w_out, w_gate, w_up, w_down = gathered
    tokens_here = residual.shape[0]
    d_branch = d_resid.astype(jnp.bfloat16)
    grad_down = outer_sum(hidden, d_branch)
    d_hidden = project_back(d_branch, w_down)
    _, pullback = jax.vjp(swiglu, gate_pre, upward)
    d_gate, d_upward = pullback(d_hidden)
    d_gate = d_gate.astype(jnp.bfloat16)
    d_upward = d_upward.astype(jnp.bfloat16)
    grad_gate = outer_sum(normed_mlp, d_gate)
    grad_up = outer_sum(normed_mlp, d_upward)
    d_normed = project_back(d_gate, w_gate) + project_back(d_upward, w_up)
    d_mid, grad_gain_mlp = rms_grad(resid_mid, gain_mlp, d_normed)
    d_resid = d_resid + d_mid
    d_branch = d_resid.astype(jnp.bfloat16)
    grad_out = outer_sum(mixed_out, d_branch)
    d_mixed = project_back(d_branch, w_out).reshape(attended.shape)
    if mixer_kind == "based":
        d_queries, d_keys, d_values = based_backward(
            query_heads, key_heads, value_heads, segment, live_keys, attended, block_stats, d_mixed
        )
    else:
        d_queries, d_keys, d_values = window_backward(
            query_heads,
            key_heads,
            value_heads,
            segment,
            live_keys,
            block_stats,
            d_mixed.astype(jnp.bfloat16),
        )
    d_queries = d_queries.reshape(tokens_here, -1).astype(jnp.bfloat16)
    d_keys = d_keys.reshape(tokens_here, -1).astype(jnp.bfloat16)
    d_values = d_values.reshape(tokens_here, -1).astype(jnp.bfloat16)
    grad_query = outer_sum(normed, d_queries)
    grad_key = outer_sum(normed, d_keys)
    grad_value = outer_sum(normed, d_values)
    d_normed = (
        project_back(d_queries, w_query)
        + project_back(d_keys, w_key)
        + project_back(d_values, w_value)
    )
    d_first, grad_gain_att = rms_grad(residual, gain_att, d_normed)
    return (
        d_resid + d_first,
        (grad_query, grad_key, grad_value, grad_out, grad_gate, grad_up, grad_down),
        (grad_gain_att, grad_gain_mlp),
    )


def route_plan(dest_slot, block_tokens):
    row_count = lax.axis_size("row")
    col_count = lax.axis_size("col")
    per_peer = block_tokens // row_count
    row_at = lax.axis_index("row")
    col_at = lax.axis_index("col")
    slot_table = dest_slot.reshape(row_count, col_count, block_tokens)
    column = lax.dynamic_index_in_dim(slot_table, col_at, 1, False)
    own_slots = lax.dynamic_index_in_dim(column, row_at, 0, False)
    send_order = jnp.argsort(own_slots)
    arrived = jnp.sort(column, axis=1)
    incoming = lax.dynamic_slice_in_dim(arrived, row_at * per_peer, per_peer, 1)
    local_slots = incoming.reshape(-1) - (row_at * col_count + col_at) * block_tokens
    placing = jnp.argsort(local_slots)
    return (send_order, local_slots, placing)


def body(
    tokens,
    cotangent,
    dest_slot,
    lengths,
    pad_mask,
    based_gain,
    based_query,
    based_key,
    based_value,
    based_output,
    mlp_gain_one,
    mlp_gate_one,
    mlp_up_one,
    mlp_down_one,
    window_gain,
    window_query,
    window_key,
    window_value,
    window_output,
    mlp_gain_two,
    mlp_gate_two,
    mlp_up_two,
    mlp_down_two,
):
    block_tokens = tokens.shape[0]
    model_width = tokens.shape[1]
    row_count = lax.axis_size("row")
    per_peer = block_tokens // row_count
    send_order, local_slots, placing = route_plan(dest_slot, block_tokens)
    arrived_pair = (
        lax.all_to_all(
            tokens[send_order].reshape(row_count, per_peer, model_width),
            "row",
            split_axis=0,
            concat_axis=0,
            tiled=True,
        ),
        lax.all_to_all(
            cotangent[send_order].reshape(row_count, per_peer, model_width),
            "row",
            split_axis=0,
            concat_axis=0,
            tiled=True,
        ),
    )
    start_resid = arrived_pair[0].reshape(block_tokens, model_width)[placing].astype(jnp.float32)
    d_top = arrived_pair[1].reshape(block_tokens, model_width)[placing].astype(jnp.float32)
    sequence_ends = jnp.cumsum(lengths[0])
    positions = jnp.arange(block_tokens, dtype=jnp.int32)
    segment = jnp.sum((positions[:, None] >= sequence_ends[None, :]).astype(jnp.int32), axis=1)
    first_shards = (
        based_query,
        based_key,
        based_value,
        based_output,
        mlp_gate_one,
        mlp_up_one,
        mlp_down_one,
    )
    second_shards = (
        window_query,
        window_key,
        window_value,
        window_output,
        mlp_gate_two,
        mlp_up_two,
        mlp_down_two,
    )
    first_full = fetch_layer(first_shards)
    resid_one, state_one = layer_forward(
        start_resid, based_gain, mlp_gain_one, first_full, segment, pad_mask, "based"
    )
    second_full = fetch_layer(second_shards)
    resid_two, state_two = layer_forward(
        resid_one, window_gain, mlp_gain_two, second_full, segment, pad_mask, "window"
    )
    d_mid, grads_two, gains_two = layer_backward(
        d_top, state_two, second_full, window_gain, mlp_gain_two, segment, pad_mask, "window"
    )
    sums_two = reduce_layer(grads_two)
    d_start, grads_one, gains_one = layer_backward(
        d_mid, state_one, first_full, based_gain, mlp_gain_one, segment, pad_mask, "based"
    )
    sums_one = reduce_layer(grads_one)
    gain_totals = lax.psum((gains_one[0], gains_one[1], gains_two[0], gains_two[1]), ("row", "col"))
    result = resid_two.astype(jnp.bfloat16)
    d_tokens = d_start.astype(jnp.bfloat16)
    back_pair = (
        lax.all_to_all(
            result[local_slots].reshape(row_count, per_peer, model_width),
            "row",
            split_axis=0,
            concat_axis=0,
            tiled=True,
        ),
        lax.all_to_all(
            d_tokens[local_slots].reshape(row_count, per_peer, model_width),
            "row",
            split_axis=0,
            concat_axis=0,
            tiled=True,
        ),
    )
    restore = jnp.argsort(send_order)
    output = back_pair[0].reshape(block_tokens, model_width)[restore]
    tokens_grad = back_pair[1].reshape(block_tokens, model_width)[restore]
    return (
        output,
        tokens_grad,
        gain_totals[0],
        sums_one[0],
        sums_one[1],
        sums_one[2],
        sums_one[3],
        gain_totals[1],
        sums_one[4],
        sums_one[5],
        sums_one[6],
        gain_totals[2],
        sums_two[0],
        sums_two[1],
        sums_two[2],
        sums_two[3],
        gain_totals[3],
        sums_two[4],
        sums_two[5],
        sums_two[6],
    )


def solution(mesh):
    placed = (
        P(("row", "col"), None),
        P(("row", "col"), None),
        P(),
        P(("row", "col"), None),
        P(("row", "col")),
        P(),
        P("row", "col"),
        P("row", "col"),
        P("row", "col"),
        P("row", "col"),
        P(),
        P("row", "col"),
        P("row", "col"),
        P("row", "col"),
        P(),
        P("row", "col"),
        P("row", "col"),
        P("row", "col"),
        P("row", "col"),
        P(),
        P("row", "col"),
        P("row", "col"),
        P("row", "col"),
    )
    return jax.shard_map(
        body,
        mesh=mesh,
        in_specs=placed,
        out_specs=(
            P(("row", "col"), None),
            P(("row", "col"), None),
            P(),
            P("row", "col"),
            P("row", "col"),
            P("row", "col"),
            P("row", "col"),
            P(),
            P("row", "col"),
            P("row", "col"),
            P("row", "col"),
            P(),
            P("row", "col"),
            P("row", "col"),
            P("row", "col"),
            P("row", "col"),
            P(),
            P("row", "col"),
            P("row", "col"),
            P("row", "col"),
        ),
        check_vma=False,
    )
```

profile of v0, /device:TPU:0, one launch (start us, length us, event | category | flops | bytes accessed | tf_op | source)
XLA Modules:
  0.0 2646.7 jit_solution(8821391708634465165)
XLA Ops:
  149.3 60.5 %all_gather.89 = bf16[1024,256]{0,1:T(8,128)(2,1)S(1)} all-gather(bf16[128,256]{0,1:T(8,128)(2,1)S(1)} %all_gather.88), channel_id=1, replica_groups=mesh['row'=8,'col'=4] {'row'}, dimensions={0}, use_global_device_ids=true | all-gather | bytes 589824 | tf_op jit(solution)/shard_map/all_gather | solution.py:208
  209.8 34.6 %all_gather.87 = bf16[1024,256]{0,1:T(8,128)(2,1)S(1)} all-gather(bf16[128,256]{0,1:T(8,128)(2,1)S(1)} %all_gather.86), channel_id=1, replica_groups=mesh['row'=8,'col'=4] {'row'}, dimensions={0}, use_global_device_ids=true | all-gather | bytes 589824 | tf_op jit(solution)/shard_map/all_gather | solution.py:207
  303.6 43.0 %all-gather.19.cloned.1.call-done = bf16[1024,2752]{0,1:T(8,128)(2,1)} async-done(((bf16[128,2752]{0,1:T(8,128)(2,1)}), bf16[1024,2752]{0,1:T(8,128)(2,1)}) %all-gather.19.cloned.1.call-update) | async-done | bytes 5636112 | tf_op jit(solution)/shard_map/all_gather | solution.py:212
  356.1 81.7 %all-gather.21.cloned.1.call-done = bf16[2752,1024]{1,0:T(8,128)(2,1)} async-done(((bf16[344,1024]{1,0:T(8,128)(2,1)}), bf16[2752,1024]{1,0:T(8,128)(2,1)}) %all-gather.21.cloned.1.call-update) | async-done | bytes 5636112 | tf_op jit(solution)/shard_map/all_gather | solution.py:213
  445.6 41.8 %all-gather.27.cloned.1.call-done = bf16[1024,1024]{1,0:T(8,128)(2,1)} async-done(((bf16[128,1024]{1,0:T(8,128)(2,1)}), bf16[1024,1024]{1,0:T(8,128)(2,1)}) %all-gather.27.cloned.1.call-update) | async-done | bytes 2097168 | tf_op jit(solution)/shard_map/all_gather | solution.py:208
  492.7 44.4 %all-gather.25.cloned.1.call-done = bf16[1024,1024]{1,0:T(8,128)(2,1)} async-done(((bf16[128,1024]{1,0:T(8,128)(2,1)}), bf16[1024,1024]{1,0:T(8,128)(2,1)}) %all-gather.25.cloned.1.call-update) | async-done | bytes 2097168 | tf_op jit(solution)/shard_map/all_gather | solution.py:207
  543.5 43.3 %all-gather.23.cloned.1.call-done = bf16[1024,1024]{1,0:T(8,128)(2,1)} async-done(((bf16[128,1024]{1,0:T(8,128)(2,1)}), bf16[1024,1024]{1,0:T(8,128)(2,1)}) %all-gather.23.cloned.1.call-update) | async-done | bytes 2097168 | tf_op jit(solution)/shard_map/all_gather | solution.py:209
  643.1 85.7 %all-gather.33.cloned.1.call-done = bf16[1024,2752]{0,1:T(8,128)(2,1)} async-done(((bf16[128,2752]{0,1:T(8,128)(2,1)}), bf16[1024,2752]{0,1:T(8,128)(2,1)}) %all-gather.33.cloned.1.call-update) | async-done | bytes 5636112 | tf_op jit(solution)/shard_map/all_gather | solution.py:212
  737.3 83.2 %all-gather.31.cloned.1.call-done = bf16[1024,2752]{0,1:T(8,128)(2,1)} async-done(((bf16[128,2752]{0,1:T(8,128)(2,1)}), bf16[1024,2752]{0,1:T(8,128)(2,1)}) %all-gather.31.cloned.1.call-update) | async-done | bytes 5636112 | tf_op jit(solution)/shard_map/all_gather | solution.py:211
  829.0 82.7 %all-gather.35.cloned.1.call-done = bf16[2752,1024]{1,0:T(8,128)(2,1)} async-done(((bf16[344,1024]{1,0:T(8,128)(2,1)}), bf16[2752,1024]{1,0:T(8,128)(2,1)}) %all-gather.35.cloned.1.call-update) | async-done | bytes 5636112 | tf_op jit(solution)/shard_map/all_gather | solution.py:213
  1169.9 65.1 %reduce-scatter.73.cloned.1.call-done = bf16[128,1024]{1,0:T(8,128)(2,1)} async-done(((bf16[1024,1024]{1,0:T(8,128)(2,1)}), bf16[128,1024]{1,0:T(8,128)(2,1)}) %reduce-scatter.73.cloned.1.call-update) | async-done | bytes 262160 | tf_op jit(solution)/shard_map/reduce_scatter | solution.py:229
  1235.1 70.4 %reduce-scatter.69.cloned.1.call-done = bf16[128,1024]{1,0:T(8,128)(2,1)} async-done(((bf16[1024,1024]{1,0:T(8,128)(2,1)}), bf16[128,1024]{1,0:T(8,128)(2,1)}) %reduce-scatter.69.cloned.1.call-update) | async-done | bytes 262160 | tf_op jit(solution)/shard_map/reduce_scatter | solution.py:226
  1305.5 70.5 %reduce-scatter.49.cloned.1.call-done = bf16[128,1024]{1,0:T(8,128)(2,1)} async-done(((bf16[1024,1024]{1,0:T(8,128)(2,1)}), bf16[128,1024]{1,0:T(8,128)(2,1)}) %reduce-scatter.49.cloned.1.call-update) | async-done | bytes 262160 | tf_op jit(solution)/shard_map/reduce_scatter | solution.py:229
  1376.1 70.4 %reduce-scatter.65.cloned.1.call-done = bf16[128,1024]{1,0:T(8,128)(2,1)} async-done(((bf16[1024,1024]{1,0:T(8,128)(2,1)}), bf16[128,1024]{1,0:T(8,128)(2,1)}) %reduce-scatter.65.cloned.1.call-update) | async-done | bytes 262160 | tf_op jit(solution)/shard_map/reduce_scatter | solution.py:223
  1446.6 69.9 %reduce-scatter.61.cloned.1.call-done = bf16[128,1024]{1,0:T(8,128)(2,1)} async-done(((bf16[1024,1024]{1,0:T(8,128)(2,1)}), bf16[128,1024]{1,0:T(8,128)(2,1)}) %reduce-scatter.61.cloned.1.call-update) | async-done | bytes 262160 | tf_op jit(solution)/shard_map/reduce_scatter | solution.py:220
  1516.5 70.1 %reduce-scatter.45.cloned.1.call-done = bf16[128,1024]{1,0:T(8,128)(2,1)} async-done(((bf16[1024,1024]{1,0:T(8,128)(2,1)}), bf16[128,1024]{1,0:T(8,128)(2,1)}) %reduce-scatter.45.cloned.1.call-update) | async-done | bytes 262160 | tf_op jit(solution)/shard_map/reduce_scatter | solution.py:226
  1586.7 110.7 %reduce-scatter.81.cloned.1.call-done = bf16[344,1024]{1,0:T(8,128)(2,1)} async-done(((bf16[2752,1024]{1,0:T(8,128)(2,1)}), bf16[344,1024]{1,0:T(8,128)(2,1)}) %reduce-scatter.81.cloned.1.call-update) | async-done | bytes 704528 | tf_op jit(solution)/shard_map/reduce_scatter | solution.py:238
  1697.6 113.0 %reduce-scatter.95.cloned.1.call-done = bf16[128,2752]{1,0:T(8,128)(2,1)} async-done(((bf16[1024,2752]{1,0:T(8,128)(2,1)}), bf16[128,2752]{1,0:T(8,128)(2,1)}) %reduce-scatter.95.cloned.1.call-update) | async-done | bytes 704528
  1812.8 110.7 %reduce-scatter.93.cloned.1.call-done = bf16[128,2752]{1,0:T(8,128)(2,1)} async-done(((bf16[1024,2752]{1,0:T(8,128)(2,1)}), bf16[128,2752]{1,0:T(8,128)(2,1)}) %reduce-scatter.93.cloned.1.call-update) | async-done | bytes 704528
  1926.2 108.6 %reduce-scatter.57.cloned.1.call-done = bf16[344,1024]{1,0:T(8,128)(2,1)} async-done(((bf16[2752,1024]{1,0:T(8,128)(2,1)}), bf16[344,1024]{1,0:T(8,128)(2,1)}) %reduce-scatter.57.cloned.1.call-update) | async-done | bytes 704528 | tf_op jit(solution)/shard_map/reduce_scatter | solution.py:238
  2055.1 115.5 %reduce-scatter.91.cloned.1.call-done = bf16[128,2752]{1,0:T(8,128)(2,1)} async-done(((bf16[1024,2752]{1,0:T(8,128)(2,1)}), bf16[128,2752]{1,0:T(8,128)(2,1)}) %reduce-scatter.91.cloned.1.call-update) | async-done | bytes 704528
  2183.8 122.8 %reduce-scatter.89.cloned.1.call-done = bf16[128,2752]{1,0:T(8,128)(2,1)} async-done(((bf16[1024,2752]{1,0:T(8,128)(2,1)}), bf16[128,2752]{1,0:T(8,128)(2,1)}) %reduce-scatter.89.cloned.1.call-update) | async-done | bytes 704528
  2312.7 40.0 %all-reduce.8 = (f32[1024]{0:T(1024)}, f32[1024]{0:T(1024)}, f32[1024]{0:T(1024)}, f32[1024]{0:T(1024)}) all-reduce(f32[1024]{0:T(1024)S(1)} %get-tuple-element.192, f32[1024]{0:T(1024)S(1)} %get-tuple-element.190, f32[1024]{0:T(1024)S(1)} %copy-done.73, f32[1024]{0:T(1024)S(1)} %copy-done.72), channel_id=1, replica_groups=mesh['row'=8,'col'=4] {'row','col'}, use_global_device_ids=true, to_apply=%region_20.21 | all-reduce | flops 4096 | bytes 32768 | tf_op jit(solution)/shard_map/psum | solution.py:482
  2512.4 23.8 reduce-scatter.79.cloned.1.call-done
  (454 shorter events, 866.7 us)
Async XLA Ops:
  73.0 563.6 %all-gather.29.cloned.1.call-start = ((), (), s32[]{:S(2)}) async-start(), calls=%async_computation.40 | async-start | bytes 2359296 | tf_op jit(solution)/shard_map/all_gather | solution.py:210
  79.4 649.4 %all-gather.33.cloned.1.call-start = ((), (), s32[]{:S(2)}) async-start(), calls=%async_computation.42 | async-start | bytes 6340608 | tf_op jit(solution)/shard_map/all_gather | solution.py:212
  88.2 732.3 %all-gather.31.cloned.1.call-start = ((), (), s32[]{:S(2)}) async-start(), calls=%async_computation.41 | async-start | bytes 6340608 | tf_op jit(solution)/shard_map/all_gather | solution.py:211
  110.1 801.6 %all-gather.35.cloned.1.call-start = ((), (), s32[]{:S(2)}) async-start(), calls=%async_computation.43 | async-start | bytes 6340608 | tf_op jit(solution)/shard_map/all_gather | solution.py:213
  149.2 1017.4 %reduce-scatter.41.cloned.1.call-start = ((), (), s32[]{:S(2)}) async-start(), calls=%async_computation.44 | async-start | bytes 589824 | tf_op jit(solution)/shard_map/reduce_scatter | solution.py:220
  1087.8 609.7 %reduce-scatter.81.cloned.1.call-start = ((), (), s32[]{:S(2)}) async-start(), calls=%async_computation.64 | async-start | bytes 6340608 | tf_op jit(solution)/shard_map/reduce_scatter | solution.py:238
  1095.7 714.8 %reduce-scatter.95.cloned.1.call-start = ((), (), s32[]{:S(2)}) async-start(), calls=%async_computation.71 | async-start | bytes 6488064
  1111.9 811.6 %reduce-scatter.93.cloned.1.call-start = ((), (), s32[]{:S(2)}) async-start(), calls=%async_computation.70 | async-start | bytes 6488064
  1127.1 907.8 %reduce-scatter.57.cloned.1.call-start = ((), (), s32[]{:S(2)}) async-start(), calls=%async_computation.52 | async-start | bytes 6340608 | tf_op jit(solution)/shard_map/reduce_scatter | solution.py:238
  1135.1 1035.5 %reduce-scatter.91.cloned.1.call-start = ((), (), s32[]{:S(2)}) async-start(), calls=%async_computation.69 | async-start | bytes 6488064
  1151.4 1155.3 %reduce-scatter.89.cloned.1.call-start = ((), (), s32[]{:S(2)}) async-start(), calls=%async_computation.68 | async-start | bytes 6488064
  1166.5 1186.3 %reduce-scatter.85.cloned.1.call-start = ((), (), s32[]{:S(2)}) async-start(), calls=%async_computation.66 | async-start | bytes 81920
  1168.2 1186.1 %reduce-scatter.87.cloned.1.call-start = ((), (), s32[]{:S(2)}) async-start(), calls=%async_computation.67 | async-start | bytes 81920
  1169.9 1203.4 %reduce-scatter.75.cloned.1.call-start = ((), (), s32[]{:S(2)}) async-start(), calls=%async_computation.61 | async-start | bytes 327680 | tf_op jit(solution)/shard_map/reduce_scatter | solution.py:252
  1235.0 1160.8 %reduce-scatter.71.cloned.1.call-start = ((), (), s32[]{:S(2)}) async-start(), calls=%async_computation.59 | async-start | bytes 327680 | tf_op jit(solution)/shard_map/reduce_scatter | solution.py:249
  1305.5 1112.7 %reduce-scatter.51.cloned.1.call-start = ((), (), s32[]{:S(2)}) async-start(), calls=%async_computation.49 | async-start | bytes 327680 | tf_op jit(solution)/shard_map/reduce_scatter | solution.py:252
  1376.0 1064.6 %reduce-scatter.67.cloned.1.call-start = ((), (), s32[]{:S(2)}) async-start(), calls=%async_computation.57 | async-start | bytes 327680 | tf_op jit(solution)/shard_map/reduce_scatter | solution.py:246
  1446.5 1016.6 %reduce-scatter.63.cloned.1.call-start = ((), (), s32[]{:S(2)}) async-start(), calls=%async_computation.55 | async-start | bytes 327680 | tf_op jit(solution)/shard_map/reduce_scatter | solution.py:243
  1516.5 969.2 %reduce-scatter.47.cloned.1.call-start = ((), (), s32[]{:S(2)}) async-start(), calls=%async_computation.47 | async-start | bytes 327680 | tf_op jit(solution)/shard_map/reduce_scatter | solution.py:249
  1586.7 924.0 %reduce-scatter.83.cloned.1.call-start = ((), (), s32[]{:S(2)}) async-start(), calls=%async_computation.65 | async-start | bytes 880640 | tf_op jit(solution)/shard_map/reduce_scatter | solution.py:261
  1697.5 838.6 %reduce-scatter.79.cloned.1.call-start = ((), (), s32[]{:S(2)}) async-start(), calls=%async_computation.63 | async-start | bytes 880640 | tf_op jit(solution)/shard_map/reduce_scatter | solution.py:258
  1812.8 748.6 %reduce-scatter.77.cloned.1.call-start = ((), (), s32[]{:S(2)}) async-start(), calls=%async_computation.62 | async-start | bytes 880640 | tf_op jit(solution)/shard_map/reduce_scatter | solution.py:255
  1925.8 660.9 %reduce-scatter.59.cloned.1.call-start = ((), (), s32[]{:S(2)}) async-start(), calls=%async_computation.53 | async-start | bytes 880640 | tf_op jit(solution)/shard_map/reduce_scatter | solution.py:261
  2049.0 562.9 %reduce-scatter.55.cloned.1.call-start = ((), (), s32[]{:S(2)}) async-start(), calls=%async_computation.51 | async-start | bytes 880640 | tf_op jit(solution)/shard_map/reduce_scatter | solution.py:258
  (110 other events, 8193.2 us)
Sparse Core Ops, SparseCore 0:
  11.8 2.9 sort.60.cloned.1.call-done
  (1 shorter events, 0.0 us)
Sparse Core Ops, SparseCore 1:
  18.7 49.5 all-gather.12
  70.3 50.4 all-gather.14
  122.7 128.9 all-gather.16
  253.8 92.7 all-gather.18
  348.8 88.9 all-gather.20
  489.3 47.7 all-gather.24
  588.8 47.8 all-gather.28
  638.7 90.0 all-gather.32
  730.7 89.7 all-gather.30
  822.7 88.9 all-gather.34
  1039.3 60.2 reduce-scatter.40
  1103.2 61.0 reduce-scatter.42
  1167.8 67.1 reduce-scatter.72
  1238.6 66.9 reduce-scatter.68
  1309.0 66.9 reduce-scatter.48
  1379.6 66.9 reduce-scatter.64
  1449.9 66.5 reduce-scatter.60
  1520.0 66.6 reduce-scatter.44
  1590.2 107.3 reduce-scatter.80
  1701.0 109.5 reduce-scatter.94
  1814.0 109.4 reduce-scatter.92
  1927.2 107.6 reduce-scatter.56
  2038.3 132.2 reduce-scatter.90
  2174.3 132.3 reduce-scatter.88
  (16 shorter events, 388.7 us)
where the time goes:
time: 2660 us; the launch traced here: 2650 us
  waiting for transfers between devices  1890 us (71%)
  matrix products  316 us (12%)
  blocking collectives  240 us (9%)
  local copies, waits for them, and re-layouts  104 us (4%)
  other arithmetic  61 us (2%)
    unnamed x46, waiting for transfers between devices  463 us
    reduce_scatter x2, waiting for transfers between devices, reduce_layer(): lax.psum_scatter(grads[6].astype(jnp.bfloat16), 'row', scatter_dimension=...  219 us
    all_gather x2, waiting for transfers between devices, fetch_layer(): lax.all_gather(wide_parts[6], 'row', axis=0, tiled=True)  164 us
    reduce_scatter x2, waiting for transfers between devices, reduce_layer(): lax.psum_scatter(grads[2].astype(jnp.bfloat16), 'row', scatter_dimension=...  141 us
    reduce_scatter x2, waiting for transfers between devices, reduce_layer(): lax.psum_scatter(grads[3].astype(jnp.bfloat16), 'row', scatter_dimension=...  136 us
    all_gather x2, waiting for transfers between devices, fetch_layer(): lax.all_gather(wide_parts[5], 'row', axis=0, tiled=True)  129 us
    all_gather x2, waiting for transfers between devices, fetch_layer(): lax.all_gather(wide_parts[4], 'row', axis=0, tiled=True)  83.3 us
    dot_general x14, matrix products, project(): return jnp.dot(left_side, right_side, preferred_element_type=jnp.float32)  72.4 us
  transfers between devices with their start and end apart: 44, of which 34 were waited for; matrix products, arithmetic and copies ran while one was open for 13% of the time, Pallas kernels for 0%

commit v1 on v0

v1 whole, which is shorter than its diff:
```python
import functools

import jax
import jax.numpy as jnp
from jax import lax
from jax.experimental import pallas as pl
from jax.experimental.pallas import tpu as pltpu
from jax.sharding import Mesh, PartitionSpec as P

HEADS = 16
FEAT = 16
HEAD_DIM = 64
WINDOW = 64
MAX_LEN = 256
D = 1024
T = 512
HALF = 256
EPS = 1e-05
NEG = -1e30
ROWS = 8
COLS = 4
FB = 344
FBP = 352
FFP = ROWS * FBP
FC = FFP // COLS

bf16, f32, i32 = jnp.bfloat16, jnp.float32, jnp.int32
NN, NT, TN = ((1,), (0,)), ((1,), (1,)), ((0,), (0,))


def dot(a, b, dims):
    return lax.dot_general(a, b, (dims, ((), ())), preferred_element_type=f32)


def call(body, grid, ins, outs, scratch=(), flops=0, prefetch=None):
    extra = 0 if prefetch is None else 1

    def spec(block, index):
        if block is None:
            return pl.BlockSpec(memory_space=pl.ANY)
        return pl.BlockSpec(block, index)

    in_specs, args = [], []
    for item in ins:
        if not isinstance(item, tuple):
            nd = item.ndim
            item = (item, item.shape, functools.partial(lambda n, *_: (0,) * n, nd))
        args.append(item[0])
        in_specs.append(spec(item[1], item[2]))
    out_specs = [spec(o[2], o[3]) for o in outs]
    out_shape = [jax.ShapeDtypeStruct(o[0], o[1]) for o in outs]
    moved = sum(a.size * a.dtype.itemsize for a in args)
    moved += sum(s.size * s.dtype.itemsize for s in out_shape)
    cost = pl.CostEstimate(flops=int(flops), bytes_accessed=int(moved), transcendentals=0)
    got = pl.pallas_call(
        body,
        out_shape=out_shape,
        grid_spec=pltpu.PrefetchScalarGridSpec(
            num_scalar_prefetch=extra,
            grid=grid,
            in_specs=in_specs,
            out_specs=out_specs,
            scratch_shapes=list(scratch),
        ),
        compiler_params=pltpu.CompilerParams(vmem_limit_bytes=56 * 2**20),
        cost_estimate=cost,
    )(*(([prefetch] if extra else []) + args))
    return got


def whole_map(*shape):
    zeros = (0,) * len(shape)
    return lambda *_: zeros


def norm_factor(h):
    return lax.rsqrt(jnp.mean(h * h, axis=-1, keepdims=True) + EPS)


def norm_proj(h, gain, weights):
    n = len(weights)

    def body(h_ref, gain_ref, *refs):
        xa_ref, outs = refs[n], refs[n + 1 :]

        @pl.when(pl.program_id(0) == 0)
        def _():
            hv = h_ref[...].astype(f32)
            xa_ref[...] = (hv * norm_factor(hv) * gain_ref[...]).astype(bf16)

        for w_ref, o_ref in zip(refs[:n], outs):
            o_ref[...] = dot(xa_ref[...], w_ref[...], NN).astype(bf16)

    ins = [h, gain.reshape(1, D)]
    outs = [((T, D), bf16, (T, D), whole_map(T, D))]
    for w in weights:
        wide = w.shape[1] // COLS
        ins.append((w, (D, wide), lambda i: (0, i)))
        outs.append(((T, w.shape[1]), bf16, (T, wide), lambda i: (0, i)))
    total = sum(w.shape[1] for w in weights)
    return call(body, (COLS,), ins, outs, flops=2 * T * D * total)


def lanes(shape, width):
    return lax.broadcasted_iota(i32, shape, len(shape) - 1) // width


def fill_mask(mask_ref, seg_q, seg_k, live_k, q_axis, window):
    q = lax.broadcasted_iota(i32, (T, T), q_axis)
    k = lax.broadcasted_iota(i32, (T, T), 1 - q_axis)
    ok = (k <= q) & (k > q - window) & (seg_q == seg_k) & ((live_k > 0) | (k == q))
    mask_ref[...] = jnp.where(ok, 1.0, 0.0)


def based_fwd(qk, v, seg_row, seg_col, live_row):
    def body(qk_ref, v_ref, sr_ref, sc_ref, lr_ref, o_ref, ou_ref, rden_ref, mask_ref):
        @pl.when(pl.program_id(0) == 0)
        def _():
            fill_mask(mask_ref, sc_ref[...], sr_ref[...], lr_ref[...], 0, MAX_LEN)

        q4, k4 = qk_ref[:, 0:64], qk_ref[:, 64:128]
        qlane = lanes((T, 64), FEAT)
        first = lanes((HALF, 128), HEAD_DIM) == 0
        scaled = q4.astype(f32) * (FEAT**-0.5)
        for pair in range(2):
            v2 = v_ref[:, pair * 128 : pair * 128 + 128]
            for tb in range(2):
                t0, s1 = tb * HALF, (tb + 1) * HALF
                got = []
                for e in range(2):
                    qm = jnp.where(qlane == pair * 2 + e, scaled, 0.0).astype(bf16)
                    a = dot(qm[t0 : t0 + HALF], k4[0:s1], NT)
                    p = (1.0 + a * (1.0 + 0.5 * a)) * mask_ref[t0 : t0 + HALF, 0:s1]
                    den = jnp.sum(p, axis=-1, keepdims=True)
                    got.append((dot(p.astype(bf16), v2[0:s1], NN), den))
                rden = 1.0 / jnp.where(first, got[0][1], got[1][1])
                ou = jnp.where(first, got[0][0], got[1][0]) * rden
                at = (slice(t0, t0 + HALF), slice(pair * 128, pair * 128 + 128))
                ou_ref[at] = ou
                rden_ref[at] = rden
                o_ref[at] = ou.astype(bf16)

    wide = (T, 256)
    col = lambda c: (0, c)
    return call(
        body,
        (4,),
        [(qk, (T, 128), col), (v, wide, col), seg_row, seg_col, live_row],
        [((T, D), bf16, wide, col), ((T, D), f32, wide, col), ((T, D), f32, wide, col)],
        scratch=[pltpu.VMEM((T, T), f32)],
        flops=HEADS * T * T * 2 * 192,
    )


def based_bwd(qk, v, dou, ou, rden, seg_row, seg_col, live_col):
    def body(qk_ref, v_ref, dou_ref, ou_ref, rden_ref, sr_ref, sc_ref, lc_ref, dqk_ref, dv_ref, mask_ref, dk_ref, dva_ref):
        @pl.when(pl.program_id(0) == 0)
        def _():
            fill_mask(mask_ref, sr_ref[...], sc_ref[...], lc_ref[...], 1, MAX_LEN)

        q4, k4 = qk_ref[:, 0:64], qk_ref[:, 64:128]
        qlane = lanes((T, 64), FEAT)
        q_scaled = q4.astype(f32) * (FEAT**-0.5)
        k_scaled = k4.astype(f32) * (FEAT**-0.5)
        vlane = lanes((T, 128), HEAD_DIM)
        dnum_f = dou_ref[...] * rden_ref[...]
        term = dnum_f * ou_ref[...]
        high = term.astype(bf16)
        low = (term - high.astype(f32)).astype(bf16)
        pick = jnp.where(
            lax.broadcasted_iota(i32, (8, 256), 0) == lanes((8, 256), HEAD_DIM), 1.0, 0.0
        ).astype(bf16)
        dden = -(dot(pick, high, NT) + dot(pick, low, NT))
        dk_ref[...] = jnp.zeros((T, 64), f32)
        dva_ref[...] = jnp.zeros((T, 256), f32)
        dq = [jnp.zeros((HALF, 64), f32), jnp.zeros((HALF, 64), f32)]
        for pair in range(2):
            cols = slice(pair * 128, pair * 128 + 128)
            v2 = v_ref[:, cols]
            for e in range(2):
                head = pair * 2 + e
                qm = jnp.where(qlane == head, q_scaled, 0.0).astype(bf16)
                km = jnp.where(qlane == head, k_scaled, 0.0).astype(bf16)
                dn = jnp.where(vlane == e, dnum_f[:, cols], 0.0).astype(bf16)
                for tb in range(2):
                    t0, s1 = tb * HALF, (tb + 1) * HALF
                    at = slice(t0, t0 + HALF)
                    a = dot(k4[0:s1], qm[at], NT)
                    m = mask_ref[0:s1, at]
                    p = (1.0 + a * (1.0 + 0.5 * a)) * m
                    dp = dot(v2[0:s1], dn[at], NT) + dden[head : head + 1, at]
                    da = (dp * m * (1.0 + a)).astype(bf16)
                    dk_ref[0:s1, :] += dot(da, qm[at], NN)
                    dva_ref[0:s1, cols] += dot(p.astype(bf16), dn[at], NN)
                    dq[tb] += dot(da, km[0:s1], TN)
        for tb in range(2):
            at = slice(tb * HALF, tb * HALF + HALF)
            dqk_ref[at, 0:64] = dq[tb].astype(bf16)
        dqk_ref[:, 64:128] = dk_ref[...].astype(bf16)
        dv_ref[...] = dva_ref[...].astype(bf16)

    wide = (T, 256)
    col = lambda c: (0, c)
    return call(
        body,
        (4,),
        [(qk, (T, 128), col), (v, wide, col), (dou, wide, col), (ou, wide, col), (rden, wide, col), seg_row, seg_col, live_col],
        [((T, 512), bf16, (T, 128), col), ((T, D), bf16, wide, col)],
        scratch=[pltpu.VMEM((T, T), f32), pltpu.VMEM((T, 64), f32), pltpu.VMEM((T, 256), f32)],
        flops=HEADS * T * T * 2 * 480,
    )


SPAN = ((0, HALF), (HALF - WINDOW, T))


def window_fwd(q, k, v, seg_row, seg_col, live_row):
    def body(q_ref, k_ref, v_ref, sr_ref, sc_ref, lr_ref, o_ref, mask_ref):
        @pl.when(pl.program_id(0) == 0)
        def _():
            fill_mask(mask_ref, sc_ref[...], sr_ref[...], lr_ref[...], 0, WINDOW)

        first = lanes((HALF, 128), HEAD_DIM) == 0
        qlane = lanes((T, 128), HEAD_DIM)
        scaled = q_ref[...].astype(f32) * (HEAD_DIM**-0.5)
        for tb in range(2):
            t0 = tb * HALF
            s0, s1 = SPAN[tb]
            ok = mask_ref[t0 : t0 + HALF, s0:s1] > 0.5
            got = []
            for e in range(2):
                qm = jnp.where(qlane == e, scaled, 0.0).astype(bf16)
                c = dot(qm[t0 : t0 + HALF], k_ref[s0:s1, :], NT)
                c = jnp.where(ok, c, NEG)
                w = jnp.exp(c - jnp.max(c, axis=-1, keepdims=True))
                w = w * (1.0 / jnp.sum(w, axis=-1, keepdims=True))
                got.append(dot(w.astype(bf16), v_ref[s0:s1, :], NN))
            o_ref[t0 : t0 + HALF, :] = jnp.where(first, got[0], got[1]).astype(bf16)

    blk = (T, 128)
    col = lambda c: (0, c)
    return call(
        body,
        (8,),
        [(q, blk, col), (k, blk, col), (v, blk, col), seg_row, seg_col, live_row],
        [((T, D), bf16, blk, col)],
        scratch=[pltpu.VMEM((T, T), f32)],
        flops=HEADS * T * T * 2 * 192,
    )[0]


def window_bwd(q, k, v, dor, seg_row, seg_col, live_col):
    def body(q_ref, k_ref, v_ref, do_ref, sr_ref, sc_ref, lc_ref, dq_ref, dk_ref, dv_ref, mask_ref, dka_ref, dva_ref):
        @pl.when(pl.program_id(0) == 0)
        def _():
            fill_mask(mask_ref, sr_ref[...], sc_ref[...], lc_ref[...], 1, WINDOW)

        lane = lanes((T, 128), HEAD_DIM)
        q_scaled = q_ref[...].astype(f32) * (HEAD_DIM**-0.5)
        k_scaled = k_ref[...].astype(f32) * (HEAD_DIM**-0.5)
        do = do_ref[...]
        dka_ref[...] = jnp.zeros((T, 128), f32)
        dva_ref[...] = jnp.zeros((T, 128), f32)
        for tb in range(2):
            at = slice(tb * HALF, tb * HALF + HALF)
            s0, s1 = SPAN[tb]
            ok = mask_ref[s0:s1, at] > 0.5
            dq = jnp.zeros((HALF, 128), f32)
            for e in range(2):
                qm = jnp.where(lane == e, q_scaled, 0.0).astype(bf16)
                km = jnp.where(lane == e, k_scaled, 0.0).astype(bf16)
                dm = jnp.where(lane == e, do, jnp.zeros_like(do))
                c = dot(k_ref[s0:s1, :], qm[at], NT)
                c = jnp.where(ok, c, NEG)
                w = jnp.exp(c - jnp.max(c, axis=0, keepdims=True))
                w = w * (1.0 / jnp.sum(w, axis=0, keepdims=True))
                dw = dot(v_ref[s0:s1, :], dm[at], NT)
                ds = (w * (dw - jnp.sum(w * dw, axis=0, keepdims=True))).astype(bf16)
                dka_ref[s0:s1, :] += dot(ds, qm[at], NN)
                dva_ref[s0:s1, :] += dot(w.astype(bf16), dm[at], NN)
                dq += dot(ds, km[s0:s1], TN)
            dq_ref[at, :] = dq.astype(bf16)
        dk_ref[...] = dka_ref[...].astype(bf16)
        dv_ref[...] = dva_ref[...].astype(bf16)

    blk = (T, 128)
    col = lambda c: (0, c)
    return call(
        body,
        (8,),
        [(q, blk, col), (k, blk, col), (v, blk, col), (dor, blk, col), seg_row, seg_col, live_col],
        [((T, D), bf16, blk, col)] * 3,
        scratch=[pltpu.VMEM((T, T), f32), pltpu.VMEM((T, 128), f32), pltpu.VMEM((T, 128), f32)],
        flops=HEADS * T * T * 2 * 480,
    )


def attn_out(h, o, w_out, gain):
    def body(h_ref, o_ref, w_ref, gain_ref, hm_ref, xf_ref):
        hm = h_ref[...].astype(f32) + dot(o_ref[...], w_ref[...], NN)
        hm_ref[...] = hm
        xf_ref[...] = (hm * norm_factor(hm) * gain_ref[...]).astype(bf16)

    full = whole_map(T, D)
    return call(
        body,
        (1,),
        [h, o, w_out, gain.reshape(1, D)],
        [((T, D), f32, (T, D), full), ((T, D), bf16, (T, D), full)],
        flops=2 * T * D * D,
    )


def gate_up(xf, w_gate, w_up):
    def body(xf_ref, wg_ref, wu_ref, g_ref, u_ref, hid_ref):
        xfv = xf_ref[...]
        g = dot(wg_ref[...], xfv, NT)
        u = dot(wu_ref[...], xfv, NT)
        g_ref[...] = g.astype(bf16)
        u_ref[...] = u.astype(bf16)
        hid_ref[...] = (g * (1.0 / (1.0 + jnp.exp(-g))) * u).astype(bf16)

    wblk, oblk, row = (FC, D), (FC, T), lambda i: (i, 0)
    return call(
        body,
        (COLS,),
        [xf, (w_gate, wblk, row), (w_up, wblk, row)],
        [((FFP, T), bf16, oblk, row)] * 3,
        flops=4 * T * D * FFP,
    )


def down(hm, hid, w_down):
    def body(hm_ref, hid_ref, w_ref, h_ref):
        part = dot(hid_ref[...], w_ref[...], TN)

        @pl.when(pl.program_id(0) == 0)
        def _():
            h_ref[...] = hm_ref[...] + part

        @pl.when(pl.program_id(0) > 0)
        def _():
            h_ref[...] += part

    row = lambda i: (i, 0)
    return call(
        body,
        (COLS,),
        [hm, (hid, (FC, T), row), (w_down, (FC, D), row)],
        [((T, D), f32, (T, D), whole_map(T, D))],
        flops=2 * T * D * FFP,
    )[0]


def relative(me, z, y, x, core):
    return z ^ me[0], y ^ me[1], x ^ me[2], core ^ me[3]


def down_bwd(me, bd, w_down, hid, g, u):
    def body(me_ref, bd_ref, w_ref, hid_ref, g_ref, u_ref, dg_ref, du_ref, p1_ref, p2_ref):
        bdv = bd_ref[...]
        gwd = dot(hid_ref[...], bdv, NN).astype(bf16)
        for x in range(2):
            for core in range(2):
                _, _, xr, cr = relative(me_ref, 0, 0, x, core)
                at = (x * 2 + core) * 256
                p1_ref[cr, xr, 0, 0] = gwd[:, at : at + 128]
                p2_ref[cr, 0, xr, 0] = gwd[:, at + 128 : at + 256]
        dhid = dot(w_ref[...], bdv, NT)
        gv, uv = g_ref[...].astype(f32), u_ref[...].astype(f32)
        sig = 1.0 / (1.0 + jnp.exp(-gv))
        act = gv * sig
        du_ref[...] = (dhid * act).astype(bf16)
        dg_ref[...] = (dhid * uv * (sig + act * (1.0 - sig))).astype(bf16)

    row = lambda i, me: (i, 0)
    hblk = (FBP, T)
    return call(
        body,
        (ROWS,),
        [bd, (w_down, (FBP, D), row), (hid, hblk, row), (g, hblk, row), (u, hblk, row)],
        [
            ((FFP, T), bf16, hblk, row),
            ((FFP, T), bf16, hblk, row),
            ((2, 2, 2, 4, FBP, 128), bf16, (2, 2, 1, 1, FBP, 128), lambda i, me: (0, 0, (i % 2) ^ me[1], (i // 2) ^ me[0], 0, 0)),
            ((2, 2, 2, 4, FBP, 128), bf16, (2, 1, 2, 1, FBP, 128), lambda i, me: (0, (i % 2) ^ me[1], 0, (i // 2) ^ me[0], 0, 0)),
        ],
        flops=4 * T * D * FFP,
        prefetch=me,
    )


def store_col(me_ref, out_ref, swapped, tile, rows, at):
    for z in range(4):
        for y in range(2):
            zr, yr, _, _ = relative(me_ref, z, y, 0, 0)
            r = (z * 2 + y) * 128
            part = tile[r : r + 128]
            if swapped:
                out_ref[0, yr, 0, zr, at : at + rows] = part
            else:
                out_ref[0, 0, yr, zr, at : at + rows] = part


def gate_up_bwd(me, xf, dg, du):
    def body(me_ref, xf_ref, dg_ref, du_ref, p1_ref, p2_ref):
        xfv = xf_ref[...]
        gwg = dot(dg_ref[...], xfv, NN).astype(bf16)
        gwu = dot(du_ref[...], xfv, NN).astype(bf16)
        for z in range(4):
            for y in range(2):
                zr, yr, _, _ = relative(me_ref, z, y, 0, 0)
                r = (z * 2 + y) * 128
                p1_ref[0, 0, yr, zr] = gwg[:, r : r + 128]
                p2_ref[0, yr, 0, zr] = gwu[:, r : r + 128]

    row = lambda i, me: (i, 0)
    return call(
        body,
        (COLS,),
        [xf, (dg, (FC, T), row), (du, (FC, T), row)],
        [
            ((2, 2, 2, 4, FC, 128), bf16, (1, 1, 2, 4, FC, 128), lambda i, me: ((i % 2) ^ me[3], (i // 2) ^ me[2], 0, 0, 0, 0)),
            ((2, 2, 2, 4, FC, 128), bf16, (1, 2, 1, 4, FC, 128), lambda i, me: ((i % 2) ^ me[3], 0, (i // 2) ^ me[2], 0, 0, 0)),
        ],
        flops=4 * T * D * FFP,
        prefetch=me,
    )


def norm_bwd(dx, h, gain, g):
    rf = norm_factor(h)
    hr = h * rf
    dgain = jnp.sum(dx * hr, axis=0, keepdims=True)
    gd = gain * dx
    mean = jnp.sum(gd * hr, axis=-1, keepdims=True) * (1.0 / D)
    return dgain, g + rf * (gd - hr * mean)


def mlp_dx(dg, du, w_gate, w_up, hm, gain, g):
    def body(dg_ref, du_ref, wg_ref, wu_ref, hm_ref, gain_ref, g_ref, gm_ref, bo_ref, gg_ref):
        part = dot(dg_ref[...], wg_ref[...], TN) + dot(du_ref[...], wu_ref[...], TN)
        i = pl.program_id(0)

        @pl.when(i == 0)
        def _():
            gm_ref[...] = part

        @pl.when((i > 0) & (i < COLS - 1))
        def _():
            gm_ref[...] += part

        @pl.when(i == COLS - 1)
        def _():
            gg, gm = norm_bwd(gm_ref[...] + part, hm_ref[...], gain_ref[...], g_ref[...].astype(f32))
            gg_ref[...] = gg
            gm_ref[...] = gm
            bo_ref[...] = gm.astype(bf16)

    row = lambda i: (i, 0)
    full = whole_map(T, D)
    return call(
        body,
        (COLS,),
        [(dg, (FC, T), row), (du, (FC, T), row), (w_gate, (FC, D), row), (w_up, (FC, D), row), hm, gain.reshape(1, D), g],
        [((T, D), f32, (T, D), full), ((T, D), bf16, (T, D), full), ((1, D), f32, (1, D), full)],
        flops=4 * T * D * FFP,
    )


def attn_dout(bo, w_out, kind):
    def body(bo_ref, w_ref, dou_ref):
        dou_ref[...] = dot(bo_ref[...], w_ref[...], NT).astype(kind)

    return call(
        body,
        (COLS,),
        [bo, (w_out, (256, D), lambda i: (i, 0))],
        [((T, D), kind, (T, 256), lambda i: (0, i))],
        flops=2 * T * D * D,
    )[0]


def attn_bwd(me, xa, grads, weights, o, bo, h, gain, gm, halves):
    n = len(grads)
    first, second = halves

    def body(me_ref, xa_ref, o_ref, h_ref, gain_ref, gm_ref, bo_ref, *refs):
        d_refs, w_refs = refs[:n], refs[n : 2 * n]
        p1_ref, p2_ref, g_ref, gg_ref = refs[2 * n :]
        xav = xa_ref[...]
        tiles = [dot(xav, d[...], TN).astype(bf16) for d in d_refs]
        tiles.append(dot(o_ref[...], bo_ref[...], TN).astype(bf16))
        for ref, strips, swapped in ((p1_ref, first, False), (p2_ref, second, True)):
            for j, (which, at) in enumerate(strips):
                store_col(me_ref, ref, swapped, tiles[which][:, at : at + 128], 128, j * 128)
        part = dot(d_refs[0][...], w_refs[0][...], NT)
        for d, w in zip(d_refs[1:], w_refs[1:]):
            part += dot(d[...], w[...], NT)
        i = pl.program_id(0)

        @pl.when(i == 0)
        def _():
            g_ref[...] = part

        @pl.when((i > 0) & (i < COLS - 1))
        def _():
            g_ref[...] += part

        @pl.when(i == COLS - 1)
        def _():
            gg, g = norm_bwd(g_ref[...] + part, h_ref[...].astype(f32), gain_ref[...], gm_ref[...])
            gg_ref[...] = gg
            g_ref[...] = g

    col = lambda i, me: (0, i)
    full = whole_map(T, D)
    n1, n2 = 128 * len(first), 128 * len(second)
    ins = [xa, o, h, gain.reshape(1, D), gm, (bo, (T, 256), col)]
    ins += [(d, (T, d.shape[1] // COLS), col) for d in grads]
    ins += [(w, (D, w.shape[1] // COLS), col) for w in weights]
    total = sum(w.shape[1] for w in weights)
    return call(
        body,
        (COLS,),
        ins,
        [
            ((2, 2, 2, 4, n1, 128), bf16, (1, 1, 2, 4, n1, 128), lambda i, me: ((i % 2) ^ me[3], (i // 2) ^ me[2], 0, 0, 0, 0)),
            ((2, 2, 2, 4, n2, 128), bf16, (1, 2, 1, 4, n2, 128), lambda i, me: ((i % 2) ^ me[3], 0, (i // 2) ^ me[2], 0, 0, 0)),
            ((T, D), f32, (T, D), full),
            ((1, D), f32, (1, D), full),
        ],
        flops=4 * T * D * total + 2 * T * D * D,
        prefetch=me,
    )


def assemble(me, bufs, jobs, shapes):
    n_out = len(shapes)

    def body(me_ref, *refs):
        halves = (refs[0:4], refs[4:8])
        outs, sems = refs[8 : 8 + n_out], refs[8 + n_out]
        for core_rel in range(2):
            for hi in range(2):

                @pl.loop(0, 8)
                def _(i):
                    lo, zr = i // 4, i % 4
                    for half, src, rows, out, rs, cs, cb in jobs:
                        yr, xr = (hi, lo) if half == 0 else (lo, hi)
                        z, y, x, core = relative(me_ref, zr, yr, xr, core_rel)
                        r, c = z * 2 + y, x * 2 + core
                        r0 = pl.multiple_of(r * rs[0] + c * rs[1], 16)
                        c0 = pl.multiple_of(r * cs[0] + c * cs[1] + cb, 128)
                        pltpu.make_async_copy(
                            halves[half][core_rel * 2 + hi].at[lo, zr, pl.ds(src, rows)],
                            outs[out].at[pl.ds(r0, rows), pl.ds(c0, 128)],
                            sems.at[out],
                        ).start()
        for j in range(n_out):
            pltpu.make_async_copy(outs[j], outs[j], sems.at[j]).wait()

    ins = [(b, None, None) for half in bufs for b in half]
    outs = [(s, bf16, None, None) for s in shapes]
    return call(body, (1,), ins, outs, scratch=[pltpu.SemaphoreType.DMA((n_out,))], prefetch=me)


HALVES_ONE = (((1, 0), (1, 128)), ((0, 0), (2, 0), (2, 128)))
HALVES_TWO = (((0, 0), (0, 128), (1, 0), (1, 128)), ((2, 0), (2, 128), (3, 0), (3, 128)))


def attn_jobs(halves, widths):
    jobs = []
    for half, strips in enumerate(halves):
        for j, (which, at) in enumerate(strips):
            jobs.append((half, j * 128, 128, which, (128, 0), (0, widths[which]), at))
    return jobs


GU_JOBS = [(0, 0, FC, 0, (0, FC), (128, 0), 0), (1, 0, FC, 1, (0, FC), (128, 0), 0)]
DOWN_JOBS = [(0, 0, FBP, 0, (FBP, 0), (0, 256), 0), (1, 0, FBP, 0, (FBP, 0), (0, 256), 128)]


def pad_hidden(w):
    k = w.shape[0]
    return jnp.pad(w.reshape(k, -1, FB), ((0, 0), (0, 0), (0, FBP - FB))).reshape(k, -1).T


def pad_rows(w):
    n = w.shape[1]
    return jnp.pad(w.reshape(-1, FB, n), ((0, 0), (0, FBP - FB), (0, 0))).reshape(-1, n)


def strips_of(blocks, halves):
    return tuple(
        jnp.concatenate([blocks[which][:, at : at + 128] for which, at in strips], axis=0) for strips in halves
    )


class Ring:
    def __init__(self):
        self.axes = ("row", "col")

    def swap(self, value, axis, by=1):
        pairs = []
        for i in range(32):
            z, y, x, c = i >> 3, (i >> 2) & 1, (i >> 1) & 1, i & 1
            if axis == "z":
                z ^= by
            elif axis == "y":
                y ^= 1
            elif axis == "x":
                x ^= 1
            else:
                c ^= 1
            pairs.append((i, (z << 3) | (y << 2) | (x << 1) | c))
        return lax.ppermute(value, self.axes, pairs)

    def gather(self, one, two):
        n1 = one.shape[0]
        both = jnp.concatenate([one, two], axis=0)
        near = [both] + [self.swap(both, "z", by) for by in (1, 2, 3)]
        full = []
        for part, (lo, hi) in ((slice(0, n1), "xy"), (slice(n1, None), "yx")):
            mine = jnp.stack([b[part] for b in near])
            own = jnp.stack([mine, self.swap(mine, lo)])
            far = self.swap(own, hi)
            full.append([own, far, self.swap(own, "core"), self.swap(far, "core")])
        return full

    def reduce(self, one, two):
        done = []
        for g, (lo, hi) in ((one, "xy"), (two, "yx")):
            h = g[0] + self.swap(g[1], "core")
            h = h[0] + self.swap(h[1], lo)
            h = h[0] + self.swap(h[1], hi)
            done.append(h)
        n1 = done[0].shape[1]
        both = jnp.concatenate(done, axis=1)
        total = both[0].astype(f32)
        for by in (1, 2, 3):
            total = total + self.swap(both[by], "z", by).astype(f32)
        return total[:n1], total[n1:]


def fetch_ring(ring, me, shards, halves):
    *attn, gate, up, dn = shards
    widths = [w.shape[1] for w in attn]
    a = ring.gather(*strips_of(attn, halves))
    attn_full = assemble(me, a, attn_jobs(halves, widths), [(D, w * COLS) for w in widths])
    gu = ring.gather(pad_hidden(gate), pad_hidden(up))
    gu_full = assemble(me, gu, GU_JOBS, [(FFP, D)] * 2)
    dp = pad_rows(dn)
    d = ring.gather(dp[:, 0:128], dp[:, 128:256])
    d_full = assemble(me, d, DOWN_JOBS, [(FFP, D)])
    return list(attn_full) + list(gu_full) + list(d_full)


def fetch_any(shards):
    full = [
        lax.all_gather(lax.all_gather(w, "col", axis=1, tiled=True), "row", axis=0, tiled=True) for w in shards
    ]
    return full[:-3] + [pad_hidden(full[-3]), pad_hidden(full[-2]), pad_rows(full[-1])]


def unpad_hidden(g):
    k = g.shape[1]
    return g.reshape(-1, FBP, k)[:, :FB].reshape(-1, k).T


def unpad_rows(g):
    n = g.shape[1]
    return g.reshape(-1, FBP, n)[:, :FB].reshape(-1, n)


def whole_grad(p, swapped):
    if swapped:
        p = jnp.swapaxes(p, 1, 2)
    core, x, y, z, n, w = p.shape
    return p.transpose(3, 2, 1, 0, 4, 5).reshape(z * y, x * core, n, w)


def join_strips(one, two, halves, widths):
    out = []
    for which, width in enumerate(widths):
        got = {}
        for src, strips in ((one, halves[0]), (two, halves[1])):
            for j, (w, at) in enumerate(strips):
                if w == which:
                    got[at] = src[..., j * 128 : j * 128 + 128, :]
        out.append(jnp.concatenate([got[a] for a in sorted(got)], axis=-1))
    return out


def scatter_any(w):
    part = lax.psum_scatter(w, "row", scatter_dimension=0, tiled=True)
    return lax.psum_scatter(part, "col", scatter_dimension=1, tiled=True).astype(f32)


def natural(blocks):
    r, c, n, w = blocks.shape
    return blocks.transpose(0, 2, 1, 3).reshape(r * n, c * w)


def sum_down(ring, one, two):
    if ring:
        a, b = ring.reduce(one, two)
        return unpad_rows(jnp.concatenate([a, b], axis=1))
    whole = jnp.concatenate([whole_grad(one, False), whole_grad(two, True)], axis=-1)
    return scatter_any(unpad_rows(natural(whole)))


def sum_gate_up(ring, one, two):
    if ring:
        a, b = ring.reduce(one, two)
        return unpad_hidden(a), unpad_hidden(b)
    out = []
    for g, swapped in ((one, False), (two, True)):
        whole = whole_grad(g, swapped).transpose(1, 2, 0, 3).reshape(FFP, D)
        out.append(scatter_any(unpad_hidden(whole)))
    return tuple(out)


def sum_attn(ring, one, two, halves, widths):
    if ring:
        a, b = ring.reduce(one, two)
        return join_strips(a, b, halves, widths)
    blocks = join_strips(whole_grad(one, False), whole_grad(two, True), halves, widths)
    return [scatter_any(natural(b)) for b in blocks]


def join_qk(q, k, parts):
    n = q.shape[0]
    both = jnp.concatenate([q.reshape(n, parts, -1), k.reshape(n, parts, -1)], axis=2)
    return both.reshape(n, -1)


def route_plan(dest_slot, block_tokens):
    row_count = lax.axis_size("row")
    col_count = lax.axis_size("col")
    per_peer = block_tokens // row_count
    row_at = lax.axis_index("row")
    col_at = lax.axis_index("col")
    slot_table = dest_slot.reshape(row_count, col_count, block_tokens)
    column = lax.dynamic_index_in_dim(slot_table, col_at, 1, False)
    own_slots = lax.dynamic_index_in_dim(column, row_at, 0, False)
    send_order = jnp.argsort(own_slots)
    arrived = jnp.sort(column, axis=1)
    incoming = lax.dynamic_slice_in_dim(arrived, row_at * per_peer, per_peer, 1)
    local_slots = incoming.reshape(-1) - (row_at * col_count + col_at) * block_tokens
    placing = jnp.argsort(local_slots)
    return (send_order, local_slots, placing)


def exchange(rows, row_count):
    n, width = rows.shape
    got = lax.all_to_all(rows.reshape(row_count, n // row_count, width), "row", split_axis=0, concat_axis=0, tiled=True)
    return got.reshape(n, width)


def body(tokens, cotangent, dest_slot, lengths, pad_mask, *params):
    n_rows, n_cols = lax.axis_size("row"), lax.axis_size("col")
    ring = Ring() if (n_rows, n_cols) == (ROWS, COLS) else None
    gain_a1, bq, bk, bv, bo_w, gain_m1, wg1, wu1, wd1 = params[:9]
    gain_a2, wq, wk, wv, wo2, gain_m2, wg2, wu2, wd2 = params[9:]
    if ring:
        row, col = lax.axis_index("row"), lax.axis_index("col")
        me = jnp.stack([row // 2, row % 2, col // 2, col % 2]).astype(i32)
        one = fetch_ring(ring, me, [join_qk(bq, bk, 1), bv, bo_w, wg1, wu1, wd1], HALVES_ONE)
        two = fetch_ring(ring, me, [wq, wk, wv, wo2, wg2, wu2, wd2], HALVES_TWO)
    else:
        me = jnp.zeros((4,), i32)
        got = fetch_any([bq, bk, bv, bo_w, wg1, wu1, wd1])
        one = [join_qk(got[0], got[1], COLS)] + got[2:]
        two = fetch_any([wq, wk, wv, wo2, wg2, wu2, wd2])
    send_order, local_slots, placing = route_plan(dest_slot, T)
    start = exchange(tokens[send_order], n_rows)[placing]
    cot = exchange(cotangent[send_order], n_rows)[placing]
    position = jnp.arange(T, dtype=i32)
    segment, end = jnp.zeros((T,), i32), jnp.zeros((), i32)
    for j in range(lengths.shape[1]):
        end = end + lengths[0, j]
        segment = segment + (position >= end).astype(i32)
    seg_row, seg_col = segment.reshape(1, T), segment.reshape(T, 1)
    live_row, live_col = pad_mask.reshape(1, T), pad_mask.reshape(T, 1)

    w_qk, w_v, w_o, w_g, w_u, w_d = one
    xa1, qk1, v1 = norm_proj(start, gain_a1, [w_qk, w_v])
    o1, ou1, rden1 = based_fwd(qk1, v1, seg_row, seg_col, live_row)
    hm1, xf1 = attn_out(start, o1, w_o, gain_m1)
    g1, u1, hid1 = gate_up(xf1, w_g, w_u)
    h1 = down(hm1, hid1, w_d)
    v_q, v_k, v_v, v_o, v_g, v_u, v_d = two
    xa2, q2, k2, v2 = norm_proj(h1, gain_a2, [v_q, v_k, v_v])
    o2 = window_fwd(q2, k2, v2, seg_row, seg_col, live_row)
    hm2, xf2 = attn_out(h1, o2, v_o, gain_m2)
    g2, u2, hid2 = gate_up(xf2, v_g, v_u)
    h2 = down(hm2, hid2, v_d)
    dg2, du2, *pd2 = down_bwd(me, cot, v_d, hid2, g2, u2)
    sum_d2 = sum_down(ring, *pd2)
    pgu2 = gate_up_bwd(me, xf2, dg2, du2)
    sum_g2, sum_u2 = sum_gate_up(ring, *pgu2)
    gm2, bo2, gg_m2 = mlp_dx(dg2, du2, v_g, v_u, hm2, gain_m2, cot)
    dor2 = attn_dout(bo2, v_o, bf16)
    dq2, dk2, dv2 = window_bwd(q2, k2, v2, dor2, seg_row, seg_col, live_col)
    *pa2, gh1, gg_a2 = attn_bwd(me, xa2, [dq2, dk2, dv2], [v_q, v_k, v_v], o2, bo2, h1, gain_a2, gm2, HALVES_TWO)
    sum_q2, sum_k2, sum_v2, sum_o2 = sum_attn(ring, *pa2, HALVES_TWO, [256] * 4)
    dg1, du1, *pd1 = down_bwd(me, gh1.astype(bf16), w_d, hid1, g1, u1)
    sum_d1 = sum_down(ring, *pd1)
    pgu1 = gate_up_bwd(me, xf1, dg1, du1)
    sum_g1, sum_u1 = sum_gate_up(ring, *pgu1)
    gm1, bo1, gg_m1 = mlp_dx(dg1, du1, w_g, w_u, hm1, gain_m1, gh1)
    dou1 = attn_dout(bo1, w_o, f32)
    dqk1, dv1 = based_bwd(qk1, v1, dou1, ou1, rden1, seg_row, seg_col, live_col)
    *pa1, g0, gg_a1 = attn_bwd(me, xa1, [dqk1, dv1], [w_qk, w_v], o1, bo1, start, gain_a1, gm1, HALVES_ONE)
    sums = sum_attn(ring, *pa1, HALVES_ONE, [128, 256, 256])
    if ring:
        sum_q1, sum_k1 = sums[0][:, :64], sums[0][:, 64:]
    else:
        wide = sums[0].shape[1] // 2
        sum_q1, sum_k1 = sums[0][:, :wide], sums[0][:, wide:]
    sum_v1, sum_o1 = sums[1:]

    gains = lax.psum(jnp.concatenate([gg_a1, gg_m1, gg_a2, gg_m2], axis=0), ("row", "col"))
    restore = jnp.argsort(send_order)
    output = exchange(h2.astype(bf16)[local_slots], n_rows)[restore]
    tokens_grad = exchange(g0.astype(bf16)[local_slots], n_rows)[restore]
    return (
        output, tokens_grad,
        gains[0], sum_q1, sum_k1, sum_v1, sum_o1, gains[1], sum_g1, sum_u1, sum_d1,
        gains[2], sum_q2, sum_k2, sum_v2, sum_o2, gains[3], sum_g2, sum_u2, sum_d2,
    )


def solution(mesh):
    block, weight = P(("row", "col"), None), P("row", "col")
    layer_in = (P(),) + (weight,) * 4 + (P(),) + (weight,) * 3
    return jax.shard_map(
        body,
        mesh=mesh,
        in_specs=(block, block, P(), block, P(("row", "col"))) + layer_in * 2,
        out_specs=(block, block) + layer_in * 2,
        check_vma=False,
    )
```

time: 2660 us -> 2580 us (0.970)
  Pallas kernels: 0 us -> 1730 us
  waiting for transfers between devices: 1890 us -> 431 us
  matrix products: 316 us -> 0 us
  blocking collectives: 240 us -> 39.9 us
  starting transfers between devices: 20 us -> 173 us
    pallas_call x0 -> x28, Pallas kernels: none -> 1730 us  [call(): pl.pallas_call(body, out_shape=out_shape, grid_spec=pltpu.PrefetchScalarG...]
    reduce_scatter x22 -> x0, waiting for transfers between devices: 894 us -> none  [the longest x2 219 us: reduce_layer(): lax.psum_scatter(grads[6].astype(jnp.bfloat16), 'row', scatter_dimension=...]
    all_gather x12 -> x0, waiting for transfers between devices: 517 us -> none  [the longest x2 164 us: fetch_layer(): lax.all_gather(wide_parts[6], 'row', axis=0, tiled=True)]
    unnamed x46 -> x0, waiting for transfers between devices: 463 us -> none
    ppermute x0 -> x120, waiting for transfers between devices: none -> 421 us  [swap(): return lax.ppermute(value, self.axes, pairs)]
    dot_general x54 -> x0, matrix products: 316 us -> none  [the longest x14 72.4 us: project(): return jnp.dot(left_side, right_side, preferred_element_type=jnp.float32)]
    all_gather x16 -> x0, blocking collectives: 200 us -> none  [the longest x1 60.5 us: fetch_layer(): lax.all_gather(wide_parts[1], 'row', axis=0, tiled=True)]
    ppermute x0 -> x120, starting transfers between devices: none -> 155 us  [swap(): return lax.ppermute(value, self.axes, pairs)]
  transfers between devices with their start and end apart: 44 -> 124, of which waited for: 34 -> 50; matrix products, arithmetic and copies ran while one was open for 13% -> 6% of each run, Pallas kernels for 0% -> 48%
where the time goes in v1:
time: 2580 us; the launch traced here: 2570 us
  Pallas kernels  1730 us (67%)
  waiting for transfers between devices  431 us (17%)
  starting transfers between devices  173 us (7%)
  local copies, waits for them, and re-layouts  91 us (4%)
  other arithmetic  80.1 us (3%)
  blocking collectives  39.9 us (2%)
    pallas_call x28, Pallas kernels, call(): pl.pallas_call(body, out_shape=out_shape, grid_spec=pltpu.PrefetchScalarG...  1730 us
    ppermute x120, waiting for transfers between devices, swap(): return lax.ppermute(value, self.axes, pairs)  421 us
    ppermute x120, starting transfers between devices, swap(): return lax.ppermute(value, self.axes, pairs)  155 us
  transfers between devices with their start and end apart: 124, of which 50 were waited for; matrix products, arithmetic and copies ran while one was open for 6% of the time, Pallas kernels for 48%

profile of v1, /device:TPU:0, one launch (start us, length us, event | category | flops | bytes accessed | tf_op | source)
XLA Modules:
  0.0 2565.4 jit_solution(2334834685407851432)
XLA Ops:
  30.2 17.5 collective-permute-done.1
  57.1 18.2 collective-permute-start.22
  208.2 14.9 collective-permute-done.51
  316.3 28.7 %collective-permute-done.15.refs_1_ = bf16[2,4,704,128]{3,2,1,0:T(8,128)(2,1)} collective-permute-done((bf16[2,4,704,128]{3,2,1,0:T(8,128)(2,1)}, bf16[2,4,704,128]{3,2,1,0:T(8,128)(2,1)}, u32[]{:S(2)}, u32[]{:S(2)}) %collective-permute-start.15) | collective-permute-done | bytes 1441824 | tf_op jit(solution)/shard_map/ppermute | solution.py:618
  356.4 19.3 collective-permute-done.48.refs_1_
  388.0 176.5 %shard_map.380.w_ref = bf16[2816,1024]{1,0:T(8,128)(2,1)} custom-call(s32[4]{0:T(128)} %pad_add_fusion.me_ref, bf16[2,4,352,128]{3,2,1,0:T(8,128)(2,1)} %copy-done.32, bf16[2,4,352,128]{3,2,1,0:T(8,128)(2,1)} %copy-done.50, bf16[2,4,352,128]{3,2,1,0:T(8,128)(2,1)} %copy-done.51, bf16[2,4,352,128]{3,2,1,0:T(8,128)(2,1)} %copy-done.58, ...), custom_call_target="tpu_custom_call" | custom-call | bytes 11534336 | tf_op jit(solution)/shard_map/pallas_call | solution.py:55
  564.5 176.5 %shard_map.388.w_ref = bf16[2816,1024]{1,0:T(8,128)(2,1)} custom-call(s32[4]{0:T(128)} %pad_add_fusion.me_ref, bf16[2,4,352,128]{3,2,1,0:T(8,128)(2,1)} %copy-done.33, bf16[2,4,352,128]{3,2,1,0:T(8,128)(2,1)} %collective-permute-done.59.refs_1_, bf16[2,4,352,128]{3,2,1,0:T(8,128)(2,1)} %collective-permute-done.60.refs_2_, ...), custom_call_target="tpu_custom_call" | custom-call | bytes 11534336 | tf_op jit(solution)/shard_map/pallas_call | solution.py:55
  741.0 160.6 %shard_map.374 = (bf16[1024,512]{1,0:T(8,128)(2,1)}, bf16[1024,1024]{1,0:T(8,128)(2,1)}, bf16[1024,1024]{1,0:T(8,128)(2,1)}) custom-call(s32[4]{0:T(128)} %pad_add_fusion.me_ref, bf16[2,4,256,128]{3,2,1,0:T(8,128)(2,1)} %copy-done.42, bf16[2,4,256,128]{3,2,1,0:T(8,128)(2,1)} %copy-done.64, bf16[2,4,256,128]{3,2,1,0:T(8,128)(2,1)} %copy-done.65, ...), custom_call_target="tpu_custom_call" | custom-call | bytes 10485760 | tf_op jit(solution)/shard_map/pallas_call | solution.py:55
  923.1 255.9 %shard_map.382 = (bf16[1024,1024]{1,0:T(8,128)(2,1)}, bf16[1024,1024]{1,0:T(8,128)(2,1)}, bf16[1024,1024]{1,0:T(8,128)(2,1)}, bf16[1024,1024]{1,0:T(8,128)(2,1)}) custom-call(s32[4]{0:T(128)} %pad_add_fusion.me_ref, bf16[2,4,512,128]{3,2,1,0:T(8,128)(2,1)} %copy-done.23, bf16[2,4,512,128]{3,2,1,0:T(8,128)(2,1)} %collective-permute-done.37.refs_1_, ...), custom_call_target="tpu_custom_call" | custom-call | bytes 16777216 | tf_op jit(solution)/shard_map/pallas_call | solution.py:55
  1179.1 351.2 %shard_map.378 = (bf16[2816,1024]{1,0:T(8,128)(2,1)}, bf16[2816,1024]{1,0:T(8,128)(2,1)}) custom-call(s32[4]{0:T(128)} %pad_add_fusion.me_ref, bf16[2,4,704,128]{3,2,1,0:T(8,128)(2,1)} %pad_maximum_fusion.refs_0_, bf16[2,4,704,128]{3,2,1,0:T(8,128)(2,1)} %collective-permute-done.15.refs_1_, bf16[2,4,704,128]{3,2,1,0:T(8,128)(2,1)} %collective-permute-done.16.refs_2_, ...), custom_call_target="tpu_custom_call" | custom-call | bytes 23068672 | tf_op jit(solution)/shard_map/pallas_call | solution.py:55
  1558.3 24.7 shard_map.384.o_ref
  1591.8 351.2 %shard_map.386 = (bf16[2816,1024]{1,0:T(8,128)(2,1)}, bf16[2816,1024]{1,0:T(8,128)(2,1)}) custom-call(s32[4]{0:T(128)} %pad_add_fusion.me_ref, bf16[2,4,704,128]{3,2,1,0:T(8,128)(2,1)} %copy-done.16, bf16[2,4,704,128]{3,2,1,0:T(8,128)(2,1)} %collective-permute-done.48.refs_1_, bf16[2,4,704,128]{3,2,1,0:T(8,128)(2,1)} %copy-done.43, ...), custom_call_target="tpu_custom_call" | custom-call | bytes 23068672 | tf_op jit(solution)/shard_map/pallas_call | solution.py:55
  1962.9 15.9 shard_map.390
  1978.8 14.3 shard_map.391
  1997.9 18.6 shard_map.393
  2016.6 17.9 shard_map.394
  2037.2 15.9 shard_map.395
  2053.2 14.8 shard_map.396
  2105.3 15.8 shard_map.398
  2139.8 39.9 %psum.7 = f32[4,1024]{1,0:T(4,128)S(1)} all-reduce(f32[4,1024]{1,0:T(4,128)S(1)} %pad_maximum_fusion.40), channel_id=1, replica_groups=mesh['row'=8,'col'=4] {'row','col'}, use_global_device_ids=true, to_apply=%region_4.5 | all-reduce | flops 4096 | bytes 32768 | tf_op jit(solution)/shard_map/psum | solution.py:825
  2287.7 16.2 collective-permute-done.70
  2400.3 25.7 %collective-permute-done.98 = bf16[4,512,128]{2,1,0:T(8,128)(2,1)S(1)} collective-permute-done((bf16[4,512,128]{2,1,0:T(8,128)(2,1)S(1)}, bf16[4,512,128]{2,1,0:T(8,128)(2,1)S(1)}, u32[]{:S(2)}, u32[]{:S(2)}) %collective-permute-start.98) | collective-permute-done | bytes 524320 | tf_op jit(solution)/shard_map/ppermute | solution.py:618
  2485.7 14.4 collective-permute-done.77
  2528.2 14.9 collective-permute-done.82
  (662 shorter events, 726.8 us)
Async XLA Ops:
  20.0 111.6 %collective-permute-start.13 = (bf16[1408,128]{1,0:T(8,128)(2,1)S(1)}, bf16[1408,128]{1,0:T(8,128)(2,1)S(1)}, u32[]{:S(2)}, u32[]{:S(2)}) collective-permute-start(bf16[1408,128]{1,0:T(8,128)(2,1)S(1)} %pad_maximum_fusion.21), channel_id=1, source_target_pairs={{0,24},{1,25},{2,26},{3,27},{4,28},{5,29},{6,30},{7,31},{8,16},{9,... | collective-permute-start | bytes 1081352 | tf_op jit(solution)/shard_map/ppermute | solution.py:618
  23.8 108.9 %collective-permute-start.12 = (bf16[1408,128]{1,0:T(8,128)(2,1)S(1)}, bf16[1408,128]{1,0:T(8,128)(2,1)S(1)}, u32[]{:S(2)}, u32[]{:S(2)}) collective-permute-start(bf16[1408,128]{1,0:T(8,128)(2,1)S(1)} %pad_maximum_fusion.21), channel_id=1, source_target_pairs={{0,16},{1,17},{2,18},{3,19},{4,20},{5,21},{6,22},{7,23},{8,24},{9,... | collective-permute-start | bytes 1081352 | tf_op jit(solution)/shard_map/ppermute | solution.py:618
  24.4 109.9 %collective-permute-start.11 = (bf16[1408,128]{1,0:T(8,128)(2,1)S(1)}, bf16[1408,128]{1,0:T(8,128)(2,1)S(1)}, u32[]{:S(2)}, u32[]{:S(2)}) collective-permute-start(bf16[1408,128]{1,0:T(8,128)(2,1)S(1)} %pad_maximum_fusion.21), channel_id=1, source_target_pairs={{0,8},{1,9},{2,10},{3,11},{4,12},{5,13},{6,14},{7,15},{8,0},{9,1},... | collective-permute-start | bytes 1081352 | tf_op jit(solution)/shard_map/ppermute | solution.py:618
  194.4 45.2 %collective-permute-start.27 = (bf16[2,4,352,128]{3,2,1,0:T(8,128)(2,1)S(1)}, bf16[2,4,352,128]{3,2,1,0:T(8,128)(2,1)S(1)}, u32[]{:S(2)}, u32[]{:S(2)}) collective-permute-start(bf16[2,4,352,128]{3,2,1,0:T(8,128)(2,1)S(1)} %pad_maximum_fusion.9.refs_0_), channel_id=1, source_target_pairs={{0,1},{1,0},{2,3},{3,2},{4,5},{5,4},{6,7},{7,6},{8,9},{9,8},{10,11... | collective-permute-start | bytes 2162696 | tf_op jit(solution)/shard_map/ppermute | solution.py:618
  304.6 51.8 %collective-permute-start.20 = (bf16[2,4,704,128]{3,2,1,0:T(8,128)(2,1)}, bf16[2,4,704,128]{3,2,1,0:T(8,128)(2,1)}, u32[]{:S(2)}, u32[]{:S(2)}) collective-permute-start(bf16[2,4,704,128]{3,2,1,0:T(8,128)(2,1)} %pad_maximum_fusion.1.refs_4_), channel_id=1, source_target_pairs={{0,1},{1,0},{2,3},{3,2},{4,5},{5,4},{6,7},{7,6},{8,9},{9,8},{10,11... | collective-permute-start | bytes 4325384 | tf_op jit(solution)/shard_map/ppermute | solution.py:618
  305.5 70.3 %collective-permute-start.48 = (bf16[2,4,704,128]{3,2,1,0:T(8,128)(2,1)S(1)}, bf16[2,4,704,128]{3,2,1,0:T(8,128)(2,1)}, u32[]{:S(2)}, u32[]{:S(2)}) collective-permute-start(bf16[2,4,704,128]{3,2,1,0:T(8,128)(2,1)S(1)} %pad_maximum_fusion.2.refs_0_), channel_id=1, source_target_pairs={{0,4},{1,5},{2,6},{3,7},{4,0},{5,1},{6,2},{7,3},{8,12},{9,13},{10,... | collective-permute-start | bytes 4325384 | tf_op jit(solution)/shard_map/ppermute | solution.py:618
  309.6 75.6 %all-to-all-start.2 = ((bf16[8,64,1024]{2,1,0:T(8,128)(2,1)}), bf16[8,64,1024]{2,1,0:T(8,128)(2,1)S(1)}, u32[]{:S(2)}, u32[]{:S(2)}) async-start(bf16[8,64,1024]{2,1,0:T(8,128)(2,1)} %bitcast.486), calls=%async_computation.2 | async-start | bytes 2097152 | tf_op jit(solution)/shard_map/all_to_all | solution.py:758
  344.9 571.7 %collective-permute-start.52 = (bf16[2,4,704,128]{3,2,1,0:T(8,128)(2,1)}, bf16[2,4,704,128]{3,2,1,0:T(8,128)(2,1)}, u32[]{:S(2)}, u32[]{:S(2)}) collective-permute-start(bf16[2,4,704,128]{3,2,1,0:T(8,128)(2,1)} %pad_maximum_fusion.3.refs_4_), channel_id=1, source_target_pairs={{0,2},{1,3},{2,0},{3,1},{4,6},{5,7},{6,4},{7,5},{8,10},{9,11},{10,... | collective-permute-start | bytes 4325384 | tf_op jit(solution)/shard_map/ppermute | solution.py:618
  345.5 572.2 %collective-permute-start.17 = (bf16[2,4,704,128]{3,2,1,0:T(8,128)(2,1)}, bf16[2,4,704,128]{3,2,1,0:T(8,128)(2,1)}, u32[]{:S(2)}, u32[]{:S(2)}) collective-permute-start(bf16[2,4,704,128]{3,2,1,0:T(8,128)(2,1)} %collective-permute-done.15.refs_1_), channel_id=1, source_target_pairs={{0,1},{1,0},{2,3},{3,2},{4,5},{5,4},{6,7},{7,6},{8,9},{9,8},{10,11... | collective-permute-start | bytes 4325384 | tf_op jit(solution)/shard_map/ppermute | solution.py:618
  345.5 833.6 %collective-permute-start.21 = (bf16[2,4,704,128]{3,2,1,0:T(8,128)(2,1)}, bf16[2,4,704,128]{3,2,1,0:T(8,128)(2,1)}, u32[]{:S(2)}, u32[]{:S(2)}) collective-permute-start(bf16[2,4,704,128]{3,2,1,0:T(8,128)(2,1)} %collective-permute-done.19.refs_5_), channel_id=1, source_target_pairs={{0,1},{1,0},{2,3},{3,2},{4,5},{5,4},{6,7},{7,6},{8,9},{9,8},{10,11... | collective-permute-start | bytes 4325384 | tf_op jit(solution)/shard_map/ppermute | solution.py:618
  356.3 560.9 %collective-permute-start.39 = (bf16[2,4,512,128]{3,2,1,0:T(8,128)(2,1)}, bf16[2,4,512,128]{3,2,1,0:T(8,128)(2,1)}, u32[]{:S(2)}, u32[]{:S(2)}) collective-permute-start(bf16[2,4,512,128]{3,2,1,0:T(8,128)(2,1)} %collective-permute-done.37.refs_1_), channel_id=1, source_target_pairs={{0,1},{1,0},{2,3},{3,2},{4,5},{5,4},{6,7},{7,6},{8,9},{9,8},{10,11... | collective-permute-start | bytes 3145736 | tf_op jit(solution)/shard_map/ppermute | solution.py:618
  375.7 541.6 %collective-permute-start.43 = (bf16[2,4,512,128]{3,2,1,0:T(8,128)(2,1)}, bf16[2,4,512,128]{3,2,1,0:T(8,128)(2,1)}, u32[]{:S(2)}, u32[]{:S(2)}) collective-permute-start(bf16[2,4,512,128]{3,2,1,0:T(8,128)(2,1)} %collective-permute-done.41.refs_5_), channel_id=1, source_target_pairs={{0,1},{1,0},{2,3},{3,2},{4,5},{5,4},{6,7},{7,6},{8,9},{9,8},{10,11... | collective-permute-start | bytes 3145736 | tf_op jit(solution)/shard_map/ppermute | solution.py:618
  916.6 672.0 %collective-permute-start.49 = (bf16[2,4,704,128]{3,2,1,0:T(8,128)(2,1)S(1)}, bf16[2,4,704,128]{3,2,1,0:T(8,128)(2,1)S(1)}, u32[]{:S(2)}, u32[]{:S(2)}) collective-permute-start(bf16[2,4,704,128]{3,2,1,0:T(8,128)(2,1)S(1)} %pad_maximum_fusion.2.refs_0_), channel_id=1, source_target_pairs={{0,1},{1,0},{2,3},{3,2},{4,5},{5,4},{6,7},{7,6},{8,9},{9,8},{10,11... | collective-permute-start | bytes 4325384 | tf_op jit(solution)/shard_map/ppermute | solution.py:618
  917.2 671.4 %collective-permute-start.53 = (bf16[2,4,704,128]{3,2,1,0:T(8,128)(2,1)}, bf16[2,4,704,128]{3,2,1,0:T(8,128)(2,1)S(1)}, u32[]{:S(2)}, u32[]{:S(2)}) collective-permute-start(bf16[2,4,704,128]{3,2,1,0:T(8,128)(2,1)} %pad_maximum_fusion.3.refs_4_), channel_id=1, source_target_pairs={{0,1},{1,0},{2,3},{3,2},{4,5},{5,4},{6,7},{7,6},{8,9},{9,8},{10,11... | collective-permute-start | bytes 4325384 | tf_op jit(solution)/shard_map/ppermute | solution.py:618
  917.3 671.3 %collective-permute-start.50 = (bf16[2,4,704,128]{3,2,1,0:T(8,128)(2,1)}, bf16[2,4,704,128]{3,2,1,0:T(8,128)(2,1)S(1)}, u32[]{:S(2)}, u32[]{:S(2)}) collective-permute-start(bf16[2,4,704,128]{3,2,1,0:T(8,128)(2,1)} %collective-permute-done.48.refs_1_), channel_id=1, source_target_pairs={{0,1},{1,0},{2,3},{3,2},{4,5},{5,4},{6,7},{7,6},{8,9},{9,8},{10,11... | collective-permute-start | bytes 4325384 | tf_op jit(solution)/shard_map/ppermute | solution.py:618
  917.7 670.9 %collective-permute-start.54 = (bf16[2,4,704,128]{3,2,1,0:T(8,128)(2,1)}, bf16[2,4,704,128]{3,2,1,0:T(8,128)(2,1)S(1)}, u32[]{:S(2)}, u32[]{:S(2)}) collective-permute-start(bf16[2,4,704,128]{3,2,1,0:T(8,128)(2,1)} %collective-permute-done.52.refs_5_), channel_id=1, source_target_pairs={{0,1},{1,0},{2,3},{3,2},{4,5},{5,4},{6,7},{7,6},{8,9},{9,8},{10,11... | collective-permute-start | bytes 4325384 | tf_op jit(solution)/shard_map/ppermute | solution.py:618
  2094.7 120.4 %all-to-all-start.1 = ((bf16[8,64,1024]{2,1,0:T(8,128)(2,1)}), bf16[8,64,1024]{2,1,0:T(8,128)(2,1)S(1)}, u32[]{:S(2)}, u32[]{:S(2)}) async-start(bf16[8,64,1024]{2,1,0:T(8,128)(2,1)} %bitcast.112), calls=%async_computation.1 | async-start | bytes 2097152 | tf_op jit(solution)/shard_map/all_to_all | solution.py:758
  2182.5 46.1 %collective-permute-start.69 = (bf16[2,2,4,384,128]{4,3,2,1,0:T(8,128)(2,1)}, bf16[2,2,4,384,128]{4,3,2,1,0:T(8,128)(2,1)}, u32[]{:S(2)}, u32[]{:S(2)}) collective-permute-start(bf16[2,2,4,384,128]{4,3,2,1,0:T(8,128)(2,1)} %slice_bitcast_fusion.6), channel_id=1, source_target_pairs={{0,1},{1,0},{2,3},{3,2},{4,5},{5,4},{6,7},{7,6},{8,9},{9,8},{10,11... | collective-permute-start | bytes 4718600 | tf_op jit(solution)/shard_map/ppermute | solution.py:618
  2208.1 152.0 %collective-permute-start.75 = (bf16[2,2,4,704,128]{4,3,2,1,0:T(8,128)(2,1)}, bf16[2,2,4,704,128]{4,3,2,1,0:T(8,128)(2,1)}, u32[]{:S(2)}, u32[]{:S(2)}) collective-permute-start(bf16[2,2,4,704,128]{4,3,2,1,0:T(8,128)(2,1)} %slice_bitcast_fusion.3), channel_id=1, source_target_pairs={{0,1},{1,0},{2,3},{3,2},{4,5},{5,4},{6,7},{7,6},{8,9},{9,8},{10,11... | collective-permute-start | bytes 8650760 | tf_op jit(solution)/shard_map/ppermute | solution.py:618
  2210.2 45.1 %collective-permute-start.96 = (bf16[2,2,4,512,128]{4,3,2,1,0:T(8,128)(2,1)}, bf16[2,2,4,512,128]{4,3,2,1,0:T(8,128)(2,1)}, u32[]{:S(2)}, u32[]{:S(2)}) collective-permute-start(bf16[2,2,4,512,128]{4,3,2,1,0:T(8,128)(2,1)} %slice_bitcast_fusion.4), channel_id=1, source_target_pairs={{0,1},{1,0},{2,3},{3,2},{4,5},{5,4},{6,7},{7,6},{8,9},{9,8},{10,11... | collective-permute-start | bytes 6291464 | tf_op jit(solution)/shard_map/ppermute | solution.py:618
  2226.7 137.1 %collective-permute-start.78 = (bf16[2,2,4,704,128]{4,3,2,1,0:T(8,128)(2,1)}, bf16[2,2,4,704,128]{4,3,2,1,0:T(8,128)(2,1)}, u32[]{:S(2)}, u32[]{:S(2)}) collective-permute-start(bf16[2,2,4,704,128]{4,3,2,1,0:T(8,128)(2,1)} %slice_bitcast_fusion.2), channel_id=1, source_target_pairs={{0,1},{1,0},{2,3},{3,2},{4,5},{5,4},{6,7},{7,6},{8,9},{9,8},{10,11... | collective-permute-start | bytes 8650760 | tf_op jit(solution)/shard_map/ppermute | solution.py:618
  2321.6 45.9 %collective-permute-start.102 = (bf16[2,2,4,704,128]{4,3,2,1,0:T(8,128)(2,1)S(1)}, bf16[2,2,4,704,128]{4,3,2,1,0:T(8,128)(2,1)S(1)}, u32[]{:S(2)}, u32[]{:S(2)}) collective-permute-start(bf16[2,2,4,704,128]{4,3,2,1,0:T(8,128)(2,1)S(1)} %copy-done.26), channel_id=1, source_target_pairs={{0,1},{1,0},{2,3},{3,2},{4,5},{5,4},{6,7},{7,6},{8,9},{9,8},{10,11... | collective-permute-start | bytes 8650760 | tf_op jit(solution)/shard_map/ppermute | solution.py:618
  2382.4 71.4 %collective-permute-start.76 = (bf16[2,4,704,128]{3,2,1,0:T(8,128)(2,1)}, bf16[2,4,704,128]{3,2,1,0:T(8,128)(2,1)}, u32[]{:S(2)}, u32[]{:S(2)}) collective-permute-start(bf16[2,4,704,128]{3,2,1,0:T(8,128)(2,1)} %slice_bitcast_fusion.13), channel_id=1, source_target_pairs={{0,2},{1,3},{2,0},{3,1},{4,6},{5,7},{6,4},{7,5},{8,10},{9,11},{10,... | collective-permute-start | bytes 4325384 | tf_op jit(solution)/shard_map/ppermute | solution.py:618
  2386.8 70.9 %collective-permute-start.79 = (bf16[2,4,704,128]{3,2,1,0:T(8,128)(2,1)}, bf16[2,4,704,128]{3,2,1,0:T(8,128)(2,1)}, u32[]{:S(2)}, u32[]{:S(2)}) collective-permute-start(bf16[2,4,704,128]{3,2,1,0:T(8,128)(2,1)} %slice_bitcast_fusion.11), channel_id=1, source_target_pairs={{0,4},{1,5},{2,6},{3,7},{4,0},{5,1},{6,2},{7,3},{8,12},{9,13},{10,... | collective-permute-start | bytes 4325384 | tf_op jit(solution)/shard_map/ppermute | solution.py:618
  (191 other events, 4691.2 us)
Sparse Core Ops, SparseCore 0:
  253.6 2.9 sort.60.cloned.1.call-done
  (1 shorter events, 0.0 us)

commit v2 on v1

v2 whole, which is shorter than its diff:
```python
import functools

import jax
import jax.numpy as jnp
from jax import lax
from jax.experimental import pallas as pl
from jax.experimental.pallas import tpu as pltpu
from jax.sharding import Mesh, PartitionSpec as P

HEADS = 16
FEAT = 16
HEAD_DIM = 64
WINDOW = 64
MAX_LEN = 256
D = 1024
T = 512
HALF = 256
EPS = 1e-05
NEG = -1e30
ROWS = 8
COLS = 4
FB = 344
FBP = 352
FFP = ROWS * FBP
FC = FFP // COLS

bf16, f32, i32 = jnp.bfloat16, jnp.float32, jnp.int32
NN, NT, TN = ((1,), (0,)), ((1,), (1,)), ((0,), (0,))


def dot(a, b, dims):
    return lax.dot_general(a, b, (dims, ((), ())), preferred_element_type=f32)


def call(body, grid, ins, outs, scratch=(), flops=0, prefetch=None):
    extra = 0 if prefetch is None else 1

    def spec(block, index):
        if block is None:
            return pl.BlockSpec(memory_space=pl.ANY)
        return pl.BlockSpec(block, index)

    in_specs, args = [], []
    for item in ins:
        if not isinstance(item, tuple):
            nd = item.ndim
            item = (item, item.shape, functools.partial(lambda n, *_: (0,) * n, nd))
        args.append(item[0])
        in_specs.append(spec(item[1], item[2]))
    out_specs = [spec(o[2], o[3]) for o in outs]
    out_shape = [jax.ShapeDtypeStruct(o[0], o[1]) for o in outs]
    moved = sum(a.size * a.dtype.itemsize for a in args)
    moved += sum(s.size * s.dtype.itemsize for s in out_shape)
    cost = pl.CostEstimate(flops=int(flops), bytes_accessed=int(moved), transcendentals=0)
    got = pl.pallas_call(
        body,
        out_shape=out_shape,
        grid_spec=pltpu.PrefetchScalarGridSpec(
            num_scalar_prefetch=extra,
            grid=grid,
            in_specs=in_specs,
            out_specs=out_specs,
            scratch_shapes=list(scratch),
        ),
        compiler_params=pltpu.CompilerParams(vmem_limit_bytes=56 * 2**20),
        cost_estimate=cost,
    )(*(([prefetch] if extra else []) + args))
    return got


def whole_map(*shape):
    zeros = (0,) * len(shape)
    return lambda *_: zeros


def norm_factor(h):
    return lax.rsqrt(jnp.mean(h * h, axis=-1, keepdims=True) + EPS)


class Strips:
    def __init__(self, half, swapped, at, n):
        self.bufs, self.swapped, self.at, self.n = half, swapped, at, n

    def ins(self):
        return [(b, None, None) for b in self.bufs]

    def scratch(self):
        return [pltpu.VMEM((2, 2, 2, 4, self.n, 128), bf16), pltpu.SemaphoreType.DMA((2, 2, 2))]

    def start(self, refs, box, sems):
        order = [(core, x, y) for core in range(2) for x in range(2) for y in range(2)]
        for core, x, y in order:
            hi, lo = (x, y) if self.swapped else (y, x)
            src = refs[core * 2 + hi].at[lo]
            if self.n != self.bufs[0].shape[2]:
                src = src.at[:, pl.ds(self.at, self.n)]
            pltpu.make_async_copy(src, box.at[core, hi, lo], sems.at[core, hi, lo]).start()

    def wait(self, box, sems, core, x):
        for y in range(2):
            hi, lo = (x, y) if self.swapped else (y, x)
            there = box.at[core, hi, lo]
            pltpu.make_async_copy(there, there, sems.at[core, hi, lo]).wait()

    def wait_all(self, box, sems):
        for core in range(2):
            for x in range(2):
                self.wait(box, sems, core, x)

    def piece(self, box, z, y, x, core):
        return box.at[core, x, y, z] if self.swapped else box.at[core, y, x, z]


BLOCKS = [(z, y) for z in range(4) for y in range(2)]
PLACES = [(x, core) for x in range(2) for core in range(2)]


def step_place(i):
    return i % 2, i // 2


def step_col(i, me):
    return ((i % 2) * 2 + i // 2) ^ me[1]


def regroup(dst_ref, src_ref, count, me):
    width = D // count
    for j in range(count):
        at = pl.multiple_of((j ^ me) * width, 128)
        dst_ref[:, j * width : (j + 1) * width] = src_ref[:, pl.ds(at, width)]


class Kernel:
    def __init__(self, n_in, strips, n_out):
        self.n_in, self.strips, self.n_out = n_in, strips, n_out

    def split(self, refs):
        n, m = self.n_in, len(self.strips)
        ins, refs = refs[:n], refs[n:]
        srcs, refs = refs[: 4 * m], refs[4 * m :]
        outs, refs = refs[: self.n_out], refs[self.n_out :]
        boxes, rest = refs[: 2 * m], refs[2 * m :]
        hold = [(s, srcs[4 * j : 4 * j + 4], boxes[2 * j], boxes[2 * j + 1]) for j, s in enumerate(self.strips)]
        return ins, hold, outs, rest

    def ins(self):
        return [i for s in self.strips for i in s.ins()]

    def scratch(self):
        return [i for s in self.strips for i in s.scratch()]


def start_all(hold):
    for s, srcs, box, sems in hold:
        s.start(srcs, box, sems)


def col_block(s, box, x, core):
    strips = []
    for j in range(s.n // 128):
        strips.append(jnp.concatenate([s.piece(box, z, y, x, core)[j * 128 : (j + 1) * 128, :] for z, y in BLOCKS], axis=0))
    return strips[0] if len(strips) == 1 else jnp.concatenate(strips, axis=1)


def norm_proj(me, h, gain, strips):
    n = len(strips)
    kern = Kernel(2, strips, n + 1)

    def body(me_ref, *refs):
        (h_ref, gain_ref), hold, (xa_ref, *outs), (xr_ref,) = kern.split(refs)
        i = pl.program_id(0)

        @pl.when(i == 0)
        def _():
            start_all(hold)
            hv = h_ref[...].astype(f32)
            xa_ref[...] = (hv * norm_factor(hv) * gain_ref[...]).astype(bf16)
            regroup(xr_ref, xa_ref, ROWS, me_ref[0])

        x, core = step_place(i)
        for (s, _, box, sems), o_ref in zip(hold, outs):
            s.wait(box, sems, core, x)
            o_ref[...] = dot(xr_ref[...], col_block(s, box, x, core), NN).astype(bf16)

    outs = [((T, D), bf16, (T, D), whole_map(T, D))]
    for s in strips:
        outs.append(((T, s.n * COLS), bf16, (T, s.n), lambda i, me: (0, step_col(i, me))))
    total = sum(s.n * COLS for s in strips)
    return call(
        body, (COLS,), [h, gain.reshape(1, D)] + kern.ins(), outs,
        scratch=kern.scratch() + [pltpu.VMEM((T, D), bf16)], flops=2 * T * D * total, prefetch=me,
    )


def lanes(shape, width):
    return lax.broadcasted_iota(i32, shape, len(shape) - 1) // width


def fill_mask(mask_ref, seg_q, seg_k, live_k, q_axis, window):
    q = lax.broadcasted_iota(i32, (T, T), q_axis)
    k = lax.broadcasted_iota(i32, (T, T), 1 - q_axis)
    ok = (k <= q) & (k > q - window) & (seg_q == seg_k) & ((live_k > 0) | (k == q))
    mask_ref[...] = jnp.where(ok, 1.0, 0.0)


def based_fwd(qk, v, seg_row, seg_col, live_row):
    def body(qk_ref, v_ref, sr_ref, sc_ref, lr_ref, o_ref, ou_ref, rden_ref, mask_ref):
        @pl.when(pl.program_id(0) == 0)
        def _():
            fill_mask(mask_ref, sc_ref[...], sr_ref[...], lr_ref[...], 0, MAX_LEN)

        q4, k4 = qk_ref[:, 0:64], qk_ref[:, 64:128]
        qlane = lanes((T, 64), FEAT)
        first = lanes((HALF, 128), HEAD_DIM) == 0
        scaled = q4.astype(f32) * (FEAT**-0.5)
        for pair in range(2):
            v2 = v_ref[:, pair * 128 : pair * 128 + 128]
            for tb in range(2):
                t0, s1 = tb * HALF, (tb + 1) * HALF
                got = []
                for e in range(2):
                    qm = jnp.where(qlane == pair * 2 + e, scaled, 0.0).astype(bf16)
                    a = dot(qm[t0 : t0 + HALF], k4[0:s1], NT)
                    p = (1.0 + a * (1.0 + 0.5 * a)) * mask_ref[t0 : t0 + HALF, 0:s1]
                    den = jnp.sum(p, axis=-1, keepdims=True)
                    got.append((dot(p.astype(bf16), v2[0:s1], NN), den))
                rden = 1.0 / jnp.where(first, got[0][1], got[1][1])
                ou = jnp.where(first, got[0][0], got[1][0]) * rden
                at = (slice(t0, t0 + HALF), slice(pair * 128, pair * 128 + 128))
                ou_ref[at] = ou
                rden_ref[at] = rden
                o_ref[at] = ou.astype(bf16)

    wide = (T, 256)
    col = lambda c: (0, c)
    return call(
        body,
        (4,),
        [(qk, (T, 128), col), (v, wide, col), seg_row, seg_col, live_row],
        [((T, D), bf16, wide, col), ((T, D), f32, wide, col), ((T, D), f32, wide, col)],
        scratch=[pltpu.VMEM((T, T), f32)],
        flops=HEADS * T * T * 2 * 192,
    )


def based_bwd(qk, v, dou, ou, rden, seg_row, seg_col, live_col):
    def body(qk_ref, v_ref, dou_ref, ou_ref, rden_ref, sr_ref, sc_ref, lc_ref, dqk_ref, dv_ref, mask_ref, dk_ref, dva_ref):
        @pl.when(pl.program_id(0) == 0)
        def _():
            fill_mask(mask_ref, sr_ref[...], sc_ref[...], lc_ref[...], 1, MAX_LEN)

        q4, k4 = qk_ref[:, 0:64], qk_ref[:, 64:128]
        qlane = lanes((T, 64), FEAT)
        q_scaled = q4.astype(f32) * (FEAT**-0.5)
        k_scaled = k4.astype(f32) * (FEAT**-0.5)
        vlane = lanes((T, 128), HEAD_DIM)
        dnum_f = dou_ref[...] * rden_ref[...]
        term = dnum_f * ou_ref[...]
        high = term.astype(bf16)
        low = (term - high.astype(f32)).astype(bf16)
        pick = jnp.where(
            lax.broadcasted_iota(i32, (8, 256), 0) == lanes((8, 256), HEAD_DIM), 1.0, 0.0
        ).astype(bf16)
        dden = -(dot(pick, high, NT) + dot(pick, low, NT))
        dk_ref[...] = jnp.zeros((T, 64), f32)
        dva_ref[...] = jnp.zeros((T, 256), f32)
        dq = [jnp.zeros((HALF, 64), f32), jnp.zeros((HALF, 64), f32)]
        for pair in range(2):
            cols = slice(pair * 128, pair * 128 + 128)
            v2 = v_ref[:, cols]
            for e in range(2):
                head = pair * 2 + e
                qm = jnp.where(qlane == head, q_scaled, 0.0).astype(bf16)
                km = jnp.where(qlane == head, k_scaled, 0.0).astype(bf16)
                dn = jnp.where(vlane == e, dnum_f[:, cols], 0.0).astype(bf16)
                for tb in range(2):
                    t0, s1 = tb * HALF, (tb + 1) * HALF
                    at = slice(t0, t0 + HALF)
                    a = dot(k4[0:s1], qm[at], NT)
                    m = mask_ref[0:s1, at]
                    p = (1.0 + a * (1.0 + 0.5 * a)) * m
                    dp = dot(v2[0:s1], dn[at], NT) + dden[head : head + 1, at]
                    da = (dp * m * (1.0 + a)).astype(bf16)
                    dk_ref[0:s1, :] += dot(da, qm[at], NN)
                    dva_ref[0:s1, cols] += dot(p.astype(bf16), dn[at], NN)
                    dq[tb] += dot(da, km[0:s1], TN)
        for tb in range(2):
            at = slice(tb * HALF, tb * HALF + HALF)
            dqk_ref[at, 0:64] = dq[tb].astype(bf16)
        dqk_ref[:, 64:128] = dk_ref[...].astype(bf16)
        dv_ref[...] = dva_ref[...].astype(bf16)

    wide = (T, 256)
    col = lambda c: (0, c)
    return call(
        body,
        (4,),
        [(qk, (T, 128), col), (v, wide, col), (dou, wide, col), (ou, wide, col), (rden, wide, col), seg_row, seg_col, live_col],
        [((T, 512), bf16, (T, 128), col), ((T, D), bf16, wide, col)],
        scratch=[pltpu.VMEM((T, T), f32), pltpu.VMEM((T, 64), f32), pltpu.VMEM((T, 256), f32)],
        flops=HEADS * T * T * 2 * 480,
    )


SPAN = ((0, HALF), (HALF - WINDOW, T))


def window_fwd(q, k, v, seg_row, seg_col, live_row):
    def body(q_ref, k_ref, v_ref, sr_ref, sc_ref, lr_ref, o_ref, mask_ref):
        @pl.when(pl.program_id(0) == 0)
        def _():
            fill_mask(mask_ref, sc_ref[...], sr_ref[...], lr_ref[...], 0, WINDOW)

        first = lanes((HALF, 128), HEAD_DIM) == 0
        qlane = lanes((T, 128), HEAD_DIM)
        scaled = q_ref[...].astype(f32) * (HEAD_DIM**-0.5)
        for tb in range(2):
            t0 = tb * HALF
            s0, s1 = SPAN[tb]
            ok = mask_ref[t0 : t0 + HALF, s0:s1] > 0.5
            got = []
            for e in range(2):
                qm = jnp.where(qlane == e, scaled, 0.0).astype(bf16)
                c = dot(qm[t0 : t0 + HALF], k_ref[s0:s1, :], NT)
                c = jnp.where(ok, c, NEG)
                w = jnp.exp(c - jnp.max(c, axis=-1, keepdims=True))
                w = w * (1.0 / jnp.sum(w, axis=-1, keepdims=True))
                got.append(dot(w.astype(bf16), v_ref[s0:s1, :], NN))
            o_ref[t0 : t0 + HALF, :] = jnp.where(first, got[0], got[1]).astype(bf16)

    blk = (T, 128)
    col = lambda c: (0, c)
    return call(
        body,
        (8,),
        [(q, blk, col), (k, blk, col), (v, blk, col), seg_row, seg_col, live_row],
        [((T, D), bf16, blk, col)],
        scratch=[pltpu.VMEM((T, T), f32)],
        flops=HEADS * T * T * 2 * 192,
    )[0]


def window_bwd(q, k, v, dor, seg_row, seg_col, live_col):
    def body(q_ref, k_ref, v_ref, do_ref, sr_ref, sc_ref, lc_ref, dq_ref, dk_ref, dv_ref, mask_ref, dka_ref, dva_ref):
        @pl.when(pl.program_id(0) == 0)
        def _():
            fill_mask(mask_ref, sr_ref[...], sc_ref[...], lc_ref[...], 1, WINDOW)

        lane = lanes((T, 128), HEAD_DIM)
        q_scaled = q_ref[...].astype(f32) * (HEAD_DIM**-0.5)
        k_scaled = k_ref[...].astype(f32) * (HEAD_DIM**-0.5)
        do = do_ref[...]
        dka_ref[...] = jnp.zeros((T, 128), f32)
        dva_ref[...] = jnp.zeros((T, 128), f32)
        for tb in range(2):
            at = slice(tb * HALF, tb * HALF + HALF)
            s0, s1 = SPAN[tb]
            ok = mask_ref[s0:s1, at] > 0.5
            dq = jnp.zeros((HALF, 128), f32)
            for e in range(2):
                qm = jnp.where(lane == e, q_scaled, 0.0).astype(bf16)
                km = jnp.where(lane == e, k_scaled, 0.0).astype(bf16)
                dm = jnp.where(lane == e, do, jnp.zeros_like(do))
                c = dot(k_ref[s0:s1, :], qm[at], NT)
                c = jnp.where(ok, c, NEG)
                w = jnp.exp(c - jnp.max(c, axis=0, keepdims=True))
                w = w * (1.0 / jnp.sum(w, axis=0, keepdims=True))
                dw = dot(v_ref[s0:s1, :], dm[at], NT)
                ds = (w * (dw - jnp.sum(w * dw, axis=0, keepdims=True))).astype(bf16)
                dka_ref[s0:s1, :] += dot(ds, qm[at], NN)
                dva_ref[s0:s1, :] += dot(w.astype(bf16), dm[at], NN)
                dq += dot(ds, km[s0:s1], TN)
            dq_ref[at, :] = dq.astype(bf16)
        dk_ref[...] = dka_ref[...].astype(bf16)
        dv_ref[...] = dva_ref[...].astype(bf16)

    blk = (T, 128)
    col = lambda c: (0, c)
    return call(
        body,
        (8,),
        [(q, blk, col), (k, blk, col), (v, blk, col), (dor, blk, col), seg_row, seg_col, live_col],
        [((T, D), bf16, blk, col)] * 3,
        scratch=[pltpu.VMEM((T, T), f32), pltpu.VMEM((T, 128), f32), pltpu.VMEM((T, 128), f32)],
        flops=HEADS * T * T * 2 * 480,
    )


def attn_out(me, h, o, strip, gain):
    kern = Kernel(3, [strip], 2)

    def body(me_ref, *refs):
        (h_ref, o_ref, gain_ref), hold, (hm_ref, xf_ref), (or_ref,) = kern.split(refs)
        i = pl.program_id(0)

        @pl.when(i == 0)
        def _():
            start_all(hold)
            regroup(or_ref, o_ref, ROWS, me_ref[0])

        x, core = step_place(i)
        s, _, box, sems = hold[0]
        s.wait(box, sems, core, x)
        at = pl.ds(pl.multiple_of(step_col(i, me_ref) * 256, 256), 256)
        hm_ref[:, at] = h_ref[:, at].astype(f32) + dot(or_ref[...], col_block(s, box, x, core), NN)

        @pl.when(i == COLS - 1)
        def _():
            hm = hm_ref[...]
            xf_ref[...] = (hm * norm_factor(hm) * gain_ref[...]).astype(bf16)

    full = whole_map(T, D)
    return call(
        body, (COLS,), [h, o, gain.reshape(1, D)] + kern.ins(),
        [((T, D), f32, (T, D), full), ((T, D), bf16, (T, D), full)],
        scratch=kern.scratch() + [pltpu.VMEM((T, D), bf16)], flops=2 * T * D * D, prefetch=me,
    )


def hidden_block(s, box, x, core):
    return jnp.concatenate([s.piece(box, z, y, x, core)[...] for z, y in BLOCKS], axis=1)


def gate_up(me, xf, w_gate, w_up):
    kern = Kernel(1, [w_gate, w_up], 3)

    def body(me_ref, *refs):
        (xf_ref,), hold, (g_ref, u_ref, hid_ref), (xr_ref,) = kern.split(refs)
        i = pl.program_id(0)

        @pl.when(i == 0)
        def _():
            start_all(hold)
            regroup(xr_ref, xf_ref, ROWS, me_ref[0])

        x, core = step_place(i)
        got = []
        for s, _, box, sems in hold:
            s.wait(box, sems, core, x)
            got.append(dot(hidden_block(s, box, x, core), xr_ref[...], NT))
        g, u = got
        g_ref[...] = g.astype(bf16)
        u_ref[...] = u.astype(bf16)
        hid_ref[...] = (g * (1.0 / (1.0 + jnp.exp(-g))) * u).astype(bf16)

    row = lambda i, me: (step_col(i, me), 0)
    return call(
        body, (COLS,), [xf] + kern.ins(), [((FFP, T), bf16, (FC, T), row)] * 3,
        scratch=kern.scratch() + [pltpu.VMEM((T, D), bf16)], flops=4 * T * D * FFP, prefetch=me,
    )


def down_rows(me_ref, hold, z):
    (s1, _, box1, _), (s2, _, box2, _) = hold
    halves = []
    for y in range(2):
        yr = y ^ me_ref[0]
        parts = []
        for x, core in PLACES:
            parts += [s1.piece(box1, z, yr, x, core)[...], s2.piece(box2, z, yr, x, core)[...]]
        halves.append(jnp.concatenate(parts, axis=1))
    return jnp.concatenate(halves, axis=0)


def down(me, hm, hid, strips):
    kern = Kernel(2, strips, 1)

    def body(me_ref, *refs):
        (hm_ref, hid_ref), hold, (h_ref,), (acc_ref,) = kern.split(refs)
        i = pl.program_id(0)

        @pl.when(i == 0)
        def _():
            start_all(hold)
            regroup(acc_ref, hm_ref, COLS, me_ref[1])
            for s, _, box, sems in hold:
                s.wait_all(box, sems)

        acc_ref[...] += dot(hid_ref[...], down_rows(me_ref, hold, i), TN)

        @pl.when(i == COLS - 1)
        def _():
            regroup(h_ref, acc_ref, COLS, me_ref[1])

    return call(
        body, (COLS,), [hm, (hid, (FC, T), lambda i, me: (i, 0))] + kern.ins(),
        [((T, D), f32, (T, D), whole_map(T, D))],
        scratch=kern.scratch() + [pltpu.VMEM((T, D), f32)], flops=2 * T * D * FFP, prefetch=me,
    )[0]


def down_bwd(me, bd, strips, hid, g, u):
    kern = Kernel(4, strips, 4)

    def body(me_ref, *refs):
        (bd_ref, hid_ref, g_ref, u_ref), hold, (dg_ref, du_ref, p1_ref, p2_ref), (br_ref,) = kern.split(refs)
        i = pl.program_id(0)

        @pl.when(i == 0)
        def _():
            start_all(hold)
            regroup(br_ref, bd_ref, COLS, me_ref[1])

        bdv = br_ref[...].astype(bf16)
        gwd = dot(hid_ref[...], bdv, NN).astype(bf16)
        for x, core in PLACES:
            at = (x * 2 + core) * 256
            for y in range(2):
                yr = y ^ me_ref[0]
                rows = slice(y * FBP, (y + 1) * FBP)
                p1_ref[core, x, yr, 0] = gwd[rows, at : at + 128]
                p2_ref[core, yr, x, 0] = gwd[rows, at + 128 : at + 256]

        @pl.when(i == 0)
        def _():
            for s, _, box, sems in hold:
                s.wait_all(box, sems)

        dhid = dot(down_rows(me_ref, hold, i), bdv, NT)
        gv, uv = g_ref[...].astype(f32), u_ref[...].astype(f32)
        sig = 1.0 / (1.0 + jnp.exp(-gv))
        act = gv * sig
        du_ref[...] = (dhid * act).astype(bf16)
        dg_ref[...] = (dhid * uv * (sig + act * (1.0 - sig))).astype(bf16)

    row = lambda i, me: (i, 0)
    hblk = (FC, T)
    pieces = ((2, 2, 2, 4, FBP, 128), bf16, (2, 2, 2, 1, FBP, 128), lambda i, me: (0, 0, 0, i, 0, 0))
    return call(
        body, (COLS,), [bd, (hid, hblk, row), (g, hblk, row), (u, hblk, row)] + kern.ins(),
        [((FFP, T), bf16, hblk, row), ((FFP, T), bf16, hblk, row), pieces, pieces],
        scratch=kern.scratch() + [pltpu.VMEM((T, D), bd.dtype)], flops=4 * T * D * FFP, prefetch=me,
    )


def piece_specs(n1, n2):
    one = ((2, 2, 2, 4, n1, 128), bf16, (1, 1, 2, 4, n1, 128), lambda i, me: (i // 2, i % 2, 0, 0, 0, 0))
    two = ((2, 2, 2, 4, n2, 128), bf16, (1, 2, 1, 4, n2, 128), lambda i, me: (i // 2, 0, i % 2, 0, 0, 0))
    return [one, two]


def gate_up_bwd(me, xf, dg, du):
    def body(me_ref, xf_ref, dg_ref, du_ref, p1_ref, p2_ref, xr_ref):
        @pl.when(pl.program_id(0) == 0)
        def _():
            regroup(xr_ref, xf_ref, ROWS, me_ref[0])

        gwg = dot(dg_ref[...], xr_ref[...], NN).astype(bf16)
        gwu = dot(du_ref[...], xr_ref[...], NN).astype(bf16)
        for r, (z, y) in enumerate(BLOCKS):
            p1_ref[0, 0, y, z] = gwg[:, r * 128 : (r + 1) * 128]
            p2_ref[0, y, 0, z] = gwu[:, r * 128 : (r + 1) * 128]

    row = lambda i, me: (step_col(i, me), 0)
    return call(
        body, (COLS,), [xf, (dg, (FC, T), row), (du, (FC, T), row)], piece_specs(FC, FC),
        scratch=[pltpu.VMEM((T, D), bf16)], flops=4 * T * D * FFP, prefetch=me,
    )


def norm_bwd(dx, h, gain, g):
    rf = norm_factor(h)
    hr = h * rf
    dgain = jnp.sum(dx * hr, axis=0, keepdims=True)
    gd = gain * dx
    mean = jnp.sum(gd * hr, axis=-1, keepdims=True) * (1.0 / D)
    return dgain, g + rf * (gd - hr * mean)


def add_to(acc_ref, part):
    @pl.when(pl.program_id(0) == 0)
    def _():
        acc_ref[...] = part

    @pl.when(pl.program_id(0) > 0)
    def _():
        acc_ref[...] += part


def mlp_dx(me, dg, du, w_gate, w_up, hm, gain, g, w_out, kind):
    kern = Kernel(5, [w_gate, w_up, w_out], 4)

    def body(me_ref, *refs):
        (dg_ref, du_ref, hm_ref, gain_ref, g_ref), hold, outs, (acc_ref, un_ref, br_ref) = kern.split(refs)
        gm_ref, bo_ref, dou_ref, gg_ref = outs
        i = pl.program_id(0)

        @pl.when(i == 0)
        def _():
            start_all(hold)

        x, core = step_place(i)
        part = None
        for (s, _, box, sems), d_ref in zip(hold[:2], (dg_ref, du_ref)):
            s.wait(box, sems, core, x)
            term = dot(d_ref[...], hidden_block(s, box, x, core), TN)
            part = term if part is None else part + term
        add_to(acc_ref, part)

        @pl.when(i == COLS - 1)
        def _():
            regroup(un_ref, acc_ref, ROWS, me_ref[0])
            gg, gm = norm_bwd(un_ref[...], hm_ref[...], gain_ref[...], g_ref[...].astype(f32))
            gg_ref[...] = gg
            gm_ref[...] = gm
            bo_ref[...] = gm.astype(bf16)
            regroup(br_ref, bo_ref, COLS, me_ref[1])
            s, _, box, sems = hold[2]
            s.wait_all(box, sems)
            w = jnp.concatenate([col_block(s, box, x, core) for x, core in PLACES], axis=1)
            acc_ref[...] = dot(br_ref[...], w, NT)
            regroup(un_ref, acc_ref, ROWS, me_ref[0])
            dou_ref[...] = un_ref[...].astype(kind)

    row = lambda i, me: (step_col(i, me), 0)
    full = whole_map(T, D)
    return call(
        body, (COLS,), [(dg, (FC, T), row), (du, (FC, T), row), hm, gain.reshape(1, D), g] + kern.ins(),
        [((T, D), f32, (T, D), full), ((T, D), bf16, (T, D), full), ((T, D), kind, (T, D), full), ((1, D), f32, (1, D), full)],
        scratch=kern.scratch() + [pltpu.VMEM((T, D), f32), pltpu.VMEM((T, D), f32), pltpu.VMEM((T, D), bf16)],
        flops=4 * T * D * FFP + 2 * T * D * D, prefetch=me,
    )


def attn_bwd(me, xa, grads, strips, o, bo, h, gain, gm, halves):
    n = len(grads)
    kern = Kernel(6 + n, strips, 4)

    def body(me_ref, *refs):
        ins, hold, (p1_ref, p2_ref, g_ref, gg_ref), (xr_ref, or_ref, acc_ref) = kern.split(refs)
        xa_ref, o_ref, h_ref, gain_ref, gm_ref, bo_ref, *d_refs = ins
        i = pl.program_id(0)

        @pl.when(i == 0)
        def _():
            start_all(hold)
            regroup(xr_ref, xa_ref, ROWS, me_ref[0])
            regroup(or_ref, o_ref, ROWS, me_ref[0])

        tiles = [dot(xr_ref[...], d[...], TN).astype(bf16) for d in d_refs]
        tiles.append(dot(or_ref[...], bo_ref[...], TN).astype(bf16))
        for j, (which, at) in enumerate(halves[0]):
            for r, (z, y) in enumerate(BLOCKS):
                p1_ref[0, 0, y, z, j * 128 : (j + 1) * 128] = tiles[which][r * 128 : (r + 1) * 128, at : at + 128]
        for j, (which, at) in enumerate(halves[1]):
            for r, (z, y) in enumerate(BLOCKS):
                p2_ref[0, y, 0, z, j * 128 : (j + 1) * 128] = tiles[which][r * 128 : (r + 1) * 128, at : at + 128]
        x, core = step_place(i)
        part = None
        for (s, _, box, sems), d in zip(hold, d_refs):
            s.wait(box, sems, core, x)
            term = dot(d[...], col_block(s, box, x, core), NT)
            part = term if part is None else part + term
        add_to(acc_ref, part)

        @pl.when(i == COLS - 1)
        def _():
            regroup(g_ref, acc_ref, ROWS, me_ref[0])
            gg, g = norm_bwd(g_ref[...], h_ref[...].astype(f32), gain_ref[...], gm_ref[...])
            gg_ref[...] = gg
            g_ref[...] = g

    col = lambda i, me: (0, step_col(i, me))
    full = whole_map(T, D)
    ins = [xa, o, h, gain.reshape(1, D), gm, (bo, (T, 256), col)]
    ins += [(d, (T, d.shape[1] // COLS), col) for d in grads]
    total = sum(d.shape[1] for d in grads)
    return call(
        body, (COLS,), ins + kern.ins(),
        piece_specs(128 * len(halves[0]), 128 * len(halves[1])) + [((T, D), f32, (T, D), full), ((1, D), f32, (1, D), full)],
        scratch=kern.scratch() + [pltpu.VMEM((T, D), bf16), pltpu.VMEM((T, D), bf16), pltpu.VMEM((T, D), f32)],
        flops=4 * T * D * total + 2 * T * D * D, prefetch=me,
    )


HALVES_ONE = (((1, 0), (1, 128)), ((0, 0), (2, 0), (2, 128)))
HALVES_TWO = (((0, 0), (0, 128), (1, 0), (1, 128)), ((2, 0), (2, 128), (3, 0), (3, 128)))


def weights_of(attn, gu, dn, halves):
    out = []
    for which in range(1 + max(w for half in halves for w, _ in half)):
        for k, half in enumerate(halves):
            at = [j for j, (w, _) in enumerate(half) if w == which]
            if at:
                out.append(Strips(attn[k], k == 1, at[0] * 128, len(at) * 128))
    return out, Strips(gu[0], False, 0, FC), Strips(gu[1], True, 0, FC), [Strips(dn[0], False, 0, FBP), Strips(dn[1], True, 0, FBP)]


def pad_hidden(w):
    k = w.shape[0]
    return jnp.pad(w.reshape(k, -1, FB), ((0, 0), (0, 0), (0, FBP - FB))).reshape(k, -1).T


def pad_rows(w):
    n = w.shape[1]
    return jnp.pad(w.reshape(-1, FB, n), ((0, 0), (0, FBP - FB), (0, 0))).reshape(-1, n)


def strips_of(blocks, halves):
    return tuple(
        jnp.concatenate([blocks[which][..., at : at + 128] for which, at in strips], axis=-2) for strips in halves
    )


def tie(value, *after):
    got = lax.optimization_barrier((value, *after))
    return got[0], got[1:]


class Ring:
    def __init__(self, names):
        self.axes = names
        self.z = lax.axis_index(names[0])

    def swap(self, value, axis, by=1):
        shift = {"z": 3, "y": 2, "x": 1, "core": 0}[axis]
        return lax.ppermute(value, self.axes, [(i, i ^ (by << shift)) for i in range(32)])

    def gather_z(self, both):
        near = [both] + [self.swap(both, "z", by) for by in (1, 2, 3)]
        low, high = self.z % 2 == 1, self.z >= 2
        a, b = jnp.where(low, near[1], near[0]), jnp.where(low, near[0], near[1])
        c, d = jnp.where(low, near[3], near[2]), jnp.where(low, near[2], near[3])
        pick = lambda p, q: jnp.where(high, q, p)
        return jnp.stack([pick(a, c), pick(b, d), pick(c, a), pick(d, b)])

    def gather_z_all(self, both):
        return lax.all_gather(both, self.axes[0], axis=0, tiled=False)

    def gather_lo(self, one, two):
        return [jnp.stack([one, self.swap(one, "x")]), jnp.stack([two, self.swap(two, "y")])]

    def gather_hi(self, pair):
        return [[pair[0], self.swap(pair[0], "y")], [pair[1], self.swap(pair[1], "x")]]

    def gather_core(self, full):
        return [half + [self.swap(b, "core") for b in half] for half in full]

    def reduce_core(self, pair):
        return [g[0] + self.swap(g[1], "core") for g in pair]

    def reduce_lo(self, pair):
        return [pair[0][0] + self.swap(pair[0][1], "x"), pair[1][0] + self.swap(pair[1][1], "y")]

    def reduce_hi(self, pair):
        return [pair[0][0] + self.swap(pair[0][1], "y"), pair[1][0] + self.swap(pair[1][1], "x")]

    def reduce_z(self, pair):
        n1 = pair[0].shape[1]
        both = jnp.concatenate(pair, axis=1)
        here = lambda by: lax.dynamic_index_in_dim(both, self.z ^ by, 0, False)
        total = here(0).astype(f32)
        for by in (1, 2, 3):
            total = total + self.swap(here(by), "z", by).astype(f32)
        return total[:n1], total[n1:]

    def reduce_z_all(self, pair):
        n1 = pair[0].shape[1]
        both = jnp.concatenate(pair, axis=1)
        total = lax.psum_scatter(both, self.axes[0], scatter_dimension=0, tiled=False).astype(f32)
        return total[:n1], total[n1:]


def pack(shards, halves):
    *attn, gate, up, dn = shards
    dp = pad_rows(dn)
    return [strips_of(attn, halves), (pad_hidden(gate), pad_hidden(up)), (dp[:, :128], dp[:, 128:])]


def boxes_any(weights, halves):
    *attn, gate, up, dn = weights

    def cut(w, rows, cols):
        return w.reshape(4, 2, rows, 2, 2, cols).transpose(0, 1, 3, 4, 2, 5)

    def boxes(one, two):
        first = [one[:, y, :, core].transpose(1, 0, 2, 3) for core in range(2) for y in range(2)]
        second = [two[:, :, x, core].transpose(1, 0, 2, 3) for core in range(2) for x in range(2)]
        return first, second

    a = boxes(*strips_of([cut(w, D // ROWS, w.shape[1] // COLS) for w in attn], halves))
    hidden = lambda w: pad_hidden(w).reshape(2, 2, FC, 4, 2, 128).transpose(3, 4, 0, 1, 2, 5)
    d = cut(pad_rows(dn), FBP, 256)
    return [a, boxes(hidden(gate), hidden(up)), boxes(d[..., :128], d[..., 128:])]


def unpad_hidden(g):
    k = g.shape[1]
    return g.reshape(-1, FBP, k)[:, :FB].reshape(-1, k).T


def unpad_rows(g):
    n = g.shape[1]
    return g.reshape(-1, FBP, n)[:, :FB].reshape(-1, n)


def whole_grad(p, swapped):
    if swapped:
        p = jnp.swapaxes(p, 1, 2)
    core, x, y, z, n, w = p.shape
    return p.transpose(3, 2, 1, 0, 4, 5).reshape(z * y, x * core, n, w)


def join_strips(one, two, halves):
    out = []
    for which in range(1 + max(w for half in halves for w, _ in half)):
        got = {}
        for src, strips in ((one, halves[0]), (two, halves[1])):
            for j, (w, at) in enumerate(strips):
                if w == which:
                    got[at] = src[..., j * 128 : j * 128 + 128, :]
        out.append(jnp.concatenate([got[a] for a in sorted(got)], axis=-1))
    return out


def scatter_any(w):
    part = lax.psum_scatter(w, "row", scatter_dimension=0, tiled=True)
    return lax.psum_scatter(part, "col", scatter_dimension=1, tiled=True).astype(f32)


def natural(blocks):
    r, c, n, w = blocks.shape
    return blocks.transpose(0, 2, 1, 3).reshape(r * n, c * w)


def sum_any(pd, pgu, pa, halves):
    whole = jnp.concatenate([whole_grad(pd[0], False), whole_grad(pd[1], True)], axis=-1)
    dn = scatter_any(unpad_rows(natural(whole)))
    gu = []
    for g, swapped in ((pgu[0], False), (pgu[1], True)):
        gu.append(scatter_any(unpad_hidden(whole_grad(g, swapped).transpose(1, 2, 0, 3).reshape(FFP, D))))
    blocks = join_strips(whole_grad(pa[0], False), whole_grad(pa[1], True), halves)
    if len(blocks) == 3:
        blocks = [blocks[0][..., :64], blocks[0][..., 64:]] + blocks[1:]
    return [scatter_any(natural(b)) for b in blocks] + gu + [dn]


def join_qk(q, k, parts):
    n = q.shape[0]
    both = jnp.concatenate([q.reshape(n, parts, -1), k.reshape(n, parts, -1)], axis=2)
    return both.reshape(n, -1)

def route_plan(dest_slot, block_tokens, rows, cols):
    row_count = lax.axis_size(rows)
    col_count = lax.axis_size(cols)
    per_peer = block_tokens // row_count
    row_at = lax.axis_index(rows)
    col_at = lax.axis_index(cols)
    slot_table = dest_slot.reshape(row_count, col_count, block_tokens)
    column = lax.dynamic_index_in_dim(slot_table, col_at, 1, False)
    own_slots = lax.dynamic_index_in_dim(column, row_at, 0, False)
    send_order = jnp.argsort(own_slots)
    arrived = jnp.sort(column, axis=1)
    incoming = lax.dynamic_slice_in_dim(arrived, row_at * per_peer, per_peer, 1)
    local_slots = incoming.reshape(-1) - (row_at * col_count + col_at) * block_tokens
    placing = jnp.argsort(local_slots)
    return (send_order, local_slots, placing)


def exchange(value, axis):
    n, width = value.shape
    row_count = lax.axis_size(axis)
    got = lax.all_to_all(value.reshape(row_count, n // row_count, width), axis, split_axis=0, concat_axis=0, tiled=True)
    return got.reshape(n, width)


def gather_all(shards):
    return [lax.all_gather(lax.all_gather(w, "col", axis=1, tiled=True), "row", axis=0, tiled=True) for w in shards]


def body(names, tokens, cotangent, dest_slot, lengths, pad_mask, *params):
    ring = Ring(names) if len(names) == 4 else None
    rows, cols = (names[:2], names[2:]) if ring else names
    gain_a1, bq, bk, bv, bo_w, gain_m1, wg1, wu1, wd1 = params[:9]
    gain_a2, wq, wk, wv, wo2, gain_m2, wg2, wu2, wd2 = params[9:]
    shards1, shards2 = [bq, bk, bv, bo_w, wg1, wu1, wd1], [wq, wk, wv, wo2, wg2, wu2, wd2]
    send_order, local_slots, placing = route_plan(dest_slot, T, rows, cols)
    start = exchange(tokens[send_order], rows)[placing]
    cot = exchange(cotangent[send_order], rows)[placing]
    restore = jnp.argsort(send_order)
    if ring:
        me = jnp.stack([lax.axis_index(names[1]), lax.axis_index(cols)]).astype(i32)
        packs = pack([join_qk(bq, bk, 1)] + shards1[2:], HALVES_ONE) + pack(shards2, HALVES_TWO)
        flat = [jnp.concatenate(p, axis=0) for p in packs]
        near = [ring.gather_z(f) for f in flat[:2]]
        rest = ring.gather_z_all(jnp.concatenate(flat[2:], axis=0))
        at = 0
        for f in flat[2:]:
            near.append(rest[:, at : at + f.shape[0]])
            at += f.shape[0]
        full = []
        for p, v in zip(packs, near):
            n1 = p[0].shape[0]
            full.append(ring.gather_core(ring.gather_hi(ring.gather_lo(v[:, :n1], v[:, n1:]))))
    else:
        me = jnp.zeros((2,), i32)
        one, two = gather_all(shards1), gather_all(shards2)
        full = boxes_any([join_qk(one[0], one[1], COLS)] + one[2:], HALVES_ONE) + boxes_any(two, HALVES_TWO)
    (w_qk, w_v, w_o), w_g, w_u, w_d = weights_of(*full[:3], HALVES_ONE)
    (v_q, v_k, v_v, v_o), v_g, v_u, v_d = weights_of(*full[3:], HALVES_TWO)
    position = jnp.arange(T, dtype=i32)
    segment, end = jnp.zeros((T,), i32), jnp.zeros((), i32)
    for j in range(lengths.shape[1]):
        end = end + lengths[0, j]
        segment = segment + (position >= end).astype(i32)
    seg_row, seg_col = segment.reshape(1, T), segment.reshape(T, 1)
    live_row, live_col = pad_mask.reshape(1, T), pad_mask.reshape(T, 1)

    xa1, qk1, v1 = norm_proj(me, start, gain_a1, [w_qk, w_v])
    o1, ou1, rden1 = based_fwd(qk1, v1, seg_row, seg_col, live_row)
    hm1, xf1 = attn_out(me, start, o1, w_o, gain_m1)
    g1, u1, hid1 = gate_up(me, xf1, w_g, w_u)
    h1 = down(me, hm1, hid1, w_d)
    xa2, q2, k2, v2 = norm_proj(me, h1, gain_a2, [v_q, v_k, v_v])
    o2 = window_fwd(q2, k2, v2, seg_row, seg_col, live_row)
    hm2, xf2 = attn_out(me, h1, o2, v_o, gain_m2)
    g2, u2, hid2 = gate_up(me, xf2, v_g, v_u)
    h2 = down(me, hm2, hid2, v_d)
    output = exchange(h2.astype(bf16)[local_slots], rows)[restore]

    tied = tie if ring else (lambda value, *after: (value, after))
    step = (lambda f, v: f(v)) if ring else (lambda f, v: v)
    core, low, high = (ring.reduce_core, ring.reduce_lo, ring.reduce_hi) if ring else (None,) * 3
    dg2, du2, *d2 = down_bwd(me, cot, v_d, hid2, g2, u2)
    gu2 = gate_up_bwd(me, xf2, dg2, du2)
    d2 = step(core, d2)
    dg2, d2 = tied(dg2, *d2)
    gm2, bo2, dor2, gg_m2 = mlp_dx(me, dg2, du2, v_g, v_u, hm2, gain_m2, cot, v_o, bf16)
    d2, gu2 = step(low, d2), step(core, gu2)
    dor2, (*d2, gu2a, gu2b) = tied(dor2, *d2, *gu2)
    dq2, dk2, dv2 = window_bwd(q2, k2, v2, dor2, seg_row, seg_col, live_col)
    d2, gu2 = step(high, d2), step(low, [gu2a, gu2b])
    dq2, d2 = tied(dq2, *d2)
    a2a, a2b, gh1, gg_a2 = attn_bwd(me, xa2, [dq2, dk2, dv2], [v_q, v_k, v_v], o2, bo2, h1, gain_a2, gm2, HALVES_TWO)
    gh1, gu2 = tied(gh1, *gu2)
    dg1, du1, *d1 = down_bwd(me, gh1, w_d, hid1, g1, u1)
    gu2, a2 = step(high, gu2), step(core, [a2a, a2b])
    dg1, a2 = tied(dg1, *a2)
    gu1 = gate_up_bwd(me, xf1, dg1, du1)
    d1 = step(core, d1)
    dg1, (*gu2, d1a, d1b) = tied(dg1, *gu2, *d1)
    gm1, bo1, dou1, gg_m1 = mlp_dx(me, dg1, du1, w_g, w_u, hm1, gain_m1, gh1, w_o, f32)
    a2, gu1 = step(low, a2), step(core, gu1)
    dou1, (*a2, gu1a, gu1b) = tied(dou1, *a2, *gu1)
    dqk1, dv1 = based_bwd(qk1, v1, dou1, ou1, rden1, seg_row, seg_col, live_col)
    d1 = step(low, [d1a, d1b])
    dqk1, d1 = tied(dqk1, *d1)
    a1a, a1b, g0, gg_a1 = attn_bwd(me, xa1, [dqk1, dv1], [w_qk, w_v], o1, bo1, start, gain_a1, gm1, HALVES_ONE)
    gains = jnp.concatenate([gg_a1, gg_m1, gg_a2, gg_m2], axis=0)
    if ring:
        a1 = core([a1a, a1b])
        gu1 = low([gu1a, gu1b])
        d1, a2, gu1, a1 = high(d1), high(a2), high(gu1), high(low(a1))
        sums = []
        for a, gu, d, halves in ((a1, gu1, d1, HALVES_ONE), (a2, gu2, d2, HALVES_TWO)):
            last = halves is HALVES_ONE
            sa = (ring.reduce_z if last else ring.reduce_z_all)(a)
            sgu = (ring.reduce_z if last else ring.reduce_z_all)(gu)
            sd = ring.reduce_z_all(d)
            sums.append(join_strips(*sa, halves) + [unpad_hidden(sgu[0]), unpad_hidden(sgu[1]), unpad_rows(jnp.concatenate(sd, axis=1))])
        sums1, sums2 = sums
        sums1 = [sums1[0][:, :64], sums1[0][:, 64:]] + sums1[1:]
        for axis, by in (("core", 1), ("x", 1), ("y", 1), ("z", 1), ("z", 2)):
            gains = gains + ring.swap(gains, axis, by)
    else:
        sums1 = sum_any(d1, [gu1a, gu1b], [a1a, a1b], HALVES_ONE)
        sums2 = sum_any(d2, gu2, a2, HALVES_TWO)
        gains = lax.psum(gains, ("row", "col"))
    tokens_grad = exchange(g0.astype(bf16)[local_slots], rows)[restore]
    return (
        output, tokens_grad,
        gains[0], *sums1[:4], gains[1], *sums1[4:],
        gains[2], *sums2[:4], gains[3], *sums2[4:],
    )


def solution(mesh):
    names, rows, cols = ("row", "col"), "row", "col"
    if (mesh.shape["row"], mesh.shape["col"]) == (ROWS, COLS):
        names = ("z", "y", "x", "core")
        rows, cols = names[:2], names[2:]
        mesh = Mesh(mesh.devices.reshape(4, 2, 2, 2), names)
    block, weight = P(names, None), P(rows, cols)
    layer_in = (P(),) + (weight,) * 4 + (P(),) + (weight,) * 3
    return jax.shard_map(
        functools.partial(body, names),
        mesh=mesh,
        in_specs=(block, block, P(), block, P(names)) + layer_in * 2,
        out_specs=(block, block) + layer_in * 2,
        check_vma=False,
    )
```

time: 2580 us -> 979 us (0.38)
  Pallas kernels: 1730 us -> 288 us
  waiting for transfers between devices: 431 us -> 359 us
  starting transfers between devices: 173 us -> 104 us
  blocking collectives: 39.9 us -> 0 us
    pallas_call x28 -> x20, Pallas kernels: 1730 us -> 288 us  [call(): pl.pallas_call(body, out_shape=out_shape, grid_spec=pltpu.PrefetchScalarG...]
    ppermute x120 -> x101, starting transfers between devices: 155 us -> 82.8 us  [swap(): lax.ppermute(value, self.axes, [(i, i ^ by << shift) for i in range(32)])]
    ppermute x120 -> x101, waiting for transfers between devices: 421 us -> 359 us  [swap(): lax.ppermute(value, self.axes, [(i, i ^ by << shift) for i in range(32)])]
    psum x1 -> x0, blocking collectives: 39.9 us -> none  [body(): lax.psum(jnp.concatenate([gg_a1, gg_m1, gg_a2, gg_m2], axis=0), ('row', '...]
  transfers between devices with their start and end apart: 124 -> 110, of which waited for: 50 -> 27; matrix products, arithmetic and copies ran while one was open for 6% -> 18% of each run, Pallas kernels for 48% -> 28%
where the time goes in v2:
time: 979 us; the launch traced here: 969 us
  waiting for transfers between devices  359 us (37%)
  Pallas kernels  288 us (29%)
  local copies, waits for them, and re-layouts  106 us (11%)
  starting transfers between devices  104 us (11%)
  other arithmetic  92.2 us (9%)
  between operations  19.8 us (2%)
    ppermute x101, waiting for transfers between devices, swap(): lax.ppermute(value, self.axes, [(i, i ^ by << shift) for i in range(32)])  359 us
    pallas_call x20, Pallas kernels, call(): pl.pallas_call(body, out_shape=out_shape, grid_spec=pltpu.PrefetchScalarG...  288 us
    ppermute x101, starting transfers between devices, swap(): lax.ppermute(value, self.axes, [(i, i ^ by << shift) for i in range(32)])  82.8 us
    add x12, other arithmetic, reduce_core(): return [g[0] + self.swap(g[1], 'core') for g in pair]  27 us
    squeeze x12, local copies, waits for them, and re-layouts, reduce_core(): return [g[0] + self.swap(g[1], 'core') for g in pair]  26.5 us
    all_to_all x4, starting transfers between devices, exchange(): lax.all_to_all(value.reshape(row_count, n // row_count, width), axis, spl...  20.9 us
    unnamed x188, local copies, waits for them, and re-layouts  20.9 us
  transfers between devices with their start and end apart: 110, of which 27 were waited for; matrix products, arithmetic and copies ran while one was open for 18% of the time, Pallas kernels for 28%

profile of v2, /device:TPU:0, one launch (start us, length us, event | category | flops | bytes accessed | tf_op | source)
XLA Modules:
  0.0 969.1 jit_solution(10108547873942017440)
XLA Ops:
  33.9 59.2 %collective-permute-done.12 = bf16[1408,128]{1,0:T(8,128)(2,1)S(1)} collective-permute-done((bf16[1408,128]{1,0:T(8,128)(2,1)S(1)}, bf16[1408,128]{1,0:T(8,128)(2,1)S(1)}, u32[]{:S(2)}, u32[]{:S(2)}) %collective-permute-start.12) | collective-permute-done | bytes 360480 | tf_op jit(solution)/shard_map/ppermute | solution.py:718
  108.1 14.4 %collective-permute-done.1 = bf16[640,128]{1,0:T(8,128)(2,1)S(1)} collective-permute-done((bf16[640,128]{1,0:T(8,128)(2,1)S(1)}, bf16[640,128]{1,0:T(8,128)(2,1)S(1)}, u32[]{:S(2)}, u32[]{:S(2)}) %collective-permute-start.1) | collective-permute-done | bytes 163872 | tf_op jit(solution)/shard_map/ppermute | solution.py:718
  132.7 35.9 %collective-permute-done.3 = bf16[4,384,128]{2,1,0:T(8,128)(2,1)S(1)} collective-permute-done((bf16[4,384,128]{2,1,0:T(8,128)(2,1)S(1)}, bf16[4,384,128]{2,1,0:T(8,128)(2,1)S(1)}, u32[]{:S(2)}, u32[]{:S(2)}) %collective-permute-start.3) | collective-permute-done | bytes 393248 | tf_op jit(solution)/shard_map/ppermute | solution.py:718
  229.8 36.2 %collective-permute-done.34 = bf16[4,512,128]{2,1,0:T(8,128)(2,1)S(1)} collective-permute-done((bf16[4,512,128]{2,1,0:T(8,128)(2,1)S(1)}, bf16[4,512,128]{2,1,0:T(8,128)(2,1)S(1)}, u32[]{:S(2)}, u32[]{:S(2)}) %collective-permute-start.34) | collective-permute-done | bytes 524320 | tf_op jit(solution)/shard_map/ppermute | solution.py:718
  291.6 26.8 %collective-permute-done.47.refs_3_.refs_5_ = bf16[2,4,352,128]{3,2,1,0:T(8,128)(2,1)} collective-permute-done((bf16[2,4,352,128]{3,2,1,0:T(8,128)(2,1)}, bf16[2,4,352,128]{3,2,1,0:T(8,128)(2,1)}, u32[]{:S(2)}, u32[]{:S(2)}) %collective-permute-start.47) | collective-permute-done | bytes 720928 | tf_op jit(solution)/shard_map/ppermute | solution.py:718
  371.7 13.6 %shard_map.377 = (bf16[2816,512]{1,0:T(8,128)(2,1)}, bf16[2816,512]{1,0:T(8,128)(2,1)}, bf16[2816,512]{1,0:T(8,128)(2,1)}) custom-call(s32[2]{0:T(128)} %pad_add_fusion.me_ref, bf16[512,1024]{1,0:T(8,128)(2,1)} %get-tuple-element.112.refs_0_.xf_ref, bf16[2,4,704,128]{3,2,1,0:T(8,128)(2,1)} %pad_maximum_fusion.1.refs_1_.refs_5_, ...), custom_call_target="tpu_custom_call" | custom-call | flops 5905580032 | bytes 21233664 | tf_op jit(solution)/shard_map/pallas_call | solution.py:55
  396.3 12.9 %shard_map.379 = (bf16[512,1024]{1,0:T(8,128)(2,1)}, bf16[512,1024]{1,0:T(8,128)(2,1)}, bf16[512,1024]{1,0:T(8,128)(2,1)}, bf16[512,1024]{1,0:T(8,128)(2,1)}) custom-call(s32[2]{0:T(128)} %pad_add_fusion.me_ref, f32[512,1024]{1,0:T(8,128)} %shard_map.378.refs_0_.refs_2_, f32[1,1024]{1,0:T(1,128)} %bitcast.387, bf16[2,4,512,128]{3,2,1,0:T(8,128)(2,1)} %copy-done.9, ...), custom_call_target="tpu_custom_call" | custom-call | flops 3221225472 | bytes 18878464 | tf_op jit(solution)/shard_map/pallas_call | solution.py:55
  410.5 24.3 %shard_map.380.refs_1_ = bf16[512,1024]{1,0:T(8,128)(2,1)} custom-call(bf16[512,1024]{1,0:T(8,128)(2,1)} %get-tuple-element.114.q_ref, bf16[512,1024]{1,0:T(8,128)(2,1)} %get-tuple-element.115.k_ref, bf16[512,1024]{1,0:T(8,128)(2,1)} %get-tuple-element.116.v_ref, s32[1,512]{1,0:T(1,128)} %fusion.29.sr_ref, s32[512,1]{1,0:T(8,128)} %convert_add_fusion.2.sc_ref, ...), custom_call_target="tpu_custom_call" | custom-call | flops 1610612736 | bytes 4200448 | tf_op jit(solution)/shard_map/pallas_call | solution.py:55
  442.3 13.6 %shard_map.382 = (bf16[2816,512]{1,0:T(8,128)(2,1)}, bf16[2816,512]{1,0:T(8,128)(2,1)}, bf16[2816,512]{1,0:T(8,128)(2,1)}) custom-call(s32[2]{0:T(128)} %pad_add_fusion.me_ref, bf16[512,1024]{1,0:T(8,128)(2,1)} %get-tuple-element.118.refs_0_.xf_ref, bf16[2,4,704,128]{3,2,1,0:T(8,128)(2,1)} %pad_maximum_fusion.3.refs_1_.refs_5_, ...), custom_call_target="tpu_custom_call" | custom-call | flops 5905580032 | bytes 21233664 | tf_op jit(solution)/shard_map/pallas_call | solution.py:55
  457.5 16.4 %shard_map.384 = (bf16[2816,512]{1,0:T(8,128)(2,1)}, bf16[2816,512]{1,0:T(8,128)(2,1)}, bf16[2,2,2,4,352,128]{5,4,3,2,1,0:T(8,128)(2,1)}, bf16[2,2,2,4,352,128]{5,4,3,2,1,0:T(8,128)(2,1)}) custom-call(s32[2]{0:T(128)} %pad_add_fusion.me_ref, bf16[512,1024]{1,0:T(8,128)(2,1)} %gather_fusion.5, bf16[2816,512]{1,0:T(8,128)(2,1)} %get-tuple-element.119.refs_1_, ...), custom_call_target="tpu_custom_call" | custom-call | flops 5905580032 | bytes 27000832 | tf_op jit(solution)/shard_map/pallas_call | solution.py:55
  477.5 11.5 %shard_map.386 = (bf16[2,2,2,4,704,128]{5,4,3,2,1,0:T(8,128)(2,1)}, bf16[2,2,2,4,704,128]{5,4,3,2,1,0:T(8,128)(2,1)}) custom-call(s32[2]{0:T(128)} %pad_add_fusion.me_ref, bf16[512,1024]{1,0:T(8,128)(2,1)} %get-tuple-element.118.refs_0_.xf_ref, bf16[2816,512]{1,0:T(8,128)(2,1)} %get-tuple-element.128.refs_0_.dg_ref, ...), custom_call_target="tpu_custom_call" | custom-call | flops 5905580032 | bytes 18350080 | tf_op jit(solution)/shard_map/pallas_call | solution.py:55
  526.5 18.6 %shard_map.385 = (f32[512,1024]{1,0:T(8,128)}, bf16[512,1024]{1,0:T(8,128)(2,1)}, bf16[512,1024]{1,0:T(8,128)(2,1)}, f32[1,1024]{1,0:T(1,128)}) custom-call(s32[2]{0:T(128)} %pad_add_fusion.me_ref, bf16[2816,512]{1,0:T(8,128)(2,1)} %get-tuple-element.128.refs_0_.dg_ref, bf16[2816,512]{1,0:T(8,128)(2,1)} %get-tuple-element.129.refs_1_.du_ref, ...), custom_call_target="tpu_custom_call" | custom-call | flops 6979321856 | bytes 28844032 | tf_op jit(solution)/shard_map/pallas_call | solution.py:55
  562.8 18.6 %shard_map.387 = (bf16[512,1024]{1,0:T(8,128)(2,1)}, bf16[512,1024]{1,0:T(8,128)(2,1)}, bf16[512,1024]{1,0:T(8,128)(2,1)}) custom-call(bf16[512,1024]{1,0:T(8,128)(2,1)} %get-tuple-element.114.q_ref, bf16[512,1024]{1,0:T(8,128)(2,1)} %get-tuple-element.115.k_ref, bf16[512,1024]{1,0:T(8,128)(2,1)} %get-tuple-element.116.v_ref, ...), custom_call_target="tpu_custom_call" | custom-call | flops 4026531840 | bytes 7346176 | tf_op jit(solution)/shard_map/pallas_call | solution.py:55
  581.5 18.7 %shard_map.388 = (bf16[2,2,2,4,512,128]{5,4,3,2,1,0:T(8,128)(2,1)}, bf16[2,2,2,4,512,128]{5,4,3,2,1,0:T(8,128)(2,1)}, f32[512,1024]{1,0:T(8,128)}, f32[1,1024]{1,0:T(1,128)}) custom-call(s32[2]{0:T(128)} %pad_add_fusion.me_ref, bf16[512,1024]{1,0:T(8,128)(2,1)} %get-tuple-element.122.refs_0_, bf16[512,1024]{1,0:T(8,128)(2,1)} %shard_map.380.refs_1_, ...), custom_call_target="tpu_custom_call" | custom-call | flops 7516192768 | bytes 33562624 | tf_op jit(solution)/shard_map/pallas_call | solution.py:55
  613.6 17.2 %shard_map.389 = (bf16[2816,512]{1,0:T(8,128)(2,1)}, bf16[2816,512]{1,0:T(8,128)(2,1)}, bf16[2,2,2,4,352,128]{5,4,3,2,1,0:T(8,128)(2,1)}, bf16[2,2,2,4,352,128]{5,4,3,2,1,0:T(8,128)(2,1)}) custom-call(s32[2]{0:T(128)} %pad_add_fusion.me_ref, f32[512,1024]{1,0:T(8,128)} %get-tuple-element.147.refs_0_.refs_4_, bf16[2816,512]{1,0:T(8,128)(2,1)} %get-tuple-element.113.refs_1_, ...), custom_call_target="tpu_custom_call" | custom-call | flops 5905580032 | bytes 28049408 | tf_op jit(solution)/shard_map/pallas_call | solution.py:55
  649.3 11.5 %shard_map.391 = (bf16[2,2,2,4,704,128]{5,4,3,2,1,0:T(8,128)(2,1)}, bf16[2,2,2,4,704,128]{5,4,3,2,1,0:T(8,128)(2,1)}) custom-call(s32[2]{0:T(128)} %pad_add_fusion.me_ref, bf16[512,1024]{1,0:T(8,128)(2,1)} %get-tuple-element.112.refs_0_.xf_ref, bf16[2816,512]{1,0:T(8,128)(2,1)} %get-tuple-element.158.refs_0_.dg_ref, ...), custom_call_target="tpu_custom_call" | custom-call | flops 5905580032 | bytes 18350080 | tf_op jit(solution)/shard_map/pallas_call | solution.py:55
  676.4 19.5 %shard_map.390 = (f32[512,1024]{1,0:T(8,128)}, bf16[512,1024]{1,0:T(8,128)(2,1)}, f32[512,1024]{1,0:T(8,128)}, f32[1,1024]{1,0:T(1,128)}) custom-call(s32[2]{0:T(128)} %pad_add_fusion.me_ref, bf16[2816,512]{1,0:T(8,128)(2,1)} %get-tuple-element.158.refs_0_.dg_ref, bf16[2816,512]{1,0:T(8,128)(2,1)} %get-tuple-element.159.refs_1_.du_ref, ...), custom_call_target="tpu_custom_call" | custom-call | flops 6979321856 | bytes 29892608 | tf_op jit(solution)/shard_map/pallas_call | solution.py:55
  702.3 11.3 %collective-permute-done.75 = bf16[2,4,352,128]{3,2,1,0:T(8,128)(2,1)S(1)} collective-permute-done((bf16[2,4,352,128]{3,2,1,0:T(8,128)(2,1)S(1)}, bf16[2,4,352,128]{3,2,1,0:T(8,128)(2,1)S(1)}, u32[]{:S(2)}, u32[]{:S(2)}) %collective-permute-start.75) | collective-permute-done | bytes 720928 | tf_op jit(solution)/shard_map/ppermute | solution.py:718
  722.3 15.9 %shard_map.392 = (bf16[512,512]{1,0:T(8,128)(2,1)}, bf16[512,1024]{1,0:T(8,128)(2,1)}) custom-call(bf16[512,512]{1,0:T(8,128)(2,1)} %get-tuple-element.108.qk_ref, bf16[512,1024]{1,0:T(8,128)(2,1)} %get-tuple-element.109.v_ref, f32[512,1024]{1,0:T(8,128)} %get-tuple-element.167.dou_ref, f32[512,1024]{1,0:T(8,128)} %get-tuple-element.168.ou_ref, ...), custom_call_target="tpu_custom_call" | custom-call | flops 4026531840 | bytes 9443328 | tf_op jit(solution)/shard_map/pallas_call | solution.py:55
  738.2 19.6 %shard_map.393 = (bf16[2,2,2,4,256,128]{5,4,3,2,1,0:T(8,128)(2,1)}, bf16[2,2,2,4,384,128]{5,4,3,2,1,0:T(8,128)(2,1)}, f32[512,1024]{1,0:T(8,128)}, f32[1,1024]{1,0:T(1,128)}) custom-call(s32[2]{0:T(128)} %pad_add_fusion.me_ref, bf16[512,1024]{1,0:T(8,128)(2,1)} %get-tuple-element.121.refs_0_, bf16[512,1024]{1,0:T(8,128)(2,1)} %get-tuple-element.110.refs_1_, ...), custom_call_target="tpu_custom_call" | custom-call | flops 4294967296 | bytes 20455424 | tf_op jit(solution)/shard_map/pallas_call | solution.py:55
  805.0 30.0 %collective-permute-done.100 = bf16[4,512,128]{2,1,0:T(8,128)(2,1)} collective-permute-done((bf16[4,512,128]{2,1,0:T(8,128)(2,1)}, bf16[4,512,128]{2,1,0:T(8,128)(2,1)}, u32[]{:S(2)}, u32[]{:S(2)}) %collective-permute-start.100) | collective-permute-done | bytes 524320 | tf_op jit(solution)/shard_map/ppermute | solution.py:718
  846.0 23.8 %collective-permute-done.92 = bf16[2,4,704,128]{3,2,1,0:T(8,128)(2,1)} collective-permute-done((bf16[2,4,704,128]{3,2,1,0:T(8,128)(2,1)}, bf16[2,4,704,128]{3,2,1,0:T(8,128)(2,1)}, u32[]{:S(2)}, u32[]{:S(2)}) %collective-permute-start.92) | collective-permute-done | bytes 1441824 | tf_op jit(solution)/shard_map/ppermute | solution.py:718
  884.4 21.5 %collective-permute-done.83 = bf16[4,256,128]{2,1,0:T(8,128)(2,1)} collective-permute-done((bf16[4,256,128]{2,1,0:T(8,128)(2,1)}, bf16[4,256,128]{2,1,0:T(8,128)(2,1)}, u32[]{:S(2)}, u32[]{:S(2)}) %collective-permute-start.83) | collective-permute-done | bytes 262176 | tf_op jit(solution)/shard_map/ppermute | solution.py:718
  922.9 19.7 %collective-permute-done.95 = bf16[1408,128]{1,0:T(8,128)(2,1)S(1)} collective-permute-done((bf16[1408,128]{1,0:T(8,128)(2,1)S(1)}, bf16[1408,128]{1,0:T(8,128)(2,1)S(1)}, u32[]{:S(2)}, u32[]{:S(2)}) %collective-permute-start.95) | collective-permute-done | bytes 360480 | tf_op jit(solution)/shard_map/ppermute | solution.py:718
  (588 shorter events, 438.8 us)
Async XLA Ops:
  8.1 186.5 %all-gather.3.cloned.1.call-start = ((), (), s32[]{:S(2)}) async-start(), calls=%async_computation.12 | async-start | bytes 4915200 | tf_op jit(solution)/shard_map/all_gather | solution.py:729
  22.7 70.4 %collective-permute-start.12 = (bf16[1408,128]{1,0:T(8,128)(2,1)S(1)}, bf16[1408,128]{1,0:T(8,128)(2,1)S(1)}, u32[]{:S(2)}, u32[]{:S(2)}) collective-permute-start(bf16[1408,128]{1,0:T(8,128)(2,1)S(1)} %pad_maximum_fusion.18), channel_id=1, source_target_pairs={{0,16},{1,17},{2,18},{3,19},{4,20},{5,21},{6,22},{7,23},{8,24},{9,... | collective-permute-start | bytes 1081352 | tf_op jit(solution)/shard_map/ppermute | solution.py:718
  22.7 70.4 %collective-permute-start.13 = (bf16[1408,128]{1,0:T(8,128)(2,1)S(1)}, bf16[1408,128]{1,0:T(8,128)(2,1)S(1)}, u32[]{:S(2)}, u32[]{:S(2)}) collective-permute-start(bf16[1408,128]{1,0:T(8,128)(2,1)S(1)} %pad_maximum_fusion.18), channel_id=1, source_target_pairs={{0,8},{1,9},{2,10},{3,11},{4,12},{5,13},{6,14},{7,15},{8,0},{9,1},... | collective-permute-start | bytes 1081352 | tf_op jit(solution)/shard_map/ppermute | solution.py:718
  125.4 56.2 %collective-permute-start.15 = (bf16[2,4,704,128]{3,2,1,0:T(8,128)(2,1)}, bf16[2,4,704,128]{3,2,1,0:T(8,128)(2,1)}, u32[]{:S(2)}, u32[]{:S(2)}) collective-permute-start(bf16[2,4,704,128]{3,2,1,0:T(8,128)(2,1)} %pad_maximum_fusion.1.refs_1_.refs_5_), channel_id=1, source_target_pairs={{0,4},{1,5},{2,6},{3,7},{4,0},{5,1},{6,2},{7,3},{8,12},{9,13},{10,... | collective-permute-start | bytes 4325384 | tf_op jit(solution)/shard_map/ppermute | solution.py:718
  128.2 53.5 %collective-permute-start.19 = (bf16[2,4,704,128]{3,2,1,0:T(8,128)(2,1)}, bf16[2,4,704,128]{3,2,1,0:T(8,128)(2,1)}, u32[]{:S(2)}, u32[]{:S(2)}) collective-permute-start(bf16[2,4,704,128]{3,2,1,0:T(8,128)(2,1)} %pad_maximum_fusion.2.refs_5_.refs_9_), channel_id=1, source_target_pairs={{0,2},{1,3},{2,0},{3,1},{4,6},{5,7},{6,4},{7,5},{8,10},{9,11},{10,... | collective-permute-start | bytes 4325384 | tf_op jit(solution)/shard_map/ppermute | solution.py:718
  190.0 92.6 %all-to-all-start = ((bf16[8,64,1024]{2,1,0:T(8,128)(2,1)}), bf16[8,64,1024]{2,1,0:T(8,128)(2,1)S(1)}, u32[]{:S(2)}, u32[]{:S(2)}) async-start(bf16[8,64,1024]{2,1,0:T(8,128)(2,1)} %bitcast.3), calls=%async_computation | async-start | bytes 2097152 | tf_op jit(solution)/shard_map/all_to_all | solution.py:864
  207.8 59.4 %collective-permute-start.38 = (bf16[4,704,128]{2,1,0:T(8,128)(2,1)S(1)}, bf16[4,704,128]{2,1,0:T(8,128)(2,1)S(1)}, u32[]{:S(2)}, u32[]{:S(2)}) collective-permute-start(bf16[4,704,128]{2,1,0:T(8,128)(2,1)S(1)} %get-tuple-element.263), channel_id=1, source_target_pairs={{0,2},{1,3},{2,0},{3,1},{4,6},{5,7},{6,4},{7,5},{8,10},{9,11},{10,... | collective-permute-start | bytes 2162696 | tf_op jit(solution)/shard_map/ppermute | solution.py:718
  216.7 51.6 %collective-permute-start.42 = (bf16[4,704,128]{2,1,0:T(8,128)(2,1)S(1)}, bf16[4,704,128]{2,1,0:T(8,128)(2,1)S(1)}, u32[]{:S(2)}, u32[]{:S(2)}) collective-permute-start(bf16[4,704,128]{2,1,0:T(8,128)(2,1)S(1)} %get-tuple-element.262), channel_id=1, source_target_pairs={{0,4},{1,5},{2,6},{3,7},{4,0},{5,1},{6,2},{7,3},{8,12},{9,13},{10,... | collective-permute-start | bytes 2162696 | tf_op jit(solution)/shard_map/ppermute | solution.py:718
  282.6 53.5 %all-to-all-start.2 = ((bf16[8,64,1024]{2,1,0:T(8,128)(2,1)}), bf16[8,64,1024]{2,1,0:T(8,128)(2,1)S(1)}, u32[]{:S(2)}, u32[]{:S(2)}) async-start(bf16[8,64,1024]{2,1,0:T(8,128)(2,1)} %bitcast.344), calls=%async_computation.2 | async-start | bytes 2097152 | tf_op jit(solution)/shard_map/all_to_all | solution.py:864
  349.1 60.3 %collective-permute-start.40 = (bf16[2,4,704,128]{3,2,1,0:T(8,128)(2,1)}, bf16[2,4,704,128]{3,2,1,0:T(8,128)(2,1)S(1)}, u32[]{:S(2)}, u32[]{:S(2)}) collective-permute-start(bf16[2,4,704,128]{3,2,1,0:T(8,128)(2,1)} %pad_maximum_fusion.3.refs_1_.refs_5_), channel_id=1, source_target_pairs={{0,1},{1,0},{2,3},{3,2},{4,5},{5,4},{6,7},{7,6},{8,9},{9,8},{10,11... | collective-permute-start | bytes 4325384 | tf_op jit(solution)/shard_map/ppermute | solution.py:718
  354.0 56.0 %collective-permute-start.44 = (bf16[2,4,704,128]{3,2,1,0:T(8,128)(2,1)}, bf16[2,4,704,128]{3,2,1,0:T(8,128)(2,1)}, u32[]{:S(2)}, u32[]{:S(2)}) collective-permute-start(bf16[2,4,704,128]{3,2,1,0:T(8,128)(2,1)} %pad_maximum_fusion.4.refs_5_.refs_9_), channel_id=1, source_target_pairs={{0,1},{1,0},{2,3},{3,2},{4,5},{5,4},{6,7},{7,6},{8,9},{9,8},{10,11... | collective-permute-start | bytes 4325384 | tf_op jit(solution)/shard_map/ppermute | solution.py:718
  354.0 56.0 %collective-permute-start.41 = (bf16[2,4,704,128]{3,2,1,0:T(8,128)(2,1)}, bf16[2,4,704,128]{3,2,1,0:T(8,128)(2,1)}, u32[]{:S(2)}, u32[]{:S(2)}) collective-permute-start(bf16[2,4,704,128]{3,2,1,0:T(8,128)(2,1)} %collective-permute-done.39.refs_2_.refs_6_), channel_id=1, source_target_pairs={{0,1},{1,0},{2,3},{3,2},{4,5},{5,4},{6,7},{7,6},{8,9},{9,8},{10,11... | collective-permute-start | bytes 4325384 | tf_op jit(solution)/shard_map/ppermute | solution.py:718
  370.5 71.8 %collective-permute-start.45 = (bf16[2,4,704,128]{3,2,1,0:T(8,128)(2,1)}, bf16[2,4,704,128]{3,2,1,0:T(8,128)(2,1)}, u32[]{:S(2)}, u32[]{:S(2)}) collective-permute-start(bf16[2,4,704,128]{3,2,1,0:T(8,128)(2,1)} %collective-permute-done.43.refs_6_.refs_10_), channel_id=1, source_target_pairs={{0,1},{1,0},{2,3},{3,2},{4,5},{5,4},{6,7},{7,6},{8,9},{9,8},{10,11... | collective-permute-start | bytes 4325384 | tf_op jit(solution)/shard_map/ppermute | solution.py:718
  492.7 56.8 %collective-permute-start.58 = (bf16[2,2,4,704,128]{4,3,2,1,0:T(8,128)(2,1)}, bf16[2,2,4,704,128]{4,3,2,1,0:T(8,128)(2,1)}, u32[]{:S(2)}, u32[]{:S(2)}) collective-permute-start(bf16[2,2,4,704,128]{4,3,2,1,0:T(8,128)(2,1)} %slice_bitcast_fusion.3), channel_id=1, source_target_pairs={{0,1},{1,0},{2,3},{3,2},{4,5},{5,4},{6,7},{7,6},{8,9},{9,8},{10,11... | collective-permute-start | bytes 8650760 | tf_op jit(solution)/shard_map/ppermute | solution.py:718
  495.1 57.6 %collective-permute-start.59 = (bf16[2,2,4,704,128]{4,3,2,1,0:T(8,128)(2,1)}, bf16[2,2,4,704,128]{4,3,2,1,0:T(8,128)(2,1)}, u32[]{:S(2)}, u32[]{:S(2)}) collective-permute-start(bf16[2,2,4,704,128]{4,3,2,1,0:T(8,128)(2,1)} %slice_bitcast_fusion.2), channel_id=1, source_target_pairs={{0,1},{1,0},{2,3},{3,2},{4,5},{5,4},{6,7},{7,6},{8,9},{9,8},{10,11... | collective-permute-start | bytes 8650760 | tf_op jit(solution)/shard_map/ppermute | solution.py:718
  517.6 117.1 %reduce-scatter.11.cloned.1.call-start = ((), (), s32[]{:S(2)}) async-start(), calls=%async_computation.11 | async-start | bytes 901120 | tf_op jit(solution)/shard_map/reduce_scatter | solution.py:761
  606.5 196.0 %reduce-scatter.9.cloned.1.call-start = ((), (), s32[]{:S(2)}) async-start(), calls=%async_computation.10 | async-start | bytes 1802240 | tf_op jit(solution)/shard_map/reduce_scatter | solution.py:761
  762.3 119.3 %all-to-all-start.3 = ((bf16[8,64,1024]{2,1,0:T(8,128)(2,1)}), bf16[8,64,1024]{2,1,0:T(8,128)(2,1)S(1)}, u32[]{:S(2)}, u32[]{:S(2)}) async-start(bf16[8,64,1024]{2,1,0:T(8,128)(2,1)} %bitcast.116), calls=%async_computation.3 | async-start | bytes 2097152 | tf_op jit(solution)/shard_map/all_to_all | solution.py:864
  767.1 111.6 %reduce-scatter.5.cloned.1.call-start = ((), (), s32[]{:S(2)}) async-start(), calls=%async_computation.8 | async-start | bytes 901120 | tf_op jit(solution)/shard_map/reduce_scatter | solution.py:761
  770.2 103.1 %collective-permute-start.84 = (bf16[2,2,4,384,128]{4,3,2,1,0:T(8,128)(2,1)}, bf16[2,2,4,384,128]{4,3,2,1,0:T(8,128)(2,1)}, u32[]{:S(2)}, u32[]{:S(2)}) collective-permute-start(bf16[2,2,4,384,128]{4,3,2,1,0:T(8,128)(2,1)} %slice_bitcast_fusion.6), channel_id=1, source_target_pairs={{0,1},{1,0},{2,3},{3,2},{4,5},{5,4},{6,7},{7,6},{8,9},{9,8},{10,11... | collective-permute-start | bytes 4718600 | tf_op jit(solution)/shard_map/ppermute | solution.py:718
  771.8 66.5 %collective-permute-start.81 = (bf16[2,2,4,256,128]{4,3,2,1,0:T(8,128)(2,1)}, bf16[2,2,4,256,128]{4,3,2,1,0:T(8,128)(2,1)}, u32[]{:S(2)}, u32[]{:S(2)}) collective-permute-start(bf16[2,2,4,256,128]{4,3,2,1,0:T(8,128)(2,1)} %slice_bitcast_fusion.15), channel_id=1, source_target_pairs={{0,1},{1,0},{2,3},{3,2},{4,5},{5,4},{6,7},{7,6},{8,9},{9,8},{10,11... | collective-permute-start | bytes 3145736 | tf_op jit(solution)/shard_map/ppermute | solution.py:718
  789.9 51.4 %collective-permute-start.90 = (bf16[2,4,704,128]{3,2,1,0:T(8,128)(2,1)}, bf16[2,4,704,128]{3,2,1,0:T(8,128)(2,1)}, u32[]{:S(2)}, u32[]{:S(2)}) collective-permute-start(bf16[2,4,704,128]{3,2,1,0:T(8,128)(2,1)} %slice_bitcast_fusion.8), channel_id=1, source_target_pairs={{0,2},{1,3},{2,0},{3,1},{4,6},{5,7},{6,4},{7,5},{8,10},{9,11},{10,... | collective-permute-start | bytes 4325384 | tf_op jit(solution)/shard_map/ppermute | solution.py:718
  794.4 150.0 %reduce-scatter.7.cloned.1.call-start = ((), (), s32[]{:S(2)}) async-start(), calls=%async_computation.9 | async-start | bytes 1310720 | tf_op jit(solution)/shard_map/reduce_scatter | solution.py:761
  844.0 62.9 %collective-permute-start.91 = (bf16[4,704,128]{2,1,0:T(8,128)(2,1)}, bf16[4,704,128]{2,1,0:T(8,128)(2,1)}, u32[]{:S(2)}, u32[]{:S(2)}) collective-permute-start(bf16[4,704,128]{2,1,0:T(8,128)(2,1)} %slice_bitcast_fusion.22), channel_id=1, source_target_pairs={{0,4},{1,5},{2,6},{3,7},{4,0},{5,1},{6,2},{7,3},{8,12},{9,13},{10,... | collective-permute-start | bytes 2162696 | tf_op jit(solution)/shard_map/ppermute | solution.py:718
  (170 other events, 3567.8 us)
Sparse Core Ops, SparseCore 0:
  17.6 113.6 all-gather.2
  606.6 22.6 reduce-scatter.10
  676.5 32.4 reduce-scatter.8
  794.5 21.3 reduce-scatter.4
  838.4 27.1 reduce-scatter.6
Sparse Core Ops, SparseCore 1:
  273.8 2.9 sort.60.cloned.1.call-done
  (1 shorter events, 0.0 us)

commit v3 on v2

--- a/solution.py
+++ b/solution.py
@@ -490,10 +490,10 @@
 
 
 def down_bwd(me, bd, strips, hid, g, u):
-    kern = Kernel(4, strips, 4)
+    kern = Kernel(4, strips, 6)
 
     def body(me_ref, *refs):
-        (bd_ref, hid_ref, g_ref, u_ref), hold, (dg_ref, du_ref, p1_ref, p2_ref), (br_ref,) = kern.split(refs)
+        (bd_ref, hid_ref, g_ref, u_ref), hold, (dg_ref, du_ref, *p_refs), (br_ref,) = kern.split(refs)
         i = pl.program_id(0)
 
         @pl.when(i == 0)
@@ -508,8 +508,8 @@
             for y in range(2):
                 yr = y ^ me_ref[0]
                 rows = slice(y * FBP, (y + 1) * FBP)
-                p1_ref[core, x, yr, 0] = gwd[rows, at : at + 128]
-                p2_ref[core, yr, x, 0] = gwd[rows, at + 128 : at + 256]
+                p_refs[core][x, yr, 0] = gwd[rows, at : at + 128]
+                p_refs[2 + core][yr, x, 0] = gwd[rows, at + 128 : at + 256]
 
         @pl.when(i == 0)
         def _():
@@ -525,31 +525,48 @@
 
     row = lambda i, me: (i, 0)
     hblk = (FC, T)
-    pieces = ((2, 2, 2, 4, FBP, 128), bf16, (2, 2, 2, 1, FBP, 128), lambda i, me: (0, 0, 0, i, 0, 0))
+    pieces = ((2, 2, 4, FBP, 128), bf16, (2, 2, 1, FBP, 128), lambda i, me: (0, 0, i, 0, 0))
     return call(
         body, (COLS,), [bd, (hid, hblk, row), (g, hblk, row), (u, hblk, row)] + kern.ins(),
-        [((FFP, T), bf16, hblk, row), ((FFP, T), bf16, hblk, row), pieces, pieces],
+        [((FFP, T), bf16, hblk, row), ((FFP, T), bf16, hblk, row)] + [pieces] * 4,
         scratch=kern.scratch() + [pltpu.VMEM((T, D), bd.dtype)], flops=4 * T * D * FFP, prefetch=me,
     )
 
 
 def piece_specs(n1, n2):
-    one = ((2, 2, 2, 4, n1, 128), bf16, (1, 1, 2, 4, n1, 128), lambda i, me: (i // 2, i % 2, 0, 0, 0, 0))
-    two = ((2, 2, 2, 4, n2, 128), bf16, (1, 2, 1, 4, n2, 128), lambda i, me: (i // 2, 0, i % 2, 0, 0, 0))
-    return [one, two]
+    out = []
+    for n, block, place in ((n1, (1, 2, 4), lambda j: (j, 0)), (n2, (2, 1, 4), lambda j: (0, j))):
+        for step in (lambda i: jnp.minimum(i, 1), lambda i: jnp.maximum(i - 2, 0)):
+            index = functools.partial(lambda place, step, i, me: (*place(step(i)), 0, 0, 0), place, step)
+            out.append(((2, 2, 4, n, 128), bf16, (*block, n, 128), index))
+    return out
+
+
+def for_core(refs, write):
+    for core in range(2):
+
+        @pl.when(pl.program_id(0) // 2 == core)
+        def _():
+            write(refs[core], refs[2 + core])
 
 
 def gate_up_bwd(me, xf, dg, du):
-    def body(me_ref, xf_ref, dg_ref, du_ref, p1_ref, p2_ref, xr_ref):
+    def body(me_ref, xf_ref, dg_ref, du_ref, *refs):
+        *p_refs, xr_ref = refs
+
         @pl.when(pl.program_id(0) == 0)
         def _():
             regroup(xr_ref, xf_ref, ROWS, me_ref[0])
 
         gwg = dot(dg_ref[...], xr_ref[...], NN).astype(bf16)
         gwu = dot(du_ref[...], xr_ref[...], NN).astype(bf16)
-        for r, (z, y) in enumerate(BLOCKS):
-            p1_ref[0, 0, y, z] = gwg[:, r * 128 : (r + 1) * 128]
-            p2_ref[0, y, 0, z] = gwu[:, r * 128 : (r + 1) * 128]
+
+        def write(one, two):
+            for r, (z, y) in enumerate(BLOCKS):
+                one[0, y, z] = gwg[:, r * 128 : (r + 1) * 128]
+                two[y, 0, z] = gwu[:, r * 128 : (r + 1) * 128]
+
+        for_core(p_refs, write)
 
     row = lambda i, me: (step_col(i, me), 0)
     return call(
@@ -624,10 +641,10 @@
 
 def attn_bwd(me, xa, grads, strips, o, bo, h, gain, gm, halves):
     n = len(grads)
-    kern = Kernel(6 + n, strips, 4)
+    kern = Kernel(6 + n, strips, 6)
 
     def body(me_ref, *refs):
-        ins, hold, (p1_ref, p2_ref, g_ref, gg_ref), (xr_ref, or_ref, acc_ref) = kern.split(refs)
+        ins, hold, (*p_refs, g_ref, gg_ref), (xr_ref, or_ref, acc_ref) = kern.split(refs)
         xa_ref, o_ref, h_ref, gain_ref, gm_ref, bo_ref, *d_refs = ins
         i = pl.program_id(0)
 
@@ -639,12 +656,16 @@
 
         tiles = [dot(xr_ref[...], d[...], TN).astype(bf16) for d in d_refs]
         tiles.append(dot(or_ref[...], bo_ref[...], TN).astype(bf16))
-        for j, (which, at) in enumerate(halves[0]):
-            for r, (z, y) in enumerate(BLOCKS):
-                p1_ref[0, 0, y, z, j * 128 : (j + 1) * 128] = tiles[which][r * 128 : (r + 1) * 128, at : at + 128]
-        for j, (which, at) in enumerate(halves[1]):
-            for r, (z, y) in enumerate(BLOCKS):
-                p2_ref[0, y, 0, z, j * 128 : (j + 1) * 128] = tiles[which][r * 128 : (r + 1) * 128, at : at + 128]
+
+        def write(one, two):
+            for j, (which, at) in enumerate(halves[0]):
+                for r, (z, y) in enumerate(BLOCKS):
+                    one[0, y, z, j * 128 : (j + 1) * 128] = tiles[which][r * 128 : (r + 1) * 128, at : at + 128]
+            for j, (which, at) in enumerate(halves[1]):
+                for r, (z, y) in enumerate(BLOCKS):
+                    two[y, 0, z, j * 128 : (j + 1) * 128] = tiles[which][r * 128 : (r + 1) * 128, at : at + 128]
+
+        for_core(p_refs, write)
         x, core = step_place(i)
         part = None
         for (s, _, box, sems), d in zip(hold, d_refs):
@@ -677,14 +698,22 @@
 HALVES_TWO = (((0, 0), (0, 128), (1, 0), (1, 128)), ((2, 0), (2, 128), (3, 0), (3, 128)))
 
 
-def weights_of(attn, gu, dn, halves):
+def attn_weights(bufs, halves):
     out = []
     for which in range(1 + max(w for half in halves for w, _ in half)):
         for k, half in enumerate(halves):
             at = [j for j, (w, _) in enumerate(half) if w == which]
             if at:
-                out.append(Strips(attn[k], k == 1, at[0] * 128, len(at) * 128))
-    return out, Strips(gu[0], False, 0, FC), Strips(gu[1], True, 0, FC), [Strips(dn[0], False, 0, FBP), Strips(dn[1], True, 0, FBP)]
+                out.append(Strips(bufs[k], k == 1, at[0] * 128, len(at) * 128))
+    return out
+
+
+def gate_weights(bufs):
+    return Strips(bufs[0], False, 0, FC), Strips(bufs[1], True, 0, FC)
+
+
+def down_weights(bufs):
+    return [Strips(bufs[0], False, 0, FBP), Strips(bufs[1], True, 0, FBP)]
 
 
 def pad_hidden(w):
@@ -703,9 +732,8 @@
     )
 
 
-def tie(value, *after):
-    got = lax.optimization_barrier((value, *after))
-    return got[0], got[1:]
+def after(value, *arrays):
+    return lax.optimization_barrier((value, *arrays))[0] if arrays else value
 
 
 class Ring:
@@ -728,23 +756,33 @@
     def gather_z_all(self, both):
         return lax.all_gather(both, self.axes[0], axis=0, tiled=False)
 
-    def gather_lo(self, one, two):
-        return [jnp.stack([one, self.swap(one, "x")]), jnp.stack([two, self.swap(two, "y")])]
-
-    def gather_hi(self, pair):
-        return [[pair[0], self.swap(pair[0], "y")], [pair[1], self.swap(pair[1], "x")]]
-
-    def gather_core(self, full):
-        return [half + [self.swap(b, "core") for b in half] for half in full]
-
-    def reduce_core(self, pair):
-        return [g[0] + self.swap(g[1], "core") for g in pair]
-
-    def reduce_lo(self, pair):
-        return [pair[0][0] + self.swap(pair[0][1], "x"), pair[1][0] + self.swap(pair[1][1], "y")]
-
-    def reduce_hi(self, pair):
-        return [pair[0][0] + self.swap(pair[0][1], "y"), pair[1][0] + self.swap(pair[1][1], "x")]
+    def gather_lo(self, pair, *behind):
+        got = [after(self.swap(v, axis), *behind) for v, axis in zip(pair, ("x", "y"))]
+        return [jnp.stack([v, g]) for v, g in zip(pair, got)]
+
+    def gather_hi(self, pair, *behind):
+        return [[v, after(self.swap(v, axis), *behind)] for v, axis in zip(pair, ("y", "x"))]
+
+    def gather_core(self, full, *behind):
+        return [half + [after(self.swap(b, "core"), *behind) for b in half] for half in full]
+
+    def reduce_core(self, four, *behind):
+        out = []
+        for own, send in (four[:2], four[2:]):
+            got = after(self.swap(send, "core"), *behind)
+            out += [own[0] + got[0], own[1] + got[1]]
+        return out
+
+    def reduce_lo(self, four, *behind):
+        out = []
+        for (keep, go), axis in ((four[:2], "x"), (four[2:], "y")):
+            got = after(self.swap(go, axis), *behind)
+            out += [keep[0] + got[0], keep[1] + got[1]]
+        return out
+
+    def reduce_hi(self, four, *behind):
+        pairs = ((four[:2], "y"), (four[2:], "x"))
+        return [keep + after(self.swap(go, axis), *behind) for (keep, go), axis in pairs]
 
     def reduce_z(self, pair):
         n1 = pair[0].shape[1]
@@ -795,7 +833,8 @@
     return g.reshape(-1, FBP, n)[:, :FB].reshape(-1, n)
 
 
-def whole_grad(p, swapped):
+def whole_grad(own, send, swapped):
+    p = jnp.stack([own, send])
     if swapped:
         p = jnp.swapaxes(p, 1, 2)
     core, x, y, z, n, w = p.shape
@@ -825,12 +864,10 @@
 
 
 def sum_any(pd, pgu, pa, halves):
-    whole = jnp.concatenate([whole_grad(pd[0], False), whole_grad(pd[1], True)], axis=-1)
-    dn = scatter_any(unpad_rows(natural(whole)))
-    gu = []
-    for g, swapped in ((pgu[0], False), (pgu[1], True)):
-        gu.append(scatter_any(unpad_hidden(whole_grad(g, swapped).transpose(1, 2, 0, 3).reshape(FFP, D))))
-    blocks = join_strips(whole_grad(pa[0], False), whole_grad(pa[1], True), halves)
+    pairs = lambda p: (whole_grad(*p[:2], False), whole_grad(*p[2:], True))
+    dn = scatter_any(unpad_rows(natural(jnp.concatenate(pairs(pd), axis=-1))))
+    gu = [scatter_any(unpad_hidden(g.transpose(1, 2, 0, 3).reshape(FFP, D))) for g in pairs(pgu)]
+    blocks = join_strips(*pairs(pa), halves)
     if len(blocks) == 3:
         blocks = [blocks[0][..., :64], blocks[0][..., 64:]] + blocks[1:]
     return [scatter_any(natural(b)) for b in blocks] + gu + [dn]
@@ -876,29 +913,25 @@
     gain_a2, wq, wk, wv, wo2, gain_m2, wg2, wu2, wd2 = params[9:]
     shards1, shards2 = [bq, bk, bv, bo_w, wg1, wu1, wd1], [wq, wk, wv, wo2, wg2, wu2, wd2]
     send_order, local_slots, placing = route_plan(dest_slot, T, rows, cols)
-    start = exchange(tokens[send_order], rows)[placing]
-    cot = exchange(cotangent[send_order], rows)[placing]
     restore = jnp.argsort(send_order)
+    outgoing = tokens[send_order]
+    cot_going = cotangent[send_order]
     if ring:
         me = jnp.stack([lax.axis_index(names[1]), lax.axis_index(cols)]).astype(i32)
         packs = pack([join_qk(bq, bk, 1)] + shards1[2:], HALVES_ONE) + pack(shards2, HALVES_TWO)
         flat = [jnp.concatenate(p, axis=0) for p in packs]
-        near = [ring.gather_z(f) for f in flat[:2]]
-        rest = ring.gather_z_all(jnp.concatenate(flat[2:], axis=0))
-        at = 0
-        for f in flat[2:]:
-            near.append(rest[:, at : at + f.shape[0]])
-            at += f.shape[0]
-        full = []
-        for p, v in zip(packs, near):
-            n1 = p[0].shape[0]
-            full.append(ring.gather_core(ring.gather_hi(ring.gather_lo(v[:, :n1], v[:, n1:]))))
+        near = [ring.gather_z(flat[0])]
+        for f in flat[1:4]:
+            near.append(ring.gather_z(after(f, near[-1], outgoing)))
+        rest = ring.gather_z_all(after(jnp.concatenate(flat[4:], axis=0), near[1]))
+        near += [rest[:, : flat[4].shape[0]], rest[:, flat[4].shape[0] :]]
+        near = [[v[:, : p[0].shape[0]], v[:, p[0].shape[0] :]] for p, v in zip(packs, near)]
+        start = exchange(outgoing, rows)[placing]
     else:
         me = jnp.zeros((2,), i32)
         one, two = gather_all(shards1), gather_all(shards2)
         full = boxes_any([join_qk(one[0], one[1], COLS)] + one[2:], HALVES_ONE) + boxes_any(two, HALVES_TWO)
-    (w_qk, w_v, w_o), w_g, w_u, w_d = weights_of(*full[:3], HALVES_ONE)
-    (v_q, v_k, v_v, v_o), v_g, v_u, v_d = weights_of(*full[3:], HALVES_TWO)
+        start = exchange(outgoing, rows)[placing]
     position = jnp.arange(T, dtype=i32)
     segment, end = jnp.zeros((T,), i32), jnp.zeros((), i32)
     for j in range(lengths.shape[1]):
@@ -907,51 +940,93 @@
     seg_row, seg_col = segment.reshape(1, T), segment.reshape(T, 1)
     live_row, live_col = pad_mask.reshape(1, T), pad_mask.reshape(T, 1)
 
+    tied = after if ring else (lambda value, *arrays: value)
+    if ring:
+        near_a1, near_gu1, near_d1, near_a2, near_gu2, near_d2 = near
+        each = lambda pair, *arrays: [after(v, *arrays) for v in pair]
+        far = lambda halves: [half[1] for half in halves]
+        hi_a1 = ring.gather_hi(ring.gather_lo(near_a1))
+        lo_gu1 = ring.gather_lo(each(near_gu1, *far(hi_a1)))
+        full_a1 = ring.gather_core(hi_a1)
+        start = after(start, *lo_gu1)
+    else:
+        full_a1 = full[0]
+    w_qk, w_v, w_o = attn_weights(full_a1, HALVES_ONE)
     xa1, qk1, v1 = norm_proj(me, start, gain_a1, [w_qk, w_v])
     o1, ou1, rden1 = based_fwd(qk1, v1, seg_row, seg_col, live_row)
-    hm1, xf1 = attn_out(me, start, o1, w_o, gain_m1)
-    g1, u1, hid1 = gate_up(me, xf1, w_g, w_u)
-    h1 = down(me, hm1, hid1, w_d)
-    xa2, q2, k2, v2 = norm_proj(me, h1, gain_a2, [v_q, v_k, v_v])
+    if ring:
+        hi_gu1 = ring.gather_hi(lo_gu1, o1)
+        lo_d1 = ring.gather_lo(each(near_d1, *lo_gu1), o1)
+    hm1, xf1 = attn_out(me, start, tied(o1, *(far(hi_gu1) + lo_d1 if ring else [])), w_o, gain_m1)
+    if ring:
+        full_gu1 = ring.gather_core(hi_gu1, xf1)
+        hi_d1 = ring.gather_hi(lo_d1, xf1)
+        lo_a2 = ring.gather_lo(each(near_a2, *far(hi_gu1)), xf1)
+        cot_going = after(cot_going, xf1)
+        xf1_late = after(xf1, *far(hi_d1), *lo_a2)
+    else:
+        full_gu1, xf1_late = full[1], xf1
+    cot = exchange(cot_going, rows)[placing]
+    w_g, w_u = gate_weights(full_gu1)
+    g1, u1, hid1 = gate_up(me, xf1_late, w_g, w_u)
+    if ring:
+        full_d1 = ring.gather_core(hi_d1, hid1)
+        hi_a2 = ring.gather_hi(lo_a2, hid1)
+        lo_gu2 = each(near_gu2, *far(hi_d1))
+        hid1_late = after(hid1, *far(hi_a2))
+    else:
+        full_d1, hid1_late = full[2], hid1
+    w_d = down_weights(full_d1)
+    h1 = down(me, hm1, hid1_late, w_d)
+    if ring:
+        full_a2 = ring.gather_core(hi_a2, h1)
+        lo_gu2 = ring.gather_lo(lo_gu2, h1)
+        h1_late = after(h1, *lo_gu2)
+    else:
+        full_a2, h1_late = full[3], h1
+    v_q, v_k, v_v, v_o = attn_weights(full_a2, HALVES_TWO)
+    xa2, q2, k2, v2 = norm_proj(me, h1_late, gain_a2, [v_q, v_k, v_v])
     o2 = window_fwd(q2, k2, v2, seg_row, seg_col, live_row)
-    hm2, xf2 = attn_out(me, h1, o2, v_o, gain_m2)
-    g2, u2, hid2 = gate_up(me, xf2, v_g, v_u)
-    h2 = down(me, hm2, hid2, v_d)
-    output = exchange(h2.astype(bf16)[local_slots], rows)[restore]
-
-    tied = tie if ring else (lambda value, *after: (value, after))
-    step = (lambda f, v: f(v)) if ring else (lambda f, v: v)
+    if ring:
+        hi_gu2 = ring.gather_hi(lo_gu2, o2)
+        lo_d2 = ring.gather_lo(each(near_d2, *lo_gu2), o2)
+    hm2, xf2 = attn_out(me, h1, tied(o2, *(far(hi_gu2) + lo_d2 if ring else [])), v_o, gain_m2)
+    if ring:
+        full_gu2 = ring.gather_core(hi_gu2, xf2)
+        hi_d2 = ring.gather_hi(lo_d2, xf2)
+        xf2_late = after(xf2, *far(hi_d2))
+    else:
+        full_gu2, xf2_late = full[4], xf2
+    v_g, v_u = gate_weights(full_gu2)
+    g2, u2, hid2 = gate_up(me, xf2_late, v_g, v_u)
+    v_d = down_weights(ring.gather_core(hi_d2, hid2) if ring else full[5])
+
+    step = (lambda f, v, *behind: f(v, *behind)) if ring else (lambda f, v, *behind: v)
     core, low, high = (ring.reduce_core, ring.reduce_lo, ring.reduce_hi) if ring else (None,) * 3
     dg2, du2, *d2 = down_bwd(me, cot, v_d, hid2, g2, u2)
     gu2 = gate_up_bwd(me, xf2, dg2, du2)
-    d2 = step(core, d2)
-    dg2, d2 = tied(dg2, *d2)
-    gm2, bo2, dor2, gg_m2 = mlp_dx(me, dg2, du2, v_g, v_u, hm2, gain_m2, cot, v_o, bf16)
-    d2, gu2 = step(low, d2), step(core, gu2)
-    dor2, (*d2, gu2a, gu2b) = tied(dor2, *d2, *gu2)
-    dq2, dk2, dv2 = window_bwd(q2, k2, v2, dor2, seg_row, seg_col, live_col)
-    d2, gu2 = step(high, d2), step(low, [gu2a, gu2b])
-    dq2, d2 = tied(dq2, *d2)
-    a2a, a2b, gh1, gg_a2 = attn_bwd(me, xa2, [dq2, dk2, dv2], [v_q, v_k, v_v], o2, bo2, h1, gain_a2, gm2, HALVES_TWO)
-    gh1, gu2 = tied(gh1, *gu2)
-    dg1, du1, *d1 = down_bwd(me, gh1, w_d, hid1, g1, u1)
-    gu2, a2 = step(high, gu2), step(core, [a2a, a2b])
-    dg1, a2 = tied(dg1, *a2)
-    gu1 = gate_up_bwd(me, xf1, dg1, du1)
-    d1 = step(core, d1)
-    dg1, (*gu2, d1a, d1b) = tied(dg1, *gu2, *d1)
-    gm1, bo1, dou1, gg_m1 = mlp_dx(me, dg1, du1, w_g, w_u, hm1, gain_m1, gh1, w_o, f32)
-    a2, gu1 = step(low, a2), step(core, gu1)
-    dou1, (*a2, gu1a, gu1b) = tied(dou1, *a2, *gu1)
-    dqk1, dv1 = based_bwd(qk1, v1, dou1, ou1, rden1, seg_row, seg_col, live_col)
-    d1 = step(low, [d1a, d1b])
-    dqk1, d1 = tied(dqk1, *d1)
-    a1a, a1b, g0, gg_a1 = attn_bwd(me, xa1, [dqk1, dv1], [w_qk, w_v], o1, bo1, start, gain_a1, gm1, HALVES_ONE)
+    d2 = step(core, d2, gu2[0])
+    gm2, bo2, dor2, gg_m2 = mlp_dx(me, tied(dg2, *d2, *gu2), du2, v_g, v_u, hm2, gain_m2, cot, v_o, bf16)
+    d2, gu2 = step(low, d2, gm2), step(core, gu2, gm2)
+    dq2, dk2, dv2 = window_bwd(q2, k2, v2, tied(dor2, *d2, *gu2), seg_row, seg_col, live_col)
+    d2 = step(high, d2, dq2)
+    *a2, gh1, gg_a2 = attn_bwd(me, xa2, [tied(dq2, *d2), dk2, dv2], [v_q, v_k, v_v], o2, bo2, h1, gain_a2, gm2, HALVES_TWO)
+    gu2 = step(low, gu2, gh1)
+    dg1, du1, *d1 = down_bwd(me, tied(gh1, *gu2), w_d, hid1, g1, u1)
+    gu2, a2 = step(high, gu2, dg1), step(core, a2, dg1)
+    gu1 = gate_up_bwd(me, xf1, tied(dg1, *gu2, *a2), du1)
+    a2, d1 = step(low, a2, gu1[0]), step(core, d1, gu1[0])
+    gm1, bo1, dou1, gg_m1 = mlp_dx(me, tied(dg1, *a2, *d1, *gu1), du1, w_g, w_u, hm1, gain_m1, gh1, w_o, f32)
+    a2, d1, gu1 = step(high, a2, gm1), step(low, d1, gm1), step(core, gu1, gm1)
+    dqk1, dv1 = based_bwd(qk1, v1, tied(dou1, *a2, *d1, *gu1), ou1, rden1, seg_row, seg_col, live_col)
+    d1 = step(high, d1, dqk1)
+    *a1, g0, gg_a1 = attn_bwd(me, xa1, [tied(dqk1, *d1), dv1], [w_qk, w_v], o1, bo1, start, gain_a1, gm1, HALVES_ONE)
+    gu1 = step(low, gu1, g0)
+    h2 = down(me, tied(hm2, g0), hid2, v_d)
+    output = exchange(h2.astype(bf16)[local_slots], rows)[restore]
     gains = jnp.concatenate([gg_a1, gg_m1, gg_a2, gg_m2], axis=0)
     if ring:
-        a1 = core([a1a, a1b])
-        gu1 = low([gu1a, gu1b])
-        d1, a2, gu1, a1 = high(d1), high(a2), high(gu1), high(low(a1))
+        gu1, a1 = high(gu1), high(low(core(a1)))
         sums = []
         for a, gu, d, halves in ((a1, gu1, d1, HALVES_ONE), (a2, gu2, d2, HALVES_TWO)):
             last = halves is HALVES_ONE
@@ -964,7 +1039,7 @@
         for axis, by in (("core", 1), ("x", 1), ("y", 1), ("z", 1), ("z", 2)):
             gains = gains + ring.swap(gains, axis, by)
     else:
-        sums1 = sum_any(d1, [gu1a, gu1b], [a1a, a1b], HALVES_ONE)
+        sums1 = sum_any(d1, gu1, a1, HALVES_ONE)
         sums2 = sum_any(d2, gu2, a2, HALVES_TWO)
         gains = lax.psum(gains, ("row", "col"))
     tokens_grad = exchange(g0.astype(bf16)[local_slots], rows)[restore]

time: 979 us -> 789 us (0.81)
  waiting for transfers between devices: 359 us -> 175 us
  local copies, waits for them, and re-layouts: 106 us -> 55.2 us
  starting transfers between devices: 104 us -> 126 us
  other arithmetic: 92.2 us -> 110 us
    ppermute x101 -> x107, waiting for transfers between devices: 359 us -> 170 us  [swap(): lax.ppermute(value, self.axes, [(i, i ^ by << shift) for i in range(32)])]
    squeeze x36 -> x0, local copies, waits for them, and re-layouts: 45.9 us -> none  [the longest x12 26.5 us: reduce_core(): return [g[0] + self.swap(g[1], 'core') for g in pair]]
    ppermute x101 -> x107, starting transfers between devices: 82.8 us -> 107 us  [swap(): lax.ppermute(value, self.axes, [(i, i ^ by << shift) for i in range(32)])]
    unnamed x188 -> x140, local copies, waits for them, and re-layouts: 20.9 us -> 15.5 us
  transfers between devices with their start and end apart: 110 -> 116, of which waited for: 27 -> 31; matrix products, arithmetic and copies ran while one was open for 18% -> 19% of each run, Pallas kernels for 28% -> 36%
where the time goes in v3:
time: 789 us; the launch traced here: 782 us
  Pallas kernels  295 us (37%)
  waiting for transfers between devices  175 us (22%)
  starting transfers between devices  126 us (16%)
  other arithmetic  110 us (14%)
  local copies, waits for them, and re-layouts  55.2 us (7%)
  between operations  20.2 us (3%)
    pallas_call x20, Pallas kernels, call(): pl.pallas_call(body, out_shape=out_shape, grid_spec=pltpu.PrefetchScalarG...  295 us
    ppermute x107, waiting for transfers between devices, swap(): lax.ppermute(value, self.axes, [(i, i ^ by << shift) for i in range(32)])  170 us
    ppermute x107, starting transfers between devices, swap(): lax.ppermute(value, self.axes, [(i, i ^ by << shift) for i in range(32)])  107 us
    add x12, other arithmetic, reduce_core(): out += [own[0] + got[0], own[1] + got[1]]  32 us
    all_to_all x4, starting transfers between devices, exchange(): lax.all_to_all(value.reshape(row_count, n // row_count, width), axis, spl...  18.3 us
    add x12, other arithmetic, reduce_lo(): out += [keep[0] + got[0], keep[1] + got[1]]  18.1 us
  transfers between devices with their start and end apart: 116, of which 31 were waited for; matrix products, arithmetic and copies ran while one was open for 19% of the time, Pallas kernels for 36%

profile of v3, /device:TPU:0, one launch (start us, length us, event | category | flops | bytes accessed | tf_op | source)
XLA Modules:
  0.0 781.6 jit_solution(15097887181675012635)
XLA Ops:
  63.4 26.4 %collective-permute-done.4 = bf16[1408,128]{1,0:T(8,128)(2,1)S(1)} collective-permute-done((bf16[1408,128]{1,0:T(8,128)(2,1)S(1)}, bf16[1408,128]{1,0:T(8,128)(2,1)S(1)}, u32[]{:S(2)}, u32[]{:S(2)}) %collective-permute-start.4) | collective-permute-done | bytes 360480 | tf_op jit(solution)/shard_map/ppermute | solution.py:746
  115.8 10.3 %collective-permute-start.27 = (bf16[1024,128]{1,0:T(8,128)(2,1)}, bf16[1024,128]{1,0:T(8,128)(2,1)}, u32[]{:S(2)}, u32[]{:S(2)}) collective-permute-start(bf16[1024,128]{1,0:T(8,128)(2,1)} %slice_dynamic-update-slice_fusion), channel_id=1, source_target_pairs={{0,8},{1,9},{2,10},{3,11},{4,12},{5,13},{6,14},{7,15},{8,0},{9,1},... | collective-permute-start | bytes 786440 | tf_op jit(solution)/shard_map/ppermute | solution.py:746
  145.9 10.2 %shard_map.374 = (bf16[512,1024]{1,0:T(8,128)(2,1)}, bf16[512,512]{1,0:T(8,128)(2,1)}, bf16[512,1024]{1,0:T(8,128)(2,1)}) custom-call(s32[2]{0:T(128)} %pad_add_fusion.me_ref, bf16[512,1024]{1,0:T(8,128)(2,1)} %gather_fusion.1, f32[1,1024]{1,0:T(1,128)} %bitcast.460, bf16[2,4,384,128]{3,2,1,0:T(8,128)(2,1)} %copy-done.5, ...), custom_call_target="tpu_custom_call" | custom-call | flops 1610612736 | bytes 8916992 | tf_op jit(solution)/shard_map/pallas_call | solution.py:55
  164.8 10.8 %collective-permute-done.21 = bf16[4,352,128]{2,1,0:T(8,128)(2,1)} collective-permute-done((bf16[4,352,128]{2,1,0:T(8,128)(2,1)}, bf16[4,352,128]{2,1,0:T(8,128)(2,1)}, u32[]{:S(2)}, u32[]{:S(2)}) %collective-permute-start.21) | collective-permute-done | bytes 360480 | tf_op jit(solution)/shard_map/ppermute | solution.py:746
  181.9 12.3 %collective-permute-done.23.refs_3_.refs_5_ = bf16[2,4,352,128]{3,2,1,0:T(8,128)(2,1)} collective-permute-done((bf16[2,4,352,128]{3,2,1,0:T(8,128)(2,1)S(1)}, bf16[2,4,352,128]{3,2,1,0:T(8,128)(2,1)}, u32[]{:S(2)}, u32[]{:S(2)}) %collective-permute-start.23) | collective-permute-done | bytes 720928 | tf_op jit(solution)/shard_map/ppermute | solution.py:746
  222.9 13.6 %shard_map.377 = (bf16[2816,512]{1,0:T(8,128)(2,1)}, bf16[2816,512]{1,0:T(8,128)(2,1)}, bf16[2816,512]{1,0:T(8,128)(2,1)}) custom-call(s32[2]{0:T(128)} %pad_add_fusion.me_ref, bf16[512,1024]{1,0:T(8,128)(2,1)} %get-tuple-element.211.refs_0_.xf_ref, bf16[2,4,704,128]{3,2,1,0:T(8,128)(2,1)} %pad_maximum_fusion.1.refs_1_.refs_5_, ...), custom_call_target="tpu_custom_call" | custom-call | flops 5905580032 | bytes 21233664 | tf_op jit(solution)/shard_map/pallas_call | solution.py:55
  244.6 11.0 %shard_map.378.refs_0_.refs_2_ = f32[512,1024]{1,0:T(8,128)} custom-call(s32[2]{0:T(128)} %pad_add_fusion.me_ref, f32[512,1024]{1,0:T(8,128)} %get-tuple-element.202.refs_0_.refs_2_, bf16[2816,512]{1,0:T(8,128)(2,1)} %get-tuple-element.219.refs_1_, bf16[2,4,352,128]{3,2,1,0:T(8,128)(2,1)} %copy-done.17, ...), custom_call_target="tpu_custom_call" | custom-call | flops 2952790016 | bytes 12845056 | tf_op jit(solution)/shard_map/pallas_call | solution.py:55
  275.2 12.6 %shard_map.379 = (bf16[512,1024]{1,0:T(8,128)(2,1)}, bf16[512,1024]{1,0:T(8,128)(2,1)}, bf16[512,1024]{1,0:T(8,128)(2,1)}, bf16[512,1024]{1,0:T(8,128)(2,1)}) custom-call(s32[2]{0:T(128)} %pad_add_fusion.me_ref, f32[512,1024]{1,0:T(8,128)} %shard_map.378.refs_0_.refs_2_, f32[1,1024]{1,0:T(1,128)} %bitcast.452, bf16[2,4,512,128]{3,2,1,0:T(8,128)(2,1)} %copy-done.3, ...), custom_call_target="tpu_custom_call" | custom-call | flops 3221225472 | bytes 18878464 | tf_op jit(solution)/shard_map/pallas_call | solution.py:55
  287.8 24.3 %shard_map.380.refs_1_ = bf16[512,1024]{1,0:T(8,128)(2,1)} custom-call(bf16[512,1024]{1,0:T(8,128)(2,1)} %get-tuple-element.234.q_ref, bf16[512,1024]{1,0:T(8,128)(2,1)} %get-tuple-element.235.k_ref, bf16[512,1024]{1,0:T(8,128)(2,1)} %get-tuple-element.236.v_ref, s32[1,512]{1,0:T(1,128)} %fusion.74.sr_ref, s32[512,1]{1,0:T(8,128)} %convert_add_fusion.2.sc_ref, ...), custom_call_target="tpu_custom_call" | custom-call | flops 1610612736 | bytes 4200448 | tf_op jit(solution)/shard_map/pallas_call | solution.py:55
  313.5 16.0 %collective-permute-done.50.refs_5_.refs_3_ = bf16[2,4,352,128]{3,2,1,0:T(8,128)(2,1)} collective-permute-done((bf16[2,4,352,128]{3,2,1,0:T(8,128)(2,1)S(1)}, bf16[2,4,352,128]{3,2,1,0:T(8,128)(2,1)}, u32[]{:S(2)}, u32[]{:S(2)}) %collective-permute-start.50) | collective-permute-done | bytes 720928 | tf_op jit(solution)/shard_map/ppermute | solution.py:746
  350.5 13.6 %shard_map.382 = (bf16[2816,512]{1,0:T(8,128)(2,1)}, bf16[2816,512]{1,0:T(8,128)(2,1)}, bf16[2816,512]{1,0:T(8,128)(2,1)}) custom-call(s32[2]{0:T(128)} %pad_add_fusion.me_ref, bf16[512,1024]{1,0:T(8,128)(2,1)} %get-tuple-element.251.refs_0_.xf_ref, bf16[2,4,704,128]{3,2,1,0:T(8,128)(2,1)} %pad_maximum_fusion.3.refs_1_.refs_5_, ...), custom_call_target="tpu_custom_call" | custom-call | flops 5905580032 | bytes 21233664 | tf_op jit(solution)/shard_map/pallas_call | solution.py:55
  364.1 16.2 %shard_map.383 = (bf16[2816,512]{1,0:T(8,128)(2,1)}, bf16[2816,512]{1,0:T(8,128)(2,1)}, bf16[2,2,4,352,128]{4,3,2,1,0:T(8,128)(2,1)}, bf16[2,2,4,352,128]{4,3,2,...) custom-call(s32[2]{0:T(128)} %pad_add_fusion.me_ref, ...), custom_call_target="tpu_custom_call" | custom-call | flops 5905580032 | bytes 27000832 | tf_op jit(solution)/shard_map/pallas_call | solution.py:55
  380.9 14.4 %shard_map.384 = (bf16[2,2,4,704,128]{4,3,2,1,0:T(8,128)(2,1)}, bf16[2,2,4,704,128]{4,3,2,1,0:T(8,128)(2,1)}, bf16[2,2,4,704,128]{4,3,2,1,0:T(8,128)(2,1)}, bf16[2,2,4,704,128]{4,3,2,1,0:T(8,128)(2,1)}) custom-call(s32[2]{0:T(128)} %pad_add_fusion.me_ref, bf16[512,1024]{1,0:T(8,128)(2,1)} %get-tuple-element.251.refs_0_.xf_ref, ...), custom_call_target="tpu_custom_call" | custom-call | flops 5905580032 | bytes 18350080 | tf_op jit(solution)/shard_map/pallas_call | solution.py:55
  401.2 18.7 %shard_map.385 = (f32[512,1024]{1,0:T(8,128)}, bf16[512,1024]{1,0:T(8,128)(2,1)}, bf16[512,1024]{1,0:T(8,128)(2,1)}, f32[1,1024]{1,0:T(1,128)}) custom-call(s32[2]{0:T(128)} %pad_add_fusion.me_ref, bf16[2816,512]{1,0:T(8,128)(2,1)} %get-tuple-element.275.dg_ref.refs_0_, bf16[2816,512]{1,0:T(8,128)(2,1)} %get-tuple-element.266.du_ref.refs_1_, ...), custom_call_target="tpu_custom_call" | custom-call | flops 6979321856 | bytes 28844032 | tf_op jit(solution)/shard_map/pallas_call | solution.py:55
  431.7 18.6 %shard_map.386 = (bf16[512,1024]{1,0:T(8,128)(2,1)}, bf16[512,1024]{1,0:T(8,128)(2,1)}, bf16[512,1024]{1,0:T(8,128)(2,1)}) custom-call(bf16[512,1024]{1,0:T(8,128)(2,1)} %get-tuple-element.234.q_ref, bf16[512,1024]{1,0:T(8,128)(2,1)} %get-tuple-element.235.k_ref, bf16[512,1024]{1,0:T(8,128)(2,1)} %get-tuple-element.236.v_ref, ...), custom_call_target="tpu_custom_call" | custom-call | flops 4026531840 | bytes 7346176 | tf_op jit(solution)/shard_map/pallas_call | solution.py:55
  450.5 20.7 %shard_map.387 = (bf16[2,2,4,512,128]{4,3,2,1,0:T(8,128)(2,1)}, bf16[2,2,4,512,128]{4,3,2,1,0:T(8,128)(2,1)}, bf16[2,2,4,512,128]{4,3,2,1,0:T(8,128)(2,1)}, bf16...) custom-call(s32[2]{0:T(128)} %pad_add_fusion.me_ref, ...), custom_call_target="tpu_custom_call" | custom-call | flops 7516192768 | bytes 33562624 | tf_op jit(solution)/shard_map/pallas_call | solution.py:55
  484.1 16.7 %shard_map.388 = (bf16[2816,512]{1,0:T(8,128)(2,1)}, bf16[2816,512]{1,0:T(8,128)(2,1)}, bf16[2,2,4,352,128]{4,3,2,1,0:T(8,128)(2,1)}, bf16[2,2,4,352,128]{4,3,2,...) custom-call(s32[2]{0:T(128)} %pad_add_fusion.me_ref, ...), custom_call_target="tpu_custom_call" | custom-call | flops 5905580032 | bytes 28049408 | tf_op jit(solution)/shard_map/pallas_call | solution.py:55
  510.9 13.9 %shard_map.389 = (bf16[2,2,4,704,128]{4,3,2,1,0:T(8,128)(2,1)}, bf16[2,2,4,704,128]{4,3,2,1,0:T(8,128)(2,1)}, bf16[2,2,4,704,128]{4,3,2,1,0:T(8,128)(2,1)}, bf16[2,2,4,704,128]{4,3,2,1,0:T(8,128)(2,1)}) custom-call(s32[2]{0:T(128)} %pad_add_fusion.me_ref, bf16[512,1024]{1,0:T(8,128)(2,1)} %get-tuple-element.211.refs_0_.xf_ref, ...), custom_call_target="tpu_custom_call" | custom-call | flops 5905580032 | bytes 18350080 | tf_op jit(solution)/shard_map/pallas_call | solution.py:55
  549.1 19.4 %shard_map.390 = (f32[512,1024]{1,0:T(8,128)}, bf16[512,1024]{1,0:T(8,128)(2,1)}, f32[512,1024]{1,0:T(8,128)}, f32[1,1024]{1,0:T(1,128)}) custom-call(s32[2]{0:T(128)} %pad_add_fusion.me_ref, bf16[2816,512]{1,0:T(8,128)(2,1)} %get-tuple-element.319.dg_ref.refs_0_, bf16[2816,512]{1,0:T(8,128)(2,1)} %get-tuple-element.306.du_ref.refs_1_, ...), custom_call_target="tpu_custom_call" | custom-call | flops 6979321856 | bytes 29892608 | tf_op jit(solution)/shard_map/pallas_call | solution.py:55
  584.4 15.8 %shard_map.391 = (bf16[512,512]{1,0:T(8,128)(2,1)}, bf16[512,1024]{1,0:T(8,128)(2,1)}) custom-call(bf16[512,512]{1,0:T(8,128)(2,1)} %get-tuple-element.191.qk_ref, bf16[512,1024]{1,0:T(8,128)(2,1)} %get-tuple-element.192.v_ref, f32[512,1024]{1,0:T(8,128)} %get-tuple-element.329.dou_ref, f32[512,1024]{1,0:T(8,128)} %get-tuple-element.330.ou_ref, ...), custom_call_target="tpu_custom_call" | custom-call | flops 4026531840 | bytes 9443328 | tf_op jit(solution)/shard_map/pallas_call | solution.py:55
  603.2 20.9 %shard_map.392 = (bf16[2,2,4,256,128]{4,3,2,1,0:T(8,128)(2,1)}, bf16[2,2,4,256,128]{4,3,2,1,0:T(8,128)(2,1)}, bf16[2,2,4,384,128]{4,3,2,1,0:T(8,128)(2,1)}, bf16...) custom-call(s32[2]{0:T(128)} %pad_add_fusion.me_ref, ...), custom_call_target="tpu_custom_call" | custom-call | flops 4294967296 | bytes 20455424 | tf_op jit(solution)/shard_map/pallas_call | solution.py:55
  624.9 11.1 %shard_map.393 = f32[512,1024]{1,0:T(8,128)} custom-call(s32[2]{0:T(128)} %pad_add_fusion.me_ref, f32[512,1024]{1,0:T(8,128)} %get-tuple-element.338.refs_2_.refs_0_, bf16[2816,512]{1,0:T(8,128)(2,1)} %get-tuple-element.256.refs_1_, bf16[2,4,352,128]{3,2,1,0:T(8,128)(2,1)} %copy-done.15, bf16[2,4,352,128]{3,2,1,0:T(8,128)(2,1)} %collective-permute-done.50.refs_5_.refs_3_, ...), custom_call_target="tpu_custom_call" | custom-call | flops 2952790016 | bytes 12845056 | tf_op jit(solution)/shard_map/pallas_call | solution.py:55
  726.6 13.6 %collective-permute-done.93 = bf16[4,256,128]{2,1,0:T(8,128)(2,1)} collective-permute-done((bf16[4,256,128]{2,1,0:T(8,128)(2,1)}, bf16[4,256,128]{2,1,0:T(8,128)(2,1)}, u32[]{:S(2)}, u32[]{:S(2)}) %collective-permute-start.93) | collective-permute-done | bytes 262176 | tf_op jit(solution)/shard_map/ppermute | solution.py:746
  743.4 9.9 %collective-permute-done.105 = bf16[1408,128]{1,0:T(8,128)(2,1)S(1)} collective-permute-done((bf16[1408,128]{1,0:T(8,128)(2,1)S(1)}, bf16[1408,128]{1,0:T(8,128)(2,1)S(1)}, u32[]{:S(2)}, u32[]{:S(2)}) %collective-permute-start.105) | collective-permute-done | bytes 360480 | tf_op jit(solution)/shard_map/ppermute | solution.py:746
  (525 shorter events, 390.5 us)
Async XLA Ops:
  27.3 115.7 %all-to-all-start = ((bf16[8,64,1024]{2,1,0:T(8,128)(2,1)}), bf16[8,64,1024]{2,1,0:T(8,128)(2,1)S(1)}, u32[]{:S(2)}, u32[]{:S(2)}) async-start(bf16[8,64,1024]{2,1,0:T(8,128)(2,1)} %bitcast.3), calls=%async_computation | async-start | bytes 2097152 | tf_op jit(solution)/shard_map/all_to_all | solution.py:901
  34.2 185.7 %all-gather.3.cloned.1.call-start = ((), (), s32[]{:S(2)}) async-start(), calls=%async_computation.12 | async-start | bytes 2703360 | tf_op jit(solution)/shard_map/all_gather | solution.py:757
  57.0 38.8 %collective-permute-start.7 = (bf16[2,4,256,128]{3,2,1,0:T(8,128)(2,1)}, bf16[2,4,256,128]{3,2,1,0:T(8,128)(2,1)S(1)}, u32[]{:S(2)}, u32[]{:S(2)}) collective-permute-start(bf16[2,4,256,128]{3,2,1,0:T(8,128)(2,1)} %pad_maximum_fusion.20.refs_6_.refs_12_), channel_id=1, source_target_pairs={{0,4},{1,5},{2,6},{3,7},{4,0},{5,1},{6,2},{7,3},{8,12},{9,13},{10,... | collective-permute-start | bytes 1572872 | tf_op jit(solution)/shard_map/ppermute | solution.py:746
  131.7 49.0 %collective-permute-start.16 = (bf16[2,4,704,128]{3,2,1,0:T(8,128)(2,1)}, bf16[2,4,704,128]{3,2,1,0:T(8,128)(2,1)}, u32[]{:S(2)}, u32[]{:S(2)}) collective-permute-start(bf16[2,4,704,128]{3,2,1,0:T(8,128)(2,1)} %pad_maximum_fusion.1.refs_1_.refs_5_), channel_id=1, source_target_pairs={{0,4},{1,5},{2,6},{3,7},{4,0},{5,1},{6,2},{7,3},{8,12},{9,13},{10,... | collective-permute-start | bytes 4325384 | tf_op jit(solution)/shard_map/ppermute | solution.py:746
  134.4 46.4 %collective-permute-start.17 = (bf16[2,4,704,128]{3,2,1,0:T(8,128)(2,1)}, bf16[2,4,704,128]{3,2,1,0:T(8,128)(2,1)}, u32[]{:S(2)}, u32[]{:S(2)}) collective-permute-start(bf16[2,4,704,128]{3,2,1,0:T(8,128)(2,1)} %pad_maximum_fusion.2.refs_5_.refs_9_), channel_id=1, source_target_pairs={{0,2},{1,3},{2,0},{3,1},{4,6},{5,7},{6,4},{7,5},{8,10},{9,11},{10,... | collective-permute-start | bytes 4325384 | tf_op jit(solution)/shard_map/ppermute | solution.py:746
  137.9 37.7 %collective-permute-start.21 = (bf16[4,352,128]{2,1,0:T(8,128)(2,1)}, bf16[4,352,128]{2,1,0:T(8,128)(2,1)}, u32[]{:S(2)}, u32[]{:S(2)}) collective-permute-start(bf16[4,352,128]{2,1,0:T(8,128)(2,1)} %get-tuple-element.197), channel_id=1, source_target_pairs={{0,2},{1,3},{2,0},{3,1},{4,6},{5,7},{6,4},{7,5},{8,10},{9,11},{10,... | collective-permute-start | bytes 1081352 | tf_op jit(solution)/shard_map/ppermute | solution.py:746
  221.4 37.6 %collective-permute-start.40 = (bf16[4,704,128]{2,1,0:T(8,128)(2,1)S(1)}, bf16[4,704,128]{2,1,0:T(8,128)(2,1)S(1)}, u32[]{:S(2)}, u32[]{:S(2)}) collective-permute-start(bf16[4,704,128]{2,1,0:T(8,128)(2,1)S(1)} %get-tuple-element.225), channel_id=1, source_target_pairs={{0,2},{1,3},{2,0},{3,1},{4,6},{5,7},{6,4},{7,5},{8,10},{9,11},{10,... | collective-permute-start | bytes 2162696 | tf_op jit(solution)/shard_map/ppermute | solution.py:746
  222.0 38.2 %collective-permute-start.41 = (bf16[4,704,128]{2,1,0:T(8,128)(2,1)S(1)}, bf16[4,704,128]{2,1,0:T(8,128)(2,1)S(1)}, u32[]{:S(2)}, u32[]{:S(2)}) collective-permute-start(bf16[4,704,128]{2,1,0:T(8,128)(2,1)S(1)} %get-tuple-element.227), channel_id=1, source_target_pairs={{0,4},{1,5},{2,6},{3,7},{4,0},{5,1},{6,2},{7,3},{8,12},{9,13},{10,... | collective-permute-start | bytes 2162696 | tf_op jit(solution)/shard_map/ppermute | solution.py:746
  222.9 39.6 %collective-permute-start.42 = (bf16[2,4,512,128]{3,2,1,0:T(8,128)(2,1)S(1)}, bf16[2,4,512,128]{3,2,1,0:T(8,128)(2,1)S(1)}, u32[]{:S(2)}, u32[]{:S(2)}) collective-permute-start(bf16[2,4,512,128]{3,2,1,0:T(8,128)(2,1)S(1)} %pad_maximum_fusion.7.refs_2_.refs_6_.refs_9_.refs_13_), channel_id=1, source_target_pairs={{0,1},{1,0},{2,3},{3,2},{4,5},{5,4},{6,7},{7,6},{8,9},{9,8},{10,11... | collective-permute-start | bytes 3145736 | tf_op jit(solution)/shard_map/ppermute | solution.py:746
  260.2 52.2 %collective-permute-start.46 = (bf16[2,4,704,128]{3,2,1,0:T(8,128)(2,1)}, bf16[2,4,704,128]{3,2,1,0:T(8,128)(2,1)}, u32[]{:S(2)}, u32[]{:S(2)}) collective-permute-start(bf16[2,4,704,128]{3,2,1,0:T(8,128)(2,1)} %pad_maximum_fusion.3.refs_1_.refs_5_), channel_id=1, source_target_pairs={{0,4},{1,5},{2,6},{3,7},{4,0},{5,1},{6,2},{7,3},{8,12},{9,13},{10,... | collective-permute-start | bytes 4325384 | tf_op jit(solution)/shard_map/ppermute | solution.py:746
  263.4 49.5 %collective-permute-start.47 = (bf16[2,4,704,128]{3,2,1,0:T(8,128)(2,1)}, bf16[2,4,704,128]{3,2,1,0:T(8,128)(2,1)}, u32[]{:S(2)}, u32[]{:S(2)}) collective-permute-start(bf16[2,4,704,128]{3,2,1,0:T(8,128)(2,1)} %pad_maximum_fusion.4.refs_5_.refs_9_), channel_id=1, source_target_pairs={{0,2},{1,3},{2,0},{3,1},{4,6},{5,7},{6,4},{7,5},{8,10},{9,11},{10,... | collective-permute-start | bytes 4325384 | tf_op jit(solution)/shard_map/ppermute | solution.py:746
  267.7 80.0 %all-to-all-start.1 = ((bf16[8,64,1024]{2,1,0:T(8,128)(2,1)}), bf16[8,64,1024]{2,1,0:T(8,128)(2,1)S(1)}, u32[]{:S(2)}, u32[]{:S(2)}) async-start(bf16[8,64,1024]{2,1,0:T(8,128)(2,1)} %bitcast.411), calls=%async_computation.1 | async-start | bytes 2097152 | tf_op jit(solution)/shard_map/all_to_all | solution.py:901
  271.3 255.1 %reduce-scatter.11.cloned.1.call-start = ((), (), s32[]{:S(2)}) async-start(), calls=%async_computation.11 | async-start | bytes 901120 | tf_op jit(solution)/shard_map/reduce_scatter | solution.py:799
  272.7 39.4 %collective-permute-start.48 = (bf16[4,352,128]{2,1,0:T(8,128)(2,1)S(1)}, bf16[4,352,128]{2,1,0:T(8,128)(2,1)S(1)}, u32[]{:S(2)}, u32[]{:S(2)}) collective-permute-start(bf16[4,352,128]{2,1,0:T(8,128)(2,1)S(1)} %get-tuple-element.239), channel_id=1, source_target_pairs={{0,2},{1,3},{2,0},{3,1},{4,6},{5,7},{6,4},{7,5},{8,10},{9,11},{10,... | collective-permute-start | bytes 1081352 | tf_op jit(solution)/shard_map/ppermute | solution.py:746
  273.3 40.1 %collective-permute-start.49 = (bf16[4,352,128]{2,1,0:T(8,128)(2,1)S(1)}, bf16[4,352,128]{2,1,0:T(8,128)(2,1)S(1)}, u32[]{:S(2)}, u32[]{:S(2)}) collective-permute-start(bf16[4,352,128]{2,1,0:T(8,128)(2,1)S(1)} %get-tuple-element.241), channel_id=1, source_target_pairs={{0,4},{1,5},{2,6},{3,7},{4,0},{5,1},{6,2},{7,3},{8,12},{9,13},{10,... | collective-permute-start | bytes 1081352 | tf_op jit(solution)/shard_map/ppermute | solution.py:746
  429.3 47.9 %collective-permute-start.68 = (bf16[2,4,704,128]{3,2,1,0:T(8,128)(2,1)}, bf16[2,4,704,128]{3,2,1,0:T(8,128)(2,1)}, u32[]{:S(2)}, u32[]{:S(2)}) collective-permute-start(bf16[2,4,704,128]{3,2,1,0:T(8,128)(2,1)} %get-tuple-element.417), channel_id=1, source_target_pairs={{0,2},{1,3},{2,0},{3,1},{4,6},{5,7},{6,4},{7,5},{8,10},{9,11},{10,... | collective-permute-start | bytes 4325384 | tf_op jit(solution)/shard_map/ppermute | solution.py:746
  430.8 46.5 %collective-permute-start.69 = (bf16[2,4,704,128]{3,2,1,0:T(8,128)(2,1)}, bf16[2,4,704,128]{3,2,1,0:T(8,128)(2,1)}, u32[]{:S(2)}, u32[]{:S(2)}) collective-permute-start(bf16[2,4,704,128]{3,2,1,0:T(8,128)(2,1)} %get-tuple-element.415), channel_id=1, source_target_pairs={{0,4},{1,5},{2,6},{3,7},{4,0},{5,1},{6,2},{7,3},{8,12},{9,13},{10,... | collective-permute-start | bytes 4325384 | tf_op jit(solution)/shard_map/ppermute | solution.py:746
  477.2 191.5 %reduce-scatter.9.cloned.1.call-start = ((), (), s32[]{:S(2)}) async-start(), calls=%async_computation.10 | async-start | bytes 1802240 | tf_op jit(solution)/shard_map/reduce_scatter | solution.py:799
  524.8 51.4 %collective-permute-start.82 = (bf16[2,2,4,704,128]{4,3,2,1,0:T(8,128)(2,1)}, bf16[2,2,4,704,128]{4,3,2,1,0:T(8,128)(2,1)}, u32[]{:S(2)}, u32[]{:S(2)}) collective-permute-start(bf16[2,2,4,704,128]{4,3,2,1,0:T(8,128)(2,1)} %get-tuple-element.316), channel_id=1, source_target_pairs={{0,1},{1,0},{2,3},{3,2},{4,5},{5,4},{6,7},{7,6},{8,9},{9,8},{10,11... | collective-permute-start | bytes 8650760 | tf_op jit(solution)/shard_map/ppermute | solution.py:746
  526.0 146.8 %reduce-scatter.7.cloned.1.call-start = ((), (), s32[]{:S(2)}) async-start(), calls=%async_computation.9 | async-start | bytes 1310720 | tf_op jit(solution)/shard_map/reduce_scatter | solution.py:799
  527.4 53.0 %collective-permute-start.83 = (bf16[2,2,4,704,128]{4,3,2,1,0:T(8,128)(2,1)}, bf16[2,2,4,704,128]{4,3,2,1,0:T(8,128)(2,1)}, u32[]{:S(2)}, u32[]{:S(2)}) collective-permute-start(bf16[2,2,4,704,128]{4,3,2,1,0:T(8,128)(2,1)} %get-tuple-element.318), channel_id=1, source_target_pairs={{0,1},{1,0},{2,3},{3,2},{4,5},{5,4},{6,7},{7,6},{8,9},{9,8},{10,11... | collective-permute-start | bytes 8650760 | tf_op jit(solution)/shard_map/ppermute | solution.py:746
  645.2 51.2 %reduce-scatter.5.cloned.1.call-start = ((), (), s32[]{:S(2)}) async-start(), calls=%async_computation.8 | async-start | bytes 901120 | tf_op jit(solution)/shard_map/reduce_scatter | solution.py:799
  652.6 40.6 %collective-permute-start.102 = (bf16[2,4,704,128]{3,2,1,0:T(8,128)(2,1)}, bf16[2,4,704,128]{3,2,1,0:T(8,128)(2,1)}, u32[]{:S(2)}, u32[]{:S(2)}) collective-permute-start(bf16[2,4,704,128]{3,2,1,0:T(8,128)(2,1)} %get-tuple-element.411), channel_id=1, source_target_pairs={{0,4},{1,5},{2,6},{3,7},{4,0},{5,1},{6,2},{7,3},{8,12},{9,13},{10,... | collective-permute-start | bytes 4325384 | tf_op jit(solution)/shard_map/ppermute | solution.py:746
  701.1 40.2 %collective-permute-start.95 = (bf16[2,4,384,128]{3,2,1,0:T(8,128)(2,1)}, bf16[2,4,384,128]{3,2,1,0:T(8,128)(2,1)}, u32[]{:S(2)}, u32[]{:S(2)}) collective-permute-start(bf16[2,4,384,128]{3,2,1,0:T(8,128)(2,1)} %get-tuple-element.423), channel_id=1, source_target_pairs={{0,4},{1,5},{2,6},{3,7},{4,0},{5,1},{6,2},{7,3},{8,12},{9,13},{10,... | collective-permute-start | bytes 2359304 | tf_op jit(solution)/shard_map/ppermute | solution.py:746
  (155 other events, 2903.1 us)
Sparse Core Ops, SparseCore 0:
  37.3 2.9 sort.60.cloned.1.call-done
  (1 shorter events, 0.0 us)
Sparse Core Ops, SparseCore 1:
  136.0 45.1 all-gather.2
  477.3 22.3 reduce-scatter.10
  526.1 33.1 reduce-scatter.8
  576.3 26.5 reduce-scatter.6
  671.4 24.7 reduce-scatter.4

commit v4 on v3

--- a/solution.py
+++ b/solution.py
@@ -81,9 +81,6 @@
     def __init__(self, half, swapped, at, n):
         self.bufs, self.swapped, self.at, self.n = half, swapped, at, n
 
-    def ins(self):
-        return [(b, None, None) for b in self.bufs]
-
     def scratch(self):
         return [pltpu.VMEM((2, 2, 2, 4, self.n, 128), bf16), pltpu.SemaphoreType.DMA((2, 2, 2))]
 
@@ -111,6 +108,36 @@
         return box.at[core, x, y, z] if self.swapped else box.at[core, y, x, z]
 
 
+class DownRows:
+    def __init__(self, bufs):
+        self.bufs = bufs
+
+    def scratch(self):
+        return [pltpu.VMEM((2, 4, FFP, 128), bf16), pltpu.SemaphoreType.DMA((2, 4))]
+
+    def start(self, refs, box, sems):
+        for z in range(4):
+            for core in range(2):
+                pltpu.make_async_copy(refs[core].at[z], box.at[core, z], sems.at[core, z]).start()
+
+    def rows(self, box, sems, z, my):
+        for core in range(2):
+            there = box.at[core, z]
+            pltpu.make_async_copy(there, there, sems.at[core, z]).wait()
+        halves = []
+        for y in range(2):
+            parts = []
+            for x, core in PLACES:
+                for at in down_places(x, y ^ my):
+                    parts.append(box[core, z, pl.ds(at, FBP), :])
+            halves.append(jnp.concatenate(parts, axis=1))
+        return jnp.concatenate(halves, axis=0)
+
+
+def down_places(x, y):
+    return [pl.multiple_of(p * FBP, 16) for p in (y * 2 + x, 4 + x * 2 + y)]
+
+
 BLOCKS = [(z, y) for z in range(4) for y in range(2)]
 PLACES = [(x, core) for x in range(2) for core in range(2)]
 
@@ -135,16 +162,17 @@
         self.n_in, self.strips, self.n_out = n_in, strips, n_out
 
     def split(self, refs):
-        n, m = self.n_in, len(self.strips)
-        ins, refs = refs[:n], refs[n:]
-        srcs, refs = refs[: 4 * m], refs[4 * m :]
+        ins, refs = refs[: self.n_in], refs[self.n_in :]
+        srcs = []
+        for s in self.strips:
+            srcs.append(refs[: len(s.bufs)])
+            refs = refs[len(s.bufs) :]
         outs, refs = refs[: self.n_out], refs[self.n_out :]
-        boxes, rest = refs[: 2 * m], refs[2 * m :]
-        hold = [(s, srcs[4 * j : 4 * j + 4], boxes[2 * j], boxes[2 * j + 1]) for j, s in enumerate(self.strips)]
-        return ins, hold, outs, rest
+        hold = [(s, srcs[j], refs[2 * j], refs[2 * j + 1]) for j, s in enumerate(self.strips)]
+        return ins, hold, outs, refs[2 * len(self.strips) :]
 
     def ins(self):
-        return [i for s in self.strips for i in s.ins()]
+        return [(b, None, None) for s in self.strips for b in s.bufs]
 
     def scratch(self):
         return [i for s in self.strips for i in s.scratch()]
@@ -305,35 +333,35 @@
 SPAN = ((0, HALF), (HALF - WINDOW, T))
 
 
-def window_fwd(q, k, v, seg_row, seg_col, live_row):
-    def body(q_ref, k_ref, v_ref, sr_ref, sc_ref, lr_ref, o_ref, mask_ref):
+def window_fwd(q, k, v, seg_row, seg_col, live_col):
+    def body(q_ref, k_ref, v_ref, sr_ref, sc_ref, lc_ref, o_ref, mask_ref):
         @pl.when(pl.program_id(0) == 0)
         def _():
-            fill_mask(mask_ref, sc_ref[...], sr_ref[...], lr_ref[...], 0, WINDOW)
+            fill_mask(mask_ref, sr_ref[...], sc_ref[...], lc_ref[...], 1, WINDOW)
 
         first = lanes((HALF, 128), HEAD_DIM) == 0
         qlane = lanes((T, 128), HEAD_DIM)
         scaled = q_ref[...].astype(f32) * (HEAD_DIM**-0.5)
         for tb in range(2):
-            t0 = tb * HALF
+            at = slice(tb * HALF, tb * HALF + HALF)
             s0, s1 = SPAN[tb]
-            ok = mask_ref[t0 : t0 + HALF, s0:s1] > 0.5
+            ok = mask_ref[s0:s1, at] > 0.5
             got = []
             for e in range(2):
                 qm = jnp.where(qlane == e, scaled, 0.0).astype(bf16)
-                c = dot(qm[t0 : t0 + HALF], k_ref[s0:s1, :], NT)
+                c = dot(k_ref[s0:s1, :], qm[at], NT)
                 c = jnp.where(ok, c, NEG)
-                w = jnp.exp(c - jnp.max(c, axis=-1, keepdims=True))
-                w = w * (1.0 / jnp.sum(w, axis=-1, keepdims=True))
-                got.append(dot(w.astype(bf16), v_ref[s0:s1, :], NN))
-            o_ref[t0 : t0 + HALF, :] = jnp.where(first, got[0], got[1]).astype(bf16)
+                w = jnp.exp(c - jnp.max(c, axis=0, keepdims=True))
+                w = w * (1.0 / jnp.sum(w, axis=0, keepdims=True))
+                got.append(dot(w.astype(bf16), v_ref[s0:s1, :], TN))
+            o_ref[at, :] = jnp.where(first, got[0], got[1]).astype(bf16)
 
     blk = (T, 128)
     col = lambda c: (0, c)
     return call(
         body,
         (8,),
-        [(q, blk, col), (k, blk, col), (v, blk, col), seg_row, seg_col, live_row],
+        [(q, blk, col), (k, blk, col), (v, blk, col), seg_row, seg_col, live_col],
         [((T, D), bf16, blk, col)],
         scratch=[pltpu.VMEM((T, T), f32)],
         flops=HEADS * T * T * 2 * 192,
@@ -450,20 +478,8 @@
     )
 
 
-def down_rows(me_ref, hold, z):
-    (s1, _, box1, _), (s2, _, box2, _) = hold
-    halves = []
-    for y in range(2):
-        yr = y ^ me_ref[0]
-        parts = []
-        for x, core in PLACES:
-            parts += [s1.piece(box1, z, yr, x, core)[...], s2.piece(box2, z, yr, x, core)[...]]
-        halves.append(jnp.concatenate(parts, axis=1))
-    return jnp.concatenate(halves, axis=0)
-
-
-def down(me, hm, hid, strips):
-    kern = Kernel(2, strips, 1)
+def down(me, hm, hid, w_down):
+    kern = Kernel(2, [w_down], 1)
 
     def body(me_ref, *refs):
         (hm_ref, hid_ref), hold, (h_ref,), (acc_ref,) = kern.split(refs)
@@ -473,10 +489,9 @@
         def _():
             start_all(hold)
             regroup(acc_ref, hm_ref, COLS, me_ref[1])
-            for s, _, box, sems in hold:
-                s.wait_all(box, sems)
-
-        acc_ref[...] += dot(hid_ref[...], down_rows(me_ref, hold, i), TN)
+
+        s, _, box, sems = hold[0]
+        acc_ref[...] += dot(hid_ref[...], s.rows(box, sems, i, me_ref[0]), TN)
 
         @pl.when(i == COLS - 1)
         def _():
@@ -489,8 +504,8 @@
     )[0]
 
 
-def down_bwd(me, bd, strips, hid, g, u):
-    kern = Kernel(4, strips, 6)
+def down_bwd(me, bd, w_down, hid, g, u):
+    kern = Kernel(4, [w_down], 4)
 
     def body(me_ref, *refs):
         (bd_ref, hid_ref, g_ref, u_ref), hold, (dg_ref, du_ref, *p_refs), (br_ref,) = kern.split(refs)
@@ -506,17 +521,11 @@
         for x, core in PLACES:
             at = (x * 2 + core) * 256
             for y in range(2):
-                yr = y ^ me_ref[0]
                 rows = slice(y * FBP, (y + 1) * FBP)
-                p_refs[core][x, yr, 0] = gwd[rows, at : at + 128]
-                p_refs[2 + core][yr, x, 0] = gwd[rows, at + 128 : at + 256]
-
-        @pl.when(i == 0)
-        def _():
-            for s, _, box, sems in hold:
-                s.wait_all(box, sems)
-
-        dhid = dot(down_rows(me_ref, hold, i), bdv, NT)
+                for half, to in enumerate(down_places(x, y ^ me_ref[0])):
+                    p_refs[core][0, pl.ds(to, FBP), :] = gwd[rows, at + half * 128 : at + half * 128 + 128]
+        s, _, box, sems = hold[0]
+        dhid = dot(s.rows(box, sems, i, me_ref[0]), bdv, NT)
         gv, uv = g_ref[...].astype(f32), u_ref[...].astype(f32)
         sig = 1.0 / (1.0 + jnp.exp(-gv))
         act = gv * sig
@@ -525,10 +534,10 @@
 
     row = lambda i, me: (i, 0)
     hblk = (FC, T)
-    pieces = ((2, 2, 4, FBP, 128), bf16, (2, 2, 1, FBP, 128), lambda i, me: (0, 0, i, 0, 0))
+    pieces = ((4, FFP, 128), bf16, (1, FFP, 128), lambda i, me: (i, 0, 0))
     return call(
         body, (COLS,), [bd, (hid, hblk, row), (g, hblk, row), (u, hblk, row)] + kern.ins(),
-        [((FFP, T), bf16, hblk, row), ((FFP, T), bf16, hblk, row)] + [pieces] * 4,
+        [((FFP, T), bf16, hblk, row), ((FFP, T), bf16, hblk, row)] + [pieces] * 2,
         scratch=kern.scratch() + [pltpu.VMEM((T, D), bd.dtype)], flops=4 * T * D * FFP, prefetch=me,
     )
 
@@ -712,10 +721,6 @@
     return Strips(bufs[0], False, 0, FC), Strips(bufs[1], True, 0, FC)
 
 
-def down_weights(bufs):
-    return [Strips(bufs[0], False, 0, FBP), Strips(bufs[1], True, 0, FBP)]
-
-
 def pad_hidden(w):
     k = w.shape[0]
     return jnp.pad(w.reshape(k, -1, FB), ((0, 0), (0, 0), (0, FBP - FB))).reshape(k, -1).T
@@ -734,6 +739,34 @@
 
 def after(value, *arrays):
     return lax.optimization_barrier((value, *arrays))[0] if arrays else value
+
+
+def sync(*groups):
+    flat, tree = jax.tree.flatten(groups)
+    return jax.tree.unflatten(tree, lax.optimization_barrier(flat))
+
+
+def add_core(four, got):
+    keep = [four[0][0] + got[0][0], four[2][0] + got[1][0]]
+    return keep, [four[0][1] + got[0][1], four[2][1] + got[1][1]]
+
+
+def add_two(keep, got):
+    return [k[0] + g[0] for k, g in zip(keep, got)], [k[1] + g[1] for k, g in zip(keep, got)]
+
+
+def add_one(keep, got):
+    return [k + g for k, g in zip(keep, got)]
+
+
+def far_rows(total):
+    parts = jnp.split(total, 4, axis=0)
+    return parts[0::2], parts[1::2]
+
+
+def near_rows(halves):
+    parts = [jnp.split(h, 2, axis=0) for h in halves]
+    return [p[0] for p in parts], [p[1] for p in parts]
 
 
 class Ring:
@@ -745,8 +778,8 @@
         shift = {"z": 3, "y": 2, "x": 1, "core": 0}[axis]
         return lax.ppermute(value, self.axes, [(i, i ^ (by << shift)) for i in range(32)])
 
-    def gather_z(self, both):
-        near = [both] + [self.swap(both, "z", by) for by in (1, 2, 3)]
+    def gather_z(self, both, *behind):
+        near = [both] + [after(self.swap(both, "z", by), *behind) for by in (1, 2, 3)]
         low, high = self.z % 2 == 1, self.z >= 2
         a, b = jnp.where(low, near[1], near[0]), jnp.where(low, near[0], near[1])
         c, d = jnp.where(low, near[3], near[2]), jnp.where(low, near[2], near[3])
@@ -766,31 +799,22 @@
     def gather_core(self, full, *behind):
         return [half + [after(self.swap(b, "core"), *behind) for b in half] for half in full]
 
-    def reduce_core(self, four, *behind):
-        out = []
-        for own, send in (four[:2], four[2:]):
-            got = after(self.swap(send, "core"), *behind)
-            out += [own[0] + got[0], own[1] + got[1]]
-        return out
-
-    def reduce_lo(self, four, *behind):
-        out = []
-        for (keep, go), axis in ((four[:2], "x"), (four[2:], "y")):
-            got = after(self.swap(go, axis), *behind)
-            out += [keep[0] + got[0], keep[1] + got[1]]
-        return out
-
-    def reduce_hi(self, four, *behind):
-        pairs = ((four[:2], "y"), (four[2:], "x"))
-        return [keep + after(self.swap(go, axis), *behind) for (keep, go), axis in pairs]
-
-    def reduce_z(self, pair):
+    def gather_down(self, pair):
+        return jnp.stack([jnp.stack(half) for half in self.gather_hi(self.gather_lo(pair))]).reshape(-1, 128)
+
+    def scatter_z(self, value):
+        return lax.psum_scatter(value, self.axes[0], scatter_dimension=0, tiled=False)
+
+    def send(self, values, axes):
+        return [self.swap(v, axis) for v, axis in zip(values, axes)]
+
+    def reduce_z(self, pair, *behind):
         n1 = pair[0].shape[1]
         both = jnp.concatenate(pair, axis=1)
         here = lambda by: lax.dynamic_index_in_dim(both, self.z ^ by, 0, False)
         total = here(0).astype(f32)
         for by in (1, 2, 3):
-            total = total + self.swap(here(by), "z", by).astype(f32)
+            total = total + after(self.swap(here(by), "z", by), *behind).astype(f32)
         return total[:n1], total[n1:]
 
     def reduce_z_all(self, pair):
@@ -820,7 +844,10 @@
     a = boxes(*strips_of([cut(w, D // ROWS, w.shape[1] // COLS) for w in attn], halves))
     hidden = lambda w: pad_hidden(w).reshape(2, 2, FC, 4, 2, 128).transpose(3, 4, 0, 1, 2, 5)
     d = cut(pad_rows(dn), FBP, 256)
-    return [a, boxes(hidden(gate), hidden(up)), boxes(d[..., :128], d[..., 128:])]
+    one = d[..., :128].transpose(3, 0, 1, 2, 4, 5)
+    two = d[..., 128:].transpose(3, 0, 2, 1, 4, 5)
+    d = jnp.stack([one, two], axis=2).reshape(2, 4, FFP, 128)
+    return [a, boxes(hidden(gate), hidden(up)), [d[0], d[1]]]
 
 
 def unpad_hidden(g):
@@ -853,6 +880,10 @@
     return out
 
 
+def sum_parts(a, gu, d, halves):
+    return join_strips(*a, halves) + [unpad_hidden(gu[0]), unpad_hidden(gu[1]), unpad_rows(jnp.concatenate(d, axis=1))]
+
+
 def scatter_any(w):
     part = lax.psum_scatter(w, "row", scatter_dimension=0, tiled=True)
     return lax.psum_scatter(part, "col", scatter_dimension=1, tiled=True).astype(f32)
@@ -865,7 +896,10 @@
 
 def sum_any(pd, pgu, pa, halves):
     pairs = lambda p: (whole_grad(*p[:2], False), whole_grad(*p[2:], True))
-    dn = scatter_any(unpad_rows(natural(jnp.concatenate(pairs(pd), axis=-1))))
+    one, two = jnp.split(jnp.stack(pd).reshape(2, 4, 2, 2, 2, FBP, 128), 2, axis=2)
+    dn = jnp.concatenate([one[:, :, 0], jnp.swapaxes(two[:, :, 0], 2, 3)], axis=-1)
+    dn = dn.transpose(1, 2, 3, 0, 4, 5).reshape(ROWS, COLS, FBP, 256)
+    dn = scatter_any(unpad_rows(natural(dn)))
     gu = [scatter_any(unpad_hidden(g.transpose(1, 2, 0, 3).reshape(FFP, D))) for g in pairs(pgu)]
     blocks = join_strips(*pairs(pa), halves)
     if len(blocks) == 3:
@@ -914,19 +948,24 @@
     shards1, shards2 = [bq, bk, bv, bo_w, wg1, wu1, wd1], [wq, wk, wv, wo2, wg2, wu2, wd2]
     send_order, local_slots, placing = route_plan(dest_slot, T, rows, cols)
     restore = jnp.argsort(send_order)
-    outgoing = tokens[send_order]
+    outgoing = after(tokens[send_order], restore) if ring else tokens[send_order]
     cot_going = cotangent[send_order]
     if ring:
         me = jnp.stack([lax.axis_index(names[1]), lax.axis_index(cols)]).astype(i32)
         packs = pack([join_qk(bq, bk, 1)] + shards1[2:], HALVES_ONE) + pack(shards2, HALVES_TWO)
         flat = [jnp.concatenate(p, axis=0) for p in packs]
-        near = [ring.gather_z(flat[0])]
-        for f in flat[1:4]:
-            near.append(ring.gather_z(after(f, near[-1], outgoing)))
-        rest = ring.gather_z_all(after(jnp.concatenate(flat[4:], axis=0), near[1]))
-        near += [rest[:, : flat[4].shape[0]], rest[:, flat[4].shape[0] :]]
-        near = [[v[:, : p[0].shape[0]], v[:, p[0].shape[0] :]] for p, v in zip(packs, near)]
-        start = exchange(outgoing, rows)[placing]
+        mid_d2 = ring.gather_down(packs[5])
+        split = lambda k, v: [v[:, : packs[k][0].shape[0]], v[:, packs[k][0].shape[0] :]]
+        each = lambda pair, *arrays: [after(v, *arrays) for v in pair]
+        far = lambda halves: [half[1] for half in halves]
+        near_a1 = ring.gather_z(flat[0])
+        hi_a1 = ring.gather_hi(ring.gather_lo(each(split(0, near_a1), mid_d2)))
+        near_gu1 = ring.gather_z(after(flat[1], near_a1))
+        lo_gu1 = ring.gather_lo(each(split(1, near_gu1), *far(hi_a1)))
+        outgoing = after(outgoing, near_gu1, *far(hi_a1))
+        arrived = exchange(outgoing, rows)
+        near_d1 = ring.gather_z(after(flat[2], arrived))
+        start = arrived[placing]
     else:
         me = jnp.zeros((2,), i32)
         one, two = gather_all(shards1), gather_all(shards2)
@@ -942,11 +981,6 @@
 
     tied = after if ring else (lambda value, *arrays: value)
     if ring:
-        near_a1, near_gu1, near_d1, near_a2, near_gu2, near_d2 = near
-        each = lambda pair, *arrays: [after(v, *arrays) for v in pair]
-        far = lambda halves: [half[1] for half in halves]
-        hi_a1 = ring.gather_hi(ring.gather_lo(near_a1))
-        lo_gu1 = ring.gather_lo(each(near_gu1, *far(hi_a1)))
         full_a1 = ring.gather_core(hi_a1)
         start = after(start, *lo_gu1)
     else:
@@ -956,93 +990,148 @@
     o1, ou1, rden1 = based_fwd(qk1, v1, seg_row, seg_col, live_row)
     if ring:
         hi_gu1 = ring.gather_hi(lo_gu1, o1)
-        lo_d1 = ring.gather_lo(each(near_d1, *lo_gu1), o1)
-    hm1, xf1 = attn_out(me, start, tied(o1, *(far(hi_gu1) + lo_d1 if ring else [])), w_o, gain_m1)
+        near_a2 = ring.gather_z(after(flat[3], near_d1), o1)
+    hm1, xf1 = attn_out(me, start, tied(o1, *(far(hi_gu1) + [near_a2] if ring else [])), w_o, gain_m1)
     if ring:
         full_gu1 = ring.gather_core(hi_gu1, xf1)
-        hi_d1 = ring.gather_hi(lo_d1, xf1)
-        lo_a2 = ring.gather_lo(each(near_a2, *far(hi_gu1)), xf1)
-        cot_going = after(cot_going, xf1)
-        xf1_late = after(xf1, *far(hi_d1), *lo_a2)
+        lo_d1 = ring.gather_lo(each(split(2, near_d1), *far(hi_gu1)), xf1)
+        xf1_late = after(xf1, *lo_d1)
     else:
         full_gu1, xf1_late = full[1], xf1
-    cot = exchange(cot_going, rows)[placing]
     w_g, w_u = gate_weights(full_gu1)
     g1, u1, hid1 = gate_up(me, xf1_late, w_g, w_u)
     if ring:
-        full_d1 = ring.gather_core(hi_d1, hid1)
-        hi_a2 = ring.gather_hi(lo_a2, hid1)
-        lo_gu2 = each(near_gu2, *far(hi_d1))
-        hid1_late = after(hid1, *far(hi_a2))
+        hi_d1 = ring.gather_hi(lo_d1, hid1)
+        lo_a2 = ring.gather_lo(each(split(3, near_a2), *lo_d1), hid1)
+        near_gu2 = ring.gather_z(after(flat[4], near_a2), hid1)
+        own_d1 = jnp.stack([jnp.stack(half) for half in hi_d1]).transpose(3, 0, 1, 2, 4, 5).reshape(4, FFP, 128)
+        full_d1 = [own_d1, ring.swap(own_d1, "core")]
+        hid1_late = after(hid1, *lo_a2)
+        all_d2 = ring.gather_z_all(after(mid_d2, near_gu2))
+        cot_going = after(cot_going, near_gu2)
     else:
         full_d1, hid1_late = full[2], hid1
-    w_d = down_weights(full_d1)
+    cot = exchange(cot_going, rows)[placing]
+    w_d = DownRows(full_d1)
     h1 = down(me, hm1, hid1_late, w_d)
     if ring:
-        full_a2 = ring.gather_core(hi_a2, h1)
-        lo_gu2 = ring.gather_lo(lo_gu2, h1)
-        h1_late = after(h1, *lo_gu2)
+        hi_a2 = ring.gather_hi(lo_a2, h1)
+        full_a2 = ring.gather_core(hi_a2)
+        lo_gu2 = each(split(4, near_gu2), *far(hi_a2))
     else:
-        full_a2, h1_late = full[3], h1
+        full_a2 = full[3]
     v_q, v_k, v_v, v_o = attn_weights(full_a2, HALVES_TWO)
-    xa2, q2, k2, v2 = norm_proj(me, h1_late, gain_a2, [v_q, v_k, v_v])
-    o2 = window_fwd(q2, k2, v2, seg_row, seg_col, live_row)
-    if ring:
-        hi_gu2 = ring.gather_hi(lo_gu2, o2)
-        lo_d2 = ring.gather_lo(each(near_d2, *lo_gu2), o2)
-    hm2, xf2 = attn_out(me, h1, tied(o2, *(far(hi_gu2) + lo_d2 if ring else [])), v_o, gain_m2)
-    if ring:
-        full_gu2 = ring.gather_core(hi_gu2, xf2)
-        hi_d2 = ring.gather_hi(lo_d2, xf2)
-        xf2_late = after(xf2, *far(hi_d2))
+    xa2, q2, k2, v2 = norm_proj(me, h1, gain_a2, [v_q, v_k, v_v])
+    if ring:
+        lo_gu2 = ring.gather_lo(lo_gu2, q2)
+    o2 = window_fwd(tied(q2, *(lo_gu2 if ring else [])), k2, v2, seg_row, seg_col, live_col)
+    hm2, xf2 = attn_out(me, h1, o2, v_o, gain_m2)
+    if ring:
+        full_gu2 = ring.gather_core(ring.gather_hi(lo_gu2, xf2))
     else:
-        full_gu2, xf2_late = full[4], xf2
+        full_gu2 = full[4]
     v_g, v_u = gate_weights(full_gu2)
-    g2, u2, hid2 = gate_up(me, xf2_late, v_g, v_u)
-    v_d = down_weights(ring.gather_core(hi_d2, hid2) if ring else full[5])
-
-    step = (lambda f, v, *behind: f(v, *behind)) if ring else (lambda f, v, *behind: v)
-    core, low, high = (ring.reduce_core, ring.reduce_lo, ring.reduce_hi) if ring else (None,) * 3
+    v_d = DownRows([all_d2, after(ring.swap(all_d2, "core"), xf2)] if ring else full[5])
+    g2, u2, hid2 = gate_up(me, xf2, v_g, v_u)
+
     dg2, du2, *d2 = down_bwd(me, cot, v_d, hid2, g2, u2)
+    if ring:
+        r_d2 = ring.send(d2[1:], ("core",))
     gu2 = gate_up_bwd(me, xf2, dg2, du2)
-    d2 = step(core, d2, gu2[0])
-    gm2, bo2, dor2, gg_m2 = mlp_dx(me, tied(dg2, *d2, *gu2), du2, v_g, v_u, hm2, gain_m2, cot, v_o, bf16)
-    d2, gu2 = step(low, d2, gm2), step(core, gu2, gm2)
-    dq2, dk2, dv2 = window_bwd(q2, k2, v2, tied(dor2, *d2, *gu2), seg_row, seg_col, live_col)
-    d2 = step(high, d2, dq2)
-    *a2, gh1, gg_a2 = attn_bwd(me, xa2, [tied(dq2, *d2), dk2, dv2], [v_q, v_k, v_v], o2, bo2, h1, gain_a2, gm2, HALVES_TWO)
-    gu2 = step(low, gu2, gh1)
-    dg1, du1, *d1 = down_bwd(me, tied(gh1, *gu2), w_d, hid1, g1, u1)
-    gu2, a2 = step(high, gu2, dg1), step(core, a2, dg1)
-    gu1 = gate_up_bwd(me, xf1, tied(dg1, *gu2, *a2), du1)
-    a2, d1 = step(low, a2, gu1[0]), step(core, d1, gu1[0])
-    gm1, bo1, dou1, gg_m1 = mlp_dx(me, tied(dg1, *a2, *d1, *gu1), du1, w_g, w_u, hm1, gain_m1, gh1, w_o, f32)
-    a2, d1, gu1 = step(high, a2, gm1), step(low, d1, gm1), step(core, gu1, gm1)
-    dqk1, dv1 = based_bwd(qk1, v1, tied(dou1, *a2, *d1, *gu1), ou1, rden1, seg_row, seg_col, live_col)
-    d1 = step(high, d1, dqk1)
-    *a1, g0, gg_a1 = attn_bwd(me, xa1, [tied(dqk1, *d1), dv1], [w_qk, w_v], o1, bo1, start, gain_a1, gm1, HALVES_ONE)
-    gu1 = step(low, gu1, g0)
-    h2 = down(me, tied(hm2, g0), hid2, v_d)
-    output = exchange(h2.astype(bf16)[local_slots], rows)[restore]
+    if ring:
+        dg2, du2, gu2, r_d2 = sync(dg2, du2, gu2, r_d2)
+        z_d2 = ring.scatter_z(d2[0] + r_d2[0])
+        r_gu2 = ring.send(gu2[1::2], ("core", "core"))
+    gm2, bo2, dor2, gg_m2 = mlp_dx(me, dg2, du2, v_g, v_u, hm2, gain_m2, cot, v_o, bf16)
+    if ring:
+        gm2, bo2, dor2, gg_m2, r_gu2 = sync(gm2, bo2, dor2, gg_m2, r_gu2)
+        keep_gu2, go = add_core(gu2, r_gu2)
+        r_gu2 = ring.send(go, ("x", "y"))
+    dq2, dk2, dv2 = window_bwd(q2, k2, v2, dor2, seg_row, seg_col, live_col)
+    *a2, gh1, gg_a2 = attn_bwd(me, xa2, [dq2, dk2, dv2], [v_q, v_k, v_v], o2, bo2, h1, gain_a2, gm2, HALVES_TWO)
+    if ring:
+        a2, gh1, gg_a2, r_gu2, z_d2 = sync(a2, gh1, gg_a2, r_gu2, z_d2)
+        keep_gu2, go = add_two(keep_gu2, r_gu2)
+        r_gu2 = ring.send(go, ("y", "x"))
+        r_a2 = ring.send(a2[1::2], ("core", "core"))
+        keep_d2, go = far_rows(z_d2)
+        r_d2 = ring.send(go, ("y", "x"))
+    dg1, du1, *d1 = down_bwd(me, gh1, w_d, hid1, g1, u1)
+    if ring:
+        dg1, du1, d1, r_gu2, r_a2, r_d2 = sync(dg1, du1, d1, r_gu2, r_a2, r_d2)
+        z_gu2 = ring.scatter_z(jnp.concatenate(add_one(keep_gu2, r_gu2), axis=1))
+        keep_a2, go = add_core(a2, r_a2)
+        r_a2 = ring.send(go, ("x", "y"))
+        r_d1 = ring.send(d1[1:], ("core",))
+        keep_d2, go = near_rows(add_one(keep_d2, r_d2))
+        r_d2 = ring.send(go, ("x", "y"))
+    gu1 = gate_up_bwd(me, xf1, dg1, du1)
+    h2 = down(me, tied(hm2, gu1[0]), hid2, v_d)
+    if ring:
+        gu1, h2, r_a2, r_d1, r_d2 = sync(gu1, h2, r_a2, r_d1, r_d2)
+        sum_d2 = add_one(keep_d2, r_d2)
+        keep_a2, go = add_two(keep_a2, r_a2)
+        r_a2 = ring.send(go, ("y", "x"))
+        r_gu1 = ring.send(gu1[1::2], ("core", "core"))
+        z_d1 = ring.scatter_z(d1[0] + r_d1[0])
+    output = exchange(h2.astype(bf16)[local_slots], rows)
+    gm1, bo1, dou1, gg_m1 = mlp_dx(me, dg1, du1, w_g, w_u, hm1, gain_m1, gh1, w_o, f32)
+    if ring:
+        gm1, bo1, dou1, gg_m1, r_a2, r_gu1 = sync(gm1, bo1, dou1, gg_m1, r_a2, r_gu1)
+        done_a2 = add_one(keep_a2, r_a2)
+        keep_gu1, go = add_core(gu1, r_gu1)
+        r_gu1 = ring.send(go, ("x", "y"))
+    dqk1, dv1 = based_bwd(qk1, v1, dou1, ou1, rden1, seg_row, seg_col, live_col)
+    if ring:
+        dqk1, dv1, output, r_gu1 = sync(dqk1, dv1, output, r_gu1)
+        keep_gu1, go = add_two(keep_gu1, r_gu1)
+        r_gu1 = ring.send(go, ("y", "x"))
+    *a1, g0, gg_a1 = attn_bwd(me, xa1, [dqk1, dv1], [w_qk, w_v], o1, bo1, start, gain_a1, gm1, HALVES_ONE)
+    output = output[restore]
     gains = jnp.concatenate([gg_a1, gg_m1, gg_a2, gg_m2], axis=0)
     if ring:
-        gu1, a1 = high(gu1), high(low(core(a1)))
-        sums = []
-        for a, gu, d, halves in ((a1, gu1, d1, HALVES_ONE), (a2, gu2, d2, HALVES_TWO)):
-            last = halves is HALVES_ONE
-            sa = (ring.reduce_z if last else ring.reduce_z_all)(a)
-            sgu = (ring.reduce_z if last else ring.reduce_z_all)(gu)
-            sd = ring.reduce_z_all(d)
-            sums.append(join_strips(*sa, halves) + [unpad_hidden(sgu[0]), unpad_hidden(sgu[1]), unpad_rows(jnp.concatenate(sd, axis=1))])
-        sums1, sums2 = sums
+        a1, g0, gains, r_gu1, z_gu2, z_d1 = sync(a1, g0, gains, r_gu1, z_gu2, z_d1)
+        gu1 = add_one(keep_gu1, r_gu1)
+        arrived = exchange(g0.astype(bf16)[local_slots], rows)
+        r_a1 = ring.send(a1[1::2], ("core", "core"))
+        r_gains = ring.send([gains], ("core",))
+        keep_d1, go = far_rows(z_d1)
+        r_d1 = ring.send(go, ("y", "x"))
+        r_a1, r_gains, r_d1 = sync(r_a1, r_gains, r_d1)
+        keep_a1, go = add_core(a1, r_a1)
+        r_a1 = ring.send(go, ("x", "y"))
+        gains = gains + r_gains[0]
+        r_gains = ring.send([gains], ("x",))
+        keep_d1, go = near_rows(add_one(keep_d1, r_d1))
+        r_d1 = ring.send(go, ("x", "y"))
+        r_a1, r_gains, r_d1 = sync(r_a1, r_gains, r_d1)
+        keep_a1, go = add_two(keep_a1, r_a1)
+        r_a1 = ring.send(go, ("y", "x"))
+        gains = gains + r_gains[0]
+        r_gains = ring.send([gains], ("y",))
+        sum_d1 = add_one(keep_d1, r_d1)
+        gu1, r_a1, r_gains, arrived = sync(gu1, r_a1, r_gains, arrived)
+        a1 = add_one(keep_a1, r_a1)
+        gains = gains + r_gains[0]
+        last = ring.reduce_z([jnp.concatenate(gu1, axis=1), jnp.concatenate(a1, axis=1)])
+        far_z = [ring.swap(gains, "z", by) for by in (1, 2, 3)]
+        gains = (gains + far_z[0]) + (far_z[1] + far_z[2])
+        z_a2 = ring.scatter_z(jnp.concatenate([after(v, z_d1) for v in done_a2], axis=1))
+        cut = lambda v, n: [v[:n].astype(f32), v[n:].astype(f32)]
+        sum_gu1, sum_a1 = cut(last[0], FC), cut(last[1], a1[0].shape[1])
+        sum_gu2, sum_a2 = cut(z_gu2, FC), cut(z_a2, done_a2[0].shape[1])
+        tokens_grad = arrived
+        wide = lambda halves: [h.astype(f32) for h in halves]
+        sum_d1, sum_d2 = wide(sum_d1), wide(sum_d2)
+        rest = sum_parts(sum_a2, sum_gu2, sum_d2, HALVES_TWO)
+        sums1, sums2 = sum_parts(sum_a1, sum_gu1, sum_d1, HALVES_ONE), rest
         sums1 = [sums1[0][:, :64], sums1[0][:, 64:]] + sums1[1:]
-        for axis, by in (("core", 1), ("x", 1), ("y", 1), ("z", 1), ("z", 2)):
-            gains = gains + ring.swap(gains, axis, by)
+        tokens_grad = tokens_grad[restore]
     else:
         sums1 = sum_any(d1, gu1, a1, HALVES_ONE)
         sums2 = sum_any(d2, gu2, a2, HALVES_TWO)
         gains = lax.psum(gains, ("row", "col"))
-    tokens_grad = exchange(g0.astype(bf16)[local_slots], rows)[restore]
+        tokens_grad = exchange(g0.astype(bf16)[local_slots], rows)[restore]
     return (
         output, tokens_grad,
         gains[0], *sums1[:4], gains[1], *sums1[4:],

time: 789 us -> 772 us (0.978)
  waiting for transfers between devices: 175 us -> 195 us
  Pallas kernels: 295 us -> 278 us
  other arithmetic: 110 us -> 101 us
  starting transfers between devices: 126 us -> 118 us
    ppermute x107 -> x100, starting transfers between devices: 107 us -> 89.2 us  [swap(): lax.ppermute(value, self.axes, [(i, i ^ by << shift) for i in range(32)])]
    pallas_call x20, Pallas kernels: 295 us -> 278 us  [call(): pl.pallas_call(body, out_shape=out_shape, grid_spec=pltpu.PrefetchScalarG...]
    all_to_all x4, starting transfers between devices: 18.3 us -> 28.5 us  [exchange(): lax.all_to_all(value.reshape(row_count, n // row_count, width), axis, spl...]
    all_to_all x4, waiting for transfers between devices: 4.66 us -> 14.7 us  [exchange(): lax.all_to_all(value.reshape(row_count, n // row_count, width), axis, spl...]
    ppermute x107 -> x100, waiting for transfers between devices: 170 us -> 175 us  [swap(): lax.ppermute(value, self.axes, [(i, i ^ by << shift) for i in range(32)])]
    add x43 -> x37, other arithmetic: 61.4 us -> 56.2 us  [the longest x14 15.8 us: add_one(): return [k + g for k, g in zip(keep, got)]]
    unnamed x140 -> x184, local copies, waits for them, and re-layouts: 15.5 us -> 17.5 us
  transfers between devices with their start and end apart: 116 -> 109, of which waited for: 31 -> 32; matrix products, arithmetic and copies ran while one was open for 19% -> 17% of each run, Pallas kernels for 36% -> 35%
where the time goes in v4:
time: 772 us; the launch traced here: 764 us
  Pallas kernels  278 us (36%)
  waiting for transfers between devices  195 us (25%)
  starting transfers between devices  118 us (15%)
  other arithmetic  101 us (13%)
  local copies, waits for them, and re-layouts  52.9 us (7%)
  between operations  18.6 us (2%)
    pallas_call x20, Pallas kernels, call(): pl.pallas_call(body, out_shape=out_shape, grid_spec=pltpu.PrefetchScalarG...  278 us
    ppermute x100, waiting for transfers between devices, swap(): lax.ppermute(value, self.axes, [(i, i ^ by << shift) for i in range(32)])  175 us
    ppermute x100, starting transfers between devices, swap(): lax.ppermute(value, self.axes, [(i, i ^ by << shift) for i in range(32)])  89.2 us
    all_to_all x4, starting transfers between devices, exchange(): lax.all_to_all(value.reshape(row_count, n // row_count, width), axis, spl...  28.5 us
    unnamed x184, local copies, waits for them, and re-layouts  17.5 us
    add x14, other arithmetic, add_one(): return [k + g for k, g in zip(keep, got)]  15.8 us
  transfers between devices with their start and end apart: 109, of which 32 were waited for; matrix products, arithmetic and copies ran while one was open for 17% of the time, Pallas kernels for 35%

profile of v4, /device:TPU:0, one launch (start us, length us, event | category | flops | bytes accessed | tf_op | source)
XLA Modules:
  0.0 763.8 jit_solution(10924735500808557525)
XLA Ops:
  57.6 15.7 %collective-permute-done.4 = bf16[1408,128]{1,0:T(8,128)(2,1)} collective-permute-done((bf16[1408,128]{1,0:T(8,128)(2,1)S(1)}, bf16[1408,128]{1,0:T(8,128)(2,1)}, u32[]{:S(2)}, u32[]{:S(2)}) %collective-permute-start.4) | collective-permute-done | bytes 360480 | tf_op jit(solution)/shard_map/ppermute | solution.py:779
  88.4 22.4 %collective-permute-done.15 = bf16[4,704,128]{2,1,0:T(8,128)(2,1)S(1)} collective-permute-done((bf16[4,704,128]{2,1,0:T(8,128)(2,1)S(1)}, bf16[4,704,128]{2,1,0:T(8,128)(2,1)S(1)}, u32[]{:S(2)}, u32[]{:S(2)}) %collective-permute-start.15) | collective-permute-done | bytes 720928 | tf_op jit(solution)/shard_map/ppermute | solution.py:779
  193.8 13.6 %shard_map.377 = (bf16[2816,512]{1,0:T(8,128)(2,1)}, bf16[2816,512]{1,0:T(8,128)(2,1)}, bf16[2816,512]{1,0:T(8,128)(2,1)}) custom-call(s32[2]{0:T(128)} %pad_add_fusion.me_ref, bf16[512,1024]{1,0:T(8,128)(2,1)} %get-tuple-element.244.refs_0_.xf_ref, bf16[2,4,704,128]{3,2,1,0:T(8,128)(2,1)} %pad_maximum_fusion.2.refs_1_.refs_5_, ...), custom_call_target="tpu_custom_call" | custom-call | flops 5905580032 | bytes 21233664 | tf_op jit(solution)/shard_map/pallas_call | solution.py:55
  224.0 11.4 %collective-permute-done.35 = bf16[4,512,128]{2,1,0:T(8,128)(2,1)S(1)} collective-permute-done((bf16[4,512,128]{2,1,0:T(8,128)(2,1)S(1)}, bf16[4,512,128]{2,1,0:T(8,128)(2,1)S(1)}, u32[]{:S(2)}, u32[]{:S(2)}) %collective-permute-start.35) | collective-permute-done | bytes 524320 | tf_op jit(solution)/shard_map/ppermute | solution.py:779
  240.5 10.8 %shard_map.378.refs_0_.refs_2_ = f32[512,1024]{1,0:T(8,128)} custom-call(s32[2]{0:T(128)} %pad_add_fusion.me_ref, f32[512,1024]{1,0:T(8,128)} %get-tuple-element.238.refs_0_.refs_2_, bf16[2816,512]{1,0:T(8,128)(2,1)} %get-tuple-element.254.refs_1_, bf16[4,2816,128]{2,1,0:T(8,128)(2,1)} %bitcast.391, bf16[4,2816,128]{2,1,0:T(8,128)(2,1)} %collective-permute-done.38.refs_3_.refs_5_), custom_call_target="tpu_custom_call" | custom-call | flops 2952790016 | bytes 12845056 | tf_op jit(solution)/shard_map/pallas_call | solution.py:55
  259.8 12.5 %shard_map.379 = (bf16[512,1024]{1,0:T(8,128)(2,1)}, bf16[512,1024]{1,0:T(8,128)(2,1)}, bf16[512,1024]{1,0:T(8,128)(2,1)}, bf16[512,1024]{1,0:T(8,128)(2,1)}) custom-call(s32[2]{0:T(128)} %pad_add_fusion.me_ref, f32[512,1024]{1,0:T(8,128)} %shard_map.378.refs_0_.refs_2_, f32[1,1024]{1,0:T(1,128)} %bitcast.452, bf16[2,4,512,128]{3,2,1,0:T(8,128)(2,1)} %copy-done.5, ...), custom_call_target="tpu_custom_call" | custom-call | flops 3221225472 | bytes 18878464 | tf_op jit(solution)/shard_map/pallas_call | solution.py:55
  292.8 11.7 %shard_map.380.refs_1_ = bf16[512,1024]{1,0:T(8,128)(2,1)} custom-call(bf16[512,1024]{1,0:T(8,128)(2,1)} %get-tuple-element.269.q_ref, bf16[512,1024]{1,0:T(8,128)(2,1)} %get-tuple-element.270.k_ref, bf16[512,1024]{1,0:T(8,128)(2,1)} %get-tuple-element.271.v_ref, s32[1,512]{1,0:T(1,128)} %fusion.47.sr_ref, s32[512,1]{1,0:T(8,128)} %convert_add_fusion.1.sc_ref, ...), custom_call_target="tpu_custom_call" | custom-call | flops 1610612736 | bytes 4200448 | tf_op jit(solution)/shard_map/pallas_call | solution.py:55
  325.1 13.6 %shard_map.382 = (bf16[2816,512]{1,0:T(8,128)(2,1)}, bf16[2816,512]{1,0:T(8,128)(2,1)}, bf16[2816,512]{1,0:T(8,128)(2,1)}) custom-call(s32[2]{0:T(128)} %pad_add_fusion.me_ref, bf16[512,1024]{1,0:T(8,128)(2,1)} %get-tuple-element.273.refs_0_.xf_ref, bf16[2,4,704,128]{3,2,1,0:T(8,128)(2,1)} %pad_maximum_fusion.5.refs_1_.refs_5_, ...), custom_call_target="tpu_custom_call" | custom-call | flops 5905580032 | bytes 21233664 | tf_op jit(solution)/shard_map/pallas_call | solution.py:55
  338.7 14.4 %shard_map.383 = (bf16[2816,512]{1,0:T(8,128)(2,1)}, bf16[2816,512]{1,0:T(8,128)(2,1)}, bf16[4,2816,128]{2,1,0:T(8,128)(2,1)}, bf16[4,2816,128]{2,1,0:T(8,128)(2,1)}) custom-call(s32[2]{0:T(128)} %pad_add_fusion.me_ref, bf16[512,1024]{1,0:T(8,128)(2,1)} %gather_fusion.3, bf16[2816,512]{1,0:T(8,128)(2,1)} %get-tuple-element.276.refs_1_, ...), custom_call_target="tpu_custom_call" | custom-call | flops 5905580032 | bytes 27000832 | tf_op jit(solution)/shard_map/pallas_call | solution.py:55
  353.3 14.0 %shard_map.384 = (bf16[2,2,4,704,128]{4,3,2,1,0:T(8,128)(2,1)}, bf16[2,2,4,704,128]{4,3,2,1,0:T(8,128)(2,1)}, bf16[2,2,4,704,128]{4,3,2,1,0:T(8,128)(2,1)}, bf16[2,2,4,704,128]{4,3,2,1,0:T(8,128)(2,1)}) custom-call(s32[2]{0:T(128)} %pad_add_fusion.me_ref, bf16[512,1024]{1,0:T(8,128)(2,1)} %get-tuple-element.273.refs_0_.xf_ref, ...), custom_call_target="tpu_custom_call" | custom-call | flops 5905580032 | bytes 18350080 | tf_op jit(solution)/shard_map/pallas_call | solution.py:55
  370.3 19.0 %shard_map.385 = (f32[512,1024]{1,0:T(8,128)}, bf16[512,1024]{1,0:T(8,128)(2,1)}, bf16[512,1024]{1,0:T(8,128)(2,1)}, f32[1,1024]{1,0:T(1,128)}) custom-call(s32[2]{0:T(128)} %pad_add_fusion.me_ref, bf16[2816,512]{1,0:T(8,128)(2,1)} %get-tuple-element.288.dg_ref.refs_0_, bf16[2816,512]{1,0:T(8,128)(2,1)} %get-tuple-element.289.du_ref.refs_1_, ...), custom_call_target="tpu_custom_call" | custom-call | flops 6979321856 | bytes 28844032 | tf_op jit(solution)/shard_map/pallas_call | solution.py:55
  396.0 18.7 %shard_map.386 = (bf16[512,1024]{1,0:T(8,128)(2,1)}, bf16[512,1024]{1,0:T(8,128)(2,1)}, bf16[512,1024]{1,0:T(8,128)(2,1)}) custom-call(bf16[512,1024]{1,0:T(8,128)(2,1)} %get-tuple-element.269.q_ref, bf16[512,1024]{1,0:T(8,128)(2,1)} %get-tuple-element.270.k_ref, bf16[512,1024]{1,0:T(8,128)(2,1)} %get-tuple-element.271.v_ref, ...), custom_call_target="tpu_custom_call" | custom-call | flops 4026531840 | bytes 7346176 | tf_op jit(solution)/shard_map/pallas_call | solution.py:55
  414.6 20.9 %shard_map.387 = (bf16[2,2,4,512,128]{4,3,2,1,0:T(8,128)(2,1)}, bf16[2,2,4,512,128]{4,3,2,1,0:T(8,128)(2,1)}, bf16[2,2,4,512,128]{4,3,2,1,0:T(8,128)(2,1)}, bf16...) custom-call(s32[2]{0:T(128)} %pad_add_fusion.me_ref, ...), custom_call_target="tpu_custom_call" | custom-call | flops 7516192768 | bytes 33562624 | tf_op jit(solution)/shard_map/pallas_call | solution.py:55
  445.8 14.8 %shard_map.388 = (bf16[2816,512]{1,0:T(8,128)(2,1)}, bf16[2816,512]{1,0:T(8,128)(2,1)}, bf16[4,2816,128]{2,1,0:T(8,128)(2,1)}, bf16[4,2816,128]{2,1,0:T(8,128)(2,1)}) custom-call(s32[2]{0:T(128)} %pad_add_fusion.me_ref, f32[512,1024]{1,0:T(8,128)} %get-tuple-element.315.refs_0_.refs_4_, bf16[2816,512]{1,0:T(8,128)(2,1)} %get-tuple-element.254.refs_1_, ...), custom_call_target="tpu_custom_call" | custom-call | flops 5905580032 | bytes 28049408 | tf_op jit(solution)/shard_map/pallas_call | solution.py:55
  479.7 14.1 %shard_map.390 = (bf16[2,2,4,704,128]{4,3,2,1,0:T(8,128)(2,1)}, bf16[2,2,4,704,128]{4,3,2,1,0:T(8,128)(2,1)}, bf16[2,2,4,704,128]{4,3,2,1,0:T(8,128)(2,1)}, bf16[2,2,4,704,128]{4,3,2,1,0:T(8,128)(2,1)}) custom-call(s32[2]{0:T(128)} %pad_add_fusion.me_ref, bf16[512,1024]{1,0:T(8,128)(2,1)} %get-tuple-element.244.refs_0_.xf_ref, ...), custom_call_target="tpu_custom_call" | custom-call | flops 5905580032 | bytes 18350080 | tf_op jit(solution)/shard_map/pallas_call | solution.py:55
  493.9 10.5 %shard_map.391 = f32[512,1024]{1,0:T(8,128)} custom-call(s32[2]{0:T(128)} %pad_add_fusion.me_ref, f32[512,1024]{1,0:T(8,128)} %get-tuple-element.339.refs_2_.refs_0_, bf16[2816,512]{1,0:T(8,128)(2,1)} %get-tuple-element.276.refs_1_, bf16[4,2816,128]{2,1,0:T(8,128)(2,1)} %bitcast.397, bf16[4,2816,128]{2,1,0:T(8,128)(2,1)} %collective-permute-done.56.refs_5_.refs_3_), custom_call_target="tpu_custom_call" | custom-call | flops 2952790016 | bytes 12845056 | tf_op jit(solution)/shard_map/pallas_call | solution.py:55
  514.4 19.5 %shard_map.389 = (f32[512,1024]{1,0:T(8,128)}, bf16[512,1024]{1,0:T(8,128)(2,1)}, f32[512,1024]{1,0:T(8,128)}, f32[1,1024]{1,0:T(1,128)}) custom-call(s32[2]{0:T(128)} %pad_add_fusion.me_ref, bf16[2816,512]{1,0:T(8,128)(2,1)} %get-tuple-element.327.refs_0_.dg_ref, bf16[2816,512]{1,0:T(8,128)(2,1)} %get-tuple-element.328.refs_1_.du_ref, ...), custom_call_target="tpu_custom_call" | custom-call | flops 6979321856 | bytes 29892608 | tf_op jit(solution)/shard_map/pallas_call | solution.py:55
  536.9 10.5 %all-to-all-start.2 = ((bf16[8,64,1024]{2,1,0:T(8,128)(2,1)}), bf16[8,64,1024]{2,1,0:T(8,128)(2,1)S(1)}, u32[]{:S(2)}, u32[]{:S(2)}) async-start(bf16[8,64,1024]{2,1,0:T(8,128)(2,1)} %bitcast.110), calls=%async_computation.3 | async-start | bytes 2097152 | tf_op jit(solution)/shard_map/all_to_all | solution.py:935
  562.9 15.9 %shard_map.392 = (bf16[512,512]{1,0:T(8,128)(2,1)}, bf16[512,1024]{1,0:T(8,128)(2,1)}) custom-call(bf16[512,512]{1,0:T(8,128)(2,1)} %get-tuple-element.227.qk_ref, bf16[512,1024]{1,0:T(8,128)(2,1)} %get-tuple-element.228.v_ref, f32[512,1024]{1,0:T(8,128)} %get-tuple-element.349.dou_ref, f32[512,1024]{1,0:T(8,128)} %get-tuple-element.350.ou_ref, ...), custom_call_target="tpu_custom_call" | custom-call | flops 4026531840 | bytes 9443328 | tf_op jit(solution)/shard_map/pallas_call | solution.py:55
  578.8 13.8 %all-to-all-done.2 = bf16[8,64,1024]{2,1,0:T(8,128)(2,1)S(1)} async-done(((bf16[8,64,1024]{2,1,0:T(8,128)(2,1)}), bf16[8,64,1024]{2,1,0:T(8,128)(2,1)S(1)}, u32[]{:S(2)}, u32[]{:S(2)}) %all-to-all-start.2) | async-done | bytes 1048608 | tf_op jit(solution)/shard_map/all_to_all | solution.py:935
  603.9 20.8 %shard_map.393 = (bf16[2,2,4,256,128]{4,3,2,1,0:T(8,128)(2,1)}, bf16[2,2,4,256,128]{4,3,2,1,0:T(8,128)(2,1)}, bf16[2,2,4,384,128]{4,3,2,1,0:T(8,128)(2,1)}, bf16...) custom-call(s32[2]{0:T(128)} %pad_add_fusion.me_ref, ...), custom_call_target="tpu_custom_call" | custom-call | flops 4294967296 | bytes 20455424 | tf_op jit(solution)/shard_map/pallas_call | solution.py:55
  666.5 14.1 %collective-permute-done.87 = bf16[2,4,384,128]{3,2,1,0:T(8,128)(2,1)} collective-permute-done((bf16[2,4,384,128]{3,2,1,0:T(8,128)(2,1)S(1)}, bf16[2,4,384,128]{3,2,1,0:T(8,128)(2,1)}, u32[]{:S(2)}, u32[]{:S(2)}) %collective-permute-start.87) | collective-permute-done | bytes 786464 | tf_op jit(solution)/shard_map/ppermute | solution.py:779
  711.3 14.3 %collective-permute-done.97 = bf16[2048,128]{1,0:T(8,128)(2,1)} collective-permute-done((bf16[2048,128]{1,0:T(8,128)(2,1)}, bf16[2048,128]{1,0:T(8,128)(2,1)}, u32[]{:S(2)}, u32[]{:S(2)}) %collective-permute-start.97) | collective-permute-done | bytes 524320 | tf_op jit(solution)/shard_map/ppermute | solution.py:779
  731.0 19.7 %collective-permute-done.98 = bf16[2048,128]{1,0:T(8,128)(2,1)} collective-permute-done((bf16[2048,128]{1,0:T(8,128)(2,1)}, bf16[2048,128]{1,0:T(8,128)(2,1)}, u32[]{:S(2)}, u32[]{:S(2)}) %collective-permute-start.98) | collective-permute-done | bytes 524320 | tf_op jit(solution)/shard_map/ppermute | solution.py:779
  (560 shorter events, 378.7 us)
Async XLA Ops:
  76.5 38.0 %all-to-all-start = ((bf16[8,64,1024]{2,1,0:T(8,128)(2,1)}), bf16[8,64,1024]{2,1,0:T(8,128)(2,1)S(1)}, u32[]{:S(2)}, u32[]{:S(2)}) async-start(bf16[8,64,1024]{2,1,0:T(8,128)(2,1)} %bitcast.393), calls=%async_computation | async-start | bytes 2097152 | tf_op jit(solution)/shard_map/all_to_all | solution.py:935
  84.1 198.8 %all-gather.3.cloned.1.call-start = ((), (), s32[]{:S(2)}) async-start(), calls=%async_computation.12 | async-start | bytes 3604480 | tf_op jit(solution)/shard_map/all_gather | solution.py:790
  112.0 42.2 %collective-permute-start.21 = (bf16[2,4,704,128]{3,2,1,0:T(8,128)(2,1)}, bf16[2,4,704,128]{3,2,1,0:T(8,128)(2,1)}, u32[]{:S(2)}, u32[]{:S(2)}) collective-permute-start(bf16[2,4,704,128]{3,2,1,0:T(8,128)(2,1)} %pad_maximum_fusion.3.refs_5_.refs_9_), channel_id=1, source_target_pairs={{0,2},{1,3},{2,0},{3,1},{4,6},{5,7},{6,4},{7,5},{8,10},{9,11},{10,... | collective-permute-start | bytes 4325384 | tf_op jit(solution)/shard_map/ppermute | solution.py:779
  113.5 51.3 %collective-permute-start.20 = (bf16[2,4,704,128]{3,2,1,0:T(8,128)(2,1)}, bf16[2,4,704,128]{3,2,1,0:T(8,128)(2,1)}, u32[]{:S(2)}, u32[]{:S(2)}) collective-permute-start(bf16[2,4,704,128]{3,2,1,0:T(8,128)(2,1)} %pad_maximum_fusion.2.refs_1_.refs_5_), channel_id=1, source_target_pairs={{0,4},{1,5},{2,6},{3,7},{4,0},{5,1},{6,2},{7,3},{8,12},{9,13},{10,... | collective-permute-start | bytes 4325384 | tf_op jit(solution)/shard_map/ppermute | solution.py:779
  140.9 47.4 %collective-permute-start.32 = (bf16[2,4,704,128]{3,2,1,0:T(8,128)(2,1)}, bf16[2,4,704,128]{3,2,1,0:T(8,128)(2,1)S(1)}, u32[]{:S(2)}, u32[]{:S(2)}) collective-permute-start(bf16[2,4,704,128]{3,2,1,0:T(8,128)(2,1)} %pad_maximum_fusion.3.refs_5_.refs_9_), channel_id=1, source_target_pairs={{0,1},{1,0},{2,3},{3,2},{4,5},{5,4},{6,7},{7,6},{8,9},{9,8},{10,11... | collective-permute-start | bytes 4325384 | tf_op jit(solution)/shard_map/ppermute | solution.py:779
  275.4 36.7 %collective-permute-start.53 = (bf16[2,4,704,128]{3,2,1,0:T(8,128)(2,1)}, bf16[2,4,704,128]{3,2,1,0:T(8,128)(2,1)}, u32[]{:S(2)}, u32[]{:S(2)}) collective-permute-start(bf16[2,4,704,128]{3,2,1,0:T(8,128)(2,1)} %pad_maximum_fusion.6.refs_5_.refs_9_), channel_id=1, source_target_pairs={{0,2},{1,3},{2,0},{3,1},{4,6},{5,7},{6,4},{7,5},{8,10},{9,11},{10,... | collective-permute-start | bytes 4325384 | tf_op jit(solution)/shard_map/ppermute | solution.py:779
  277.1 42.4 %collective-permute-start.50 = (bf16[2,4,704,128]{3,2,1,0:T(8,128)(2,1)}, bf16[2,4,704,128]{3,2,1,0:T(8,128)(2,1)S(1)}, u32[]{:S(2)}, u32[]{:S(2)}) collective-permute-start(bf16[2,4,704,128]{3,2,1,0:T(8,128)(2,1)} %pad_maximum_fusion.5.refs_1_.refs_5_), channel_id=1, source_target_pairs={{0,4},{1,5},{2,6},{3,7},{4,0},{5,1},{6,2},{7,3},{8,12},{9,13},{10,... | collective-permute-start | bytes 4325384 | tf_op jit(solution)/shard_map/ppermute | solution.py:779
  283.0 55.7 %collective-permute-start.56 = (bf16[4,2816,128]{2,1,0:T(8,128)(2,1)}, bf16[4,2816,128]{2,1,0:T(8,128)(2,1)}, u32[]{:S(2)}, u32[]{:S(2)}) collective-permute-start(bf16[4,2816,128]{2,1,0:T(8,128)(2,1)} %bitcast.395), channel_id=1, source_target_pairs={{0,1},{1,0},{2,3},{3,2},{4,5},{5,4},{6,7},{7,6},{8,9},{9,8},{10,11... | collective-permute-start | bytes 8650760 | tf_op jit(solution)/shard_map/ppermute | solution.py:779
  285.7 35.1 %all-to-all-start.1 = ((bf16[8,64,1024]{2,1,0:T(8,128)(2,1)}), bf16[8,64,1024]{2,1,0:T(8,128)(2,1)S(1)}, u32[]{:S(2)}, u32[]{:S(2)}) async-start(bf16[8,64,1024]{2,1,0:T(8,128)(2,1)} %bitcast.92), calls=%async_computation.1 | async-start | bytes 2097152 | tf_op jit(solution)/shard_map/all_to_all | solution.py:935
  291.4 144.2 %reduce-scatter.5.cloned.1.call-start = ((), (), s32[]{:S(2)}) async-start(), calls=%async_computation.8 | async-start | bytes 3604480 | tf_op jit(solution)/shard_map/reduce_scatter | solution.py:806
  369.6 255.8 %reduce-scatter.7.cloned.1.call-start = ((), (), s32[]{:S(2)}) async-start(), calls=%async_computation.9 | async-start | bytes 1802240 | tf_op jit(solution)/shard_map/reduce_scatter | solution.py:806
  393.1 42.4 %collective-permute-start.61 = (bf16[2,4,704,128]{3,2,1,0:T(8,128)(2,1)S(1)}, bf16[2,4,704,128]{3,2,1,0:T(8,128)(2,1)}, u32[]{:S(2)}, u32[]{:S(2)}) collective-permute-start(bf16[2,4,704,128]{3,2,1,0:T(8,128)(2,1)S(1)} %get-tuple-element.477), channel_id=1, source_target_pairs={{0,4},{1,5},{2,6},{3,7},{4,0},{5,1},{6,2},{7,3},{8,12},{9,13},{10,... | collective-permute-start | bytes 4325384 | tf_op jit(solution)/shard_map/ppermute | solution.py:779
  394.8 40.8 %collective-permute-start.60 = (bf16[2,4,704,128]{3,2,1,0:T(8,128)(2,1)S(1)}, bf16[2,4,704,128]{3,2,1,0:T(8,128)(2,1)}, u32[]{:S(2)}, u32[]{:S(2)}) collective-permute-start(bf16[2,4,704,128]{3,2,1,0:T(8,128)(2,1)S(1)} %get-tuple-element.479), channel_id=1, source_target_pairs={{0,2},{1,3},{2,0},{3,1},{4,6},{5,7},{6,4},{7,5},{8,10},{9,11},{10,... | collective-permute-start | bytes 4325384 | tf_op jit(solution)/shard_map/ppermute | solution.py:779
  465.1 40.3 %collective-permute-start.70 = (bf16[4,2816,128]{2,1,0:T(8,128)(2,1)}, bf16[4,2816,128]{2,1,0:T(8,128)(2,1)}, u32[]{:S(2)}, u32[]{:S(2)}) collective-permute-start(bf16[4,2816,128]{2,1,0:T(8,128)(2,1)} %get-tuple-element.342), channel_id=1, source_target_pairs={{0,1},{1,0},{2,3},{3,2},{4,5},{5,4},{6,7},{7,6},{8,9},{9,8},{10,11... | collective-permute-start | bytes 8650760 | tf_op jit(solution)/shard_map/ppermute | solution.py:779
  470.4 155.1 %reduce-scatter.9.cloned.1.call-start = ((), (), s32[]{:S(2)}) async-start(), calls=%async_computation.10 | async-start | bytes 3604480 | tf_op jit(solution)/shard_map/reduce_scatter | solution.py:806
  505.4 42.0 %collective-permute-start.75 = (bf16[2,2,4,704,128]{4,3,2,1,0:T(8,128)(2,1)}, bf16[2,2,4,704,128]{4,3,2,1,0:T(8,128)(2,1)}, u32[]{:S(2)}, u32[]{:S(2)}) collective-permute-start(bf16[2,2,4,704,128]{4,3,2,1,0:T(8,128)(2,1)} %get-tuple-element.347), channel_id=1, source_target_pairs={{0,1},{1,0},{2,3},{3,2},{4,5},{5,4},{6,7},{7,6},{8,9},{9,8},{10,11... | collective-permute-start | bytes 8650760 | tf_op jit(solution)/shard_map/ppermute | solution.py:779
  505.5 41.9 %collective-permute-start.76 = (bf16[2,2,4,704,128]{4,3,2,1,0:T(8,128)(2,1)}, bf16[2,2,4,704,128]{4,3,2,1,0:T(8,128)(2,1)}, u32[]{:S(2)}, u32[]{:S(2)}) collective-permute-start(bf16[2,2,4,704,128]{4,3,2,1,0:T(8,128)(2,1)} %get-tuple-element.348), channel_id=1, source_target_pairs={{0,1},{1,0},{2,3},{3,2},{4,5},{5,4},{6,7},{7,6},{8,9},{9,8},{10,11... | collective-permute-start | bytes 8650760 | tf_op jit(solution)/shard_map/ppermute | solution.py:779
  512.2 35.2 %collective-permute-start.74 = (bf16[4,512,128]{2,1,0:T(8,128)(2,1)}, bf16[4,512,128]{2,1,0:T(8,128)(2,1)}, u32[]{:S(2)}, u32[]{:S(2)}) collective-permute-start(bf16[4,512,128]{2,1,0:T(8,128)(2,1)} %fusion.29), channel_id=1, source_target_pairs={{0,2},{1,3},{2,0},{3,1},{4,6},{5,7},{6,4},{7,5},{8,10},{9,11},{10,... | collective-permute-start | bytes 1572872 | tf_op jit(solution)/shard_map/ppermute | solution.py:779
  536.9 55.8 %all-to-all-start.2 = ((bf16[8,64,1024]{2,1,0:T(8,128)(2,1)}), bf16[8,64,1024]{2,1,0:T(8,128)(2,1)S(1)}, u32[]{:S(2)}, u32[]{:S(2)}) async-start(bf16[8,64,1024]{2,1,0:T(8,128)(2,1)} %bitcast.110), calls=%async_computation.3 | async-start | bytes 2097152 | tf_op jit(solution)/shard_map/all_to_all | solution.py:935
  547.3 109.7 %reduce-scatter.11.cloned.1.call-start = ((), (), s32[]{:S(2)}) async-start(), calls=%async_computation.11 | async-start | bytes 1310720 | tf_op jit(solution)/shard_map/reduce_scatter | solution.py:806
  552.5 41.3 %collective-permute-start.78 = (bf16[2,4,704,128]{3,2,1,0:T(8,128)(2,1)}, bf16[2,4,704,128]{3,2,1,0:T(8,128)(2,1)}, u32[]{:S(2)}, u32[]{:S(2)}) collective-permute-start(bf16[2,4,704,128]{3,2,1,0:T(8,128)(2,1)} %get-tuple-element.473), channel_id=1, source_target_pairs={{0,4},{1,5},{2,6},{3,7},{4,0},{5,1},{6,2},{7,3},{8,12},{9,13},{10,... | collective-permute-start | bytes 4325384 | tf_op jit(solution)/shard_map/ppermute | solution.py:779
  558.5 35.3 %collective-permute-start.77 = (bf16[2,4,704,128]{3,2,1,0:T(8,128)(2,1)}, bf16[2,4,704,128]{3,2,1,0:T(8,128)(2,1)}, u32[]{:S(2)}, u32[]{:S(2)}) collective-permute-start(bf16[2,4,704,128]{3,2,1,0:T(8,128)(2,1)} %get-tuple-element.475), channel_id=1, source_target_pairs={{0,2},{1,3},{2,0},{3,1},{4,6},{5,7},{6,4},{7,5},{8,10},{9,11},{10,... | collective-permute-start | bytes 4325384 | tf_op jit(solution)/shard_map/ppermute | solution.py:779
  639.8 48.1 %all-to-all-start.3 = ((bf16[8,64,1024]{2,1,0:T(8,128)(2,1)}), bf16[8,64,1024]{2,1,0:T(8,128)(2,1)S(1)}, u32[]{:S(2)}, u32[]{:S(2)}) async-start(bf16[8,64,1024]{2,1,0:T(8,128)(2,1)} %bitcast.134), calls=%async_computation.6 | async-start | bytes 2097152 | tf_op jit(solution)/shard_map/all_to_all | solution.py:935
  706.5 44.1 %collective-permute-start.98 = (bf16[2048,128]{1,0:T(8,128)(2,1)}, bf16[2048,128]{1,0:T(8,128)(2,1)}, u32[]{:S(2)}, u32[]{:S(2)}) collective-permute-start(bf16[2048,128]{1,0:T(8,128)(2,1)} %get-tuple-element.488), channel_id=1, source_target_pairs={{0,16},{1,17},{2,18},{3,19},{4,20},{5,21},{6,22},{7,23},{8,24},{9,... | collective-permute-start | bytes 1572872 | tf_op jit(solution)/shard_map/ppermute | solution.py:779
  (170 other events, 2393.9 us)
Sparse Core Ops, SparseCore 0:
  19.5 2.9 sort.60.cloned.1.call-done
  220.7 62.1 all-gather.2
  369.8 61.6 reduce-scatter.4
  470.6 38.1 reduce-scatter.6
  510.9 76.7 reduce-scatter.8
  626.9 30.1 reduce-scatter.10
  (1 shorter events, 0.0 us)

commit v5 on v4

--- a/solution.py
+++ b/solution.py
@@ -653,7 +653,7 @@
     kern = Kernel(6 + n, strips, 6)
 
     def body(me_ref, *refs):
-        ins, hold, (*p_refs, g_ref, gg_ref), (xr_ref, or_ref, acc_ref) = kern.split(refs)
+        ins, hold, (*p_refs, g_ref, gg_ref), (xr_ref, or_ref, xt_ref, ot_ref, acc_ref) = kern.split(refs)
         xa_ref, o_ref, h_ref, gain_ref, gm_ref, bo_ref, *d_refs = ins
         i = pl.program_id(0)
 
@@ -662,9 +662,11 @@
             start_all(hold)
             regroup(xr_ref, xa_ref, ROWS, me_ref[0])
             regroup(or_ref, o_ref, ROWS, me_ref[0])
-
-        tiles = [dot(xr_ref[...], d[...], TN).astype(bf16) for d in d_refs]
-        tiles.append(dot(or_ref[...], bo_ref[...], TN).astype(bf16))
+            xt_ref[...] = xr_ref[...].T
+            ot_ref[...] = or_ref[...].T
+
+        tiles = [dot(xt_ref[...], d[...], NN).astype(bf16) for d in d_refs]
+        tiles.append(dot(ot_ref[...], bo_ref[...], NN).astype(bf16))
 
         def write(one, two):
             for j, (which, at) in enumerate(halves[0]):
@@ -698,7 +700,10 @@
     return call(
         body, (COLS,), ins + kern.ins(),
         piece_specs(128 * len(halves[0]), 128 * len(halves[1])) + [((T, D), f32, (T, D), full), ((1, D), f32, (1, D), full)],
-        scratch=kern.scratch() + [pltpu.VMEM((T, D), bf16), pltpu.VMEM((T, D), bf16), pltpu.VMEM((T, D), f32)],
+        scratch=kern.scratch()
+        + [pltpu.VMEM((T, D), bf16)] * 2
+        + [pltpu.VMEM((D, T), bf16)] * 2
+        + [pltpu.VMEM((T, D), f32)],
         flops=4 * T * D * total + 2 * T * D * D, prefetch=me,
     )
 
@@ -808,14 +813,15 @@
     def send(self, values, axes):
         return [self.swap(v, axis) for v, axis in zip(values, axes)]
 
-    def reduce_z(self, pair, *behind):
-        n1 = pair[0].shape[1]
-        both = jnp.concatenate(pair, axis=1)
-        here = lambda by: lax.dynamic_index_in_dim(both, self.z ^ by, 0, False)
-        total = here(0).astype(f32)
-        for by in (1, 2, 3):
-            total = total + after(self.swap(here(by), "z", by), *behind).astype(f32)
-        return total[:n1], total[n1:]
+    def send_back(self, value):
+        part = lambda by: lax.dynamic_index_in_dim(value, self.z ^ by, 0, False)
+        return [self.swap(part(by), "z", by) for by in (1, 2, 3)]
+
+    def add_back(self, value, got):
+        total = lax.dynamic_index_in_dim(value, self.z, 0, False).astype(f32)
+        for g in got:
+            total = total + g.astype(f32)
+        return total
 
     def reduce_z_all(self, pair):
         n1 = pair[0].shape[1]
@@ -948,7 +954,7 @@
     shards1, shards2 = [bq, bk, bv, bo_w, wg1, wu1, wd1], [wq, wk, wv, wo2, wg2, wu2, wd2]
     send_order, local_slots, placing = route_plan(dest_slot, T, rows, cols)
     restore = jnp.argsort(send_order)
-    outgoing = after(tokens[send_order], restore) if ring else tokens[send_order]
+    outgoing = after(tokens[send_order], restore, placing) if ring else tokens[send_order]
     cot_going = cotangent[send_order]
     if ring:
         me = jnp.stack([lax.axis_index(names[1]), lax.axis_index(cols)]).astype(i32)
@@ -1037,11 +1043,14 @@
     dg2, du2, *d2 = down_bwd(me, cot, v_d, hid2, g2, u2)
     if ring:
         r_d2 = ring.send(d2[1:], ("core",))
+    h2 = down(me, hm2, hid2, v_d)
+    outgoing = h2.astype(bf16)[local_slots]
     gu2 = gate_up_bwd(me, xf2, dg2, du2)
     if ring:
-        dg2, du2, gu2, r_d2 = sync(dg2, du2, gu2, r_d2)
+        dg2, du2, gu2, r_d2, outgoing = sync(dg2, du2, gu2, r_d2, outgoing)
         z_d2 = ring.scatter_z(d2[0] + r_d2[0])
         r_gu2 = ring.send(gu2[1::2], ("core", "core"))
+    output = exchange(outgoing, rows)
     gm2, bo2, dor2, gg_m2 = mlp_dx(me, dg2, du2, v_g, v_u, hm2, gain_m2, cot, v_o, bf16)
     if ring:
         gm2, bo2, dor2, gg_m2, r_gu2 = sync(gm2, bo2, dor2, gg_m2, r_gu2)
@@ -1050,7 +1059,7 @@
     dq2, dk2, dv2 = window_bwd(q2, k2, v2, dor2, seg_row, seg_col, live_col)
     *a2, gh1, gg_a2 = attn_bwd(me, xa2, [dq2, dk2, dv2], [v_q, v_k, v_v], o2, bo2, h1, gain_a2, gm2, HALVES_TWO)
     if ring:
-        a2, gh1, gg_a2, r_gu2, z_d2 = sync(a2, gh1, gg_a2, r_gu2, z_d2)
+        a2, gh1, gg_a2, r_gu2, z_d2, output = sync(a2, gh1, gg_a2, r_gu2, z_d2, output)
         keep_gu2, go = add_two(keep_gu2, r_gu2)
         r_gu2 = ring.send(go, ("y", "x"))
         r_a2 = ring.send(a2[1::2], ("core", "core"))
@@ -1058,23 +1067,20 @@
         r_d2 = ring.send(go, ("y", "x"))
     dg1, du1, *d1 = down_bwd(me, gh1, w_d, hid1, g1, u1)
     if ring:
-        dg1, du1, d1, r_gu2, r_a2, r_d2 = sync(dg1, du1, d1, r_gu2, r_a2, r_d2)
+        dg1, du1, d1, r_gu2, r_a2 = sync(dg1, du1, d1, r_gu2, r_a2)
         z_gu2 = ring.scatter_z(jnp.concatenate(add_one(keep_gu2, r_gu2), axis=1))
         keep_a2, go = add_core(a2, r_a2)
         r_a2 = ring.send(go, ("x", "y"))
         r_d1 = ring.send(d1[1:], ("core",))
+    gu1 = gate_up_bwd(me, xf1, dg1, du1)
+    if ring:
+        gu1, r_a2, r_d1, r_d2 = sync(gu1, r_a2, r_d1, r_d2)
+        keep_a2, go = add_two(keep_a2, r_a2)
+        r_a2 = ring.send(go, ("y", "x"))
         keep_d2, go = near_rows(add_one(keep_d2, r_d2))
         r_d2 = ring.send(go, ("x", "y"))
-    gu1 = gate_up_bwd(me, xf1, dg1, du1)
-    h2 = down(me, tied(hm2, gu1[0]), hid2, v_d)
-    if ring:
-        gu1, h2, r_a2, r_d1, r_d2 = sync(gu1, h2, r_a2, r_d1, r_d2)
-        sum_d2 = add_one(keep_d2, r_d2)
-        keep_a2, go = add_two(keep_a2, r_a2)
-        r_a2 = ring.send(go, ("y", "x"))
         r_gu1 = ring.send(gu1[1::2], ("core", "core"))
         z_d1 = ring.scatter_z(d1[0] + r_d1[0])
-    output = exchange(h2.astype(bf16)[local_slots], rows)
     gm1, bo1, dou1, gg_m1 = mlp_dx(me, dg1, du1, w_g, w_u, hm1, gain_m1, gh1, w_o, f32)
     if ring:
         gm1, bo1, dou1, gg_m1, r_a2, r_gu1 = sync(gm1, bo1, dou1, gg_m1, r_a2, r_gu1)
@@ -1083,7 +1089,8 @@
         r_gu1 = ring.send(go, ("x", "y"))
     dqk1, dv1 = based_bwd(qk1, v1, dou1, ou1, rden1, seg_row, seg_col, live_col)
     if ring:
-        dqk1, dv1, output, r_gu1 = sync(dqk1, dv1, output, r_gu1)
+        dqk1, dv1, r_gu1, r_d2 = sync(dqk1, dv1, r_gu1, r_d2)
+        sum_d2 = add_one(keep_d2, r_d2)
         keep_gu1, go = add_two(keep_gu1, r_gu1)
         r_gu1 = ring.send(go, ("y", "x"))
     *a1, g0, gg_a1 = attn_bwd(me, xa1, [dqk1, dv1], [w_qk, w_v], o1, bo1, start, gain_a1, gm1, HALVES_ONE)
@@ -1091,34 +1098,38 @@
     gains = jnp.concatenate([gg_a1, gg_m1, gg_a2, gg_m2], axis=0)
     if ring:
         a1, g0, gains, r_gu1, z_gu2, z_d1 = sync(a1, g0, gains, r_gu1, z_gu2, z_d1)
-        gu1 = add_one(keep_gu1, r_gu1)
-        arrived = exchange(g0.astype(bf16)[local_slots], rows)
+        gu1 = jnp.concatenate(add_one(keep_gu1, r_gu1), axis=1)
         r_a1 = ring.send(a1[1::2], ("core", "core"))
         r_gains = ring.send([gains], ("core",))
         keep_d1, go = far_rows(z_d1)
         r_d1 = ring.send(go, ("y", "x"))
-        r_a1, r_gains, r_d1 = sync(r_a1, r_gains, r_d1)
+        r_z = ring.send_back(gu1)
+        outgoing = g0.astype(bf16)[local_slots]
+        r_a1, r_gains, r_d1, outgoing = sync(r_a1, r_gains, r_d1, outgoing)
+        arrived = exchange(outgoing, rows)
         keep_a1, go = add_core(a1, r_a1)
         r_a1 = ring.send(go, ("x", "y"))
         gains = gains + r_gains[0]
         r_gains = ring.send([gains], ("x",))
         keep_d1, go = near_rows(add_one(keep_d1, r_d1))
         r_d1 = ring.send(go, ("x", "y"))
-        r_a1, r_gains, r_d1 = sync(r_a1, r_gains, r_d1)
+        r_a1, r_gains, r_d1, r_z = sync(r_a1, r_gains, r_d1, r_z)
         keep_a1, go = add_two(keep_a1, r_a1)
         r_a1 = ring.send(go, ("y", "x"))
         gains = gains + r_gains[0]
         r_gains = ring.send([gains], ("y",))
         sum_d1 = add_one(keep_d1, r_d1)
-        gu1, r_a1, r_gains, arrived = sync(gu1, r_a1, r_gains, arrived)
-        a1 = add_one(keep_a1, r_a1)
+        last_gu1 = ring.add_back(gu1, r_z)
+        r_a1, r_gains, arrived = sync(r_a1, r_gains, arrived)
+        a1 = jnp.concatenate(add_one(keep_a1, r_a1), axis=1)
+        last_a1 = ring.add_back(a1, ring.send_back(a1))
         gains = gains + r_gains[0]
-        last = ring.reduce_z([jnp.concatenate(gu1, axis=1), jnp.concatenate(a1, axis=1)])
         far_z = [ring.swap(gains, "z", by) for by in (1, 2, 3)]
         gains = (gains + far_z[0]) + (far_z[1] + far_z[2])
         z_a2 = ring.scatter_z(jnp.concatenate([after(v, z_d1) for v in done_a2], axis=1))
+        z_a2 = after(z_a2, *far_z)
         cut = lambda v, n: [v[:n].astype(f32), v[n:].astype(f32)]
-        sum_gu1, sum_a1 = cut(last[0], FC), cut(last[1], a1[0].shape[1])
+        sum_gu1, sum_a1 = cut(last_gu1, FC), cut(last_a1, 128 * len(HALVES_ONE[0]))
         sum_gu2, sum_a2 = cut(z_gu2, FC), cut(z_a2, done_a2[0].shape[1])
         tokens_grad = arrived
         wide = lambda halves: [h.astype(f32) for h in halves]

time: 772 us -> 756 us (0.979)
  waiting for transfers between devices: 195 us -> 168 us
  starting transfers between devices: 118 us -> 128 us
    ppermute x100 -> x103, waiting for transfers between devices: 175 us -> 155 us  [swap(): lax.ppermute(value, self.axes, [(i, i ^ by << shift) for i in range(32)])]
    ppermute x100 -> x103, starting transfers between devices: 89.2 us -> 102 us  [swap(): lax.ppermute(value, self.axes, [(i, i ^ by << shift) for i in range(32)])]
    unnamed x184 -> x168, local copies, waits for them, and re-layouts: 17.5 us -> 18.4 us
  transfers between devices with their start and end apart: 109 -> 112, of which waited for: 32 -> 31; matrix products, arithmetic and copies ran while one was open for 17% -> 17% of each run, Pallas kernels for 35% -> 35%
where the time goes in v5:
time: 756 us; the launch traced here: 749 us
  Pallas kernels  280 us (37%)
  waiting for transfers between devices  168 us (22%)
  starting transfers between devices  128 us (17%)
  other arithmetic  102 us (13%)
  local copies, waits for them, and re-layouts  52.2 us (7%)
  between operations  18.6 us (2%)
    pallas_call x20, Pallas kernels, call(): pl.pallas_call(body, out_shape=out_shape, grid_spec=pltpu.PrefetchScalarG...  280 us
    ppermute x103, waiting for transfers between devices, swap(): lax.ppermute(value, self.axes, [(i, i ^ by << shift) for i in range(32)])  155 us
    ppermute x103, starting transfers between devices, swap(): lax.ppermute(value, self.axes, [(i, i ^ by << shift) for i in range(32)])  102 us
    all_to_all x4, starting transfers between devices, exchange(): lax.all_to_all(value.reshape(row_count, n // row_count, width), axis, spl...  26.2 us
    add x6, other arithmetic, add_core(): keep = [four[0][0] + got[0][0], four[2][0] + got[1][0]]  19.8 us
    unnamed x168, local copies, waits for them, and re-layouts  18.4 us
  transfers between devices with their start and end apart: 112, of which 31 were waited for; matrix products, arithmetic and copies ran while one was open for 17% of the time, Pallas kernels for 35%

profile of v5, /device:TPU:0, one launch (start us, length us, event | category | flops | bytes accessed | tf_op | source)
XLA Modules:
  0.0 748.7 jit_solution(846951438337019909)
XLA Ops:
  60.0 17.9 %collective-permute-done.4 = bf16[1408,128]{1,0:T(8,128)(2,1)S(1)} collective-permute-done((bf16[1408,128]{1,0:T(8,128)(2,1)S(1)}, bf16[1408,128]{1,0:T(8,128)(2,1)S(1)}, u32[]{:S(2)}, u32[]{:S(2)}) %collective-permute-start.4) | collective-permute-done | bytes 360480 | tf_op jit(solution)/shard_map/ppermute | solution.py:784
  90.0 21.7 %collective-permute-done.15 = bf16[4,704,128]{2,1,0:T(8,128)(2,1)S(1)} collective-permute-done((bf16[4,704,128]{2,1,0:T(8,128)(2,1)S(1)}, bf16[4,704,128]{2,1,0:T(8,128)(2,1)S(1)}, u32[]{:S(2)}, u32[]{:S(2)}) %collective-permute-start.15) | collective-permute-done | bytes 720928 | tf_op jit(solution)/shard_map/ppermute | solution.py:784
  144.5 10.1 %shard_map.374 = (bf16[512,1024]{1,0:T(8,128)(2,1)}, bf16[512,512]{1,0:T(8,128)(2,1)}, bf16[512,1024]{1,0:T(8,128)(2,1)}) custom-call(s32[2]{0:T(128)} %pad_add_fusion.me_ref, bf16[512,1024]{1,0:T(8,128)(2,1)} %gather_fusion.1, f32[1,1024]{1,0:T(1,128)} %bitcast.459, bf16[2,4,384,128]{3,2,1,0:T(8,128)(2,1)} %copy-done.6, ...), custom_call_target="tpu_custom_call" | custom-call | flops 1610612736 | bytes 8916992 | tf_op jit(solution)/shard_map/pallas_call | solution.py:55
  166.1 10.4 %collective-permute-done.28 = bf16[4,352,128]{2,1,0:T(8,128)(2,1)S(1)} collective-permute-done((bf16[4,352,128]{2,1,0:T(8,128)(2,1)S(1)}, bf16[4,352,128]{2,1,0:T(8,128)(2,1)S(1)}, u32[]{:S(2)}, u32[]{:S(2)}) %collective-permute-start.28) | collective-permute-done | bytes 360480 | tf_op jit(solution)/shard_map/ppermute | solution.py:784
  193.9 13.5 %shard_map.377 = (bf16[2816,512]{1,0:T(8,128)(2,1)}, bf16[2816,512]{1,0:T(8,128)(2,1)}, bf16[2816,512]{1,0:T(8,128)(2,1)}) custom-call(s32[2]{0:T(128)} %pad_add_fusion.me_ref, bf16[512,1024]{1,0:T(8,128)(2,1)} %get-tuple-element.246.refs_0_.xf_ref, bf16[2,4,704,128]{3,2,1,0:T(8,128)(2,1)} %pad_maximum_fusion.1.refs_1_.refs_5_, ...), custom_call_target="tpu_custom_call" | custom-call | flops 5905580032 | bytes 21233664 | tf_op jit(solution)/shard_map/pallas_call | solution.py:55
  225.2 9.4 %collective-permute-done.35 = bf16[4,512,128]{2,1,0:T(8,128)(2,1)S(1)} collective-permute-done((bf16[4,512,128]{2,1,0:T(8,128)(2,1)S(1)}, bf16[4,512,128]{2,1,0:T(8,128)(2,1)S(1)}, u32[]{:S(2)}, u32[]{:S(2)}) %collective-permute-start.35) | collective-permute-done | bytes 524320 | tf_op jit(solution)/shard_map/ppermute | solution.py:784
  241.7 10.7 %shard_map.378.refs_0_.refs_2_ = f32[512,1024]{1,0:T(8,128)} custom-call(s32[2]{0:T(128)} %pad_add_fusion.me_ref, f32[512,1024]{1,0:T(8,128)} %get-tuple-element.240.refs_0_.refs_2_, bf16[2816,512]{1,0:T(8,128)(2,1)} %get-tuple-element.256.refs_1_, bf16[4,2816,128]{2,1,0:T(8,128)(2,1)} %bitcast.389, bf16[4,2816,128]{2,1,0:T(8,128)(2,1)} %collective-permute-done.38.refs_3_.refs_5_), custom_call_target="tpu_custom_call" | custom-call | flops 2952790016 | bytes 12845056 | tf_op jit(solution)/shard_map/pallas_call | solution.py:55
  260.6 12.5 %shard_map.379 = (bf16[512,1024]{1,0:T(8,128)(2,1)}, bf16[512,1024]{1,0:T(8,128)(2,1)}, bf16[512,1024]{1,0:T(8,128)(2,1)}, bf16[512,1024]{1,0:T(8,128)(2,1)}) custom-call(s32[2]{0:T(128)} %pad_add_fusion.me_ref, f32[512,1024]{1,0:T(8,128)} %shard_map.378.refs_0_.refs_2_, f32[1,1024]{1,0:T(1,128)} %bitcast.451, bf16[2,4,512,128]{3,2,1,0:T(8,128)(2,1)} %copy-done.5, ...), custom_call_target="tpu_custom_call" | custom-call | flops 3221225472 | bytes 18878464 | tf_op jit(solution)/shard_map/pallas_call | solution.py:55
  291.7 11.7 %shard_map.380.refs_1_ = bf16[512,1024]{1,0:T(8,128)(2,1)} custom-call(bf16[512,1024]{1,0:T(8,128)(2,1)} %get-tuple-element.271.q_ref, bf16[512,1024]{1,0:T(8,128)(2,1)} %get-tuple-element.272.k_ref, bf16[512,1024]{1,0:T(8,128)(2,1)} %get-tuple-element.273.v_ref, s32[1,512]{1,0:T(1,128)} %fusion.66.sr_ref, s32[512,1]{1,0:T(8,128)} %convert_add_fusion.2.sc_ref, ...), custom_call_target="tpu_custom_call" | custom-call | flops 1610612736 | bytes 4200448 | tf_op jit(solution)/shard_map/pallas_call | solution.py:55
  323.2 13.6 %shard_map.382 = (bf16[2816,512]{1,0:T(8,128)(2,1)}, bf16[2816,512]{1,0:T(8,128)(2,1)}, bf16[2816,512]{1,0:T(8,128)(2,1)}) custom-call(s32[2]{0:T(128)} %pad_add_fusion.me_ref, bf16[512,1024]{1,0:T(8,128)(2,1)} %get-tuple-element.275.refs_0_.xf_ref, bf16[2,4,704,128]{3,2,1,0:T(8,128)(2,1)} %copy-done.32, ...), custom_call_target="tpu_custom_call" | custom-call | flops 5905580032 | bytes 21233664 | tf_op jit(solution)/shard_map/pallas_call | solution.py:55
  336.8 14.5 %shard_map.383 = (bf16[2816,512]{1,0:T(8,128)(2,1)}, bf16[2816,512]{1,0:T(8,128)(2,1)}, bf16[4,2816,128]{2,1,0:T(8,128)(2,1)}, bf16[4,2816,128]{2,1,0:T(8,128)(2,1)}) custom-call(s32[2]{0:T(128)} %pad_add_fusion.me_ref, bf16[512,1024]{1,0:T(8,128)(2,1)} %gather_fusion.3, bf16[2816,512]{1,0:T(8,128)(2,1)} %get-tuple-element.278.refs_1_, ...), custom_call_target="tpu_custom_call" | custom-call | flops 5905580032 | bytes 27000832 | tf_op jit(solution)/shard_map/pallas_call | solution.py:55
  351.5 10.2 %shard_map.385 = f32[512,1024]{1,0:T(8,128)} custom-call(s32[2]{0:T(128)} %pad_add_fusion.me_ref, f32[512,1024]{1,0:T(8,128)} %get-tuple-element.290.refs_0_.refs_2_, bf16[2816,512]{1,0:T(8,128)(2,1)} %get-tuple-element.278.refs_1_, bf16[4,2816,128]{2,1,0:T(8,128)(2,1)} %bitcast.395, bf16[4,2816,128]{2,1,0:T(8,128)(2,1)} %collective-permute-done.56.refs_5_.refs_3_), custom_call_target="tpu_custom_call" | custom-call | flops 2952790016 | bytes 12845056 | tf_op jit(solution)/shard_map/pallas_call | solution.py:55
  366.2 14.2 %shard_map.384 = (bf16[2,2,4,704,128]{4,3,2,1,0:T(8,128)(2,1)}, bf16[2,2,4,704,128]{4,3,2,1,0:T(8,128)(2,1)}, bf16[2,2,4,704,128]{4,3,2,1,0:T(8,128)(2,1)}, bf16[2,2,4,704,128]{4,3,2,1,0:T(8,128)(2,1)}) custom-call(s32[2]{0:T(128)} %pad_add_fusion.me_ref, bf16[512,1024]{1,0:T(8,128)(2,1)} %get-tuple-element.275.refs_0_.xf_ref, ...), custom_call_target="tpu_custom_call" | custom-call | flops 5905580032 | bytes 18350080 | tf_op jit(solution)/shard_map/pallas_call | solution.py:55
  393.9 19.0 %shard_map.386 = (f32[512,1024]{1,0:T(8,128)}, bf16[512,1024]{1,0:T(8,128)(2,1)}, bf16[512,1024]{1,0:T(8,128)(2,1)}, f32[1,1024]{1,0:T(1,128)}) custom-call(s32[2]{0:T(128)} %pad_add_fusion.me_ref, bf16[2816,512]{1,0:T(8,128)(2,1)} %get-tuple-element.291.dg_ref.refs_0_, bf16[2816,512]{1,0:T(8,128)(2,1)} %get-tuple-element.292.du_ref.refs_1_, ...), custom_call_target="tpu_custom_call" | custom-call | flops 6979321856 | bytes 28844032 | tf_op jit(solution)/shard_map/pallas_call | solution.py:55
  422.8 18.6 %shard_map.387 = (bf16[512,1024]{1,0:T(8,128)(2,1)}, bf16[512,1024]{1,0:T(8,128)(2,1)}, bf16[512,1024]{1,0:T(8,128)(2,1)}) custom-call(bf16[512,1024]{1,0:T(8,128)(2,1)} %get-tuple-element.271.q_ref, bf16[512,1024]{1,0:T(8,128)(2,1)} %get-tuple-element.272.k_ref, bf16[512,1024]{1,0:T(8,128)(2,1)} %get-tuple-element.273.v_ref, ...), custom_call_target="tpu_custom_call" | custom-call | flops 4026531840 | bytes 7346176 | tf_op jit(solution)/shard_map/pallas_call | solution.py:55
  441.4 21.3 %shard_map.388 = (bf16[2,2,4,512,128]{4,3,2,1,0:T(8,128)(2,1)}, bf16[2,2,4,512,128]{4,3,2,1,0:T(8,128)(2,1)}, bf16[2,2,4,512,128]{4,3,2,1,0:T(8,128)(2,1)}, bf16...) custom-call(s32[2]{0:T(128)} %pad_add_fusion.me_ref, ...), custom_call_target="tpu_custom_call" | custom-call | flops 7516192768 | bytes 33562624 | tf_op jit(solution)/shard_map/pallas_call | solution.py:55
  468.1 14.9 %shard_map.389 = (bf16[2816,512]{1,0:T(8,128)(2,1)}, bf16[2816,512]{1,0:T(8,128)(2,1)}, bf16[4,2816,128]{2,1,0:T(8,128)(2,1)}, bf16[4,2816,128]{2,1,0:T(8,128)(2,1)}) custom-call(s32[2]{0:T(128)} %pad_add_fusion.me_ref, f32[512,1024]{1,0:T(8,128)} %get-tuple-element.320.refs_0_.refs_4_, bf16[2816,512]{1,0:T(8,128)(2,1)} %get-tuple-element.256.refs_1_, ...), custom_call_target="tpu_custom_call" | custom-call | flops 5905580032 | bytes 28049408 | tf_op jit(solution)/shard_map/pallas_call | solution.py:55
  499.2 14.0 %shard_map.391 = (bf16[2,2,4,704,128]{4,3,2,1,0:T(8,128)(2,1)}, bf16[2,2,4,704,128]{4,3,2,1,0:T(8,128)(2,1)}, bf16[2,2,4,704,128]{4,3,2,1,0:T(8,128)(2,1)}, bf16[2,2,4,704,128]{4,3,2,1,0:T(8,128)(2,1)}) custom-call(s32[2]{0:T(128)} %pad_add_fusion.me_ref, bf16[512,1024]{1,0:T(8,128)(2,1)} %get-tuple-element.246.refs_0_.xf_ref, ...), custom_call_target="tpu_custom_call" | custom-call | flops 5905580032 | bytes 18350080 | tf_op jit(solution)/shard_map/pallas_call | solution.py:55
  534.4 20.4 %shard_map.390 = (f32[512,1024]{1,0:T(8,128)}, bf16[512,1024]{1,0:T(8,128)(2,1)}, f32[512,1024]{1,0:T(8,128)}, f32[1,1024]{1,0:T(1,128)}) custom-call(s32[2]{0:T(128)} %pad_add_fusion.me_ref, bf16[2816,512]{1,0:T(8,128)(2,1)} %get-tuple-element.331.refs_0_.dg_ref, bf16[2816,512]{1,0:T(8,128)(2,1)} %get-tuple-element.332.refs_1_.du_ref, ...), custom_call_target="tpu_custom_call" | custom-call | flops 6979321856 | bytes 29892608 | tf_op jit(solution)/shard_map/pallas_call | solution.py:55
  572.1 15.8 %shard_map.392 = (bf16[512,512]{1,0:T(8,128)(2,1)}, bf16[512,1024]{1,0:T(8,128)(2,1)}) custom-call(bf16[512,512]{1,0:T(8,128)(2,1)} %get-tuple-element.229.qk_ref, bf16[512,1024]{1,0:T(8,128)(2,1)} %get-tuple-element.230.v_ref, f32[512,1024]{1,0:T(8,128)} %get-tuple-element.353.dou_ref, f32[512,1024]{1,0:T(8,128)} %get-tuple-element.354.ou_ref, ...), custom_call_target="tpu_custom_call" | custom-call | flops 4026531840 | bytes 9443328 | tf_op jit(solution)/shard_map/pallas_call | solution.py:55
  589.1 9.7 %collective-permute-done.77 = bf16[352,128]{1,0:T(8,128)(2,1)S(1)} collective-permute-done((bf16[352,128]{1,0:T(8,128)(2,1)S(1)}, bf16[352,128]{1,0:T(8,128)(2,1)S(1)}, u32[]{:S(2)}, u32[]{:S(2)}) %collective-permute-start.77) | collective-permute-done | bytes 90144 | tf_op jit(solution)/shard_map/ppermute | solution.py:784
  604.2 21.1 %shard_map.393 = (bf16[2,2,4,256,128]{4,3,2,1,0:T(8,128)(2,1)}, bf16[2,2,4,256,128]{4,3,2,1,0:T(8,128)(2,1)}, bf16[2,2,4,384,128]{4,3,2,1,0:T(8,128)(2,1)}, bf16...) custom-call(s32[2]{0:T(128)} %pad_add_fusion.me_ref, ...), custom_call_target="tpu_custom_call" | custom-call | flops 4294967296 | bytes 20455424 | tf_op jit(solution)/shard_map/pallas_call | solution.py:55
  658.4 11.8 %collective-permute-done.91 = bf16[1408,128]{1,0:T(8,128)(2,1)S(1)} collective-permute-done((bf16[1408,128]{1,0:T(8,128)(2,1)}, bf16[1408,128]{1,0:T(8,128)(2,1)S(1)}, u32[]{:S(2)}, u32[]{:S(2)}) %collective-permute-start.91) | collective-permute-done | bytes 360480 | tf_op jit(solution)/shard_map/ppermute | solution.py:784
  682.1 9.5 %all-to-all-start.3 = ((bf16[8,64,1024]{2,1,0:T(8,128)(2,1)}), bf16[8,64,1024]{2,1,0:T(8,128)(2,1)S(1)}, u32[]{:S(2)}, u32[]{:S(2)}) async-start(bf16[8,64,1024]{2,1,0:T(8,128)(2,1)} %bitcast.137), calls=%async_computation.6 | async-start | bytes 2097152 | tf_op jit(solution)/shard_map/all_to_all | solution.py:941
  (551 shorter events, 383.4 us)
Async XLA Ops:
  80.9 36.5 %all-to-all-start = ((bf16[8,64,1024]{2,1,0:T(8,128)(2,1)}), bf16[8,64,1024]{2,1,0:T(8,128)(2,1)S(1)}, u32[]{:S(2)}, u32[]{:S(2)}) async-start(bf16[8,64,1024]{2,1,0:T(8,128)(2,1)} %bitcast.391), calls=%async_computation | async-start | bytes 2097152 | tf_op jit(solution)/shard_map/all_to_all | solution.py:941
  84.6 198.6 %all-gather.3.cloned.1.call-start = ((), (), s32[]{:S(2)}) async-start(), calls=%async_computation.12 | async-start | bytes 3604480 | tf_op jit(solution)/shard_map/all_gather | solution.py:795
  113.0 41.7 %collective-permute-start.21 = (bf16[2,4,704,128]{3,2,1,0:T(8,128)(2,1)}, bf16[2,4,704,128]{3,2,1,0:T(8,128)(2,1)}, u32[]{:S(2)}, u32[]{:S(2)}) collective-permute-start(bf16[2,4,704,128]{3,2,1,0:T(8,128)(2,1)} %pad_maximum_fusion.2.refs_5_.refs_9_), channel_id=1, source_target_pairs={{0,2},{1,3},{2,0},{3,1},{4,6},{5,7},{6,4},{7,5},{8,10},{9,11},{10,... | collective-permute-start | bytes 4325384 | tf_op jit(solution)/shard_map/ppermute | solution.py:784
  116.6 48.3 %collective-permute-start.20 = (bf16[2,4,704,128]{3,2,1,0:T(8,128)(2,1)}, bf16[2,4,704,128]{3,2,1,0:T(8,128)(2,1)}, u32[]{:S(2)}, u32[]{:S(2)}) collective-permute-start(bf16[2,4,704,128]{3,2,1,0:T(8,128)(2,1)} %pad_maximum_fusion.1.refs_1_.refs_5_), channel_id=1, source_target_pairs={{0,4},{1,5},{2,6},{3,7},{4,0},{5,1},{6,2},{7,3},{8,12},{9,13},{10,... | collective-permute-start | bytes 4325384 | tf_op jit(solution)/shard_map/ppermute | solution.py:784
  140.9 47.1 %collective-permute-start.32 = (bf16[2,4,704,128]{3,2,1,0:T(8,128)(2,1)}, bf16[2,4,704,128]{3,2,1,0:T(8,128)(2,1)S(1)}, u32[]{:S(2)}, u32[]{:S(2)}) collective-permute-start(bf16[2,4,704,128]{3,2,1,0:T(8,128)(2,1)} %pad_maximum_fusion.2.refs_5_.refs_9_), channel_id=1, source_target_pairs={{0,1},{1,0},{2,3},{3,2},{4,5},{5,4},{6,7},{7,6},{8,9},{9,8},{10,11... | collective-permute-start | bytes 4325384 | tf_op jit(solution)/shard_map/ppermute | solution.py:784
  208.4 33.3 %collective-permute-start.38 = (bf16[4,2816,128]{2,1,0:T(8,128)(2,1)S(1)}, bf16[4,2816,128]{2,1,0:T(8,128)(2,1)}, u32[]{:S(2)}, u32[]{:S(2)}) collective-permute-start(bf16[4,2816,128]{2,1,0:T(8,128)(2,1)S(1)} %bitcast.388), channel_id=1, source_target_pairs={{0,1},{1,0},{2,3},{3,2},{4,5},{5,4},{6,7},{7,6},{8,9},{9,8},{10,11... | collective-permute-start | bytes 8650760 | tf_op jit(solution)/shard_map/ppermute | solution.py:784
  275.8 35.2 %collective-permute-start.53 = (bf16[2,4,704,128]{3,2,1,0:T(8,128)(2,1)}, bf16[2,4,704,128]{3,2,1,0:T(8,128)(2,1)}, u32[]{:S(2)}, u32[]{:S(2)}) collective-permute-start(bf16[2,4,704,128]{3,2,1,0:T(8,128)(2,1)} %pad_maximum_fusion.5.refs_5_.refs_9_), channel_id=1, source_target_pairs={{0,2},{1,3},{2,0},{3,1},{4,6},{5,7},{6,4},{7,5},{8,10},{9,11},{10,... | collective-permute-start | bytes 4325384 | tf_op jit(solution)/shard_map/ppermute | solution.py:784
  277.2 42.0 %collective-permute-start.50 = (bf16[2,4,704,128]{3,2,1,0:T(8,128)(2,1)S(1)}, bf16[2,4,704,128]{3,2,1,0:T(8,128)(2,1)}, u32[]{:S(2)}, u32[]{:S(2)}) collective-permute-start(bf16[2,4,704,128]{3,2,1,0:T(8,128)(2,1)S(1)} %pad_maximum_fusion.4.refs_1_.refs_5_), channel_id=1, source_target_pairs={{0,4},{1,5},{2,6},{3,7},{4,0},{5,1},{6,2},{7,3},{8,12},{9,13},{10,... | collective-permute-start | bytes 4325384 | tf_op jit(solution)/shard_map/ppermute | solution.py:784
  283.2 53.6 %collective-permute-start.56 = (bf16[4,2816,128]{2,1,0:T(8,128)(2,1)}, bf16[4,2816,128]{2,1,0:T(8,128)(2,1)}, u32[]{:S(2)}, u32[]{:S(2)}) collective-permute-start(bf16[4,2816,128]{2,1,0:T(8,128)(2,1)} %bitcast.393), channel_id=1, source_target_pairs={{0,1},{1,0},{2,3},{3,2},{4,5},{5,4},{6,7},{7,6},{8,9},{9,8},{10,11... | collective-permute-start | bytes 8650760 | tf_op jit(solution)/shard_map/ppermute | solution.py:784
  286.0 34.5 %all-to-all-start.1 = ((bf16[8,64,1024]{2,1,0:T(8,128)(2,1)}), bf16[8,64,1024]{2,1,0:T(8,128)(2,1)S(1)}, u32[]{:S(2)}, u32[]{:S(2)}) async-start(bf16[8,64,1024]{2,1,0:T(8,128)(2,1)} %bitcast.92), calls=%async_computation.1 | async-start | bytes 2097152 | tf_op jit(solution)/shard_map/all_to_all | solution.py:941
  290.3 172.5 %reduce-scatter.5.cloned.1.call-start = ((), (), s32[]{:S(2)}) async-start(), calls=%async_computation.8 | async-start | bytes 3604480 | tf_op jit(solution)/shard_map/reduce_scatter | solution.py:811
  385.1 77.6 %all-to-all-start.2 = ((bf16[8,64,1024]{2,1,0:T(8,128)(2,1)}), bf16[8,64,1024]{2,1,0:T(8,128)(2,1)S(1)}, u32[]{:S(2)}, u32[]{:S(2)}) async-start(bf16[8,64,1024]{2,1,0:T(8,128)(2,1)} %bitcast.100), calls=%async_computation.3 | async-start | bytes 2097152 | tf_op jit(solution)/shard_map/all_to_all | solution.py:941
  393.8 232.3 %reduce-scatter.7.cloned.1.call-start = ((), (), s32[]{:S(2)}) async-start(), calls=%async_computation.9 | async-start | bytes 1802240 | tf_op jit(solution)/shard_map/reduce_scatter | solution.py:811
  416.2 46.5 %collective-permute-start.61 = (bf16[2,4,704,128]{3,2,1,0:T(8,128)(2,1)}, bf16[2,4,704,128]{3,2,1,0:T(8,128)(2,1)}, u32[]{:S(2)}, u32[]{:S(2)}) collective-permute-start(bf16[2,4,704,128]{3,2,1,0:T(8,128)(2,1)} %get-tuple-element.481), channel_id=1, source_target_pairs={{0,4},{1,5},{2,6},{3,7},{4,0},{5,1},{6,2},{7,3},{8,12},{9,13},{10,... | collective-permute-start | bytes 4325384 | tf_op jit(solution)/shard_map/ppermute | solution.py:784
  422.0 40.8 %collective-permute-start.60 = (bf16[2,4,704,128]{3,2,1,0:T(8,128)(2,1)}, bf16[2,4,704,128]{3,2,1,0:T(8,128)(2,1)}, u32[]{:S(2)}, u32[]{:S(2)}) collective-permute-start(bf16[2,4,704,128]{3,2,1,0:T(8,128)(2,1)} %get-tuple-element.483), channel_id=1, source_target_pairs={{0,2},{1,3},{2,0},{3,1},{4,6},{5,7},{6,4},{7,5},{8,10},{9,11},{10,... | collective-permute-start | bytes 4325384 | tf_op jit(solution)/shard_map/ppermute | solution.py:784
  486.3 39.2 %collective-permute-start.68 = (bf16[4,2816,128]{2,1,0:T(8,128)(2,1)}, bf16[4,2816,128]{2,1,0:T(8,128)(2,1)}, u32[]{:S(2)}, u32[]{:S(2)}) collective-permute-start(bf16[4,2816,128]{2,1,0:T(8,128)(2,1)} %get-tuple-element.345), channel_id=1, source_target_pairs={{0,1},{1,0},{2,3},{3,2},{4,5},{5,4},{6,7},{7,6},{8,9},{9,8},{10,11... | collective-permute-start | bytes 8650760 | tf_op jit(solution)/shard_map/ppermute | solution.py:784
  490.4 135.8 %reduce-scatter.9.cloned.1.call-start = ((), (), s32[]{:S(2)}) async-start(), calls=%async_computation.10 | async-start | bytes 3604480 | tf_op jit(solution)/shard_map/reduce_scatter | solution.py:811
  530.2 201.8 %reduce-scatter.11.cloned.1.call-start = ((), (), s32[]{:S(2)}) async-start(), calls=%async_computation.11 | async-start | bytes 1310720 | tf_op jit(solution)/shard_map/reduce_scatter | solution.py:811
  559.0 39.8 %collective-permute-start.76 = (bf16[2,4,704,128]{3,2,1,0:T(8,128)(2,1)}, bf16[2,4,704,128]{3,2,1,0:T(8,128)(2,1)}, u32[]{:S(2)}, u32[]{:S(2)}) collective-permute-start(bf16[2,4,704,128]{3,2,1,0:T(8,128)(2,1)} %get-tuple-element.477), channel_id=1, source_target_pairs={{0,4},{1,5},{2,6},{3,7},{4,0},{5,1},{6,2},{7,3},{8,12},{9,13},{10,... | collective-permute-start | bytes 4325384 | tf_op jit(solution)/shard_map/ppermute | solution.py:784
  563.6 35.2 %collective-permute-start.75 = (bf16[2,4,704,128]{3,2,1,0:T(8,128)(2,1)}, bf16[2,4,704,128]{3,2,1,0:T(8,128)(2,1)}, u32[]{:S(2)}, u32[]{:S(2)}) collective-permute-start(bf16[2,4,704,128]{3,2,1,0:T(8,128)(2,1)} %get-tuple-element.479), channel_id=1, source_target_pairs={{0,2},{1,3},{2,0},{3,1},{4,6},{5,7},{6,4},{7,5},{8,10},{9,11},{10,... | collective-permute-start | bytes 4325384 | tf_op jit(solution)/shard_map/ppermute | solution.py:784
  644.6 35.2 %collective-permute-start.93 = (bf16[1408,128]{1,0:T(8,128)(2,1)}, bf16[1408,128]{1,0:T(8,128)(2,1)S(1)}, u32[]{:S(2)}, u32[]{:S(2)}) collective-permute-start(bf16[1408,128]{1,0:T(8,128)(2,1)} %get-tuple-element.492), channel_id=1, source_target_pairs={{0,24},{1,25},{2,26},{3,27},{4,28},{5,29},{6,30},{7,31},{8,16},{9,... | collective-permute-start | bytes 1081352 | tf_op jit(solution)/shard_map/ppermute | solution.py:784
  649.4 42.3 %collective-permute-start.87 = (bf16[2,4,384,128]{3,2,1,0:T(8,128)(2,1)}, bf16[2,4,384,128]{3,2,1,0:T(8,128)(2,1)}, u32[]{:S(2)}, u32[]{:S(2)}) collective-permute-start(bf16[2,4,384,128]{3,2,1,0:T(8,128)(2,1)} %get-tuple-element.489), channel_id=1, source_target_pairs={{0,4},{1,5},{2,6},{3,7},{4,0},{5,1},{6,2},{7,3},{8,12},{9,13},{10,... | collective-permute-start | bytes 2359304 | tf_op jit(solution)/shard_map/ppermute | solution.py:784
  652.8 38.9 %collective-permute-start.86 = (bf16[2,4,256,128]{3,2,1,0:T(8,128)(2,1)}, bf16[2,4,256,128]{3,2,1,0:T(8,128)(2,1)}, u32[]{:S(2)}, u32[]{:S(2)}) collective-permute-start(bf16[2,4,256,128]{3,2,1,0:T(8,128)(2,1)} %get-tuple-element.490), channel_id=1, source_target_pairs={{0,2},{1,3},{2,0},{3,1},{4,6},{5,7},{6,4},{7,5},{8,10},{9,11},{10,... | collective-permute-start | bytes 1572872 | tf_op jit(solution)/shard_map/ppermute | solution.py:784
  682.1 35.2 %all-to-all-start.3 = ((bf16[8,64,1024]{2,1,0:T(8,128)(2,1)}), bf16[8,64,1024]{2,1,0:T(8,128)(2,1)S(1)}, u32[]{:S(2)}, u32[]{:S(2)}) async-start(bf16[8,64,1024]{2,1,0:T(8,128)(2,1)} %bitcast.137), calls=%async_computation.6 | async-start | bytes 2097152 | tf_op jit(solution)/shard_map/all_to_all | solution.py:941
  (165 other events, 2446.9 us)
Sparse Core Ops, SparseCore 0:
  23.8 2.9 sort.60.cloned.1.call-done
  221.1 62.0 all-gather.2
  384.7 77.6 reduce-scatter.4
  490.5 34.7 reduce-scatter.6
  530.3 57.5 reduce-scatter.8
  628.3 38.9 reduce-scatter.10
  (1 shorter events, 0.0 us)

commit v6 on v5

--- a/solution.py
+++ b/solution.py
@@ -607,13 +607,16 @@
     kern = Kernel(5, [w_gate, w_up, w_out], 4)
 
     def body(me_ref, *refs):
-        (dg_ref, du_ref, hm_ref, gain_ref, g_ref), hold, outs, (acc_ref, un_ref, br_ref) = kern.split(refs)
+        (dg_ref, du_ref, hm_ref, gain_ref, g_ref), hold, outs, rest = kern.split(refs)
+        acc_ref, un_ref, br_ref, hl_ref, gl_ref, late = rest
         gm_ref, bo_ref, dou_ref, gg_ref = outs
         i = pl.program_id(0)
 
         @pl.when(i == 0)
         def _():
             start_all(hold)
+            for k, (src, dst) in enumerate(((hm_ref, hl_ref), (g_ref, gl_ref))):
+                pltpu.make_async_copy(src, dst, late.at[k]).start()
 
         x, core = step_place(i)
         part = None
@@ -626,7 +629,9 @@
         @pl.when(i == COLS - 1)
         def _():
             regroup(un_ref, acc_ref, ROWS, me_ref[0])
-            gg, gm = norm_bwd(un_ref[...], hm_ref[...], gain_ref[...], g_ref[...].astype(f32))
+            for k, (src, dst) in enumerate(((hm_ref, hl_ref), (g_ref, gl_ref))):
+                pltpu.make_async_copy(src, dst, late.at[k]).wait()
+            gg, gm = norm_bwd(un_ref[...], hl_ref[...], gain_ref[...], gl_ref[...].astype(f32))
             gg_ref[...] = gg
             gm_ref[...] = gm
             bo_ref[...] = gm.astype(bf16)
@@ -641,9 +646,11 @@
     row = lambda i, me: (step_col(i, me), 0)
     full = whole_map(T, D)
     return call(
-        body, (COLS,), [(dg, (FC, T), row), (du, (FC, T), row), hm, gain.reshape(1, D), g] + kern.ins(),
+        body, (COLS,), [(dg, (FC, T), row), (du, (FC, T), row), (hm, None, None), gain.reshape(1, D), (g, None, None)] + kern.ins(),
         [((T, D), f32, (T, D), full), ((T, D), bf16, (T, D), full), ((T, D), kind, (T, D), full), ((1, D), f32, (1, D), full)],
-        scratch=kern.scratch() + [pltpu.VMEM((T, D), f32), pltpu.VMEM((T, D), f32), pltpu.VMEM((T, D), bf16)],
+        scratch=kern.scratch()
+        + [pltpu.VMEM((T, D), f32), pltpu.VMEM((T, D), f32), pltpu.VMEM((T, D), bf16)]
+        + [pltpu.VMEM((T, D), f32), pltpu.VMEM((T, D), g.dtype), pltpu.SemaphoreType.DMA((2,))],
         flops=4 * T * D * FFP + 2 * T * D * D, prefetch=me,
     )
 
@@ -653,7 +660,8 @@
     kern = Kernel(6 + n, strips, 6)
 
     def body(me_ref, *refs):
-        ins, hold, (*p_refs, g_ref, gg_ref), (xr_ref, or_ref, xt_ref, ot_ref, acc_ref) = kern.split(refs)
+        ins, hold, (*p_refs, g_ref, gg_ref), rest = kern.split(refs)
+        xr_ref, or_ref, xt_ref, ot_ref, acc_ref, hl_ref, gl_ref, late = rest
         xa_ref, o_ref, h_ref, gain_ref, gm_ref, bo_ref, *d_refs = ins
         i = pl.program_id(0)
 
@@ -662,6 +670,8 @@
             start_all(hold)
             regroup(xr_ref, xa_ref, ROWS, me_ref[0])
             regroup(or_ref, o_ref, ROWS, me_ref[0])
+            for k, (src, dst) in enumerate(((h_ref, hl_ref), (gm_ref, gl_ref))):
+                pltpu.make_async_copy(src, dst, late.at[k]).start()
             xt_ref[...] = xr_ref[...].T
             ot_ref[...] = or_ref[...].T
 
@@ -688,13 +698,15 @@
         @pl.when(i == COLS - 1)
         def _():
             regroup(g_ref, acc_ref, ROWS, me_ref[0])
-            gg, g = norm_bwd(g_ref[...], h_ref[...].astype(f32), gain_ref[...], gm_ref[...])
+            for k, (src, dst) in enumerate(((h_ref, hl_ref), (gm_ref, gl_ref))):
+                pltpu.make_async_copy(src, dst, late.at[k]).wait()
+            gg, g = norm_bwd(g_ref[...], hl_ref[...].astype(f32), gain_ref[...], gl_ref[...])
             gg_ref[...] = gg
             g_ref[...] = g
 
     col = lambda i, me: (0, step_col(i, me))
     full = whole_map(T, D)
-    ins = [xa, o, h, gain.reshape(1, D), gm, (bo, (T, 256), col)]
+    ins = [xa, o, (h, None, None), gain.reshape(1, D), (gm, None, None), (bo, (T, 256), col)]
     ins += [(d, (T, d.shape[1] // COLS), col) for d in grads]
     total = sum(d.shape[1] for d in grads)
     return call(
@@ -703,7 +715,7 @@
         scratch=kern.scratch()
         + [pltpu.VMEM((T, D), bf16)] * 2
         + [pltpu.VMEM((D, T), bf16)] * 2
-        + [pltpu.VMEM((T, D), f32)],
+        + [pltpu.VMEM((T, D), f32), pltpu.VMEM((T, D), h.dtype), pltpu.VMEM((T, D), f32), pltpu.SemaphoreType.DMA((2,))],
         flops=4 * T * D * total + 2 * T * D * D, prefetch=me,
     )
 
@@ -765,12 +777,12 @@
 
 
 def far_rows(total):
-    parts = jnp.split(total, 4, axis=0)
+    parts = jnp.split(total, 4, axis=-2)
     return parts[0::2], parts[1::2]
 
 
 def near_rows(halves):
-    parts = [jnp.split(h, 2, axis=0) for h in halves]
+    parts = [jnp.split(h, 2, axis=-2) for h in halves]
     return [p[0] for p in parts], [p[1] for p in parts]
 
 
@@ -1063,8 +1075,6 @@
         keep_gu2, go = add_two(keep_gu2, r_gu2)
         r_gu2 = ring.send(go, ("y", "x"))
         r_a2 = ring.send(a2[1::2], ("core", "core"))
-        keep_d2, go = far_rows(z_d2)
-        r_d2 = ring.send(go, ("y", "x"))
     dg1, du1, *d1 = down_bwd(me, gh1, w_d, hid1, g1, u1)
     if ring:
         dg1, du1, d1, r_gu2, r_a2 = sync(dg1, du1, d1, r_gu2, r_a2)
@@ -1074,23 +1084,21 @@
         r_d1 = ring.send(d1[1:], ("core",))
     gu1 = gate_up_bwd(me, xf1, dg1, du1)
     if ring:
-        gu1, r_a2, r_d1, r_d2 = sync(gu1, r_a2, r_d1, r_d2)
+        gu1, r_a2, r_d1 = sync(gu1, r_a2, r_d1)
         keep_a2, go = add_two(keep_a2, r_a2)
         r_a2 = ring.send(go, ("y", "x"))
-        keep_d2, go = near_rows(add_one(keep_d2, r_d2))
-        r_d2 = ring.send(go, ("x", "y"))
         r_gu1 = ring.send(gu1[1::2], ("core", "core"))
         z_d1 = ring.scatter_z(d1[0] + r_d1[0])
     gm1, bo1, dou1, gg_m1 = mlp_dx(me, dg1, du1, w_g, w_u, hm1, gain_m1, gh1, w_o, f32)
     if ring:
         gm1, bo1, dou1, gg_m1, r_a2, r_gu1 = sync(gm1, bo1, dou1, gg_m1, r_a2, r_gu1)
-        done_a2 = add_one(keep_a2, r_a2)
+        n_a2 = keep_a2[0].shape[1]
+        z_a2 = ring.scatter_z(jnp.concatenate(add_one(keep_a2, r_a2), axis=1))
         keep_gu1, go = add_core(gu1, r_gu1)
         r_gu1 = ring.send(go, ("x", "y"))
     dqk1, dv1 = based_bwd(qk1, v1, dou1, ou1, rden1, seg_row, seg_col, live_col)
     if ring:
-        dqk1, dv1, r_gu1, r_d2 = sync(dqk1, dv1, r_gu1, r_d2)
-        sum_d2 = add_one(keep_d2, r_d2)
+        dqk1, dv1, r_gu1 = sync(dqk1, dv1, r_gu1)
         keep_gu1, go = add_two(keep_gu1, r_gu1)
         r_gu1 = ring.send(go, ("y", "x"))
     *a1, g0, gg_a1 = attn_bwd(me, xa1, [dqk1, dv1], [w_qk, w_v], o1, bo1, start, gain_a1, gm1, HALVES_ONE)
@@ -1101,11 +1109,11 @@
         gu1 = jnp.concatenate(add_one(keep_gu1, r_gu1), axis=1)
         r_a1 = ring.send(a1[1::2], ("core", "core"))
         r_gains = ring.send([gains], ("core",))
-        keep_d1, go = far_rows(z_d1)
+        keep_d1, go = far_rows(jnp.stack([z_d1, z_d2]))
         r_d1 = ring.send(go, ("y", "x"))
         r_z = ring.send_back(gu1)
         outgoing = g0.astype(bf16)[local_slots]
-        r_a1, r_gains, r_d1, outgoing = sync(r_a1, r_gains, r_d1, outgoing)
+        r_a1, r_gains, r_d1, r_z, outgoing, z_a2 = sync(r_a1, r_gains, r_d1, r_z, outgoing, z_a2)
         arrived = exchange(outgoing, rows)
         keep_a1, go = add_core(a1, r_a1)
         r_a1 = ring.send(go, ("x", "y"))
@@ -1113,12 +1121,12 @@
         r_gains = ring.send([gains], ("x",))
         keep_d1, go = near_rows(add_one(keep_d1, r_d1))
         r_d1 = ring.send(go, ("x", "y"))
-        r_a1, r_gains, r_d1, r_z = sync(r_a1, r_gains, r_d1, r_z)
+        r_a1, r_gains, r_d1 = sync(r_a1, r_gains, r_d1)
         keep_a1, go = add_two(keep_a1, r_a1)
         r_a1 = ring.send(go, ("y", "x"))
         gains = gains + r_gains[0]
         r_gains = ring.send([gains], ("y",))
-        sum_d1 = add_one(keep_d1, r_d1)
+        sum_d1, sum_d2 = ([v[k] for v in add_one(keep_d1, r_d1)] for k in range(2))
         last_gu1 = ring.add_back(gu1, r_z)
         r_a1, r_gains, arrived = sync(r_a1, r_gains, arrived)
         a1 = jnp.concatenate(add_one(keep_a1, r_a1), axis=1)
@@ -1126,11 +1134,9 @@
         gains = gains + r_gains[0]
         far_z = [ring.swap(gains, "z", by) for by in (1, 2, 3)]
         gains = (gains + far_z[0]) + (far_z[1] + far_z[2])
-        z_a2 = ring.scatter_z(jnp.concatenate([after(v, z_d1) for v in done_a2], axis=1))
-        z_a2 = after(z_a2, *far_z)
         cut = lambda v, n: [v[:n].astype(f32), v[n:].astype(f32)]
         sum_gu1, sum_a1 = cut(last_gu1, FC), cut(last_a1, 128 * len(HALVES_ONE[0]))
-        sum_gu2, sum_a2 = cut(z_gu2, FC), cut(z_a2, done_a2[0].shape[1])
+        sum_gu2, sum_a2 = cut(z_gu2, FC), cut(z_a2, n_a2)
         tokens_grad = arrived
         wide = lambda halves: [h.astype(f32) for h in halves]
         sum_d1, sum_d2 = wide(sum_d1), wide(sum_d2)

time: 756 us -> 750 us (level)
  waiting for transfers between devices: 168 us -> 178 us
  starting transfers between devices: 128 us -> 119 us
    ppermute x103 -> x99, waiting for transfers between devices: 155 us -> 170 us  [swap(): lax.ppermute(value, self.axes, [(i, i ^ by << shift) for i in range(32)])]
    ppermute x103 -> x99, starting transfers between devices: 102 us -> 98.1 us  [swap(): lax.ppermute(value, self.axes, [(i, i ^ by << shift) for i in range(32)])]
    unnamed x168 -> x160, local copies, waits for them, and re-layouts: 18.4 us -> 15.2 us
  transfers between devices with their start and end apart: 112 -> 108, of which waited for: 31 -> 35; matrix products, arithmetic and copies ran while one was open for 17% -> 17% of each run, Pallas kernels for 35% -> 35%
where the time goes in v6:
time: 750 us; the launch traced here: 742 us
  Pallas kernels  276 us (37%)
  waiting for transfers between devices  178 us (24%)
  starting transfers between devices  119 us (16%)
  other arithmetic  101 us (13%)
  local copies, waits for them, and re-layouts  49.9 us (7%)
  between operations  18.8 us (3%)
    pallas_call x20, Pallas kernels, call(): pl.pallas_call(body, out_shape=out_shape, grid_spec=pltpu.PrefetchScalarG...  276 us
    ppermute x99, waiting for transfers between devices, swap(): lax.ppermute(value, self.axes, [(i, i ^ by << shift) for i in range(32)])  170 us
    ppermute x99, starting transfers between devices, swap(): lax.ppermute(value, self.axes, [(i, i ^ by << shift) for i in range(32)])  98.1 us
    all_to_all x4, starting transfers between devices, exchange(): lax.all_to_all(value.reshape(row_count, n // row_count, width), axis, spl...  20.2 us
    add x6, other arithmetic, add_core(): keep = [four[0][0] + got[0][0], four[2][0] + got[1][0]]  19.4 us
    unnamed x160, local copies, waits for them, and re-layouts  15.2 us
  transfers between devices with their start and end apart: 108, of which 35 were waited for; matrix products, arithmetic and copies ran while one was open for 17% of the time, Pallas kernels for 35%

profile of v6, /device:TPU:0, one launch (start us, length us, event | category | flops | bytes accessed | tf_op | source)
XLA Modules:
  0.0 742.5 jit_solution(12475716676814823691)
XLA Ops:
  60.0 17.9 %collective-permute-done.4 = bf16[1408,128]{1,0:T(8,128)(2,1)S(1)} collective-permute-done((bf16[1408,128]{1,0:T(8,128)(2,1)S(1)}, bf16[1408,128]{1,0:T(8,128)(2,1)S(1)}, u32[]{:S(2)}, u32[]{:S(2)}) %collective-permute-start.4) | collective-permute-done | bytes 360480 | tf_op jit(solution)/shard_map/ppermute | solution.py:796
  90.0 21.7 %collective-permute-done.15 = bf16[4,704,128]{2,1,0:T(8,128)(2,1)S(1)} collective-permute-done((bf16[4,704,128]{2,1,0:T(8,128)(2,1)S(1)}, bf16[4,704,128]{2,1,0:T(8,128)(2,1)S(1)}, u32[]{:S(2)}, u32[]{:S(2)}) %collective-permute-start.15) | collective-permute-done | bytes 720928 | tf_op jit(solution)/shard_map/ppermute | solution.py:796
  144.5 10.1 %shard_map.374 = (bf16[512,1024]{1,0:T(8,128)(2,1)}, bf16[512,512]{1,0:T(8,128)(2,1)}, bf16[512,1024]{1,0:T(8,128)(2,1)}) custom-call(s32[2]{0:T(128)} %pad_add_fusion.me_ref, bf16[512,1024]{1,0:T(8,128)(2,1)} %gather_fusion.1, f32[1,1024]{1,0:T(1,128)} %bitcast.465, bf16[2,4,384,128]{3,2,1,0:T(8,128)(2,1)} %copy-done.6, ...), custom_call_target="tpu_custom_call" | custom-call | flops 1610612736 | bytes 8916992 | tf_op jit(solution)/shard_map/pallas_call | solution.py:55
  166.1 10.4 %collective-permute-done.28 = bf16[4,352,128]{2,1,0:T(8,128)(2,1)S(1)} collective-permute-done((bf16[4,352,128]{2,1,0:T(8,128)(2,1)S(1)}, bf16[4,352,128]{2,1,0:T(8,128)(2,1)S(1)}, u32[]{:S(2)}, u32[]{:S(2)}) %collective-permute-start.28) | collective-permute-done | bytes 360480 | tf_op jit(solution)/shard_map/ppermute | solution.py:796
  194.0 13.5 %shard_map.377 = (bf16[2816,512]{1,0:T(8,128)(2,1)}, bf16[2816,512]{1,0:T(8,128)(2,1)}, bf16[2816,512]{1,0:T(8,128)(2,1)}) custom-call(s32[2]{0:T(128)} %pad_add_fusion.me_ref, bf16[512,1024]{1,0:T(8,128)(2,1)} %get-tuple-element.240.refs_0_.xf_ref, bf16[2,4,704,128]{3,2,1,0:T(8,128)(2,1)} %pad_maximum_fusion.1.refs_1_.refs_5_, ...), custom_call_target="tpu_custom_call" | custom-call | flops 5905580032 | bytes 21233664 | tf_op jit(solution)/shard_map/pallas_call | solution.py:55
  208.5 9.1 %collective-permute-done.46 = bf16[1408,128]{1,0:T(8,128)(2,1)S(1)} collective-permute-done((bf16[1408,128]{1,0:T(8,128)(2,1)S(1)}, bf16[1408,128]{1,0:T(8,128)(2,1)S(1)}, u32[]{:S(2)}, u32[]{:S(2)}) %collective-permute-start.46) | collective-permute-done | bytes 360480 | tf_op jit(solution)/shard_map/ppermute | solution.py:796
  225.2 9.4 %collective-permute-done.35 = bf16[4,512,128]{2,1,0:T(8,128)(2,1)S(1)} collective-permute-done((bf16[4,512,128]{2,1,0:T(8,128)(2,1)S(1)}, bf16[4,512,128]{2,1,0:T(8,128)(2,1)S(1)}, u32[]{:S(2)}, u32[]{:S(2)}) %collective-permute-start.35) | collective-permute-done | bytes 524320 | tf_op jit(solution)/shard_map/ppermute | solution.py:796
  241.7 10.5 %shard_map.378.refs_0_.refs_2_ = f32[512,1024]{1,0:T(8,128)} custom-call(s32[2]{0:T(128)} %pad_add_fusion.me_ref, f32[512,1024]{1,0:T(8,128)} %get-tuple-element.234.refs_0_.refs_2_, bf16[2816,512]{1,0:T(8,128)(2,1)} %get-tuple-element.250.refs_1_, bf16[4,2816,128]{2,1,0:T(8,128)(2,1)} %bitcast.399, bf16[4,2816,128]{2,1,0:T(8,128)(2,1)} %collective-permute-done.38.refs_3_.refs_5_), custom_call_target="tpu_custom_call" | custom-call | flops 2952790016 | bytes 12845056 | tf_op jit(solution)/shard_map/pallas_call | solution.py:55
  260.6 12.6 %shard_map.379 = (bf16[512,1024]{1,0:T(8,128)(2,1)}, bf16[512,1024]{1,0:T(8,128)(2,1)}, bf16[512,1024]{1,0:T(8,128)(2,1)}, bf16[512,1024]{1,0:T(8,128)(2,1)}) custom-call(s32[2]{0:T(128)} %pad_add_fusion.me_ref, f32[512,1024]{1,0:T(8,128)} %shard_map.378.refs_0_.refs_2_, f32[1,1024]{1,0:T(1,128)} %bitcast.457, bf16[2,4,512,128]{3,2,1,0:T(8,128)(2,1)} %copy-done.5, ...), custom_call_target="tpu_custom_call" | custom-call | flops 3221225472 | bytes 18878464 | tf_op jit(solution)/shard_map/pallas_call | solution.py:55
  291.6 11.7 %shard_map.380.refs_1_ = bf16[512,1024]{1,0:T(8,128)(2,1)} custom-call(bf16[512,1024]{1,0:T(8,128)(2,1)} %get-tuple-element.265.q_ref, bf16[512,1024]{1,0:T(8,128)(2,1)} %get-tuple-element.266.k_ref, bf16[512,1024]{1,0:T(8,128)(2,1)} %get-tuple-element.267.v_ref, s32[1,512]{1,0:T(1,128)} %fusion.71.sr_ref, s32[512,1]{1,0:T(8,128)} %convert_add_fusion.2.sc_ref, ...), custom_call_target="tpu_custom_call" | custom-call | flops 1610612736 | bytes 4200448 | tf_op jit(solution)/shard_map/pallas_call | solution.py:55
  323.3 13.6 %shard_map.382 = (bf16[2816,512]{1,0:T(8,128)(2,1)}, bf16[2816,512]{1,0:T(8,128)(2,1)}, bf16[2816,512]{1,0:T(8,128)(2,1)}) custom-call(s32[2]{0:T(128)} %pad_add_fusion.me_ref, bf16[512,1024]{1,0:T(8,128)(2,1)} %get-tuple-element.269.refs_0_.xf_ref, bf16[2,4,704,128]{3,2,1,0:T(8,128)(2,1)} %copy-done.35, ...), custom_call_target="tpu_custom_call" | custom-call | flops 5905580032 | bytes 21233664 | tf_op jit(solution)/shard_map/pallas_call | solution.py:55
  336.9 14.4 %shard_map.383 = (bf16[2816,512]{1,0:T(8,128)(2,1)}, bf16[2816,512]{1,0:T(8,128)(2,1)}, bf16[4,2816,128]{2,1,0:T(8,128)(2,1)}, bf16[4,2816,128]{2,1,0:T(8,128)(2,1)}) custom-call(s32[2]{0:T(128)} %pad_add_fusion.me_ref, bf16[512,1024]{1,0:T(8,128)(2,1)} %gather_fusion.3, bf16[2816,512]{1,0:T(8,128)(2,1)} %get-tuple-element.272.refs_1_, ...), custom_call_target="tpu_custom_call" | custom-call | flops 5905580032 | bytes 27000832 | tf_op jit(solution)/shard_map/pallas_call | solution.py:55
  351.5 10.2 %shard_map.385 = f32[512,1024]{1,0:T(8,128)} custom-call(s32[2]{0:T(128)} %pad_add_fusion.me_ref, f32[512,1024]{1,0:T(8,128)} %get-tuple-element.284.refs_0_.refs_2_, bf16[2816,512]{1,0:T(8,128)(2,1)} %get-tuple-element.272.refs_1_, bf16[4,2816,128]{2,1,0:T(8,128)(2,1)} %bitcast.405, bf16[4,2816,128]{2,1,0:T(8,128)(2,1)} %collective-permute-done.56.refs_5_.refs_3_), custom_call_target="tpu_custom_call" | custom-call | flops 2952790016 | bytes 12845056 | tf_op jit(solution)/shard_map/pallas_call | solution.py:55
  366.3 14.4 %shard_map.384 = (bf16[2,2,4,704,128]{4,3,2,1,0:T(8,128)(2,1)}, bf16[2,2,4,704,128]{4,3,2,1,0:T(8,128)(2,1)}, bf16[2,2,4,704,128]{4,3,2,1,0:T(8,128)(2,1)}, bf16[2,2,4,704,128]{4,3,2,1,0:T(8,128)(2,1)}) custom-call(s32[2]{0:T(128)} %pad_add_fusion.me_ref, bf16[512,1024]{1,0:T(8,128)(2,1)} %get-tuple-element.269.refs_0_.xf_ref, ...), custom_call_target="tpu_custom_call" | custom-call | flops 5905580032 | bytes 18350080 | tf_op jit(solution)/shard_map/pallas_call | solution.py:55
  394.0 18.4 %shard_map.386 = (f32[512,1024]{1,0:T(8,128)}, bf16[512,1024]{1,0:T(8,128)(2,1)}, bf16[512,1024]{1,0:T(8,128)(2,1)}, f32[1,1024]{1,0:T(1,128)}) custom-call(s32[2]{0:T(128)} %pad_add_fusion.me_ref, bf16[2816,512]{1,0:T(8,128)(2,1)} %get-tuple-element.285.dg_ref.refs_0_, bf16[2816,512]{1,0:T(8,128)(2,1)} %get-tuple-element.286.du_ref.refs_1_, ...), custom_call_target="tpu_custom_call" | custom-call | flops 6979321856 | bytes 28844032 | tf_op jit(solution)/shard_map/pallas_call | solution.py:55
  422.1 18.7 %shard_map.387 = (bf16[512,1024]{1,0:T(8,128)(2,1)}, bf16[512,1024]{1,0:T(8,128)(2,1)}, bf16[512,1024]{1,0:T(8,128)(2,1)}) custom-call(bf16[512,1024]{1,0:T(8,128)(2,1)} %get-tuple-element.265.q_ref, bf16[512,1024]{1,0:T(8,128)(2,1)} %get-tuple-element.266.k_ref, bf16[512,1024]{1,0:T(8,128)(2,1)} %get-tuple-element.267.v_ref, ...), custom_call_target="tpu_custom_call" | custom-call | flops 4026531840 | bytes 7346176 | tf_op jit(solution)/shard_map/pallas_call | solution.py:55
  440.8 20.3 %shard_map.388 = (bf16[2,2,4,512,128]{4,3,2,1,0:T(8,128)(2,1)}, bf16[2,2,4,512,128]{4,3,2,1,0:T(8,128)(2,1)}, bf16[2,2,4,512,128]{4,3,2,1,0:T(8,128)(2,1)}, bf16...) custom-call(s32[2]{0:T(128)} %pad_add_fusion.me_ref, ...), custom_call_target="tpu_custom_call" | custom-call | flops 7516192768 | bytes 33562624 | tf_op jit(solution)/shard_map/pallas_call | solution.py:55
  468.2 14.8 %shard_map.389 = (bf16[2816,512]{1,0:T(8,128)(2,1)}, bf16[2816,512]{1,0:T(8,128)(2,1)}, bf16[4,2816,128]{2,1,0:T(8,128)(2,1)}, bf16[4,2816,128]{2,1,0:T(8,128)(2,1)}) custom-call(s32[2]{0:T(128)} %pad_add_fusion.me_ref, f32[512,1024]{1,0:T(8,128)} %get-tuple-element.314.refs_0_.refs_4_, bf16[2816,512]{1,0:T(8,128)(2,1)} %get-tuple-element.250.refs_1_, ...), custom_call_target="tpu_custom_call" | custom-call | flops 5905580032 | bytes 28049408 | tf_op jit(solution)/shard_map/pallas_call | solution.py:55
  496.2 14.3 %shard_map.391 = (bf16[2,2,4,704,128]{4,3,2,1,0:T(8,128)(2,1)}, bf16[2,2,4,704,128]{4,3,2,1,0:T(8,128)(2,1)}, bf16[2,2,4,704,128]{4,3,2,1,0:T(8,128)(2,1)}, bf16[2,2,4,704,128]{4,3,2,1,0:T(8,128)(2,1)}) custom-call(s32[2]{0:T(128)} %pad_add_fusion.me_ref, bf16[512,1024]{1,0:T(8,128)(2,1)} %get-tuple-element.240.refs_0_.xf_ref, ...), custom_call_target="tpu_custom_call" | custom-call | flops 5905580032 | bytes 18350080 | tf_op jit(solution)/shard_map/pallas_call | solution.py:55
  530.2 19.3 %shard_map.390 = (f32[512,1024]{1,0:T(8,128)}, bf16[512,1024]{1,0:T(8,128)(2,1)}, f32[512,1024]{1,0:T(8,128)}, f32[1,1024]{1,0:T(1,128)}) custom-call(s32[2]{0:T(128)} %pad_add_fusion.me_ref, bf16[2816,512]{1,0:T(8,128)(2,1)} %get-tuple-element.325.refs_0_.dg_ref, bf16[2816,512]{1,0:T(8,128)(2,1)} %get-tuple-element.326.refs_1_.du_ref, ...), custom_call_target="tpu_custom_call" | custom-call | flops 6979321856 | bytes 29892608 | tf_op jit(solution)/shard_map/pallas_call | solution.py:55
  563.9 15.8 %shard_map.392 = (bf16[512,512]{1,0:T(8,128)(2,1)}, bf16[512,1024]{1,0:T(8,128)(2,1)}) custom-call(bf16[512,512]{1,0:T(8,128)(2,1)} %get-tuple-element.223.qk_ref, bf16[512,1024]{1,0:T(8,128)(2,1)} %get-tuple-element.224.v_ref, f32[512,1024]{1,0:T(8,128)} %get-tuple-element.346.dou_ref, f32[512,1024]{1,0:T(8,128)} %get-tuple-element.347.ou_ref, ...), custom_call_target="tpu_custom_call" | custom-call | flops 4026531840 | bytes 9443328 | tf_op jit(solution)/shard_map/pallas_call | solution.py:55
  598.6 20.3 %shard_map.393 = (bf16[2,2,4,256,128]{4,3,2,1,0:T(8,128)(2,1)}, bf16[2,2,4,256,128]{4,3,2,1,0:T(8,128)(2,1)}, bf16[2,2,4,384,128]{4,3,2,1,0:T(8,128)(2,1)}, bf16...) custom-call(s32[2]{0:T(128)} %pad_add_fusion.me_ref, ...), custom_call_target="tpu_custom_call" | custom-call | flops 4294967296 | bytes 20455424 | tf_op jit(solution)/shard_map/pallas_call | solution.py:55
  645.5 11.6 %collective-permute-done.83 = bf16[1408,128]{1,0:T(8,128)(2,1)} collective-permute-done((bf16[1408,128]{1,0:T(8,128)(2,1)}, bf16[1408,128]{1,0:T(8,128)(2,1)}, u32[]{:S(2)}, u32[]{:S(2)}) %collective-permute-start.83) | collective-permute-done | bytes 360480 | tf_op jit(solution)/shard_map/ppermute | solution.py:796
  688.7 12.6 %collective-permute-done.86 = bf16[2,4,384,128]{3,2,1,0:T(8,128)(2,1)} collective-permute-done((bf16[2,4,384,128]{3,2,1,0:T(8,128)(2,1)}, bf16[2,4,384,128]{3,2,1,0:T(8,128)(2,1)}, u32[]{:S(2)}, u32[]{:S(2)}) %collective-permute-start.86) | collective-permute-done | bytes 786464 | tf_op jit(solution)/shard_map/ppermute | solution.py:796
  (531 shorter events, 378.1 us)
Async XLA Ops:
  80.9 36.5 %all-to-all-start = ((bf16[8,64,1024]{2,1,0:T(8,128)(2,1)}), bf16[8,64,1024]{2,1,0:T(8,128)(2,1)S(1)}, u32[]{:S(2)}, u32[]{:S(2)}) async-start(bf16[8,64,1024]{2,1,0:T(8,128)(2,1)} %bitcast.401), calls=%async_computation | async-start | bytes 2097152 | tf_op jit(solution)/shard_map/all_to_all | solution.py:953
  84.6 198.6 %all-gather.3.cloned.1.call-start = ((), (), s32[]{:S(2)}) async-start(), calls=%async_computation.12 | async-start | bytes 3604480 | tf_op jit(solution)/shard_map/all_gather | solution.py:807
  113.0 41.7 %collective-permute-start.21 = (bf16[2,4,704,128]{3,2,1,0:T(8,128)(2,1)}, bf16[2,4,704,128]{3,2,1,0:T(8,128)(2,1)}, u32[]{:S(2)}, u32[]{:S(2)}) collective-permute-start(bf16[2,4,704,128]{3,2,1,0:T(8,128)(2,1)} %pad_maximum_fusion.2.refs_5_.refs_9_), channel_id=1, source_target_pairs={{0,2},{1,3},{2,0},{3,1},{4,6},{5,7},{6,4},{7,5},{8,10},{9,11},{10,... | collective-permute-start | bytes 4325384 | tf_op jit(solution)/shard_map/ppermute | solution.py:796
  116.7 48.3 %collective-permute-start.20 = (bf16[2,4,704,128]{3,2,1,0:T(8,128)(2,1)}, bf16[2,4,704,128]{3,2,1,0:T(8,128)(2,1)}, u32[]{:S(2)}, u32[]{:S(2)}) collective-permute-start(bf16[2,4,704,128]{3,2,1,0:T(8,128)(2,1)} %pad_maximum_fusion.1.refs_1_.refs_5_), channel_id=1, source_target_pairs={{0,4},{1,5},{2,6},{3,7},{4,0},{5,1},{6,2},{7,3},{8,12},{9,13},{10,... | collective-permute-start | bytes 4325384 | tf_op jit(solution)/shard_map/ppermute | solution.py:796
  140.9 47.1 %collective-permute-start.32 = (bf16[2,4,704,128]{3,2,1,0:T(8,128)(2,1)}, bf16[2,4,704,128]{3,2,1,0:T(8,128)(2,1)S(1)}, u32[]{:S(2)}, u32[]{:S(2)}) collective-permute-start(bf16[2,4,704,128]{3,2,1,0:T(8,128)(2,1)} %pad_maximum_fusion.2.refs_5_.refs_9_), channel_id=1, source_target_pairs={{0,1},{1,0},{2,3},{3,2},{4,5},{5,4},{6,7},{7,6},{8,9},{9,8},{10,11... | collective-permute-start | bytes 4325384 | tf_op jit(solution)/shard_map/ppermute | solution.py:796
  208.4 33.3 %collective-permute-start.38 = (bf16[4,2816,128]{2,1,0:T(8,128)(2,1)S(1)}, bf16[4,2816,128]{2,1,0:T(8,128)(2,1)}, u32[]{:S(2)}, u32[]{:S(2)}) collective-permute-start(bf16[4,2816,128]{2,1,0:T(8,128)(2,1)S(1)} %bitcast.398), channel_id=1, source_target_pairs={{0,1},{1,0},{2,3},{3,2},{4,5},{5,4},{6,7},{7,6},{8,9},{9,8},{10,11... | collective-permute-start | bytes 8650760 | tf_op jit(solution)/shard_map/ppermute | solution.py:796
  275.8 35.1 %collective-permute-start.53 = (bf16[2,4,704,128]{3,2,1,0:T(8,128)(2,1)}, bf16[2,4,704,128]{3,2,1,0:T(8,128)(2,1)}, u32[]{:S(2)}, u32[]{:S(2)}) collective-permute-start(bf16[2,4,704,128]{3,2,1,0:T(8,128)(2,1)} %pad_maximum_fusion.5.refs_5_.refs_9_), channel_id=1, source_target_pairs={{0,2},{1,3},{2,0},{3,1},{4,6},{5,7},{6,4},{7,5},{8,10},{9,11},{10,... | collective-permute-start | bytes 4325384 | tf_op jit(solution)/shard_map/ppermute | solution.py:796
  277.4 41.9 %collective-permute-start.50 = (bf16[2,4,704,128]{3,2,1,0:T(8,128)(2,1)S(1)}, bf16[2,4,704,128]{3,2,1,0:T(8,128)(2,1)}, u32[]{:S(2)}, u32[]{:S(2)}) collective-permute-start(bf16[2,4,704,128]{3,2,1,0:T(8,128)(2,1)S(1)} %pad_maximum_fusion.4.refs_1_.refs_5_), channel_id=1, source_target_pairs={{0,4},{1,5},{2,6},{3,7},{4,0},{5,1},{6,2},{7,3},{8,12},{9,13},{10,... | collective-permute-start | bytes 4325384 | tf_op jit(solution)/shard_map/ppermute | solution.py:796
  283.2 53.7 %collective-permute-start.56 = (bf16[4,2816,128]{2,1,0:T(8,128)(2,1)}, bf16[4,2816,128]{2,1,0:T(8,128)(2,1)}, u32[]{:S(2)}, u32[]{:S(2)}) collective-permute-start(bf16[4,2816,128]{2,1,0:T(8,128)(2,1)} %bitcast.403), channel_id=1, source_target_pairs={{0,1},{1,0},{2,3},{3,2},{4,5},{5,4},{6,7},{7,6},{8,9},{9,8},{10,11... | collective-permute-start | bytes 8650760 | tf_op jit(solution)/shard_map/ppermute | solution.py:796
  285.9 34.6 %all-to-all-start.1 = ((bf16[8,64,1024]{2,1,0:T(8,128)(2,1)}), bf16[8,64,1024]{2,1,0:T(8,128)(2,1)S(1)}, u32[]{:S(2)}, u32[]{:S(2)}) async-start(bf16[8,64,1024]{2,1,0:T(8,128)(2,1)} %bitcast.92), calls=%async_computation.1 | async-start | bytes 2097152 | tf_op jit(solution)/shard_map/all_to_all | solution.py:953
  290.2 172.3 %reduce-scatter.5.cloned.1.call-start = ((), (), s32[]{:S(2)}) async-start(), calls=%async_computation.8 | async-start | bytes 3604480 | tf_op jit(solution)/shard_map/reduce_scatter | solution.py:823
  291.1 32.2 %collective-permute-start.54 = (bf16[2,4,704,128]{3,2,1,0:T(8,128)(2,1)}, bf16[2,4,704,128]{3,2,1,0:T(8,128)(2,1)}, u32[]{:S(2)}, u32[]{:S(2)}) collective-permute-start(bf16[2,4,704,128]{3,2,1,0:T(8,128)(2,1)} %pad_maximum_fusion.5.refs_5_.refs_9_), channel_id=1, source_target_pairs={{0,1},{1,0},{2,3},{3,2},{4,5},{5,4},{6,7},{7,6},{8,9},{9,8},{10,11... | collective-permute-start | bytes 4325384 | tf_op jit(solution)/shard_map/ppermute | solution.py:796
  385.4 75.7 %all-to-all-start.2 = ((bf16[8,64,1024]{2,1,0:T(8,128)(2,1)}), bf16[8,64,1024]{2,1,0:T(8,128)(2,1)S(1)}, u32[]{:S(2)}, u32[]{:S(2)}) async-start(bf16[8,64,1024]{2,1,0:T(8,128)(2,1)} %bitcast.100), calls=%async_computation.3 | async-start | bytes 2097152 | tf_op jit(solution)/shard_map/all_to_all | solution.py:953
  393.9 225.7 %reduce-scatter.7.cloned.1.call-start = ((), (), s32[]{:S(2)}) async-start(), calls=%async_computation.9 | async-start | bytes 1802240 | tf_op jit(solution)/shard_map/reduce_scatter | solution.py:823
  415.7 45.4 %collective-permute-start.61 = (bf16[2,4,704,128]{3,2,1,0:T(8,128)(2,1)}, bf16[2,4,704,128]{3,2,1,0:T(8,128)(2,1)}, u32[]{:S(2)}, u32[]{:S(2)}) collective-permute-start(bf16[2,4,704,128]{3,2,1,0:T(8,128)(2,1)} %get-tuple-element.469), channel_id=1, source_target_pairs={{0,4},{1,5},{2,6},{3,7},{4,0},{5,1},{6,2},{7,3},{8,12},{9,13},{10,... | collective-permute-start | bytes 4325384 | tf_op jit(solution)/shard_map/ppermute | solution.py:796
  421.5 39.6 %collective-permute-start.60 = (bf16[2,4,704,128]{3,2,1,0:T(8,128)(2,1)}, bf16[2,4,704,128]{3,2,1,0:T(8,128)(2,1)}, u32[]{:S(2)}, u32[]{:S(2)}) collective-permute-start(bf16[2,4,704,128]{3,2,1,0:T(8,128)(2,1)} %get-tuple-element.471), channel_id=1, source_target_pairs={{0,2},{1,3},{2,0},{3,1},{4,6},{5,7},{6,4},{7,5},{8,10},{9,11},{10,... | collective-permute-start | bytes 4325384 | tf_op jit(solution)/shard_map/ppermute | solution.py:796
  485.9 35.1 %collective-permute-start.68 = (bf16[4,2816,128]{2,1,0:T(8,128)(2,1)}, bf16[4,2816,128]{2,1,0:T(8,128)(2,1)}, u32[]{:S(2)}, u32[]{:S(2)}) collective-permute-start(bf16[4,2816,128]{2,1,0:T(8,128)(2,1)} %get-tuple-element.339), channel_id=1, source_target_pairs={{0,1},{1,0},{2,3},{3,2},{4,5},{5,4},{6,7},{7,6},{8,9},{9,8},{10,11... | collective-permute-start | bytes 8650760 | tf_op jit(solution)/shard_map/ppermute | solution.py:796
  490.0 129.7 %reduce-scatter.9.cloned.1.call-start = ((), (), s32[]{:S(2)}) async-start(), calls=%async_computation.10 | async-start | bytes 3604480 | tf_op jit(solution)/shard_map/reduce_scatter | solution.py:823
  525.7 133.8 %reduce-scatter.11.cloned.1.call-start = ((), (), s32[]{:S(2)}) async-start(), calls=%async_computation.11 | async-start | bytes 1310720 | tf_op jit(solution)/shard_map/reduce_scatter | solution.py:823
  553.8 33.3 %collective-permute-start.74 = (bf16[2,4,704,128]{3,2,1,0:T(8,128)(2,1)}, bf16[2,4,704,128]{3,2,1,0:T(8,128)(2,1)}, u32[]{:S(2)}, u32[]{:S(2)}) collective-permute-start(bf16[2,4,704,128]{3,2,1,0:T(8,128)(2,1)} %get-tuple-element.465), channel_id=1, source_target_pairs={{0,4},{1,5},{2,6},{3,7},{4,0},{5,1},{6,2},{7,3},{8,12},{9,13},{10,... | collective-permute-start | bytes 4325384 | tf_op jit(solution)/shard_map/ppermute | solution.py:796
  558.7 32.9 %collective-permute-start.73 = (bf16[2,4,704,128]{3,2,1,0:T(8,128)(2,1)}, bf16[2,4,704,128]{3,2,1,0:T(8,128)(2,1)}, u32[]{:S(2)}, u32[]{:S(2)}) collective-permute-start(bf16[2,4,704,128]{3,2,1,0:T(8,128)(2,1)} %get-tuple-element.467), channel_id=1, source_target_pairs={{0,2},{1,3},{2,0},{3,1},{4,6},{5,7},{6,4},{7,5},{8,10},{9,11},{10,... | collective-permute-start | bytes 4325384 | tf_op jit(solution)/shard_map/ppermute | solution.py:796
  619.7 45.8 %collective-permute-start.78 = (bf16[2,2,4,384,128]{4,3,2,1,0:T(8,128)(2,1)}, bf16[2,2,4,384,128]{4,3,2,1,0:T(8,128)(2,1)}, u32[]{:S(2)}, u32[]{:S(2)}) collective-permute-start(bf16[2,2,4,384,128]{4,3,2,1,0:T(8,128)(2,1)} %get-tuple-element.374), channel_id=1, source_target_pairs={{0,1},{1,0},{2,3},{3,2},{4,5},{5,4},{6,7},{7,6},{8,9},{9,8},{10,11... | collective-permute-start | bytes 4718600 | tf_op jit(solution)/shard_map/ppermute | solution.py:796
  619.8 45.7 %collective-permute-start.77 = (bf16[2,2,4,256,128]{4,3,2,1,0:T(8,128)(2,1)}, bf16[2,2,4,256,128]{4,3,2,1,0:T(8,128)(2,1)}, u32[]{:S(2)}, u32[]{:S(2)}) collective-permute-start(bf16[2,2,4,256,128]{4,3,2,1,0:T(8,128)(2,1)} %get-tuple-element.373), channel_id=1, source_target_pairs={{0,1},{1,0},{2,3},{3,2},{4,5},{5,4},{6,7},{7,6},{8,9},{9,8},{10,11... | collective-permute-start | bytes 3145736 | tf_op jit(solution)/shard_map/ppermute | solution.py:796
  678.4 36.5 %all-to-all-start.3 = ((bf16[8,64,1024]{2,1,0:T(8,128)(2,1)}), bf16[8,64,1024]{2,1,0:T(8,128)(2,1)S(1)}, u32[]{:S(2)}, u32[]{:S(2)}) async-start(bf16[8,64,1024]{2,1,0:T(8,128)(2,1)} %bitcast.144), calls=%async_computation.7 | async-start | bytes 2097152 | tf_op jit(solution)/shard_map/all_to_all | solution.py:953
  (157 other events, 2237.6 us)
Sparse Core Ops, SparseCore 0:
  23.8 2.9 sort.60.cloned.1.call-done
  221.1 62.0 all-gather.2
  385.0 77.4 reduce-scatter.4
  490.1 35.2 reduce-scatter.6
  527.6 55.8 reduce-scatter.8
  598.7 28.5 reduce-scatter.10
  (1 shorter events, 0.0 us)

commit v7 on v6

--- a/solution.py
+++ b/solution.py
@@ -982,7 +982,6 @@
         lo_gu1 = ring.gather_lo(each(split(1, near_gu1), *far(hi_a1)))
         outgoing = after(outgoing, near_gu1, *far(hi_a1))
         arrived = exchange(outgoing, rows)
-        near_d1 = ring.gather_z(after(flat[2], arrived))
         start = arrived[placing]
     else:
         me = jnp.zeros((2,), i32)
@@ -1005,7 +1004,9 @@
         full_a1 = full[0]
     w_qk, w_v, w_o = attn_weights(full_a1, HALVES_ONE)
     xa1, qk1, v1 = norm_proj(me, start, gain_a1, [w_qk, w_v])
-    o1, ou1, rden1 = based_fwd(qk1, v1, seg_row, seg_col, live_row)
+    if ring:
+        near_d1 = ring.gather_z(after(flat[2], arrived), qk1)
+    o1, ou1, rden1 = based_fwd(tied(qk1, *([near_d1] if ring else [])), v1, seg_row, seg_col, live_row)
     if ring:
         hi_gu1 = ring.gather_hi(lo_gu1, o1)
         near_a2 = ring.gather_z(after(flat[3], near_d1), o1)
@@ -1112,8 +1113,9 @@
         keep_d1, go = far_rows(jnp.stack([z_d1, z_d2]))
         r_d1 = ring.send(go, ("y", "x"))
         r_z = ring.send_back(gu1)
+        r_a1, r_gains, r_d1, g0 = sync(r_a1, r_gains, r_d1, g0)
         outgoing = g0.astype(bf16)[local_slots]
-        r_a1, r_gains, r_d1, r_z, outgoing, z_a2 = sync(r_a1, r_gains, r_d1, r_z, outgoing, z_a2)
+        r_z, outgoing, z_a2 = sync(r_z, outgoing, z_a2)
         arrived = exchange(outgoing, rows)
         keep_a1, go = add_core(a1, r_a1)
         r_a1 = ring.send(go, ("x", "y"))

time: 750 us -> 738 us (0.984)
  waiting for transfers between devices: 178 us -> 150 us
  starting transfers between devices: 119 us -> 133 us
    ppermute x99, waiting for transfers between devices: 170 us -> 143 us  [swap(): lax.ppermute(value, self.axes, [(i, i ^ by << shift) for i in range(32)])]
    all_to_all x4, starting transfers between devices: 20.2 us -> 28.8 us  [exchange(): lax.all_to_all(value.reshape(row_count, n // row_count, width), axis, spl...]
    unnamed x160 -> x164, local copies, waits for them, and re-layouts: 15.2 us -> 14.9 us
  transfers between devices with their start and end apart: 108 -> 108, of which waited for: 35 -> 32; matrix products, arithmetic and copies ran while one was open for 17% -> 18% of each run, Pallas kernels for 35% -> 36%
where the time goes in v7:
time: 738 us; the launch traced here: 730 us
  Pallas kernels  277 us (38%)
  waiting for transfers between devices  150 us (20%)
  starting transfers between devices  133 us (18%)
  other arithmetic  101 us (14%)
  local copies, waits for them, and re-layouts  50.6 us (7%)
  between operations  18.5 us (3%)
    pallas_call x20, Pallas kernels, call(): pl.pallas_call(body, out_shape=out_shape, grid_spec=pltpu.PrefetchScalarG...  277 us
    ppermute x99, waiting for transfers between devices, swap(): lax.ppermute(value, self.axes, [(i, i ^ by << shift) for i in range(32)])  143 us
    ppermute x99, starting transfers between devices, swap(): lax.ppermute(value, self.axes, [(i, i ^ by << shift) for i in range(32)])  104 us
    all_to_all x4, starting transfers between devices, exchange(): lax.all_to_all(value.reshape(row_count, n // row_count, width), axis, spl...  28.8 us
    add x6, other arithmetic, add_core(): keep = [four[0][0] + got[0][0], four[2][0] + got[1][0]]  20 us
    unnamed x164, local copies, waits for them, and re-layouts  14.9 us
  transfers between devices with their start and end apart: 108, of which 32 were waited for; matrix products, arithmetic and copies ran while one was open for 18% of the time, Pallas kernels for 36%

profile of v7, /device:TPU:0, one launch (start us, length us, event | category | flops | bytes accessed | tf_op | source)
XLA Modules:
  0.0 729.9 jit_solution(3187898350402147691)
XLA Ops:
  58.3 18.0 %collective-permute-done.4 = bf16[1408,128]{1,0:T(8,128)(2,1)S(1)} collective-permute-done((bf16[1408,128]{1,0:T(8,128)(2,1)S(1)}, bf16[1408,128]{1,0:T(8,128)(2,1)S(1)}, u32[]{:S(2)}, u32[]{:S(2)}) %collective-permute-start.4) | collective-permute-done | bytes 360480 | tf_op jit(solution)/shard_map/ppermute | solution.py:796
  94.3 17.1 %collective-permute-done.15 = bf16[4,704,128]{2,1,0:T(8,128)(2,1)} collective-permute-done((bf16[4,704,128]{2,1,0:T(8,128)(2,1)}, bf16[4,704,128]{2,1,0:T(8,128)(2,1)}, u32[]{:S(2)}, u32[]{:S(2)}) %collective-permute-start.15) | collective-permute-done | bytes 720928 | tf_op jit(solution)/shard_map/ppermute | solution.py:796
  125.8 10.3 %shard_map.374 = (bf16[512,1024]{1,0:T(8,128)(2,1)}, bf16[512,512]{1,0:T(8,128)(2,1)}, bf16[512,1024]{1,0:T(8,128)(2,1)}) custom-call(s32[2]{0:T(128)} %pad_add_fusion.me_ref, bf16[512,1024]{1,0:T(8,128)(2,1)} %gather_fusion.1, f32[1,1024]{1,0:T(1,128)} %bitcast.463, bf16[2,4,384,128]{3,2,1,0:T(8,128)(2,1)} %copy-done.6, ...), custom_call_target="tpu_custom_call" | custom-call | flops 1610612736 | bytes 8916992 | tf_op jit(solution)/shard_map/pallas_call | solution.py:55
  151.7 8.8 %shard_map.375 = (bf16[512,1024]{1,0:T(8,128)(2,1)}, f32[512,1024]{1,0:T(8,128)}, f32[512,1024]{1,0:T(8,128)}) custom-call(bf16[512,512]{1,0:T(8,128)(2,1)} %get-tuple-element.233.qk_ref, bf16[512,1024]{1,0:T(8,128)(2,1)} %get-tuple-element.234.v_ref, s32[1,512]{1,0:T(1,128)} %fusion.71.sr_ref, s32[512,1]{1,0:T(8,128)} %convert_add_fusion.2.sc_ref, ...), custom_call_target="tpu_custom_call" | custom-call | flops 1610612736 | bytes 6821888 | tf_op jit(solution)/shard_map/pallas_call | solution.py:55
  162.8 9.2 %collective-permute-done.28 = bf16[4,352,128]{2,1,0:T(8,128)(2,1)S(1)} collective-permute-done((bf16[4,352,128]{2,1,0:T(8,128)(2,1)S(1)}, bf16[4,352,128]{2,1,0:T(8,128)(2,1)S(1)}, u32[]{:S(2)}, u32[]{:S(2)}) %collective-permute-start.28) | collective-permute-done | bytes 360480 | tf_op jit(solution)/shard_map/ppermute | solution.py:796
  190.3 13.6 %shard_map.377 = (bf16[2816,512]{1,0:T(8,128)(2,1)}, bf16[2816,512]{1,0:T(8,128)(2,1)}, bf16[2816,512]{1,0:T(8,128)(2,1)}) custom-call(s32[2]{0:T(128)} %pad_add_fusion.me_ref, bf16[512,1024]{1,0:T(8,128)(2,1)} %get-tuple-element.249.refs_0_.xf_ref, bf16[2,4,704,128]{3,2,1,0:T(8,128)(2,1)} %pad_maximum_fusion.1.refs_1_.refs_5_, ...), custom_call_target="tpu_custom_call" | custom-call | flops 5905580032 | bytes 21233664 | tf_op jit(solution)/shard_map/pallas_call | solution.py:55
  204.9 10.0 %collective-permute-done.46 = bf16[1408,128]{1,0:T(8,128)(2,1)S(1)} collective-permute-done((bf16[1408,128]{1,0:T(8,128)(2,1)S(1)}, bf16[1408,128]{1,0:T(8,128)(2,1)S(1)}, u32[]{:S(2)}, u32[]{:S(2)}) %collective-permute-start.46) | collective-permute-done | bytes 360480 | tf_op jit(solution)/shard_map/ppermute | solution.py:796
  236.1 10.7 %shard_map.378.refs_0_.refs_2_ = f32[512,1024]{1,0:T(8,128)} custom-call(s32[2]{0:T(128)} %pad_add_fusion.me_ref, f32[512,1024]{1,0:T(8,128)} %get-tuple-element.243.refs_0_.refs_2_, bf16[2816,512]{1,0:T(8,128)(2,1)} %get-tuple-element.259.refs_1_, bf16[4,2816,128]{2,1,0:T(8,128)(2,1)} %bitcast.399, bf16[4,2816,128]{2,1,0:T(8,128)(2,1)} %collective-permute-done.38.refs_3_.refs_5_), custom_call_target="tpu_custom_call" | custom-call | flops 2952790016 | bytes 12845056 | tf_op jit(solution)/shard_map/pallas_call | solution.py:55
  257.9 12.5 %shard_map.379 = (bf16[512,1024]{1,0:T(8,128)(2,1)}, bf16[512,1024]{1,0:T(8,128)(2,1)}, bf16[512,1024]{1,0:T(8,128)(2,1)}, bf16[512,1024]{1,0:T(8,128)(2,1)}) custom-call(s32[2]{0:T(128)} %pad_add_fusion.me_ref, f32[512,1024]{1,0:T(8,128)} %shard_map.378.refs_0_.refs_2_, f32[1,1024]{1,0:T(1,128)} %bitcast.455, bf16[2,4,512,128]{3,2,1,0:T(8,128)(2,1)} %copy-done.5, ...), custom_call_target="tpu_custom_call" | custom-call | flops 3221225472 | bytes 18878464 | tf_op jit(solution)/shard_map/pallas_call | solution.py:55
  290.3 11.7 %shard_map.380.refs_1_ = bf16[512,1024]{1,0:T(8,128)(2,1)} custom-call(bf16[512,1024]{1,0:T(8,128)(2,1)} %get-tuple-element.274.q_ref, bf16[512,1024]{1,0:T(8,128)(2,1)} %get-tuple-element.275.k_ref, bf16[512,1024]{1,0:T(8,128)(2,1)} %get-tuple-element.276.v_ref, s32[1,512]{1,0:T(1,128)} %fusion.71.sr_ref, s32[512,1]{1,0:T(8,128)} %convert_add_fusion.2.sc_ref, ...), custom_call_target="tpu_custom_call" | custom-call | flops 1610612736 | bytes 4200448 | tf_op jit(solution)/shard_map/pallas_call | solution.py:55
  320.4 13.6 %shard_map.382 = (bf16[2816,512]{1,0:T(8,128)(2,1)}, bf16[2816,512]{1,0:T(8,128)(2,1)}, bf16[2816,512]{1,0:T(8,128)(2,1)}) custom-call(s32[2]{0:T(128)} %pad_add_fusion.me_ref, bf16[512,1024]{1,0:T(8,128)(2,1)} %get-tuple-element.278.refs_0_.xf_ref, bf16[2,4,704,128]{3,2,1,0:T(8,128)(2,1)} %copy-done.36, ...), custom_call_target="tpu_custom_call" | custom-call | flops 5905580032 | bytes 21233664 | tf_op jit(solution)/shard_map/pallas_call | solution.py:55
  334.0 14.5 %shard_map.383 = (bf16[2816,512]{1,0:T(8,128)(2,1)}, bf16[2816,512]{1,0:T(8,128)(2,1)}, bf16[4,2816,128]{2,1,0:T(8,128)(2,1)}, bf16[4,2816,128]{2,1,0:T(8,128)(2,1)}) custom-call(s32[2]{0:T(128)} %pad_add_fusion.me_ref, bf16[512,1024]{1,0:T(8,128)(2,1)} %gather_fusion.3, bf16[2816,512]{1,0:T(8,128)(2,1)} %get-tuple-element.281.refs_1_, ...), custom_call_target="tpu_custom_call" | custom-call | flops 5905580032 | bytes 27000832 | tf_op jit(solution)/shard_map/pallas_call | solution.py:55
  348.6 10.2 %shard_map.385 = f32[512,1024]{1,0:T(8,128)} custom-call(s32[2]{0:T(128)} %pad_add_fusion.me_ref, f32[512,1024]{1,0:T(8,128)} %get-tuple-element.293.refs_0_.refs_2_, bf16[2816,512]{1,0:T(8,128)(2,1)} %get-tuple-element.281.refs_1_, bf16[4,2816,128]{2,1,0:T(8,128)(2,1)} %bitcast.405, bf16[4,2816,128]{2,1,0:T(8,128)(2,1)} %collective-permute-done.56.refs_5_.refs_3_), custom_call_target="tpu_custom_call" | custom-call | flops 2952790016 | bytes 12845056 | tf_op jit(solution)/shard_map/pallas_call | solution.py:55
  363.4 14.2 %shard_map.384 = (bf16[2,2,4,704,128]{4,3,2,1,0:T(8,128)(2,1)}, bf16[2,2,4,704,128]{4,3,2,1,0:T(8,128)(2,1)}, bf16[2,2,4,704,128]{4,3,2,1,0:T(8,128)(2,1)}, bf16[2,2,4,704,128]{4,3,2,1,0:T(8,128)(2,1)}) custom-call(s32[2]{0:T(128)} %pad_add_fusion.me_ref, bf16[512,1024]{1,0:T(8,128)(2,1)} %get-tuple-element.278.refs_0_.xf_ref, ...), custom_call_target="tpu_custom_call" | custom-call | flops 5905580032 | bytes 18350080 | tf_op jit(solution)/shard_map/pallas_call | solution.py:55
  382.3 10.3 %all-to-all-start.2 = ((bf16[8,64,1024]{2,1,0:T(8,128)(2,1)}), bf16[8,64,1024]{2,1,0:T(8,128)(2,1)S(1)}, u32[]{:S(2)}, u32[]{:S(2)}) async-start(bf16[8,64,1024]{2,1,0:T(8,128)(2,1)} %bitcast.100), calls=%async_computation.3 | async-start | bytes 2097152 | tf_op jit(solution)/shard_map/all_to_all | solution.py:953
  392.7 18.4 %shard_map.386 = (f32[512,1024]{1,0:T(8,128)}, bf16[512,1024]{1,0:T(8,128)(2,1)}, bf16[512,1024]{1,0:T(8,128)(2,1)}, f32[1,1024]{1,0:T(1,128)}) custom-call(s32[2]{0:T(128)} %pad_add_fusion.me_ref, bf16[2816,512]{1,0:T(8,128)(2,1)} %get-tuple-element.294.dg_ref.refs_0_, bf16[2816,512]{1,0:T(8,128)(2,1)} %get-tuple-element.295.du_ref.refs_1_, ...), custom_call_target="tpu_custom_call" | custom-call | flops 6979321856 | bytes 28844032 | tf_op jit(solution)/shard_map/pallas_call | solution.py:55
  421.2 18.7 %shard_map.387 = (bf16[512,1024]{1,0:T(8,128)(2,1)}, bf16[512,1024]{1,0:T(8,128)(2,1)}, bf16[512,1024]{1,0:T(8,128)(2,1)}) custom-call(bf16[512,1024]{1,0:T(8,128)(2,1)} %get-tuple-element.274.q_ref, bf16[512,1024]{1,0:T(8,128)(2,1)} %get-tuple-element.275.k_ref, bf16[512,1024]{1,0:T(8,128)(2,1)} %get-tuple-element.276.v_ref, ...), custom_call_target="tpu_custom_call" | custom-call | flops 4026531840 | bytes 7346176 | tf_op jit(solution)/shard_map/pallas_call | solution.py:55
  439.9 20.2 %shard_map.388 = (bf16[2,2,4,512,128]{4,3,2,1,0:T(8,128)(2,1)}, bf16[2,2,4,512,128]{4,3,2,1,0:T(8,128)(2,1)}, bf16[2,2,4,512,128]{4,3,2,1,0:T(8,128)(2,1)}, bf16...) custom-call(s32[2]{0:T(128)} %pad_add_fusion.me_ref, ...), custom_call_target="tpu_custom_call" | custom-call | flops 7516192768 | bytes 33562624 | tf_op jit(solution)/shard_map/pallas_call | solution.py:55
  467.2 14.9 %shard_map.389 = (bf16[2816,512]{1,0:T(8,128)(2,1)}, bf16[2816,512]{1,0:T(8,128)(2,1)}, bf16[4,2816,128]{2,1,0:T(8,128)(2,1)}, bf16[4,2816,128]{2,1,0:T(8,128)(2,1)}) custom-call(s32[2]{0:T(128)} %pad_add_fusion.me_ref, f32[512,1024]{1,0:T(8,128)} %get-tuple-element.323.refs_0_.refs_4_, bf16[2816,512]{1,0:T(8,128)(2,1)} %get-tuple-element.259.refs_1_, ...), custom_call_target="tpu_custom_call" | custom-call | flops 5905580032 | bytes 28049408 | tf_op jit(solution)/shard_map/pallas_call | solution.py:55
  494.9 14.3 %shard_map.391 = (bf16[2,2,4,704,128]{4,3,2,1,0:T(8,128)(2,1)}, bf16[2,2,4,704,128]{4,3,2,1,0:T(8,128)(2,1)}, bf16[2,2,4,704,128]{4,3,2,1,0:T(8,128)(2,1)}, bf16[2,2,4,704,128]{4,3,2,1,0:T(8,128)(2,1)}) custom-call(s32[2]{0:T(128)} %pad_add_fusion.me_ref, bf16[512,1024]{1,0:T(8,128)(2,1)} %get-tuple-element.249.refs_0_.xf_ref, ...), custom_call_target="tpu_custom_call" | custom-call | flops 5905580032 | bytes 18350080 | tf_op jit(solution)/shard_map/pallas_call | solution.py:55
  529.1 19.3 %shard_map.390 = (f32[512,1024]{1,0:T(8,128)}, bf16[512,1024]{1,0:T(8,128)(2,1)}, f32[512,1024]{1,0:T(8,128)}, f32[1,1024]{1,0:T(1,128)}) custom-call(s32[2]{0:T(128)} %pad_add_fusion.me_ref, bf16[2816,512]{1,0:T(8,128)(2,1)} %get-tuple-element.334.refs_0_.dg_ref, bf16[2816,512]{1,0:T(8,128)(2,1)} %get-tuple-element.335.refs_1_.du_ref, ...), custom_call_target="tpu_custom_call" | custom-call | flops 6979321856 | bytes 29892608 | tf_op jit(solution)/shard_map/pallas_call | solution.py:55
  562.8 15.9 %shard_map.392 = (bf16[512,512]{1,0:T(8,128)(2,1)}, bf16[512,1024]{1,0:T(8,128)(2,1)}) custom-call(bf16[512,512]{1,0:T(8,128)(2,1)} %get-tuple-element.233.qk_ref, bf16[512,1024]{1,0:T(8,128)(2,1)} %get-tuple-element.234.v_ref, f32[512,1024]{1,0:T(8,128)} %get-tuple-element.355.dou_ref, f32[512,1024]{1,0:T(8,128)} %get-tuple-element.356.ou_ref, ...), custom_call_target="tpu_custom_call" | custom-call | flops 4026531840 | bytes 9443328 | tf_op jit(solution)/shard_map/pallas_call | solution.py:55
  598.9 20.4 %shard_map.393 = (bf16[2,2,4,256,128]{4,3,2,1,0:T(8,128)(2,1)}, bf16[2,2,4,256,128]{4,3,2,1,0:T(8,128)(2,1)}, bf16[2,2,4,384,128]{4,3,2,1,0:T(8,128)(2,1)}, bf16...) custom-call(s32[2]{0:T(128)} %pad_add_fusion.me_ref, ...), custom_call_target="tpu_custom_call" | custom-call | flops 4294967296 | bytes 20455424 | tf_op jit(solution)/shard_map/pallas_call | solution.py:55
  652.7 9.6 %collective-permute-done.91 = bf16[1408,128]{1,0:T(8,128)(2,1)} collective-permute-done((bf16[1408,128]{1,0:T(8,128)(2,1)}, bf16[1408,128]{1,0:T(8,128)(2,1)}, u32[]{:S(2)}, u32[]{:S(2)}) %collective-permute-start.91) | collective-permute-done | bytes 360480 | tf_op jit(solution)/shard_map/ppermute | solution.py:796
  (535 shorter events, 375.4 us)
Async XLA Ops:
  79.4 39.0 %all-to-all-start = ((bf16[8,64,1024]{2,1,0:T(8,128)(2,1)}), bf16[8,64,1024]{2,1,0:T(8,128)(2,1)S(1)}, u32[]{:S(2)}, u32[]{:S(2)}) async-start(bf16[8,64,1024]{2,1,0:T(8,128)(2,1)} %bitcast.401), calls=%async_computation | async-start | bytes 2097152 | tf_op jit(solution)/shard_map/all_to_all | solution.py:953
  83.0 196.5 %all-gather.3.cloned.1.call-start = ((), (), s32[]{:S(2)}) async-start(), calls=%async_computation.12 | async-start | bytes 3604480 | tf_op jit(solution)/shard_map/all_gather | solution.py:807
  114.0 34.3 %collective-permute-start.24 = (bf16[2,4,704,128]{3,2,1,0:T(8,128)(2,1)}, bf16[2,4,704,128]{3,2,1,0:T(8,128)(2,1)}, u32[]{:S(2)}, u32[]{:S(2)}) collective-permute-start(bf16[2,4,704,128]{3,2,1,0:T(8,128)(2,1)} %pad_maximum_fusion.2.refs_5_.refs_9_), channel_id=1, source_target_pairs={{0,2},{1,3},{2,0},{3,1},{4,6},{5,7},{6,4},{7,5},{8,10},{9,11},{10,... | collective-permute-start | bytes 4325384 | tf_op jit(solution)/shard_map/ppermute | solution.py:796
  116.8 43.7 %collective-permute-start.23 = (bf16[2,4,704,128]{3,2,1,0:T(8,128)(2,1)}, bf16[2,4,704,128]{3,2,1,0:T(8,128)(2,1)}, u32[]{:S(2)}, u32[]{:S(2)}) collective-permute-start(bf16[2,4,704,128]{3,2,1,0:T(8,128)(2,1)} %pad_maximum_fusion.1.refs_1_.refs_5_), channel_id=1, source_target_pairs={{0,4},{1,5},{2,6},{3,7},{4,0},{5,1},{6,2},{7,3},{8,12},{9,13},{10,... | collective-permute-start | bytes 4325384 | tf_op jit(solution)/shard_map/ppermute | solution.py:796
  136.1 46.6 %collective-permute-start.32 = (bf16[2,4,704,128]{3,2,1,0:T(8,128)(2,1)}, bf16[2,4,704,128]{3,2,1,0:T(8,128)(2,1)S(1)}, u32[]{:S(2)}, u32[]{:S(2)}) collective-permute-start(bf16[2,4,704,128]{3,2,1,0:T(8,128)(2,1)} %pad_maximum_fusion.2.refs_5_.refs_9_), channel_id=1, source_target_pairs={{0,1},{1,0},{2,3},{3,2},{4,5},{5,4},{6,7},{7,6},{8,9},{9,8},{10,11... | collective-permute-start | bytes 4325384 | tf_op jit(solution)/shard_map/ppermute | solution.py:796
  204.8 31.3 %collective-permute-start.38 = (bf16[4,2816,128]{2,1,0:T(8,128)(2,1)S(1)}, bf16[4,2816,128]{2,1,0:T(8,128)(2,1)}, u32[]{:S(2)}, u32[]{:S(2)}) collective-permute-start(bf16[4,2816,128]{2,1,0:T(8,128)(2,1)S(1)} %bitcast.398), channel_id=1, source_target_pairs={{0,1},{1,0},{2,3},{3,2},{4,5},{5,4},{6,7},{7,6},{8,9},{9,8},{10,11... | collective-permute-start | bytes 8650760 | tf_op jit(solution)/shard_map/ppermute | solution.py:796
  273.0 36.5 %collective-permute-start.53 = (bf16[2,4,704,128]{3,2,1,0:T(8,128)(2,1)}, bf16[2,4,704,128]{3,2,1,0:T(8,128)(2,1)}, u32[]{:S(2)}, u32[]{:S(2)}) collective-permute-start(bf16[2,4,704,128]{3,2,1,0:T(8,128)(2,1)} %pad_maximum_fusion.5.refs_5_.refs_9_), channel_id=1, source_target_pairs={{0,2},{1,3},{2,0},{3,1},{4,6},{5,7},{6,4},{7,5},{8,10},{9,11},{10,... | collective-permute-start | bytes 4325384 | tf_op jit(solution)/shard_map/ppermute | solution.py:796
  274.5 41.9 %collective-permute-start.50 = (bf16[2,4,704,128]{3,2,1,0:T(8,128)(2,1)S(1)}, bf16[2,4,704,128]{3,2,1,0:T(8,128)(2,1)}, u32[]{:S(2)}, u32[]{:S(2)}) collective-permute-start(bf16[2,4,704,128]{3,2,1,0:T(8,128)(2,1)S(1)} %pad_maximum_fusion.4.refs_1_.refs_5_), channel_id=1, source_target_pairs={{0,4},{1,5},{2,6},{3,7},{4,0},{5,1},{6,2},{7,3},{8,12},{9,13},{10,... | collective-permute-start | bytes 4325384 | tf_op jit(solution)/shard_map/ppermute | solution.py:796
  279.5 54.5 %collective-permute-start.56 = (bf16[4,2816,128]{2,1,0:T(8,128)(2,1)}, bf16[4,2816,128]{2,1,0:T(8,128)(2,1)}, u32[]{:S(2)}, u32[]{:S(2)}) collective-permute-start(bf16[4,2816,128]{2,1,0:T(8,128)(2,1)} %bitcast.403), channel_id=1, source_target_pairs={{0,1},{1,0},{2,3},{3,2},{4,5},{5,4},{6,7},{7,6},{8,9},{9,8},{10,11... | collective-permute-start | bytes 8650760 | tf_op jit(solution)/shard_map/ppermute | solution.py:796
  282.3 35.4 %all-to-all-start.1 = ((bf16[8,64,1024]{2,1,0:T(8,128)(2,1)}), bf16[8,64,1024]{2,1,0:T(8,128)(2,1)S(1)}, u32[]{:S(2)}, u32[]{:S(2)}) async-start(bf16[8,64,1024]{2,1,0:T(8,128)(2,1)} %bitcast.92), calls=%async_computation.1 | async-start | bytes 2097152 | tf_op jit(solution)/shard_map/all_to_all | solution.py:953
  288.9 172.4 %reduce-scatter.5.cloned.1.call-start = ((), (), s32[]{:S(2)}) async-start(), calls=%async_computation.8 | async-start | bytes 3604480 | tf_op jit(solution)/shard_map/reduce_scatter | solution.py:823
  289.8 30.6 %collective-permute-start.54 = (bf16[2,4,704,128]{3,2,1,0:T(8,128)(2,1)}, bf16[2,4,704,128]{3,2,1,0:T(8,128)(2,1)}, u32[]{:S(2)}, u32[]{:S(2)}) collective-permute-start(bf16[2,4,704,128]{3,2,1,0:T(8,128)(2,1)} %pad_maximum_fusion.5.refs_5_.refs_9_), channel_id=1, source_target_pairs={{0,1},{1,0},{2,3},{3,2},{4,5},{5,4},{6,7},{7,6},{8,9},{9,8},{10,11... | collective-permute-start | bytes 4325384 | tf_op jit(solution)/shard_map/ppermute | solution.py:796
  382.3 77.8 %all-to-all-start.2 = ((bf16[8,64,1024]{2,1,0:T(8,128)(2,1)}), bf16[8,64,1024]{2,1,0:T(8,128)(2,1)S(1)}, u32[]{:S(2)}, u32[]{:S(2)}) async-start(bf16[8,64,1024]{2,1,0:T(8,128)(2,1)} %bitcast.100), calls=%async_computation.3 | async-start | bytes 2097152 | tf_op jit(solution)/shard_map/all_to_all | solution.py:953
  392.6 227.5 %reduce-scatter.7.cloned.1.call-start = ((), (), s32[]{:S(2)}) async-start(), calls=%async_computation.9 | async-start | bytes 1802240 | tf_op jit(solution)/shard_map/reduce_scatter | solution.py:823
  414.4 45.7 %collective-permute-start.61 = (bf16[2,4,704,128]{3,2,1,0:T(8,128)(2,1)}, bf16[2,4,704,128]{3,2,1,0:T(8,128)(2,1)}, u32[]{:S(2)}, u32[]{:S(2)}) collective-permute-start(bf16[2,4,704,128]{3,2,1,0:T(8,128)(2,1)} %get-tuple-element.479), channel_id=1, source_target_pairs={{0,4},{1,5},{2,6},{3,7},{4,0},{5,1},{6,2},{7,3},{8,12},{9,13},{10,... | collective-permute-start | bytes 4325384 | tf_op jit(solution)/shard_map/ppermute | solution.py:796
  420.2 39.9 %collective-permute-start.60 = (bf16[2,4,704,128]{3,2,1,0:T(8,128)(2,1)}, bf16[2,4,704,128]{3,2,1,0:T(8,128)(2,1)}, u32[]{:S(2)}, u32[]{:S(2)}) collective-permute-start(bf16[2,4,704,128]{3,2,1,0:T(8,128)(2,1)} %get-tuple-element.481), channel_id=1, source_target_pairs={{0,2},{1,3},{2,0},{3,1},{4,6},{5,7},{6,4},{7,5},{8,10},{9,11},{10,... | collective-permute-start | bytes 4325384 | tf_op jit(solution)/shard_map/ppermute | solution.py:796
  485.0 35.1 %collective-permute-start.68 = (bf16[4,2816,128]{2,1,0:T(8,128)(2,1)}, bf16[4,2816,128]{2,1,0:T(8,128)(2,1)}, u32[]{:S(2)}, u32[]{:S(2)}) collective-permute-start(bf16[4,2816,128]{2,1,0:T(8,128)(2,1)} %get-tuple-element.348), channel_id=1, source_target_pairs={{0,1},{1,0},{2,3},{3,2},{4,5},{5,4},{6,7},{7,6},{8,9},{9,8},{10,11... | collective-permute-start | bytes 8650760 | tf_op jit(solution)/shard_map/ppermute | solution.py:796
  489.1 131.1 %reduce-scatter.9.cloned.1.call-start = ((), (), s32[]{:S(2)}) async-start(), calls=%async_computation.10 | async-start | bytes 3604480 | tf_op jit(solution)/shard_map/reduce_scatter | solution.py:823
  524.8 139.6 %reduce-scatter.11.cloned.1.call-start = ((), (), s32[]{:S(2)}) async-start(), calls=%async_computation.11 | async-start | bytes 1310720 | tf_op jit(solution)/shard_map/reduce_scatter | solution.py:823
  552.5 33.4 %collective-permute-start.74 = (bf16[2,4,704,128]{3,2,1,0:T(8,128)(2,1)}, bf16[2,4,704,128]{3,2,1,0:T(8,128)(2,1)}, u32[]{:S(2)}, u32[]{:S(2)}) collective-permute-start(bf16[2,4,704,128]{3,2,1,0:T(8,128)(2,1)} %get-tuple-element.475), channel_id=1, source_target_pairs={{0,4},{1,5},{2,6},{3,7},{4,0},{5,1},{6,2},{7,3},{8,12},{9,13},{10,... | collective-permute-start | bytes 4325384 | tf_op jit(solution)/shard_map/ppermute | solution.py:796
  557.0 32.9 %collective-permute-start.73 = (bf16[2,4,704,128]{3,2,1,0:T(8,128)(2,1)}, bf16[2,4,704,128]{3,2,1,0:T(8,128)(2,1)}, u32[]{:S(2)}, u32[]{:S(2)}) collective-permute-start(bf16[2,4,704,128]{3,2,1,0:T(8,128)(2,1)} %get-tuple-element.477), channel_id=1, source_target_pairs={{0,2},{1,3},{2,0},{3,1},{4,6},{5,7},{6,4},{7,5},{8,10},{9,11},{10,... | collective-permute-start | bytes 4325384 | tf_op jit(solution)/shard_map/ppermute | solution.py:796
  641.3 39.7 %collective-permute-start.85 = (bf16[2,352,128]{2,1,0:T(8,128)(2,1)}, bf16[2,352,128]{2,1,0:T(8,128)(2,1)}, u32[]{:S(2)}, u32[]{:S(2)}) collective-permute-start(bf16[2,352,128]{2,1,0:T(8,128)(2,1)} %split.38), channel_id=1, source_target_pairs={{0,2},{1,3},{2,0},{3,1},{4,6},{5,7},{6,4},{7,5},{8,10},{9,11},{10,... | collective-permute-start | bytes 540680 | tf_op jit(solution)/shard_map/ppermute | solution.py:796
  642.5 38.4 %collective-permute-start.86 = (bf16[2,352,128]{2,1,0:T(8,128)(2,1)}, bf16[2,352,128]{2,1,0:T(8,128)(2,1)}, u32[]{:S(2)}, u32[]{:S(2)}) collective-permute-start(bf16[2,352,128]{2,1,0:T(8,128)(2,1)} %split.39), channel_id=1, source_target_pairs={{0,4},{1,5},{2,6},{3,7},{4,0},{5,1},{6,2},{7,3},{8,12},{9,13},{10,... | collective-permute-start | bytes 540680 | tf_op jit(solution)/shard_map/ppermute | solution.py:796
  666.1 35.6 %all-to-all-start.3 = ((bf16[8,64,1024]{2,1,0:T(8,128)(2,1)}), bf16[8,64,1024]{2,1,0:T(8,128)(2,1)S(1)}, u32[]{:S(2)}, u32[]{:S(2)}) async-start(bf16[8,64,1024]{2,1,0:T(8,128)(2,1)} %bitcast.144), calls=%async_computation.7 | async-start | bytes 2097152 | tf_op jit(solution)/shard_map/all_to_all | solution.py:953
  (159 other events, 2298.7 us)
Sparse Core Ops, SparseCore 0:
  23.8 2.9 sort.60.cloned.1.call-done
  218.3 61.1 all-gather.2
  381.9 79.3 reduce-scatter.4
  489.2 35.0 reduce-scatter.6
  526.4 55.8 reduce-scatter.8
  599.0 28.2 reduce-scatter.10
  (1 shorter events, 0.0 us)
